TPU v7x, 512 devices: a whole 4x8x8 slice. The times are simulated.
512 devices in a mesh: grp: 8 (over x, core), dev: 64 (over y, z).
Axes of the slice: x: 4, y: 8, z: 8, core: 2. Of those that a mesh axis runs over, the one named last changes fastest.
Arguments:
- coords: float32 [262144, 64], P(('grp', 'dev')), may hold values from -6 to 6
- right_side: float32 [262144, 256], P(('grp', 'dev')), may hold values from -6 to 6
- leaf_perm: int32 [512, 512], P(('grp', 'dev')), may hold values from 0 to 511, each once within a row
- near_list: int32 [512, 4], P(('grp', 'dev')), may hold values from -1 to 511, as said below
- far_leaves: int32 [512, 4], P(('grp', 'dev')), may hold values from 0 to 511, as said below
- couplings: bfloat16 [512, 4, 128, 128], P(('grp', 'dev')), may hold values from -0.5 to 0.5
- transfer: bfloat16 [512, 128, 128], P(('grp', 'dev')), may hold values from -0.5 to 0.5
- leaf_basis: bfloat16 [262144, 128], P(('grp', 'dev')), may hold values from -0.25 to 0.25
- cluster_of: int32 [512], P(('grp', 'dev')), may hold values from 0 to 31, as said below
- far_clusters: int32 [32, 4], P('grp'), may hold values from 0 to 31, as said below
- cluster_couplings: bfloat16 [32, 4, 128, 128], P('grp'), may hold values from -0.125 to 0.125
- ridge_weight: float32 [], replicated, may hold values from 0.5 to 2
Outputs:
- solution: float32 [262144, 256], P(('grp', 'dev'))
- residual: float32 [262144, 256], P(('grp', 'dev'))
Inputs may be any that keep to these rules, and one draw needn't show every extreme that they name: `near_list`: each row lists leaves of the row's group whose position within the group differs from the row's leaf by 1 to 2, each at most once, in any slot order; -1 marks an empty slot. The number of listed leaves varies from leaf to leaf. `far_leaves`: each row names 4 different leaves of the row's group whose position within the group differs from the row's leaf by more than 2 and at most 8. `cluster_of`: leaves of group g belong to clusters g * 4 to g * 4 + 3, and every cluster holds exactly 16 leaves. `far_clusters`: each row names 4 different clusters, none of them in the row's own group.
All inputs are finite; a program needn't handle non-finite values.
Results may differ from a plain program's by a relative error of at most 0.0033.
Values may be sent and summed in bfloat16 or wider, within the bound.
No kernel may reach another device: no remote copies, remote signals or barrier semaphores. Data moves between devices by JAX's collectives and lax.ppermute only.
A program may use at most 64 MiB of HBM per device.

v0:
```python
import jax
import jax.numpy as jnp
from jax import lax
from jax.sharding import PartitionSpec as P

REACH = 2
FARREACH = 8
ITERS = 2


kernel_scale = 1.0 / 32.0
spectrum_gap = 0.5
spectrum_top = 8.0


def from_behind(shard, axis, by):
    devices = lax.axis_size(axis)
    pairs = [(i, i + by) for i in range(devices) if 0 <= i + by < devices]
    return lax.ppermute(shard, axis, pairs)


def in_blocks(shard, dim, devices):
    lengths = shard.shape
    blocks = shard.reshape(*lengths[:dim], devices, lengths[dim] // devices, *lengths[dim + 1 :])
    return jnp.moveaxis(blocks, dim, 0)


def sum_at_owner(shard, axis, dim):
    blocks = in_blocks(shard, dim, lax.axis_size(axis))
    arrived = lax.all_to_all(blocks, axis, split_axis=0, concat_axis=0, tiled=True)
    return arrived.sum(axis=0)


def sent_to_all(shard, axis):
    copies = jnp.broadcast_to(shard, (lax.axis_size(axis), *shard.shape))
    return lax.all_to_all(copies, axis, split_axis=0, concat_axis=0, tiled=True)


def laid_out(blocks, dim):
    blocks = jnp.moveaxis(blocks, 0, dim)
    lengths = blocks.shape
    return blocks.reshape(*lengths[:dim], lengths[dim] * lengths[dim + 1], *lengths[dim + 2 :])


def gathered_copies(shard, axis, dim):
    blocks = sent_to_all(shard, axis)
    return laid_out(blocks, dim)


def kernel_block(left_points, right_points):
    inner_products = jnp.dot(
        left_points,
        right_points.T,
        precision=lax.Precision.HIGHEST,
        preferred_element_type=jnp.float32,
    )
    distance = (
        jnp.sum(left_points * left_points, axis=1)[:, None]
        + jnp.sum(right_points * right_points, axis=1)[None, :]
        - 2.0 * inner_products
    )
    return jnp.exp(-kernel_scale * distance).astype(jnp.bfloat16)


def body(
    coords,
    right_side,
    leaf_perm,
    near_list,
    far_leaves,
    couplings,
    transfer,
    leaf_basis,
    cluster_of,
    far_clusters,
    cluster_couplings,
    ridge_weight,
):
    dev_count = lax.axis_size("dev")
    group_index = lax.axis_index("grp")
    leaf_id = group_index * dev_count + lax.axis_index("dev")
    clusters_here = far_clusters.shape[0]
    local_cluster = cluster_of[0] - group_index * clusters_here
    ordering = leaf_perm[0]
    near_offsets = [offset for offset in range(-REACH, REACH + 1) if offset != 0]
    far_offsets = [offset for offset in range(-FARREACH, FARREACH + 1) if abs(offset) > REACH]
    neighbours = [from_behind(coords, "dev", -offset) for offset in near_offsets]
    near_flags = [
        jnp.any((near_list[0] == leaf_id + offset) & (near_list[0] >= 0)).astype(jnp.float32)
        for offset in near_offsets
    ]
    far_hits = jnp.stack(
        [far_leaves[0] == leaf_id + offset for offset in far_offsets], axis=1
    ).astype(jnp.bfloat16)
    own_block = kernel_block(coords, coords)
    near_blocks = [kernel_block(coords, neighbour_points) for neighbour_points in neighbours]
    cluster_slots = (jnp.arange(clusters_here) == local_cluster).astype(jnp.float32)

    def operate(direction):
        values = direction.astype(jnp.bfloat16)
        near_sum = jnp.dot(own_block, values, preferred_element_type=jnp.float32)
        for position in range(len(near_offsets)):
            remote = from_behind(values, "dev", -near_offsets[position])
            block_here = near_blocks[position]
            near_term = lax.cond(
                near_flags[position] > 0,
                lambda: jnp.dot(block_here, remote, preferred_element_type=jnp.float32),
                lambda: jnp.zeros(values.shape, jnp.float32),
            )
            near_sum = near_sum + near_term
        skeleton = lax.dot_general(
            leaf_basis,
            values[ordering],
            (((0,), (0,)), ((), ())),
            preferred_element_type=jnp.float32,
        ).astype(jnp.bfloat16)
        remote_skeletons = jnp.stack(
            [from_behind(skeleton, "dev", -offset) for offset in far_offsets]
        )
        chosen = jnp.einsum(
            "kj,jbo->kbo", far_hits, remote_skeletons, preferred_element_type=jnp.float32
        ).astype(jnp.bfloat16)
        level_one = jnp.einsum(
            "kab,kbo->ao", couplings[0], chosen, preferred_element_type=jnp.float32
        )
        uplift = lax.dot_general(
            transfer[0], skeleton, (((0,), (0,)), ((), ())), preferred_element_type=jnp.float32
        )
        contrib = cluster_slots[:, None, None] * uplift[None]
        column_sums = sum_at_owner(contrib, "dev", 2).astype(jnp.bfloat16)
        every_column = gathered_copies(column_sums, "grp", 0)
        picked = every_column[far_clusters]
        partial_coupled = jnp.einsum(
            "ckab,ckbo->cao", cluster_couplings, picked, preferred_element_type=jnp.float32
        ).astype(jnp.bfloat16)
        whole_columns = gathered_copies(partial_coupled, "dev", 2)
        coupled = whole_columns[local_cluster]
        downward = jnp.dot(transfer[0], coupled, preferred_element_type=jnp.float32)
        tree_rows = jnp.dot(
            leaf_basis,
            (level_one + downward).astype(jnp.bfloat16),
            preferred_element_type=jnp.float32,
        )
        far_part = jnp.zeros_like(tree_rows).at[ordering].set(tree_rows)
        return ridge_weight * direction + (near_sum + far_part)

    bottom_edge = ridge_weight + spectrum_gap
    top_edge = ridge_weight + spectrum_top
    centre = (top_edge + bottom_edge) / 2.0
    spread = (top_edge - bottom_edge) / 2.0
    sigma_ratio = centre / spread
    contraction = 1.0 / sigma_ratio
    direction = right_side / centre
    solution = direction
    residual = right_side
    for rounds in range(ITERS):
        residual = residual - operate(direction)
        rho_next = 1.0 / (2.0 * sigma_ratio - contraction)
        direction = rho_next * contraction * direction + 2.0 * rho_next / spread * residual
        solution = solution + direction
        contraction = rho_next
    return (solution, residual)


def solution(mesh):
    placed = (
        P(("grp", "dev"), None),
        P(("grp", "dev"), None),
        P(("grp", "dev"), None),
        P(("grp", "dev"), None),
        P(("grp", "dev"), None),
        P(("grp", "dev"), None, None, None),
        P(("grp", "dev"), None, None),
        P(("grp", "dev"), None),
        P(("grp", "dev")),
        P("grp", None),
        P("grp", None, None, None),
        P(),
    )
    return jax.shard_map(
        body,
        mesh=mesh,
        in_specs=placed,
        out_specs=(P(("grp", "dev"), None), P(("grp", "dev"), None)),
        check_vma=False,
    )
```

profile of v0, /device:TPU:4, one launch (start us, length us, event | category | flops | bytes accessed | tf_op | source)
XLA Modules:
  0.0 297.0 jit_solution(1542740054072501519)
XLA Ops:
  8.9 10.9 %collective-permute-start.9 = (bf16[128,256]{0,1:T(8,128)(2,1)S(1)}, bf16[128,256]{0,1:T(8,128)(2,1)S(1)}, u32[]{:S(2)}, u32[]{:S(2)}) collective-permute-start(bf16[128,256]{0,1:T(8,128)(2,1)S(1)} %bitcast.205), channel_id=1, source_target_pairs={{0,7},{1,8},{2,9},{3,10},{4,11},{5,12},{6,13},{7,14},{8,15},{9,16}... | collective-permute-start | bytes 196616 | tf_op jit(solution)/shard_map/ppermute | solution.py:19
  25.0 9.1 %collective-permute-start.12 = (bf16[128,256]{0,1:T(8,128)(2,1)S(1)}, bf16[128,256]{0,1:T(8,128)(2,1)S(1)}, u32[]{:S(2)}, u32[]{:S(2)}) collective-permute-start(bf16[128,256]{0,1:T(8,128)(2,1)S(1)} %bitcast.208), channel_id=1, source_target_pairs={{0,4},{1,5},{2,6},{3,7},{4,8},{5,9},{6,10},{7,11},{8,12},{9,13},{1... | collective-permute-start | bytes 196616 | tf_op jit(solution)/shard_map/ppermute | solution.py:19
  36.5 6.6 %all-to-all-start = ((f32[64,4,128,4]{2,3,1,0:T(4,128)}), f32[64,4,128,4]{2,3,1,0:T(4,128)}, u32[]{:S(2)}, u32[]{:S(2)}) async-start(f32[64,4,128,4]{2,3,1,0:T(4,128)} %broadcast_multiply_fusion.1), calls=%async_computation | async-start | bytes 1048576 | tf_op jit(solution)/shard_map/all_to_all | solution.py:30
  54.2 5.2 %collective-permute-start.13 = (bf16[128,256]{0,1:T(8,128)(2,1)S(1)}, bf16[128,256]{0,1:T(8,128)(2,1)S(1)}, u32[]{:S(2)}, u32[]{:S(2)}) collective-permute-start(bf16[128,256]{0,1:T(8,128)(2,1)S(1)} %bitcast.209), channel_id=1, source_target_pairs={{0,3},{1,4},{2,5},{3,6},{4,7},{5,8},{6,9},{7,10},{8,11},{9,12},{10... | collective-permute-start | bytes 196616 | tf_op jit(solution)/shard_map/ppermute | solution.py:19
  66.1 4.9 %collective-permute-done.14 = bf16[128,256]{0,1:T(8,128)(2,1)S(1)} collective-permute-done((bf16[128,256]{0,1:T(8,128)(2,1)S(1)}, bf16[128,256]{0,1:T(8,128)(2,1)S(1)}, u32[]{:S(2)}, u32[]{:S(2)}) %collective-permute-start.14) | collective-permute-done | bytes 65568 | tf_op jit(solution)/shard_map/ppermute | solution.py:19
  80.5 3.7 %collective-permute-done.19 = bf16[128,256]{0,1:T(8,128)(2,1)S(1)} collective-permute-done((bf16[128,256]{0,1:T(8,128)(2,1)S(1)}, bf16[128,256]{0,1:T(8,128)(2,1)S(1)}, u32[]{:S(2)}, u32[]{:S(2)}) %collective-permute-start.19) | collective-permute-done | bytes 65568 | tf_op jit(solution)/shard_map/ppermute | solution.py:19
  84.2 6.3 %collective-permute-start.1 = (bf16[512,256]{1,0:T(8,128)(2,1)S(1)}, bf16[512,256]{1,0:T(8,128)(2,1)}, u32[]{:S(2)}, u32[]{:S(2)}) collective-permute-start(bf16[512,256]{1,0:T(8,128)(2,1)S(1)} %fusion.41), channel_id=1, source_target_pairs={{0,2},{1,3},{2,4},{3,5},{4,6},{5,7},{6,8},{7,9},{8,10},{9,11},{10,... | collective-permute-start | bytes 786440 | tf_op jit(solution)/shard_map/ppermute | solution.py:19
  93.3 6.6 %collective-permute-start = (f32[512,64]{0,1:T(8,128)}, f32[512,64]{0,1:T(8,128)S(1)}, u32[]{:S(2)}, u32[]{:S(2)}) collective-permute-start(f32[512,64]{0,1:T(8,128)} %param.28), channel_id=1, source_target_pairs={{0,2},{1,3},{2,4},{3,5},{4,6},{5,7},{6,8},{7,9},{8,10},{9,11},{10,... | collective-permute-start | bytes 393224 | tf_op jit(solution)/shard_map/ppermute | solution.py:19
  100.0 4.0 %collective-permute-done.6 = f32[512,64]{0,1:T(8,128)} collective-permute-done((f32[512,64]{0,1:T(8,128)}, f32[512,64]{0,1:T(8,128)}, u32[]{:S(2)}, u32[]{:S(2)}) %collective-permute-start.6) | collective-permute-done | bytes 131104 | tf_op jit(solution)/shard_map/ppermute | solution.py:19
  113.0 4.8 %all-to-all-start.1 = ((bf16[8,4,128,4]{2,3,1,0:T(4,128)(2,1)}), bf16[8,4,128,4]{2,3,1,0:T(4,128)(2,1)S(1)}, u32[]{:S(2)}, u32[]{:S(2)}) async-start(bf16[8,4,128,4]{2,3,1,0:T(4,128)(2,1)} %broadcast_in_dim.10), calls=%async_computation.1 | async-start | bytes 65536 | tf_op jit(solution)/shard_map/all_to_all | solution.py:36
  117.8 4.6 %collective-permute-start.2 = (f32[512,64]{0,1:T(8,128)}, f32[512,64]{0,1:T(8,128)S(1)}, u32[]{:S(2)}, u32[]{:S(2)}) collective-permute-start(f32[512,64]{0,1:T(8,128)} %param.28), channel_id=1, source_target_pairs={{0,1},{1,2},{2,3},{3,4},{4,5},{5,6},{6,7},{7,8},{8,9},{9,10},{10,1... | collective-permute-start | bytes 393224 | tf_op jit(solution)/shard_map/ppermute | solution.py:19
  124.1 19.3 %all-to-all-start.2 = ((bf16[64,4,128,4]{2,3,1,0:T(4,128)(2,1)}), bf16[64,4,128,4]{2,3,1,0:T(4,128)(2,1)}, u32[]{:S(2)}, u32[]{:S(2)}) async-start(bf16[64,4,128,4]{2,3,1,0:T(4,128)(2,1)} %broadcast_in_dim.12), calls=%async_computation.2 | async-start | bytes 524288 | tf_op jit(solution)/shard_map/all_to_all | solution.py:36
  153.6 4.5 %all-to-all-done.2 = bf16[64,4,128,4]{2,3,1,0:T(4,128)(2,1)} async-done(((bf16[64,4,128,4]{2,3,1,0:T(4,128)(2,1)}), bf16[64,4,128,4]{2,3,1,0:T(4,128)(2,1)}, u32[]{:S(2)}, u32[]{:S(2)}) %all-to-all-start.2) | async-done | bytes 262176 | tf_op jit(solution)/shard_map/all_to_all | solution.py:36
  160.5 3.6 %scatter_custom_fusion = f32[512,256]{1,0:T(8,128)} fusion(s32[512]{0:T(512)S(1)} %bitcast.229, f32[512,256]{1,0:T(8,128)} %copy.39, f32[]{:T(128)} %constant.7.clone.1), kind=kCustom, calls=%fused_computation.48 | custom fusion | bytes 524800 | tf_op jit(solution)/shard_map/scatter | solution.py:144
  172.0 3.9 %collective-permute-start.25 = (bf16[128,256]{0,1:T(8,128)(2,1)S(1)}, bf16[128,256]{0,1:T(8,128)(2,1)}, u32[]{:S(2)}, u32[]{:S(2)}) collective-permute-start(bf16[128,256]{0,1:T(8,128)(2,1)S(1)} %bitcast.217), channel_id=1, source_target_pairs={{0,7},{1,8},{2,9},{3,10},{4,11},{5,12},{6,13},{7,14},{8,15},{9,16}... | collective-permute-start | bytes 196616 | tf_op jit(solution)/shard_map/ppermute | solution.py:19
  175.9 5.0 %collective-permute-start.26 = (bf16[128,256]{0,1:T(8,128)(2,1)S(1)}, bf16[128,256]{0,1:T(8,128)(2,1)}, u32[]{:S(2)}, u32[]{:S(2)}) collective-permute-start(bf16[128,256]{0,1:T(8,128)(2,1)S(1)} %bitcast.218), channel_id=1, source_target_pairs={{0,6},{1,7},{2,8},{3,9},{4,10},{5,11},{6,12},{7,13},{8,14},{9,15},... | collective-permute-start | bytes 196616 | tf_op jit(solution)/shard_map/ppermute | solution.py:19
  184.3 6.1 %collective-permute-start.28 = (bf16[128,256]{0,1:T(8,128)(2,1)S(1)}, bf16[128,256]{0,1:T(8,128)(2,1)}, u32[]{:S(2)}, u32[]{:S(2)}) collective-permute-start(bf16[128,256]{0,1:T(8,128)(2,1)S(1)} %bitcast.220), channel_id=1, source_target_pairs={{0,4},{1,5},{2,6},{3,7},{4,8},{5,9},{6,10},{7,11},{8,12},{9,13},{1... | collective-permute-start | bytes 196616 | tf_op jit(solution)/shard_map/ppermute | solution.py:19
  193.3 7.3 %all-to-all-start.3 = ((f32[64,4,128,4]{2,3,1,0:T(4,128)}), f32[64,4,128,4]{2,3,1,0:T(4,128)S(1)}, u32[]{:S(2)}, u32[]{:S(2)}) async-start(f32[64,4,128,4]{2,3,1,0:T(4,128)} %broadcast_multiply_fusion), calls=%async_computation.3 | async-start | bytes 1048576 | tf_op jit(solution)/shard_map/all_to_all | solution.py:30
  200.6 5.3 %collective-permute-start.29 = (bf16[128,256]{0,1:T(8,128)(2,1)S(1)}, bf16[128,256]{0,1:T(8,128)(2,1)S(1)}, u32[]{:S(2)}, u32[]{:S(2)}) collective-permute-start(bf16[128,256]{0,1:T(8,128)(2,1)S(1)} %bitcast.221), channel_id=1, source_target_pairs={{0,3},{1,4},{2,5},{3,6},{4,7},{5,8},{6,9},{7,10},{8,11},{9,12},{10... | collective-permute-start | bytes 196616 | tf_op jit(solution)/shard_map/ppermute | solution.py:19
  222.9 6.0 %collective-permute-start.20 = (bf16[512,256]{1,0:T(8,128)(2,1)S(1)}, bf16[512,256]{1,0:T(8,128)(2,1)}, u32[]{:S(2)}, u32[]{:S(2)}) collective-permute-start(bf16[512,256]{1,0:T(8,128)(2,1)S(1)} %get-tuple-element.80), channel_id=1, source_target_pairs={{0,2},{1,3},{2,4},{3,5},{4,6},{5,7},{6,8},{7,9},{8,10},{9,11},{10,... | collective-permute-start | bytes 786440 | tf_op jit(solution)/shard_map/ppermute | solution.py:19
  229.5 3.5 %collective-permute-start.21 = (bf16[512,256]{1,0:T(8,128)(2,1)S(1)}, bf16[512,256]{1,0:T(8,128)(2,1)}, u32[]{:S(2)}, u32[]{:S(2)}) collective-permute-start(bf16[512,256]{1,0:T(8,128)(2,1)S(1)} %get-tuple-element.80), channel_id=1, source_target_pairs={{0,1},{1,2},{2,3},{3,4},{4,5},{5,6},{6,7},{7,8},{8,9},{9,10},{10,1... | collective-permute-start | bytes 786440 | tf_op jit(solution)/shard_map/ppermute | solution.py:19
  236.3 5.3 %all-to-all-start.4 = ((bf16[8,4,128,4]{2,3,1,0:T(4,128)(2,1)}), bf16[8,4,128,4]{2,3,1,0:T(4,128)(2,1)S(1)}, u32[]{:S(2)}, u32[]{:S(2)}) async-start(bf16[8,4,128,4]{2,3,1,0:T(4,128)(2,1)} %broadcast_in_dim.13), calls=%async_computation.4 | async-start | bytes 65536 | tf_op jit(solution)/shard_map/all_to_all | solution.py:36
  246.2 27.9 %all-to-all-start.5 = ((bf16[64,4,128,4]{2,3,1,0:T(4,128)(2,1)}), bf16[64,4,128,4]{2,3,1,0:T(4,128)(2,1)}, u32[]{:S(2)}, u32[]{:S(2)}) async-start(bf16[64,4,128,4]{2,3,1,0:T(4,128)(2,1)} %broadcast_in_dim.14), calls=%async_computation.5 | async-start | bytes 524288 | tf_op jit(solution)/shard_map/all_to_all | solution.py:36
  284.1 4.8 %all-to-all-done.5 = bf16[64,4,128,4]{2,3,1,0:T(4,128)(2,1)} async-done(((bf16[64,4,128,4]{2,3,1,0:T(4,128)(2,1)}), bf16[64,4,128,4]{2,3,1,0:T(4,128)(2,1)}, u32[]{:S(2)}, u32[]{:S(2)}) %all-to-all-start.5) | async-done | bytes 262176 | tf_op jit(solution)/shard_map/all_to_all | solution.py:36
  (236 shorter events, 130.6 us)
Async XLA Ops:
  5.4 48.8 %collective-permute-start.8 = (bf16[128,256]{0,1:T(8,128)(2,1)S(1)}, bf16[128,256]{0,1:T(8,128)(2,1)S(1)}, u32[]{:S(2)}, u32[]{:S(2)}) collective-permute-start(bf16[128,256]{0,1:T(8,128)(2,1)S(1)} %bitcast.204), channel_id=1, source_target_pairs={{0,8},{1,9},{2,10},{3,11},{4,12},{5,13},{6,14},{7,15},{8,16},{9,17... | collective-permute-start | bytes 196616 | tf_op jit(solution)/shard_map/ppermute | solution.py:19
  8.9 50.6 %collective-permute-start.9 = (bf16[128,256]{0,1:T(8,128)(2,1)S(1)}, bf16[128,256]{0,1:T(8,128)(2,1)S(1)}, u32[]{:S(2)}, u32[]{:S(2)}) collective-permute-start(bf16[128,256]{0,1:T(8,128)(2,1)S(1)} %bitcast.205), channel_id=1, source_target_pairs={{0,7},{1,8},{2,9},{3,10},{4,11},{5,12},{6,13},{7,14},{8,15},{9,16}... | collective-permute-start | bytes 196616 | tf_op jit(solution)/shard_map/ppermute | solution.py:19
  19.9 40.9 %collective-permute-start.10 = (bf16[128,256]{0,1:T(8,128)(2,1)S(1)}, bf16[128,256]{0,1:T(8,128)(2,1)S(1)}, u32[]{:S(2)}, u32[]{:S(2)}) collective-permute-start(bf16[128,256]{0,1:T(8,128)(2,1)S(1)} %bitcast.206), channel_id=1, source_target_pairs={{0,6},{1,7},{2,8},{3,9},{4,10},{5,11},{6,12},{7,13},{8,14},{9,15},... | collective-permute-start | bytes 196616 | tf_op jit(solution)/shard_map/ppermute | solution.py:19
  23.3 38.8 %collective-permute-start.11 = (bf16[128,256]{0,1:T(8,128)(2,1)S(1)}, bf16[128,256]{0,1:T(8,128)(2,1)S(1)}, u32[]{:S(2)}, u32[]{:S(2)}) collective-permute-start(bf16[128,256]{0,1:T(8,128)(2,1)S(1)} %bitcast.207), channel_id=1, source_target_pairs={{0,5},{1,6},{2,7},{3,8},{4,9},{5,10},{6,11},{7,12},{8,13},{9,14},{... | collective-permute-start | bytes 196616 | tf_op jit(solution)/shard_map/ppermute | solution.py:19
  25.0 38.5 %collective-permute-start.12 = (bf16[128,256]{0,1:T(8,128)(2,1)S(1)}, bf16[128,256]{0,1:T(8,128)(2,1)S(1)}, u32[]{:S(2)}, u32[]{:S(2)}) collective-permute-start(bf16[128,256]{0,1:T(8,128)(2,1)S(1)} %bitcast.208), channel_id=1, source_target_pairs={{0,4},{1,5},{2,6},{3,7},{4,8},{5,9},{6,10},{7,11},{8,12},{9,13},{1... | collective-permute-start | bytes 196616 | tf_op jit(solution)/shard_map/ppermute | solution.py:19
  36.5 74.8 %all-to-all-start = ((f32[64,4,128,4]{2,3,1,0:T(4,128)}), f32[64,4,128,4]{2,3,1,0:T(4,128)}, u32[]{:S(2)}, u32[]{:S(2)}) async-start(f32[64,4,128,4]{2,3,1,0:T(4,128)} %broadcast_multiply_fusion.1), calls=%async_computation | async-start | bytes 1048576 | tf_op jit(solution)/shard_map/all_to_all | solution.py:30
  72.8 75.5 %collective-permute-start.5 = (bf16[512,256]{1,0:T(8,128)(2,1)S(1)}, bf16[512,256]{1,0:T(8,128)(2,1)}, u32[]{:S(2)}, u32[]{:S(2)}) collective-permute-start(bf16[512,256]{1,0:T(8,128)(2,1)S(1)} %fusion.41), channel_id=1, source_target_pairs={{1,0},{2,1},{3,2},{4,3},{5,4},{6,5},{7,6},{8,7},{9,8},{10,9},{11,1... | collective-permute-start | bytes 786440 | tf_op jit(solution)/shard_map/ppermute | solution.py:19
  77.0 73.6 %collective-permute-start.7 = (bf16[512,256]{1,0:T(8,128)(2,1)S(1)}, bf16[512,256]{1,0:T(8,128)(2,1)}, u32[]{:S(2)}, u32[]{:S(2)}) collective-permute-start(bf16[512,256]{1,0:T(8,128)(2,1)S(1)} %fusion.41), channel_id=1, source_target_pairs={{2,0},{3,1},{4,2},{5,3},{6,4},{7,5},{8,6},{9,7},{10,8},{11,9},{12,... | collective-permute-start | bytes 786440 | tf_op jit(solution)/shard_map/ppermute | solution.py:19
  84.2 68.5 %collective-permute-start.1 = (bf16[512,256]{1,0:T(8,128)(2,1)S(1)}, bf16[512,256]{1,0:T(8,128)(2,1)}, u32[]{:S(2)}, u32[]{:S(2)}) collective-permute-start(bf16[512,256]{1,0:T(8,128)(2,1)S(1)} %fusion.41), channel_id=1, source_target_pairs={{0,2},{1,3},{2,4},{3,5},{4,6},{5,7},{6,8},{7,9},{8,10},{9,11},{10,... | collective-permute-start | bytes 786440 | tf_op jit(solution)/shard_map/ppermute | solution.py:19
  104.0 49.5 %collective-permute-start.3 = (bf16[512,256]{1,0:T(8,128)(2,1)S(1)}, bf16[512,256]{1,0:T(8,128)(2,1)}, u32[]{:S(2)}, u32[]{:S(2)}) collective-permute-start(bf16[512,256]{1,0:T(8,128)(2,1)S(1)} %fusion.41), channel_id=1, source_target_pairs={{0,1},{1,2},{2,3},{3,4},{4,5},{5,6},{6,7},{7,8},{8,9},{9,10},{10,1... | collective-permute-start | bytes 786440 | tf_op jit(solution)/shard_map/ppermute | solution.py:19
  117.8 27.6 %collective-permute-start.2 = (f32[512,64]{0,1:T(8,128)}, f32[512,64]{0,1:T(8,128)S(1)}, u32[]{:S(2)}, u32[]{:S(2)}) collective-permute-start(f32[512,64]{0,1:T(8,128)} %param.28), channel_id=1, source_target_pairs={{0,1},{1,2},{2,3},{3,4},{4,5},{5,6},{6,7},{7,8},{8,9},{9,10},{10,1... | collective-permute-start | bytes 393224 | tf_op jit(solution)/shard_map/ppermute | solution.py:19
  124.1 33.9 %all-to-all-start.2 = ((bf16[64,4,128,4]{2,3,1,0:T(4,128)(2,1)}), bf16[64,4,128,4]{2,3,1,0:T(4,128)(2,1)}, u32[]{:S(2)}, u32[]{:S(2)}) async-start(bf16[64,4,128,4]{2,3,1,0:T(4,128)(2,1)} %broadcast_in_dim.12), calls=%async_computation.2 | async-start | bytes 524288 | tf_op jit(solution)/shard_map/all_to_all | solution.py:36
  169.2 31.4 %collective-permute-start.24 = (bf16[128,256]{0,1:T(8,128)(2,1)S(1)}, bf16[128,256]{0,1:T(8,128)(2,1)}, u32[]{:S(2)}, u32[]{:S(2)}) collective-permute-start(bf16[128,256]{0,1:T(8,128)(2,1)S(1)} %bitcast.216), channel_id=1, source_target_pairs={{0,8},{1,9},{2,10},{3,11},{4,12},{5,13},{6,14},{7,15},{8,16},{9,17... | collective-permute-start | bytes 196616 | tf_op jit(solution)/shard_map/ppermute | solution.py:19
  172.0 35.3 %collective-permute-start.25 = (bf16[128,256]{0,1:T(8,128)(2,1)S(1)}, bf16[128,256]{0,1:T(8,128)(2,1)}, u32[]{:S(2)}, u32[]{:S(2)}) collective-permute-start(bf16[128,256]{0,1:T(8,128)(2,1)S(1)} %bitcast.217), channel_id=1, source_target_pairs={{0,7},{1,8},{2,9},{3,10},{4,11},{5,12},{6,13},{7,14},{8,15},{9,16}... | collective-permute-start | bytes 196616 | tf_op jit(solution)/shard_map/ppermute | solution.py:19
  175.9 34.2 %collective-permute-start.26 = (bf16[128,256]{0,1:T(8,128)(2,1)S(1)}, bf16[128,256]{0,1:T(8,128)(2,1)}, u32[]{:S(2)}, u32[]{:S(2)}) collective-permute-start(bf16[128,256]{0,1:T(8,128)(2,1)S(1)} %bitcast.218), channel_id=1, source_target_pairs={{0,6},{1,7},{2,8},{3,9},{4,10},{5,11},{6,12},{7,13},{8,14},{9,15},... | collective-permute-start | bytes 196616 | tf_op jit(solution)/shard_map/ppermute | solution.py:19
  180.9 31.9 %collective-permute-start.27 = (bf16[128,256]{0,1:T(8,128)(2,1)S(1)}, bf16[128,256]{0,1:T(8,128)(2,1)}, u32[]{:S(2)}, u32[]{:S(2)}) collective-permute-start(bf16[128,256]{0,1:T(8,128)(2,1)S(1)} %bitcast.219), channel_id=1, source_target_pairs={{0,5},{1,6},{2,7},{3,8},{4,9},{5,10},{6,11},{7,12},{8,13},{9,14},{... | collective-permute-start | bytes 196616 | tf_op jit(solution)/shard_map/ppermute | solution.py:19
  184.3 31.3 %collective-permute-start.28 = (bf16[128,256]{0,1:T(8,128)(2,1)S(1)}, bf16[128,256]{0,1:T(8,128)(2,1)}, u32[]{:S(2)}, u32[]{:S(2)}) collective-permute-start(bf16[128,256]{0,1:T(8,128)(2,1)S(1)} %bitcast.220), channel_id=1, source_target_pairs={{0,4},{1,5},{2,6},{3,7},{4,8},{5,9},{6,10},{7,11},{8,12},{9,13},{1... | collective-permute-start | bytes 196616 | tf_op jit(solution)/shard_map/ppermute | solution.py:19
  193.3 42.3 %all-to-all-start.3 = ((f32[64,4,128,4]{2,3,1,0:T(4,128)}), f32[64,4,128,4]{2,3,1,0:T(4,128)S(1)}, u32[]{:S(2)}, u32[]{:S(2)}) async-start(f32[64,4,128,4]{2,3,1,0:T(4,128)} %broadcast_multiply_fusion), calls=%async_computation.3 | async-start | bytes 1048576 | tf_op jit(solution)/shard_map/all_to_all | solution.py:30
  220.3 53.8 %collective-permute-start.35 = (bf16[128,256]{0,1:T(8,128)(2,1)S(1)}, bf16[128,256]{0,1:T(8,128)(2,1)S(1)}, u32[]{:S(2)}, u32[]{:S(2)}) collective-permute-start(bf16[128,256]{0,1:T(8,128)(2,1)S(1)} %bitcast.227), channel_id=1, source_target_pairs={{8,0},{9,1},{10,2},{11,3},{12,4},{13,5},{14,6},{15,7},{16,8},{17,9... | collective-permute-start | bytes 196616 | tf_op jit(solution)/shard_map/ppermute | solution.py:19
  222.9 55.7 %collective-permute-start.20 = (bf16[512,256]{1,0:T(8,128)(2,1)S(1)}, bf16[512,256]{1,0:T(8,128)(2,1)}, u32[]{:S(2)}, u32[]{:S(2)}) collective-permute-start(bf16[512,256]{1,0:T(8,128)(2,1)S(1)} %get-tuple-element.80), channel_id=1, source_target_pairs={{0,2},{1,3},{2,4},{3,5},{4,6},{5,7},{6,8},{7,9},{8,10},{9,11},{10,... | collective-permute-start | bytes 786440 | tf_op jit(solution)/shard_map/ppermute | solution.py:19
  229.5 50.0 %collective-permute-start.21 = (bf16[512,256]{1,0:T(8,128)(2,1)S(1)}, bf16[512,256]{1,0:T(8,128)(2,1)}, u32[]{:S(2)}, u32[]{:S(2)}) collective-permute-start(bf16[512,256]{1,0:T(8,128)(2,1)S(1)} %get-tuple-element.80), channel_id=1, source_target_pairs={{0,1},{1,2},{2,3},{3,4},{4,5},{5,6},{6,7},{7,8},{8,9},{9,10},{10,1... | collective-permute-start | bytes 786440 | tf_op jit(solution)/shard_map/ppermute | solution.py:19
  233.7 46.3 %collective-permute-start.22 = (bf16[512,256]{1,0:T(8,128)(2,1)S(1)}, bf16[512,256]{1,0:T(8,128)(2,1)}, u32[]{:S(2)}, u32[]{:S(2)}) collective-permute-start(bf16[512,256]{1,0:T(8,128)(2,1)S(1)} %get-tuple-element.80), channel_id=1, source_target_pairs={{1,0},{2,1},{3,2},{4,3},{5,4},{6,5},{7,6},{8,7},{9,8},{10,9},{11,1... | collective-permute-start | bytes 786440 | tf_op jit(solution)/shard_map/ppermute | solution.py:19
  241.6 40.4 %collective-permute-start.23 = (bf16[512,256]{1,0:T(8,128)(2,1)S(1)}, bf16[512,256]{1,0:T(8,128)(2,1)}, u32[]{:S(2)}, u32[]{:S(2)}) collective-permute-start(bf16[512,256]{1,0:T(8,128)(2,1)S(1)} %get-tuple-element.80), channel_id=1, source_target_pairs={{2,0},{3,1},{4,2},{5,3},{6,4},{7,5},{8,6},{9,7},{10,8},{11,9},{12,... | collective-permute-start | bytes 786440 | tf_op jit(solution)/shard_map/ppermute | solution.py:19
  246.2 42.7 %all-to-all-start.5 = ((bf16[64,4,128,4]{2,3,1,0:T(4,128)(2,1)}), bf16[64,4,128,4]{2,3,1,0:T(4,128)(2,1)}, u32[]{:S(2)}, u32[]{:S(2)}) async-start(bf16[64,4,128,4]{2,3,1,0:T(4,128)(2,1)} %broadcast_in_dim.14), calls=%async_computation.5 | async-start | bytes 524288 | tf_op jit(solution)/shard_map/all_to_all | solution.py:36
  (52 other events, 762.2 us)
where the time goes:
time: 300 us; the launch traced here: 297 us
  starting transfers between devices  184 us (61%)
  local copies, waits for them, and re-layouts  44.5 us (15%)
  waiting for transfers between devices  26.6 us (9%)
  matrix products  24 us (8%)
  other arithmetic  12.4 us (4%)
  between operations  5.74 us (2%)
    ppermute x36, starting transfers between devices, from_behind(): return lax.ppermute(shard, axis, pairs)  113 us
    all_to_all x4, starting transfers between devices, sent_to_all(): return lax.all_to_all(copies, axis, split_axis=0, concat_axis=0, tiled=True)  57.2 us
    unnamed x90, local copies, waits for them, and re-layouts  19.1 us
    ppermute x36, waiting for transfers between devices, from_behind(): return lax.ppermute(shard, axis, pairs)  16.2 us
    all_to_all x2, starting transfers between devices, sum_at_owner(): lax.all_to_all(blocks, axis, split_axis=0, concat_axis=0, tiled=True)  13.9 us
    dot_general x5, matrix products, kernel_block(): jnp.dot(left_points, right_points.T, precision=lax.Precision.HIGHEST, pre...  10.7 us
    all_to_all x4, waiting for transfers between devices, sent_to_all(): return lax.all_to_all(copies, axis, split_axis=0, concat_axis=0, tiled=True)  10.4 us
    dot_general x4, matrix products, operate(): jnp.dot(block_here, remote, preferred_element_type=jnp.float32)  6.74 us
  transfers between devices with their start and end apart: 42, of which 10 were waited for; matrix products, arithmetic and copies ran while one was open for 17% of the time, Pallas kernels for 0%

commit v1 on v0

v1 whole, which is shorter than its diff:
```python
import jax
import jax.numpy as jnp
from jax import lax
from jax.experimental import pallas as pl
from jax.experimental.pallas import tpu as pltpu
from jax.sharding import PartitionSpec as P

LEAF, DIM, OUT, RANK = 512, 64, 256, 128
N_GRP, N_DEV, CPG = 8, 64, 4
FAR1, FAR2 = 4, 4
COLS = OUT // N_DEV
NEAR = (-1, 1, -2, 2)

KERNEL_LOG2 = -1.4426950408889634 / 32.0
GAP, TOP = 0.5, 8.0

F32, BF16 = jnp.float32, jnp.bfloat16
VMEM = pl.BlockSpec(memory_space=pltpu.VMEM)
SMEM = pl.BlockSpec(memory_space=pltpu.SMEM)
LIMIT = 48 * 2**20


def dot(a, b, dims=((1,), (0,))):
    return lax.dot_general(a, b, (dims, ((), ())), preferred_element_type=F32)


def call(kernel, name, outs, ins, args, scratch=(), flops=0):
    shapes = [jax.ShapeDtypeStruct(s, t) for s, t in outs]
    return pl.pallas_call(
        kernel,
        name=name,
        out_shape=shapes,
        in_specs=ins,
        out_specs=[VMEM] * len(outs),
        scratch_shapes=list(scratch),
        compiler_params=pltpu.CompilerParams(vmem_limit_bytes=LIMIT),
        cost_estimate=pl.CostEstimate(flops=flops, bytes_accessed=0, transcendentals=0),
    )(*args)


def chebyshev(ridge):
    ridge = jnp.full((1, 1), ridge, F32)
    bottom, top = ridge + GAP, ridge + TOP
    centre, spread = (top + bottom) / 2.0, (top - bottom) / 2.0
    sigma = centre / spread
    rho0 = 1.0 / sigma
    rho1 = 1.0 / (2.0 * sigma - rho0)
    rho2 = 1.0 / (2.0 * sigma - rho1)
    first = (rho1 * rho0, 2.0 * rho1 / spread)
    second = (rho2 * rho1, 2.0 * rho2 / spread)
    return ridge, centre, first, second


def to_owners(values, basis, transfer, staged, rows):
    skeleton = dot(values, basis, ((0,), (0,))).astype(BF16)
    uplift = dot(skeleton, transfer)
    skeleton = skeleton.astype(F32)
    for i in range(COLS):
        part = slice(N_DEV * i, N_DEV * (i + 1))
        staged[pl.ds(i, N_DEV, stride=rows), :] = skeleton[part]
        staged[pl.ds(COLS + i, N_DEV, stride=rows), :] = uplift[part]


def start_kernel(ridge, far, cluster, rs, coords, perm, basis, transfer, wc, sent, placed, staged):
    _, centre, _, _ = chebyshev(ridge[0])
    values = (rs[...] / centre).astype(BF16)
    point = lax.broadcasted_iota(jnp.int32, (LEAF, LEAF), 0)
    pick = jnp.where(point == perm[...], 1.0, 0.0).astype(BF16)
    basis_here = dot(pick, basis[...]).astype(BF16)
    placed[...] = basis_here
    staged[...] = jnp.zeros_like(staged)
    to_owners(values, basis_here, transfer[0], staged, 16)
    lane = lax.broadcasted_iota(jnp.int32, (N_DEV, RANK), 1)
    told = jnp.where(lane == FAR1, (cluster[0] % CPG).astype(F32), 0.0)
    for k in range(FAR1):
        told = jnp.where(lane == k, (far[0, k] % N_DEV).astype(F32), told)
    staged[pl.ds(8, N_DEV, stride=16), :] = told
    sent[...] = staged[...].astype(BF16).reshape(N_DEV, 16, RANK)
    wc[:, :OUT] = values
    high = coords[...].astype(BF16)
    low = (coords[...] - high.astype(F32)).astype(BF16)
    wc[:, OUT : OUT + 2 * DIM] = jnp.concatenate([high, low], axis=1)


def owner_sums(staged, rows, told, sums, narrow):
    lane = lax.broadcasted_iota(jnp.int32, (N_DEV, RANK), 1).astype(F32)
    member = jnp.where(lane == told[:, FAR1 : FAR1 + 1], 1.0, 0.0).astype(BF16)
    uplifts = jnp.concatenate(
        [staged[pl.ds(COLS + i, N_DEV, stride=rows), :] for i in range(COLS)], axis=1
    ).astype(BF16)
    total = dot(member, uplifts, ((0,), (0,)))
    for i in range(COLS):
        narrow[pl.ds(CPG * i, CPG), :] = total[:CPG, RANK * i : RANK * (i + 1)]
    out = narrow[...].astype(BF16)
    for g in range(N_GRP):
        sums[g] = out


def sums_first_kernel(arrived, sums, told, skeletons, staged, narrow):
    staged[...] = arrived[...].astype(F32).reshape(N_DEV * 16, RANK)
    told[...] = staged[pl.ds(8, N_DEV, stride=16), :]
    owner_sums(staged, 16, told[...], sums, narrow)
    skeletons[...] = jnp.concatenate(
        [staged[pl.ds(i, N_DEV, stride=16), :] for i in range(COLS)], axis=1
    ).astype(BF16)


def sums_kernel(arrived, told, sums, skeletons, staged, narrow):
    staged[...] = arrived[...].astype(F32).reshape(N_DEV * 8, RANK)
    owner_sums(staged, 8, told[...], sums, narrow)
    skeletons[...] = jnp.concatenate(
        [staged[pl.ds(i, N_DEV, stride=8), :] for i in range(COLS)], axis=1
    ).astype(BF16)


def partners_kernel(skeletons, told, sent, staged):
    lane = lax.broadcasted_iota(jnp.int32, (N_DEV, N_DEV), 1).astype(F32)
    pick = jnp.concatenate(
        [jnp.where(lane == told[:, k : k + 1], 1.0, 0.0) for k in range(FAR1)], axis=0
    ).astype(BF16)
    picked = dot(pick, skeletons[...])
    for k in range(FAR1):
        for i in range(COLS):
            staged[pl.ds(COLS * k + i, N_DEV, stride=16), :] = picked[
                N_DEV * k : N_DEV * (k + 1), RANK * i : RANK * (i + 1)
            ]
    sent[...] = staged[...].astype(BF16).reshape(N_DEV, 16, RANK)


def couple_kernel(far_clusters, all_sums, blocks, told, sent):
    rows = COLS * CPG
    sums = all_sums[...].reshape(N_GRP * rows, RANK)
    row = lax.broadcasted_iota(jnp.int32, (rows, N_GRP * rows), 0)
    lane = lax.broadcasted_iota(jnp.int32, (rows, N_GRP * rows), 1)
    column, cluster = row // CPG, row % CPG
    total = jnp.zeros((rows, CPG * RANK), F32)
    for k in range(FAR2):
        target = CPG * column
        for c in range(CPG):
            f = far_clusters[c, k]
            target += jnp.where(cluster == c, rows * (f // CPG) + f % CPG, 0)
        pick = jnp.where(lane == target, 1.0, 0.0).astype(BF16)
        picked = dot(pick, sums).astype(BF16)
        block = blocks[:, k].reshape(CPG * RANK, RANK)
        total += dot(picked, block, ((1,), (1,)))
    coupled = jnp.zeros((rows, RANK), F32)
    own = cluster[:, :RANK]
    for c in range(CPG):
        coupled += jnp.where(own == c, total[:, RANK * c : RANK * (c + 1)], 0.0)
    coupled = coupled.astype(BF16)
    lane = lax.broadcasted_iota(jnp.int32, (N_DEV, rows), 1).astype(F32)
    pick = jnp.concatenate(
        [jnp.where(lane == told[:, FAR1 : FAR1 + 1] + CPG * i, 1.0, 0.0) for i in range(COLS)], axis=0
    ).astype(BF16)
    out = dot(pick, coupled)
    for i in range(COLS):
        sent[:, i, :] = out[N_DEV * i : N_DEV * (i + 1)]


def far_field(partners, coupled, couplings, transfer, basis, staged):
    staged[...] = partners[...].astype(F32).reshape(N_DEV * 16, RANK)
    local = jnp.zeros((RANK, OUT), F32)
    for k in range(FAR1):
        skeleton = jnp.concatenate(
            [staged[pl.ds(COLS * k + i, N_DEV, stride=16), :] for i in range(COLS)], axis=0
        ).astype(BF16)
        local += dot(couplings[0, k], skeleton, ((1,), (1,)))
    downward = jnp.concatenate([coupled[:, i, :] for i in range(COLS)], axis=0).astype(BF16)
    local += dot(transfer[0], downward, ((1,), (1,)))
    return dot(basis[...], local.astype(BF16))


def middle_kernel(ridge, partners, coupled, couplings, transfer, basis, near, rs, w, sent, d2, r1, staged, staged_out):
    ridge, centre, (mul, add), _ = chebyshev(ridge[0])
    far = far_field(partners, coupled, couplings, transfer, basis, staged)
    d1 = rs[...] / centre
    residual = rs[...] - (ridge * d1 + (near[...] + far))
    direction = mul * d1 + add * residual
    r1[...] = residual
    d2[...] = direction
    values = direction.astype(BF16)
    w[...] = values
    to_owners(values, basis[...], transfer[0], staged_out, 8)
    sent[...] = staged_out[...].astype(BF16).reshape(N_DEV, 8, RANK)


def end_kernel(ridge, partners, coupled, couplings, transfer, basis, near, rs, d2, r1, solution, residual, staged):
    ridge, centre, _, (mul, add) = chebyshev(ridge[0])
    far = far_field(partners, coupled, couplings, transfer, basis, staged)
    r2 = r1[...] - (ridge * d2[...] + (near[...] + far))
    residual[...] = r2
    d3 = mul * d2[...] + add * r2
    solution[...] = rs[...] / centre + d2[...] + d3


def norms(points):
    square = jnp.sum(points * points, axis=1, keepdims=True) * KERNEL_LOG2
    return square, jnp.broadcast_to(square, (LEAF, RANK)).T[:1]


def listed(near_list, offset):
    leaf = lax.axis_index("grp") * N_DEV + lax.axis_index("dev")
    hit = near_list[0, 0] == leaf + offset
    for k in range(1, len(NEAR)):
        hit = hit | (near_list[0, k] == leaf + offset)
    return hit


def block_times(here, there, block, total, fresh):
    high, low = here[:, OUT : OUT + DIM], here[:, OUT + DIM : OUT + 2 * DIM]
    left = jnp.concatenate([high, high, low, low], axis=1)
    column, _ = norms(high.astype(F32) + low.astype(F32))
    high, low = there[:, OUT : OUT + DIM], there[:, OUT + DIM : OUT + 2 * DIM]
    right = jnp.concatenate([high, low, high, low], axis=1)
    _, across = norms(high.astype(F32) + low.astype(F32))
    step = 128
    for r in range(0, LEAF, step):
        part = slice(r, r + step)
        inner = dot(left[part], right, ((1,), (1,)))
        entries = jnp.exp2((column[part] + across) - (2.0 * KERNEL_LOG2) * inner).astype(BF16)
        block[part] = entries
        product = dot(entries, there[:, :OUT])
        total[part] = product if fresh else total[part] + product


def near_own_kernel(here, block, total):
    block_times(here, here, block, total, True)


def near_pair_kernel(offsets, near_list, here, before, first, second, block1, block2, total):
    total[...] = before[...]
    for offset, there, block in zip(offsets, (first, second), (block1, block2)):

        @pl.when(listed(near_list, offset))
        def _():
            block_times(here, there, block, total, False)


def again_own_kernel(w, block, total):
    total[...] = dot(block[...], w[...])


def again_pair_kernel(offsets, near_list, before, first, second, block1, block2, total):
    total[...] = before[...]
    for offset, there, block in zip(offsets, (first, second), (block1, block2)):

        @pl.when(listed(near_list, offset))
        def _():
            total[...] += dot(block[...], there[...])


def from_behind(shard, by):
    pairs = [(i, i + by) for i in range(N_DEV) if 0 <= i + by < N_DEV]
    return lax.ppermute(shard, "dev", pairs)


def exchanged(blocks, axis):
    return lax.all_to_all(blocks, axis, split_axis=0, concat_axis=0, tiled=True)


def body(
    coords,
    right_side,
    leaf_perm,
    near_list,
    far_leaves,
    couplings,
    transfer,
    leaf_basis,
    cluster_of,
    far_clusters,
    cluster_couplings,
    ridge_weight,
):
    ridge = ridge_weight.reshape(1)
    field = ((LEAF, OUT), F32)
    block = ((LEAF, LEAF), BF16)
    rows16 = pltpu.VMEM((N_DEV * 16, RANK), F32)
    rows8 = pltpu.VMEM((N_DEV * 8, RANK), F32)
    narrow = pltpu.VMEM((COLS * CPG, RANK), F32)
    pair_outs = [block, block, field]
    gmul = 2 * LEAF * LEAF * OUT

    wc, sent, basis = call(
        start_kernel,
        "start",
        [((LEAF, OUT + 2 * DIM), BF16), ((N_DEV, 16, RANK), BF16), ((LEAF, RANK), BF16)],
        [SMEM, SMEM, SMEM] + [VMEM] * 5,
        (ridge, far_leaves, cluster_of, right_side, coords, leaf_perm, leaf_basis, transfer),
        [rows16],
        gmul,
    )
    arrived = exchanged(sent, "dev")
    neighbours = [from_behind(wc, -offset) for offset in NEAR]
    own_block, near = call(near_own_kernel, "near_own", [block, field], [VMEM], (wc,), flops=2 * gmul)

    sums, told, skeletons = call(
        sums_first_kernel,
        "sums_first",
        [((N_GRP, 16, RANK), BF16), ((N_DEV, RANK), F32), ((N_DEV, COLS * RANK), BF16)],
        [VMEM],
        (arrived,),
        [rows16, narrow],
        gmul // 4,
    )

    def through_owners(sums, skeletons):
        all_sums = exchanged(sums, "grp")
        (partners,) = call(
            partners_kernel, "partners", [((N_DEV, 16, RANK), BF16)], [VMEM] * 2, (skeletons, told), [rows16], gmul // 4
        )
        partners = exchanged(partners, "dev")
        (coupled,) = call(
            couple_kernel,
            "couple",
            [((N_DEV, COLS, RANK), F32)],
            [SMEM] + [VMEM] * 3,
            (far_clusters, all_sums, cluster_couplings, told),
            flops=gmul // 4,
        )
        return partners, exchanged(coupled, "dev")

    partners, coupled = through_owners(sums, skeletons)
    blocks = []
    for at in (0, 2):
        b1, b2, near = call(
            lambda *refs, at=at: near_pair_kernel(NEAR[at : at + 2], *refs),
            f"near_pair_{at}",
            pair_outs,
            [SMEM] + [VMEM] * 4,
            (near_list, wc, near, neighbours[at], neighbours[at + 1]),
            flops=4 * gmul,
        )
        blocks += [b1, b2]

    w, sent, d2, r1 = call(
        middle_kernel,
        "middle",
        [((LEAF, OUT), BF16), ((N_DEV, 8, RANK), BF16), field, field],
        [SMEM] + [VMEM] * 7,
        (ridge, partners, coupled, couplings, transfer, basis, near, right_side),
        [rows16, rows8],
        gmul,
    )
    arrived = exchanged(sent, "dev")
    neighbours = [from_behind(w, -offset) for offset in NEAR]
    (near,) = call(again_own_kernel, "again_own", [field], [VMEM] * 2, (w, own_block), flops=gmul)
    sums, skeletons = call(
        sums_kernel,
        "sums",
        [((N_GRP, 16, RANK), BF16), ((N_DEV, COLS * RANK), BF16)],
        [VMEM] * 2,
        (arrived, told),
        [rows8, narrow],
        gmul // 4,
    )
    partners, coupled = through_owners(sums, skeletons)
    for at in (0, 2):
        (near,) = call(
            lambda *refs, at=at: again_pair_kernel(NEAR[at : at + 2], *refs),
            f"again_pair_{at}",
            [field],
            [SMEM] + [VMEM] * 5,
            (near_list, near, neighbours[at], neighbours[at + 1], blocks[at], blocks[at + 1]),
            flops=2 * gmul,
        )
    return tuple(
        call(
            end_kernel,
            "end",
            [field, field],
            [SMEM] + [VMEM] * 9,
            (ridge, partners, coupled, couplings, transfer, basis, near, right_side, d2, r1),
            [rows16],
            gmul,
        )
    )


def solution(mesh):
    placed = (
        P(("grp", "dev"), None),
        P(("grp", "dev"), None),
        P(("grp", "dev"), None),
        P(("grp", "dev"), None),
        P(("grp", "dev"), None),
        P(("grp", "dev"), None, None, None),
        P(("grp", "dev"), None, None),
        P(("grp", "dev"), None),
        P(("grp", "dev")),
        P("grp", None),
        P("grp", None, None, None),
        P(),
    )
    return jax.shard_map(
        body,
        mesh=mesh,
        in_specs=placed,
        out_specs=(P(("grp", "dev"), None), P(("grp", "dev"), None)),
        check_vma=False,
    )
```

time: 300 us -> 200 us (0.67)
  the two profiles are of different devices: /device:TPU:4 before, /device:TPU:24 now
where the time goes in v1:
time: 200 us; the launch traced here: 199 us
  blocking collectives  64.8 us (32%)
  starting transfers between devices  61.1 us (31%)
  waiting for transfers between devices  40.8 us (20%)
  Pallas kernels  23 us (12%)
  local copies, waits for them, and re-layouts  6.78 us (3%)
  between operations  2.27 us (1%)
    all_to_all x4, blocking collectives, exchanged(): return lax.all_to_all(blocks, axis, split_axis=0, concat_axis=0, tiled=True)  64.8 us
    ppermute x8, starting transfers between devices, from_behind(): return lax.ppermute(shard, 'dev', pairs)  33.6 us
    all_to_all x4, starting transfers between devices, exchanged(): return lax.all_to_all(blocks, axis, split_axis=0, concat_axis=0, tiled=True)  27.5 us
    pallas_call x15, Pallas kernels, call(): pl.pallas_call(kernel, name=name, out_shape=shapes, in_specs=ins, out_spe...  23 us
    ppermute x8, waiting for transfers between devices, from_behind(): return lax.ppermute(shard, 'dev', pairs)  21.8 us
    all_to_all x4, waiting for transfers between devices, exchanged(): return lax.all_to_all(blocks, axis, split_axis=0, concat_axis=0, tiled=True)  19 us
    unnamed x41, local copies, waits for them, and re-layouts  6.78 us
  transfers between devices with their start and end apart: 12, of which 7 were waited for; matrix products, arithmetic and copies ran while one was open for 0% of the time, Pallas kernels for 7%

profile of v1, /device:TPU:24, one launch (start us, length us, event | category | flops | bytes accessed | tf_op | source)
XLA Modules:
  0.0 198.8 jit_solution(9228031483280960747)
XLA Ops:
  6.0 29.5 %all_to_all.40.arrived = bf16[64,16,128]{2,1,0:T(8,128)(2,1)S(1)} all-to-all(bf16[64,16,128]{2,1,0:T(8,128)(2,1)S(1)} %get-tuple-element.22), channel_id=1, replica_groups=mesh['grp'=8,'dev'=64] {'dev'}, dimensions={0} | all-to-all | bytes 524288 | tf_op jit(solution)/shard_map/all_to_all | solution.py:258
  35.8 9.5 %all_to_all.41.all_sums = bf16[8,16,128]{2,1,0:T(8,128)(2,1)S(1)} all-to-all(bf16[8,16,128]{2,1,0:T(8,128)(2,1)S(1)} %get-tuple-element.25), channel_id=1, replica_groups=mesh['grp'=8,'dev'=64] {'grp'}, dimensions={0} | all-to-all | bytes 65536 | tf_op jit(solution)/shard_map/all_to_all | solution.py:258
  47.3 6.5 %all-to-all-start.3 = ((f32[64,4,128]{2,1,0:T(4,128)}), f32[64,4,128]{2,1,0:T(4,128)S(1)}, u32[]{:S(2)}, u32[]{:S(2)}) async-start(f32[64,4,128]{2,1,0:T(4,128)} %couple.2), calls=%async_computation.3 | async-start | bytes 262144 | tf_op jit(solution)/shard_map/all_to_all | solution.py:258
  54.9 9.5 %all-to-all-done.3.coupled = f32[64,4,128]{2,1,0:T(4,128)S(1)} async-done(((f32[64,4,128]{2,1,0:T(4,128)}), f32[64,4,128]{2,1,0:T(4,128)S(1)}, u32[]{:S(2)}, u32[]{:S(2)}) %all-to-all-start.3) | async-done | bytes 131104 | tf_op jit(solution)/shard_map/all_to_all | solution.py:258
  64.4 7.0 %all-to-all-start.1 = ((bf16[64,16,128]{2,1,0:T(8,128)(2,1)}), bf16[64,16,128]{2,1,0:T(8,128)(2,1)S(1)}, u32[]{:S(2)}, u32[]{:S(2)}) async-start(bf16[64,16,128]{2,1,0:T(8,128)(2,1)} %partners.2), calls=%async_computation.1 | async-start | bytes 524288 | tf_op jit(solution)/shard_map/all_to_all | solution.py:258
  71.4 3.4 %collective-permute-start = (bf16[512,384]{1,0:T(8,128)(2,1)S(1)}, bf16[512,384]{1,0:T(8,128)(2,1)S(1)}, u32[]{:S(2)}, u32[]{:S(2)}) collective-permute-start(bf16[512,384]{1,0:T(8,128)(2,1)S(1)} %get-tuple-element.27.here.refs_1_), channel_id=1, source_target_pairs={{0,1},{1,2},{2,3},{3,4},{4,5},{5,6},{6,7},{7,8},{8,9},{9,10},{10,1... | collective-permute-start | bytes 1179656 | tf_op jit(solution)/shard_map/ppermute | solution.py:254
  74.8 4.6 %collective-permute-start.1 = (bf16[512,384]{1,0:T(8,128)(2,1)S(1)}, bf16[512,384]{1,0:T(8,128)(2,1)S(1)}, u32[]{:S(2)}, u32[]{:S(2)}) collective-permute-start(bf16[512,384]{1,0:T(8,128)(2,1)S(1)} %get-tuple-element.27.here.refs_1_), channel_id=1, source_target_pairs={{1,0},{2,1},{3,2},{4,3},{5,4},{6,5},{7,6},{8,7},{9,8},{10,9},{11,1... | collective-permute-start | bytes 1179656 | tf_op jit(solution)/shard_map/ppermute | solution.py:254
  79.4 2.2 %collective-permute-start.2 = (bf16[512,384]{1,0:T(8,128)(2,1)S(1)}, bf16[512,384]{1,0:T(8,128)(2,1)S(1)}, u32[]{:S(2)}, u32[]{:S(2)}) collective-permute-start(bf16[512,384]{1,0:T(8,128)(2,1)S(1)} %get-tuple-element.27.here.refs_1_), channel_id=1, source_target_pairs={{0,2},{1,3},{2,4},{3,5},{4,6},{5,7},{6,8},{7,9},{8,10},{9,11},{10,... | collective-permute-start | bytes 1179656 | tf_op jit(solution)/shard_map/ppermute | solution.py:254
  81.6 6.7 %collective-permute-start.3 = (bf16[512,384]{1,0:T(8,128)(2,1)S(1)}, bf16[512,384]{1,0:T(8,128)(2,1)S(1)}, u32[]{:S(2)}, u32[]{:S(2)}) collective-permute-start(bf16[512,384]{1,0:T(8,128)(2,1)S(1)} %get-tuple-element.27.here.refs_1_), channel_id=1, source_target_pairs={{2,0},{3,1},{4,2},{5,3},{6,4},{7,5},{8,6},{9,7},{10,8},{11,9},{12,... | collective-permute-start | bytes 1179656 | tf_op jit(solution)/shard_map/ppermute | solution.py:254
  89.5 6.9 %collective-permute-done.refs_3_ = bf16[512,384]{1,0:T(8,128)(2,1)S(1)} collective-permute-done((bf16[512,384]{1,0:T(8,128)(2,1)S(1)}, bf16[512,384]{1,0:T(8,128)(2,1)S(1)}, u32[]{:S(2)}, u32[]{:S(2)}) %collective-permute-start) | collective-permute-done | bytes 393248 | tf_op jit(solution)/shard_map/ppermute | solution.py:254
  96.4 3.5 %near_pair_0.1 = (bf16[512,512]{1,0:T(8,128)(2,1)S(1)}, bf16[512,512]{1,0:T(8,128)(2,1)S(1)}, f32[512,256]{1,0:T(8,128)S(1)}) custom-call(s32[1,4]{1,0:T(1,128)S(1)} %copy-done.18, bf16[512,384]{1,0:T(8,128)(2,1)S(1)} %get-tuple-element.27.here.refs_1_, f32[512,256]{1,0:T(8,128)S(1)} %get-tuple-element.28.refs_2_, ...), custom_call_target="tpu_custom_call" | custom-call | flops 536870912 | tf_op jit(solution)/shard_map/near_pair_0/pallas_call | solution.py:29
  101.5 6.2 %collective-permute-done.3.refs_4_ = bf16[512,384]{1,0:T(8,128)(2,1)S(1)} collective-permute-done((bf16[512,384]{1,0:T(8,128)(2,1)S(1)}, bf16[512,384]{1,0:T(8,128)(2,1)S(1)}, u32[]{:S(2)}, u32[]{:S(2)}) %collective-permute-start.3) | collective-permute-done | bytes 393248 | tf_op jit(solution)/shard_map/ppermute | solution.py:254
  107.7 3.5 %near_pair_2.1 = (bf16[512,512]{1,0:T(8,128)(2,1)S(1)}, bf16[512,512]{1,0:T(8,128)(2,1)S(1)}, f32[512,256]{1,0:T(8,128)S(1)}) custom-call(s32[1,4]{1,0:T(1,128)S(1)} %copy-done.18, bf16[512,384]{1,0:T(8,128)(2,1)S(1)} %get-tuple-element.27.here.refs_1_, f32[512,256]{1,0:T(8,128)S(1)} %get-tuple-element.29.refs_2_, ...), custom_call_target="tpu_custom_call" | custom-call | flops 536870912 | tf_op jit(solution)/shard_map/near_pair_2/pallas_call | solution.py:29
  115.1 17.2 %all_to_all.42.arrived = bf16[64,8,128]{2,1,0:T(8,128)(2,1)S(1)} all-to-all(bf16[64,8,128]{2,1,0:T(8,128)(2,1)S(1)} %get-tuple-element.31), channel_id=1, replica_groups=mesh['grp'=8,'dev'=64] {'dev'}, dimensions={0} | all-to-all | bytes 262144 | tf_op jit(solution)/shard_map/all_to_all | solution.py:258
  132.5 8.7 %all_to_all.43.all_sums = bf16[8,16,128]{2,1,0:T(8,128)(2,1)S(1)} all-to-all(bf16[8,16,128]{2,1,0:T(8,128)(2,1)S(1)} %get-tuple-element.33), channel_id=1, replica_groups=mesh['grp'=8,'dev'=64] {'grp'}, dimensions={0} | all-to-all | bytes 65536 | tf_op jit(solution)/shard_map/all_to_all | solution.py:258
  143.2 7.0 %all-to-all-start.7 = ((f32[64,4,128]{2,1,0:T(4,128)}), f32[64,4,128]{2,1,0:T(4,128)S(1)}, u32[]{:S(2)}, u32[]{:S(2)}) async-start(f32[64,4,128]{2,1,0:T(4,128)} %couple.3), calls=%async_computation.7 | async-start | bytes 262144 | tf_op jit(solution)/shard_map/all_to_all | solution.py:258
  151.3 9.5 %all-to-all-done.7.coupled = f32[64,4,128]{2,1,0:T(4,128)S(1)} async-done(((f32[64,4,128]{2,1,0:T(4,128)}), f32[64,4,128]{2,1,0:T(4,128)S(1)}, u32[]{:S(2)}, u32[]{:S(2)}) %all-to-all-start.7) | async-done | bytes 131104 | tf_op jit(solution)/shard_map/all_to_all | solution.py:258
  160.8 7.0 %all-to-all-start.5 = ((bf16[64,16,128]{2,1,0:T(8,128)(2,1)}), bf16[64,16,128]{2,1,0:T(8,128)(2,1)S(1)}, u32[]{:S(2)}, u32[]{:S(2)}) async-start(bf16[64,16,128]{2,1,0:T(8,128)(2,1)} %partners.3), calls=%async_computation.5 | async-start | bytes 524288 | tf_op jit(solution)/shard_map/all_to_all | solution.py:258
  167.8 3.4 %collective-permute-start.4 = (bf16[512,256]{1,0:T(8,128)(2,1)}, bf16[512,256]{1,0:T(8,128)(2,1)S(1)}, u32[]{:S(2)}, u32[]{:S(2)}) collective-permute-start(bf16[512,256]{1,0:T(8,128)(2,1)} %get-tuple-element.34.w), channel_id=1, source_target_pairs={{0,1},{1,2},{2,3},{3,4},{4,5},{5,6},{6,7},{7,8},{8,9},{9,10},{10,1... | collective-permute-start | bytes 786440 | tf_op jit(solution)/shard_map/ppermute | solution.py:254
  171.2 4.6 %collective-permute-start.5 = (bf16[512,256]{1,0:T(8,128)(2,1)}, bf16[512,256]{1,0:T(8,128)(2,1)S(1)}, u32[]{:S(2)}, u32[]{:S(2)}) collective-permute-start(bf16[512,256]{1,0:T(8,128)(2,1)} %get-tuple-element.34.w), channel_id=1, source_target_pairs={{1,0},{2,1},{3,2},{4,3},{5,4},{6,5},{7,6},{8,7},{9,8},{10,9},{11,1... | collective-permute-start | bytes 786440 | tf_op jit(solution)/shard_map/ppermute | solution.py:254
  175.8 2.2 %collective-permute-start.6 = (bf16[512,256]{1,0:T(8,128)(2,1)}, bf16[512,256]{1,0:T(8,128)(2,1)S(1)}, u32[]{:S(2)}, u32[]{:S(2)}) collective-permute-start(bf16[512,256]{1,0:T(8,128)(2,1)} %get-tuple-element.34.w), channel_id=1, source_target_pairs={{0,2},{1,3},{2,4},{3,5},{4,6},{5,7},{6,8},{7,9},{8,10},{9,11},{10,... | collective-permute-start | bytes 786440 | tf_op jit(solution)/shard_map/ppermute | solution.py:254
  178.0 6.7 %collective-permute-start.7 = (bf16[512,256]{1,0:T(8,128)(2,1)}, bf16[512,256]{1,0:T(8,128)(2,1)S(1)}, u32[]{:S(2)}, u32[]{:S(2)}) collective-permute-start(bf16[512,256]{1,0:T(8,128)(2,1)} %get-tuple-element.34.w), channel_id=1, source_target_pairs={{2,0},{3,1},{4,2},{5,3},{6,4},{7,5},{8,6},{9,7},{10,8},{11,9},{12,... | collective-permute-start | bytes 786440 | tf_op jit(solution)/shard_map/ppermute | solution.py:254
  187.4 4.1 %collective-permute-done.6.refs_2_ = bf16[512,256]{1,0:T(8,128)(2,1)S(1)} collective-permute-done((bf16[512,256]{1,0:T(8,128)(2,1)}, bf16[512,256]{1,0:T(8,128)(2,1)S(1)}, u32[]{:S(2)}, u32[]{:S(2)}) %collective-permute-start.6) | collective-permute-done | bytes 262176 | tf_op jit(solution)/shard_map/ppermute | solution.py:254
  191.5 4.5 %collective-permute-done.7.refs_3_ = bf16[512,256]{1,0:T(8,128)(2,1)S(1)} collective-permute-done((bf16[512,256]{1,0:T(8,128)(2,1)}, bf16[512,256]{1,0:T(8,128)(2,1)S(1)}, u32[]{:S(2)}, u32[]{:S(2)}) %collective-permute-start.7) | collective-permute-done | bytes 262176 | tf_op jit(solution)/shard_map/ppermute | solution.py:254
  (60 shorter events, 22.9 us)
Async XLA Ops:
  1.3 1.8 copy-start.14
  1.3 1.8 copy-start.15
  6.0 39.3 %copy-start.2 = (bf16[4,4,128,128]{3,2,1,0:T(8,128)(2,1)S(1)}, bf16[4,4,128,128]{3,2,1,0:T(8,128)(2,1)}, u32[]{:S(2)}) copy-start(bf16[4,4,128,128]{3,2,1,0:T(8,128)(2,1)} %blocks.3) | copy-start | bytes 1572868
  35.8 9.6 %copy-start.16 = (s32[4,4]{1,0:T(4,128)S(1)}, s32[4,4]{1,0:T(4,128)}, u32[]{:S(2)}) copy-start(s32[4,4]{1,0:T(4,128)} %far_clusters.3) | copy-start | bytes 196
  47.3 17.0 %all-to-all-start.3 = ((f32[64,4,128]{2,1,0:T(4,128)}), f32[64,4,128]{2,1,0:T(4,128)S(1)}, u32[]{:S(2)}, u32[]{:S(2)}) async-start(f32[64,4,128]{2,1,0:T(4,128)} %couple.2), calls=%async_computation.3 | async-start | bytes 262144 | tf_op jit(solution)/shard_map/all_to_all | solution.py:258
  64.4 48.4 %all-to-all-start.1 = ((bf16[64,16,128]{2,1,0:T(8,128)(2,1)}), bf16[64,16,128]{2,1,0:T(8,128)(2,1)S(1)}, u32[]{:S(2)}, u32[]{:S(2)}) async-start(bf16[64,16,128]{2,1,0:T(8,128)(2,1)} %partners.2), calls=%async_computation.1 | async-start | bytes 524288 | tf_op jit(solution)/shard_map/all_to_all | solution.py:258
  71.4 24.9 %collective-permute-start = (bf16[512,384]{1,0:T(8,128)(2,1)S(1)}, bf16[512,384]{1,0:T(8,128)(2,1)S(1)}, u32[]{:S(2)}, u32[]{:S(2)}) collective-permute-start(bf16[512,384]{1,0:T(8,128)(2,1)S(1)} %get-tuple-element.27.here.refs_1_), channel_id=1, source_target_pairs={{0,1},{1,2},{2,3},{3,4},{4,5},{5,6},{6,7},{7,8},{8,9},{9,10},{10,1... | collective-permute-start | bytes 1179656 | tf_op jit(solution)/shard_map/ppermute | solution.py:254
  74.8 21.6 %collective-permute-start.1 = (bf16[512,384]{1,0:T(8,128)(2,1)S(1)}, bf16[512,384]{1,0:T(8,128)(2,1)S(1)}, u32[]{:S(2)}, u32[]{:S(2)}) collective-permute-start(bf16[512,384]{1,0:T(8,128)(2,1)S(1)} %get-tuple-element.27.here.refs_1_), channel_id=1, source_target_pairs={{1,0},{2,1},{3,2},{4,3},{5,4},{6,5},{7,6},{8,7},{9,8},{10,9},{11,1... | collective-permute-start | bytes 1179656 | tf_op jit(solution)/shard_map/ppermute | solution.py:254
  79.4 22.1 %collective-permute-start.2 = (bf16[512,384]{1,0:T(8,128)(2,1)S(1)}, bf16[512,384]{1,0:T(8,128)(2,1)S(1)}, u32[]{:S(2)}, u32[]{:S(2)}) collective-permute-start(bf16[512,384]{1,0:T(8,128)(2,1)S(1)} %get-tuple-element.27.here.refs_1_), channel_id=1, source_target_pairs={{0,2},{1,3},{2,4},{3,5},{4,6},{5,7},{6,8},{7,9},{8,10},{9,11},{10,... | collective-permute-start | bytes 1179656 | tf_op jit(solution)/shard_map/ppermute | solution.py:254
  81.6 26.1 %collective-permute-start.3 = (bf16[512,384]{1,0:T(8,128)(2,1)S(1)}, bf16[512,384]{1,0:T(8,128)(2,1)S(1)}, u32[]{:S(2)}, u32[]{:S(2)}) collective-permute-start(bf16[512,384]{1,0:T(8,128)(2,1)S(1)} %get-tuple-element.27.here.refs_1_), channel_id=1, source_target_pairs={{2,0},{3,1},{4,2},{5,3},{6,4},{7,5},{8,6},{9,7},{10,8},{11,9},{12,... | collective-permute-start | bytes 1179656 | tf_op jit(solution)/shard_map/ppermute | solution.py:254
  89.5 6.9 %copy-start.18 = (s32[1,4]{1,0:T(1,128)S(1)}, s32[1,4]{1,0:T(1,128)}, u32[]{:S(2)}) copy-start(s32[1,4]{1,0:T(1,128)} %refs_0_.7) | copy-start | bytes 52
  107.7 5.2 %copy-start.1 = (f32[512,256]{1,0:T(8,128)S(1)}, f32[512,256]{1,0:T(8,128)}, u32[]{:S(2)}) copy-start(f32[512,256]{1,0:T(8,128)} %rs.5) | copy-start | bytes 1572868
  107.7 5.2 %copy-start.3 = (bf16[1,4,128,128]{3,2,1,0:T(8,128)(2,1)S(1)}, bf16[1,4,128,128]{3,2,1,0:T(8,128)(2,1)}, u32[]{:S(2)}) copy-start(bf16[1,4,128,128]{3,2,1,0:T(8,128)(2,1)} %couplings.3) | copy-start | bytes 393220
  143.2 17.6 %all-to-all-start.7 = ((f32[64,4,128]{2,1,0:T(4,128)}), f32[64,4,128]{2,1,0:T(4,128)S(1)}, u32[]{:S(2)}, u32[]{:S(2)}) async-start(f32[64,4,128]{2,1,0:T(4,128)} %couple.3), calls=%async_computation.7 | async-start | bytes 262144 | tf_op jit(solution)/shard_map/all_to_all | solution.py:258
  160.8 36.4 %all-to-all-start.5 = ((bf16[64,16,128]{2,1,0:T(8,128)(2,1)}), bf16[64,16,128]{2,1,0:T(8,128)(2,1)S(1)}, u32[]{:S(2)}, u32[]{:S(2)}) async-start(bf16[64,16,128]{2,1,0:T(8,128)(2,1)} %partners.3), calls=%async_computation.5 | async-start | bytes 524288 | tf_op jit(solution)/shard_map/all_to_all | solution.py:258
  167.8 18.4 %collective-permute-start.4 = (bf16[512,256]{1,0:T(8,128)(2,1)}, bf16[512,256]{1,0:T(8,128)(2,1)S(1)}, u32[]{:S(2)}, u32[]{:S(2)}) collective-permute-start(bf16[512,256]{1,0:T(8,128)(2,1)} %get-tuple-element.34.w), channel_id=1, source_target_pairs={{0,1},{1,2},{2,3},{3,4},{4,5},{5,6},{6,7},{7,8},{8,9},{9,10},{10,1... | collective-permute-start | bytes 786440 | tf_op jit(solution)/shard_map/ppermute | solution.py:254
  171.2 15.0 %collective-permute-start.5 = (bf16[512,256]{1,0:T(8,128)(2,1)}, bf16[512,256]{1,0:T(8,128)(2,1)S(1)}, u32[]{:S(2)}, u32[]{:S(2)}) collective-permute-start(bf16[512,256]{1,0:T(8,128)(2,1)} %get-tuple-element.34.w), channel_id=1, source_target_pairs={{1,0},{2,1},{3,2},{4,3},{5,4},{6,5},{7,6},{8,7},{9,8},{10,9},{11,1... | collective-permute-start | bytes 786440 | tf_op jit(solution)/shard_map/ppermute | solution.py:254
  175.8 15.7 %collective-permute-start.6 = (bf16[512,256]{1,0:T(8,128)(2,1)}, bf16[512,256]{1,0:T(8,128)(2,1)S(1)}, u32[]{:S(2)}, u32[]{:S(2)}) collective-permute-start(bf16[512,256]{1,0:T(8,128)(2,1)} %get-tuple-element.34.w), channel_id=1, source_target_pairs={{0,2},{1,3},{2,4},{3,5},{4,6},{5,7},{6,8},{7,9},{8,10},{9,11},{10,... | collective-permute-start | bytes 786440 | tf_op jit(solution)/shard_map/ppermute | solution.py:254
  178.0 18.0 %collective-permute-start.7 = (bf16[512,256]{1,0:T(8,128)(2,1)}, bf16[512,256]{1,0:T(8,128)(2,1)S(1)}, u32[]{:S(2)}, u32[]{:S(2)}) collective-permute-start(bf16[512,256]{1,0:T(8,128)(2,1)} %get-tuple-element.34.w), channel_id=1, source_target_pairs={{2,0},{3,1},{4,2},{5,3},{6,4},{7,5},{8,6},{9,7},{10,8},{11,9},{12,... | collective-permute-start | bytes 786440 | tf_op jit(solution)/shard_map/ppermute | solution.py:254
  184.6 1.5 copy-start.11
  184.7 1.5 copy-start.13
  186.2 9.8 %copy-start.7 = (bf16[512,512]{1,0:T(8,128)(2,1)S(1)}, bf16[512,512]{1,0:T(8,128)(2,1)}, u32[]{:S(2)}) copy-start(bf16[512,512]{1,0:T(8,128)(2,1)} %copy-done.6) | copy-start | bytes 1572868
  186.2 9.8 %copy-start.9 = (bf16[512,512]{1,0:T(8,128)(2,1)S(1)}, bf16[512,512]{1,0:T(8,128)(2,1)}, u32[]{:S(2)}) copy-start(bf16[512,512]{1,0:T(8,128)(2,1)} %copy-done.8) | copy-start | bytes 1572868
  196.0 1.2 copy-start.5
  (8 other events, 6.4 us)

commit v2 on v1

--- a/solution.py
+++ b/solution.py
@@ -17,6 +17,7 @@
 F32, BF16 = jnp.float32, jnp.bfloat16
 VMEM = pl.BlockSpec(memory_space=pltpu.VMEM)
 SMEM = pl.BlockSpec(memory_space=pltpu.SMEM)
+ANY = pl.BlockSpec(memory_space=pl.ANY)
 LIMIT = 48 * 2**20
 
 
@@ -76,10 +77,12 @@
         told = jnp.where(lane == k, (far[0, k] % N_DEV).astype(F32), told)
     staged[pl.ds(8, N_DEV, stride=16), :] = told
     sent[...] = staged[...].astype(BF16).reshape(N_DEV, 16, RANK)
-    wc[:, :OUT] = values
+    wc[:LEAF] = values
     high = coords[...].astype(BF16)
     low = (coords[...] - high.astype(F32)).astype(BF16)
-    wc[:, OUT : OUT + 2 * DIM] = jnp.concatenate([high, low], axis=1)
+    parts = jnp.concatenate([high, low], axis=0)
+    wc[LEAF : LEAF + 2 * DIM] = parts[:, :OUT]
+    wc[LEAF + 2 * DIM :] = parts[:, OUT:]
 
 
 def owner_sums(staged, rows, told, sums, narrow):
@@ -96,7 +99,7 @@
         sums[g] = out
 
 
-def sums_first_kernel(arrived, sums, told, skeletons, staged, narrow):
+def sums_first_kernel(arrived, _, sums, told, skeletons, staged, narrow):
     staged[...] = arrived[...].astype(F32).reshape(N_DEV * 16, RANK)
     told[...] = staged[pl.ds(8, N_DEV, stride=16), :]
     owner_sums(staged, 16, told[...], sums, narrow)
@@ -105,7 +108,7 @@
     ).astype(BF16)
 
 
-def sums_kernel(arrived, told, sums, skeletons, staged, narrow):
+def sums_kernel(arrived, told, _, sums, skeletons, staged, narrow):
     staged[...] = arrived[...].astype(F32).reshape(N_DEV * 8, RANK)
     owner_sums(staged, 8, told[...], sums, narrow)
     skeletons[...] = jnp.concatenate(
@@ -127,7 +130,7 @@
     sent[...] = staged[...].astype(BF16).reshape(N_DEV, 16, RANK)
 
 
-def couple_kernel(far_clusters, all_sums, blocks, told, sent):
+def couple_kernel(far_clusters, all_sums, blocks, told, partners, _, sent, staged):
     rows = COLS * CPG
     sums = all_sums[...].reshape(N_GRP * rows, RANK)
     row = lax.broadcasted_iota(jnp.int32, (rows, N_GRP * rows), 0)
@@ -153,26 +156,27 @@
         [jnp.where(lane == told[:, FAR1 : FAR1 + 1] + CPG * i, 1.0, 0.0) for i in range(COLS)], axis=0
     ).astype(BF16)
     out = dot(pick, coupled)
+    staged[:, :16, :] = partners[...].astype(F32)
+    staged[:, 16:, :] = jnp.zeros((N_DEV, 8, RANK), F32)
     for i in range(COLS):
-        sent[:, i, :] = out[N_DEV * i : N_DEV * (i + 1)]
-
-
-def far_field(partners, coupled, couplings, transfer, basis, staged):
-    staged[...] = partners[...].astype(F32).reshape(N_DEV * 16, RANK)
+        staged[:, 16 + i, :] = out[N_DEV * i : N_DEV * (i + 1)]
+    sent[...] = staged[...].astype(BF16)
+
+
+def far_field(arrived, couplings, transfer, basis, staged):
+    staged[...] = arrived[...].astype(F32).reshape(N_DEV * 24, RANK)
     local = jnp.zeros((RANK, OUT), F32)
-    for k in range(FAR1):
+    for k in range(FAR1 + 1):
         skeleton = jnp.concatenate(
-            [staged[pl.ds(COLS * k + i, N_DEV, stride=16), :] for i in range(COLS)], axis=0
+            [staged[pl.ds(COLS * k + i, N_DEV, stride=24), :] for i in range(COLS)], axis=0
         ).astype(BF16)
-        local += dot(couplings[0, k], skeleton, ((1,), (1,)))
-    downward = jnp.concatenate([coupled[:, i, :] for i in range(COLS)], axis=0).astype(BF16)
-    local += dot(transfer[0], downward, ((1,), (1,)))
+        local += dot(couplings[0, k] if k < FAR1 else transfer[0], skeleton, ((1,), (1,)))
     return dot(basis[...], local.astype(BF16))
 
 
-def middle_kernel(ridge, partners, coupled, couplings, transfer, basis, near, rs, w, sent, d2, r1, staged, staged_out):
+def middle_kernel(ridge, arrived, couplings, transfer, basis, near, rs, w, sent, d2, r1, staged, staged_out):
     ridge, centre, (mul, add), _ = chebyshev(ridge[0])
-    far = far_field(partners, coupled, couplings, transfer, basis, staged)
+    far = far_field(arrived, couplings, transfer, basis, staged)
     d1 = rs[...] / centre
     residual = rs[...] - (ridge * d1 + (near[...] + far))
     direction = mul * d1 + add * residual
@@ -184,18 +188,20 @@
     sent[...] = staged_out[...].astype(BF16).reshape(N_DEV, 8, RANK)
 
 
-def end_kernel(ridge, partners, coupled, couplings, transfer, basis, near, rs, d2, r1, solution, residual, staged):
+def end_kernel(ridge, arrived, couplings, transfer, basis, near, rs, d2, r1, solution, residual, staged):
     ridge, centre, _, (mul, add) = chebyshev(ridge[0])
-    far = far_field(partners, coupled, couplings, transfer, basis, staged)
+    far = far_field(arrived, couplings, transfer, basis, staged)
     r2 = r1[...] - (ridge * d2[...] + (near[...] + far))
     residual[...] = r2
     d3 = mul * d2[...] + add * r2
     solution[...] = rs[...] / centre + d2[...] + d3
 
 
-def norms(points):
-    square = jnp.sum(points * points, axis=1, keepdims=True) * KERNEL_LOG2
-    return square, jnp.broadcast_to(square, (LEAF, RANK)).T[:1]
+def coordinates(wc):
+    parts = jnp.concatenate([wc[LEAF : LEAF + 2 * DIM], wc[LEAF + 2 * DIM :]], axis=1)
+    high, low = parts[:DIM], parts[DIM:]
+    points = high.astype(F32) + low.astype(F32)
+    return high, low, jnp.sum(points * points, axis=0, keepdims=True) * KERNEL_LOG2
 
 
 def listed(near_list, offset):
@@ -207,19 +213,18 @@
 
 
 def block_times(here, there, block, total, fresh):
-    high, low = here[:, OUT : OUT + DIM], here[:, OUT + DIM : OUT + 2 * DIM]
-    left = jnp.concatenate([high, high, low, low], axis=1)
-    column, _ = norms(high.astype(F32) + low.astype(F32))
-    high, low = there[:, OUT : OUT + DIM], there[:, OUT + DIM : OUT + 2 * DIM]
-    right = jnp.concatenate([high, low, high, low], axis=1)
-    _, across = norms(high.astype(F32) + low.astype(F32))
+    high, low, norm = coordinates(here)
+    left = jnp.concatenate([high, high, low, low], axis=0)
+    column = jnp.broadcast_to(norm, (RANK, LEAF)).T[:, :1]
+    high, low, across = coordinates(there)
+    right = jnp.concatenate([high, low, high, low], axis=0)
     step = 128
     for r in range(0, LEAF, step):
         part = slice(r, r + step)
-        inner = dot(left[part], right, ((1,), (1,)))
+        inner = dot(left[:, part], right, ((0,), (0,)))
         entries = jnp.exp2((column[part] + across) - (2.0 * KERNEL_LOG2) * inner).astype(BF16)
         block[part] = entries
-        product = dot(entries, there[:, :OUT])
+        product = dot(entries, there[:LEAF])
         total[part] = product if fresh else total[part] + product
 
 
@@ -275,103 +280,115 @@
     ridge = ridge_weight.reshape(1)
     field = ((LEAF, OUT), F32)
     block = ((LEAF, LEAF), BF16)
+    rows24 = pltpu.VMEM((N_DEV * 24, RANK), F32)
     rows16 = pltpu.VMEM((N_DEV * 16, RANK), F32)
     rows8 = pltpu.VMEM((N_DEV * 8, RANK), F32)
     narrow = pltpu.VMEM((COLS * CPG, RANK), F32)
-    pair_outs = [block, block, field]
     gmul = 2 * LEAF * LEAF * OUT
 
     wc, sent, basis = call(
         start_kernel,
         "start",
-        [((LEAF, OUT + 2 * DIM), BF16), ((N_DEV, 16, RANK), BF16), ((LEAF, RANK), BF16)],
+        [((LEAF + 4 * DIM, OUT), BF16), ((N_DEV, 16, RANK), BF16), ((LEAF, RANK), BF16)],
         [SMEM, SMEM, SMEM] + [VMEM] * 5,
-        (ridge, far_leaves, cluster_of, right_side, coords, leaf_perm, leaf_basis, transfer),
+        (ridge, far_leaves, cluster_of, right_side, coords.T, leaf_perm, leaf_basis, transfer),
         [rows16],
         gmul,
     )
     arrived = exchanged(sent, "dev")
-    neighbours = [from_behind(wc, -offset) for offset in NEAR]
+    behind, ahead = from_behind(wc, 1), from_behind(wc, -1)
     own_block, near = call(near_own_kernel, "near_own", [block, field], [VMEM], (wc,), flops=2 * gmul)
-
     sums, told, skeletons = call(
         sums_first_kernel,
         "sums_first",
         [((N_GRP, 16, RANK), BF16), ((N_DEV, RANK), F32), ((N_DEV, COLS * RANK), BF16)],
-        [VMEM],
-        (arrived,),
+        [VMEM, ANY],
+        (arrived, near),
         [rows16, narrow],
         gmul // 4,
     )
 
-    def through_owners(sums, skeletons):
-        all_sums = exchanged(sums, "grp")
+    def near_first(at, near, first, second):
+        return call(
+            lambda *refs: near_pair_kernel(NEAR[at : at + 2], *refs),
+            f"near_pair_{at}",
+            [block, block, field],
+            [SMEM] + [VMEM] * 4,
+            (near_list, wc, near, first, second),
+            flops=4 * gmul,
+        )
+
+    def near_again(at, near, first, second):
+        return call(
+            lambda *refs: again_pair_kernel(NEAR[at : at + 2], *refs),
+            f"again_pair_{at}",
+            [field],
+            [SMEM] + [VMEM] * 5,
+            (near_list, near, first, second, blocks[at], blocks[at + 1]),
+            flops=2 * gmul,
+        )
+
+    def partners_of(skeletons):
         (partners,) = call(
             partners_kernel, "partners", [((N_DEV, 16, RANK), BF16)], [VMEM] * 2, (skeletons, told), [rows16], gmul // 4
         )
-        partners = exchanged(partners, "dev")
-        (coupled,) = call(
+        return partners
+
+    def through_owners(all_sums, partners, near):
+        (sent,) = call(
             couple_kernel,
             "couple",
-            [((N_DEV, COLS, RANK), F32)],
-            [SMEM] + [VMEM] * 3,
-            (far_clusters, all_sums, cluster_couplings, told),
-            flops=gmul // 4,
+            [((N_DEV, 24, RANK), BF16)],
+            [SMEM] + [VMEM] * 4 + [ANY],
+            (far_clusters, all_sums, cluster_couplings, told, partners, near),
+            [pltpu.VMEM((N_DEV, 24, RANK), F32)],
+            gmul // 4,
         )
-        return partners, exchanged(coupled, "dev")
-
-    partners, coupled = through_owners(sums, skeletons)
-    blocks = []
-    for at in (0, 2):
-        b1, b2, near = call(
-            lambda *refs, at=at: near_pair_kernel(NEAR[at : at + 2], *refs),
-            f"near_pair_{at}",
-            pair_outs,
-            [SMEM] + [VMEM] * 4,
-            (near_list, wc, near, neighbours[at], neighbours[at + 1]),
-            flops=4 * gmul,
-        )
-        blocks += [b1, b2]
+        return exchanged(sent, "dev")
+
+    all_sums = exchanged(sums, "grp")
+    partners = partners_of(skeletons)
+    blocks = [None] * len(NEAR)
+    blocks[0], blocks[1], near = near_first(0, near, behind, ahead)
+    arrived = through_owners(all_sums, partners, near)
+    behind, ahead = from_behind(behind, 1), from_behind(ahead, -1)
+    blocks[2], blocks[3], near = near_first(2, near, behind, ahead)
 
     w, sent, d2, r1 = call(
         middle_kernel,
         "middle",
         [((LEAF, OUT), BF16), ((N_DEV, 8, RANK), BF16), field, field],
-        [SMEM] + [VMEM] * 7,
-        (ridge, partners, coupled, couplings, transfer, basis, near, right_side),
-        [rows16, rows8],
+        [SMEM] + [VMEM] * 6,
+        (ridge, arrived, couplings, transfer, basis, near, right_side),
+        [rows24, rows8],
         gmul,
     )
     arrived = exchanged(sent, "dev")
-    neighbours = [from_behind(w, -offset) for offset in NEAR]
+    behind, ahead = from_behind(w, 1), from_behind(w, -1)
     (near,) = call(again_own_kernel, "again_own", [field], [VMEM] * 2, (w, own_block), flops=gmul)
     sums, skeletons = call(
         sums_kernel,
         "sums",
         [((N_GRP, 16, RANK), BF16), ((N_DEV, COLS * RANK), BF16)],
-        [VMEM] * 2,
-        (arrived, told),
+        [VMEM, VMEM, ANY],
+        (arrived, told, near),
         [rows8, narrow],
         gmul // 4,
     )
-    partners, coupled = through_owners(sums, skeletons)
-    for at in (0, 2):
-        (near,) = call(
-            lambda *refs, at=at: again_pair_kernel(NEAR[at : at + 2], *refs),
-            f"again_pair_{at}",
-            [field],
-            [SMEM] + [VMEM] * 5,
-            (near_list, near, neighbours[at], neighbours[at + 1], blocks[at], blocks[at + 1]),
-            flops=2 * gmul,
-        )
+    all_sums = exchanged(sums, "grp")
+    partners = partners_of(skeletons)
+    (near,) = near_again(0, near, behind, ahead)
+    arrived = through_owners(all_sums, partners, near)
+    behind, ahead = from_behind(behind, 1), from_behind(ahead, -1)
+    (near,) = near_again(2, near, behind, ahead)
     return tuple(
         call(
             end_kernel,
             "end",
             [field, field],
-            [SMEM] + [VMEM] * 9,
-            (ridge, partners, coupled, couplings, transfer, basis, near, right_side, d2, r1),
-            [rows16],
+            [SMEM] + [VMEM] * 8,
+            (ridge, arrived, couplings, transfer, basis, near, right_side, d2, r1),
+            [rows24],
             gmul,
         )
     )

time: 200 us -> 157 us (0.79)
  blocking collectives: 64.8 us -> 0 us
  starting transfers between devices: 61.1 us -> 85.6 us
  local copies, waits for them, and re-layouts: 6.78 us -> 16.7 us
  Pallas kernels: 23 us -> 15.9 us
  waiting for transfers between devices: 40.8 us -> 35.3 us
    all_to_all x4 -> x0, blocking collectives: 64.8 us -> none  [exchanged(): return lax.all_to_all(blocks, axis, split_axis=0, concat_axis=0, tiled=True)]
    all_to_all x4 -> x6, starting transfers between devices: 27.5 us -> 53.7 us  [exchanged(): return lax.all_to_all(blocks, axis, split_axis=0, concat_axis=0, tiled=True)]
    unnamed x41 -> x58, local copies, waits for them, and re-layouts: 6.78 us -> 16.7 us
    all_to_all x4 -> x6, waiting for transfers between devices: 19 us -> 11.8 us  [exchanged(): return lax.all_to_all(blocks, axis, split_axis=0, concat_axis=0, tiled=True)]
    pallas_call x15, Pallas kernels: 23 us -> 15.9 us  [call(): pl.pallas_call(kernel, name=name, out_shape=shapes, in_specs=ins, out_spe...]
  transfers between devices with their start and end apart: 12 -> 14, of which waited for: 7 -> 6; matrix products, arithmetic and copies ran while one was open for 0% -> 0% of each run, Pallas kernels for 7% -> 4%
where the time goes in v2:
time: 157 us; the launch traced here: 156 us
  starting transfers between devices  85.6 us (55%)
  waiting for transfers between devices  35.3 us (22%)
  local copies, waits for them, and re-layouts  16.7 us (11%)
  Pallas kernels  15.9 us (10%)
  between operations  2.25 us (1%)
    all_to_all x6, starting transfers between devices, exchanged(): return lax.all_to_all(blocks, axis, split_axis=0, concat_axis=0, tiled=True)  53.7 us
    ppermute x8, starting transfers between devices, from_behind(): return lax.ppermute(shard, 'dev', pairs)  31.9 us
    ppermute x8, waiting for transfers between devices, from_behind(): return lax.ppermute(shard, 'dev', pairs)  23.5 us
    unnamed x58, local copies, waits for them, and re-layouts  16.7 us
    pallas_call x15, Pallas kernels, call(): pl.pallas_call(kernel, name=name, out_shape=shapes, in_specs=ins, out_spe...  15.9 us
    all_to_all x6, waiting for transfers between devices, exchanged(): return lax.all_to_all(blocks, axis, split_axis=0, concat_axis=0, tiled=True)  11.8 us
  transfers between devices with their start and end apart: 14, of which 6 were waited for; matrix products, arithmetic and copies ran while one was open for 0% of the time, Pallas kernels for 4%

profile of v2, /device:TPU:24, one launch (start us, length us, event | category | flops | bytes accessed | tf_op | source)
XLA Modules:
  0.0 155.7 jit_solution(11959811256670544045)
XLA Ops:
  6.2 2.0 %start.1 = (bf16[768,256]{1,0:T(8,128)(2,1)S(1)}, bf16[64,16,128]{2,1,0:T(8,128)(2,1)}, bf16[512,128]{1,0:T(8,128)(2,1)S(1)}) custom-call(f32[1]{0:T(128)} %bitcast.2.ridge, s32[1,4]{1,0:T(1,128)S(1)} %copy-done.25, s32[1]{0:T(128)S(6)} %copy.14.cluster, f32[512,256]{1,0:T(8,128)S(1)} %copy-done, f32[64,512]{1,0:T(8,128)S(1)} %bitcast.5, ...), custom_call_target="tpu_custom_call" | custom-call | flops 134217728 | tf_op jit(solution)/shard_map/start/pallas_call | solution.py:30
  8.2 16.4 %all-to-all-start = ((bf16[64,16,128]{2,1,0:T(8,128)(2,1)}), bf16[64,16,128]{2,1,0:T(8,128)(2,1)S(1)}, u32[]{:S(2)}, u32[]{:S(2)}) async-start(bf16[64,16,128]{2,1,0:T(8,128)(2,1)} %get-tuple-element.22), calls=%async_computation | async-start | bytes 524288 | tf_op jit(solution)/shard_map/all_to_all | solution.py:263
  24.6 3.4 %collective-permute-start = (bf16[768,256]{1,0:T(8,128)(2,1)S(1)}, bf16[768,256]{1,0:T(8,128)(2,1)S(1)}, u32[]{:S(2)}, u32[]{:S(2)}) collective-permute-start(bf16[768,256]{1,0:T(8,128)(2,1)S(1)} %get-tuple-element.23.here.refs_1_), channel_id=1, source_target_pairs={{0,1},{1,2},{2,3},{3,4},{4,5},{5,6},{6,7},{7,8},{8,9},{9,10},{10,1... | collective-permute-start | bytes 1179656 | tf_op jit(solution)/shard_map/ppermute | solution.py:259
  28.0 4.6 %collective-permute-start.1 = (bf16[768,256]{1,0:T(8,128)(2,1)S(1)}, bf16[768,256]{1,0:T(8,128)(2,1)S(1)}, u32[]{:S(2)}, u32[]{:S(2)}) collective-permute-start(bf16[768,256]{1,0:T(8,128)(2,1)S(1)} %get-tuple-element.23.here.refs_1_), channel_id=1, source_target_pairs={{1,0},{2,1},{3,2},{4,3},{5,4},{6,5},{7,6},{8,7},{9,8},{10,9},{11,1... | collective-permute-start | bytes 1179656 | tf_op jit(solution)/shard_map/ppermute | solution.py:259
  33.3 4.7 %all-to-all-done.arrived = bf16[64,16,128]{2,1,0:T(8,128)(2,1)S(1)} async-done(((bf16[64,16,128]{2,1,0:T(8,128)(2,1)}), bf16[64,16,128]{2,1,0:T(8,128)(2,1)S(1)}, u32[]{:S(2)}, u32[]{:S(2)}) %all-to-all-start) | async-done | bytes 262176 | tf_op jit(solution)/shard_map/all_to_all | solution.py:263
  38.9 4.4 %all-to-all-start.1 = ((bf16[8,16,128]{2,1,0:T(8,128)(2,1)}), bf16[8,16,128]{2,1,0:T(8,128)(2,1)S(1)}, u32[]{:S(2)}, u32[]{:S(2)}) async-start(bf16[8,16,128]{2,1,0:T(8,128)(2,1)} %get-tuple-element.25), calls=%async_computation.1 | async-start | bytes 65536 | tf_op jit(solution)/shard_map/all_to_all | solution.py:263
  46.9 1.9 %all-to-all-done.1.all_sums = bf16[8,16,128]{2,1,0:T(8,128)(2,1)S(1)} async-done(((bf16[8,16,128]{2,1,0:T(8,128)(2,1)}), bf16[8,16,128]{2,1,0:T(8,128)(2,1)S(1)}, u32[]{:S(2)}, u32[]{:S(2)}) %all-to-all-start.1) | async-done | bytes 32800 | tf_op jit(solution)/shard_map/all_to_all | solution.py:263
  48.7 2.1 %couple.2 = bf16[64,24,128]{2,1,0:T(8,128)(2,1)} custom-call(s32[4,4]{1,0:T(4,128)S(1)} %copy-done.22, bf16[8,16,128]{2,1,0:T(8,128)(2,1)S(1)} %all-to-all-done.1.all_sums, bf16[4,4,128,128]{3,2,1,0:T(8,128)(2,1)S(1)} %copy-done.2, f32[64,128]{1,0:T(8,128)S(1)} %get-tuple-element.26.told, bf16[64,16,128]{2,1,0:T(8,128)(2,1)S(1)} %partners.2, ...), custom_call_target="tpu_custom_call" | custom-call | flops 33554432 | tf_op jit(solution)/shard_map/couple/pallas_call | solution.py:30
  50.9 8.8 %all-to-all-start.2 = ((bf16[64,24,128]{2,1,0:T(8,128)(2,1)}), bf16[64,24,128]{2,1,0:T(8,128)(2,1)S(1)}, u32[]{:S(2)}, u32[]{:S(2)}) async-start(bf16[64,24,128]{2,1,0:T(8,128)(2,1)} %couple.2), calls=%async_computation.2 | async-start | bytes 786432 | tf_op jit(solution)/shard_map/all_to_all | solution.py:263
  59.7 3.5 %collective-permute-start.2 = (bf16[768,256]{1,0:T(8,128)(2,1)S(1)}, bf16[768,256]{1,0:T(8,128)(2,1)S(1)}, u32[]{:S(2)}, u32[]{:S(2)}) collective-permute-start(bf16[768,256]{1,0:T(8,128)(2,1)S(1)} %collective-permute-done.refs_3_), channel_id=1, source_target_pairs={{0,1},{1,2},{2,3},{3,4},{4,5},{5,6},{6,7},{7,8},{8,9},{9,10},{10,1... | collective-permute-start | bytes 1179656 | tf_op jit(solution)/shard_map/ppermute | solution.py:259
  63.2 4.6 %collective-permute-start.3 = (bf16[768,256]{1,0:T(8,128)(2,1)S(1)}, bf16[768,256]{1,0:T(8,128)(2,1)S(1)}, u32[]{:S(2)}, u32[]{:S(2)}) collective-permute-start(bf16[768,256]{1,0:T(8,128)(2,1)S(1)} %collective-permute-done.1.refs_4_), channel_id=1, source_target_pairs={{1,0},{2,1},{3,2},{4,3},{5,4},{6,5},{7,6},{8,7},{9,8},{10,9},{11,1... | collective-permute-start | bytes 1179656 | tf_op jit(solution)/shard_map/ppermute | solution.py:259
  67.8 12.9 %collective-permute-done.2.refs_3_ = bf16[768,256]{1,0:T(8,128)(2,1)S(1)} collective-permute-done((bf16[768,256]{1,0:T(8,128)(2,1)S(1)}, bf16[768,256]{1,0:T(8,128)(2,1)S(1)}, u32[]{:S(2)}, u32[]{:S(2)}) %collective-permute-start.2) | collective-permute-done | bytes 393248 | tf_op jit(solution)/shard_map/ppermute | solution.py:259
  85.0 1.7 %middle.1 = (bf16[512,256]{1,0:T(8,128)(2,1)S(1)}, bf16[64,8,128]{2,1,0:T(8,128)(2,1)}, f32[512,256]{1,0:T(8,128)S(1)}, f32[512,256]{1,0:T(8,128)S(1)}) custom-call(f32[1]{0:T(128)} %bitcast.3.ridge, bf16[64,24,128]{2,1,0:T(8,128)(2,1)S(1)} %all-to-all-done.2.arrived, bf16[1,4,128,128]{3,2,1,0:T(8,128)(2,1)S(1)} %copy-done.3, ...), custom_call_target="tpu_custom_call" | custom-call | flops 134217728 | tf_op jit(solution)/shard_map/middle/pallas_call | solution.py:30
  88.2 9.7 %all-to-all-start.3 = ((bf16[64,8,128]{2,1,0:T(8,128)(2,1)}), bf16[64,8,128]{2,1,0:T(8,128)(2,1)S(1)}, u32[]{:S(2)}, u32[]{:S(2)}) async-start(bf16[64,8,128]{2,1,0:T(8,128)(2,1)} %get-tuple-element.31), calls=%async_computation.3 | async-start | bytes 262144 | tf_op jit(solution)/shard_map/all_to_all | solution.py:263
  98.0 3.4 %collective-permute-start.4 = (bf16[512,256]{1,0:T(8,128)(2,1)S(1)}, bf16[512,256]{1,0:T(8,128)(2,1)}, u32[]{:S(2)}, u32[]{:S(2)}) collective-permute-start(bf16[512,256]{1,0:T(8,128)(2,1)S(1)} %get-tuple-element.32.w), channel_id=1, source_target_pairs={{0,1},{1,2},{2,3},{3,4},{4,5},{5,6},{6,7},{7,8},{8,9},{9,10},{10,1... | collective-permute-start | bytes 786440 | tf_op jit(solution)/shard_map/ppermute | solution.py:259
  101.4 4.6 %collective-permute-start.5 = (bf16[512,256]{1,0:T(8,128)(2,1)S(1)}, bf16[512,256]{1,0:T(8,128)(2,1)}, u32[]{:S(2)}, u32[]{:S(2)}) collective-permute-start(bf16[512,256]{1,0:T(8,128)(2,1)S(1)} %get-tuple-element.32.w), channel_id=1, source_target_pairs={{1,0},{2,1},{3,2},{4,3},{5,4},{6,5},{7,6},{8,7},{9,8},{10,9},{11,1... | collective-permute-start | bytes 786440 | tf_op jit(solution)/shard_map/ppermute | solution.py:259
  106.3 2.3 %all-to-all-done.3.arrived = bf16[64,8,128]{2,1,0:T(8,128)(2,1)S(1)} async-done(((bf16[64,8,128]{2,1,0:T(8,128)(2,1)}), bf16[64,8,128]{2,1,0:T(8,128)(2,1)S(1)}, u32[]{:S(2)}, u32[]{:S(2)}) %all-to-all-start.3) | async-done | bytes 131104 | tf_op jit(solution)/shard_map/all_to_all | solution.py:263
  109.4 5.3 %all-to-all-start.4 = ((bf16[8,16,128]{2,1,0:T(8,128)(2,1)}), bf16[8,16,128]{2,1,0:T(8,128)(2,1)S(1)}, u32[]{:S(2)}, u32[]{:S(2)}) async-start(bf16[8,16,128]{2,1,0:T(8,128)(2,1)} %get-tuple-element.34), calls=%async_computation.4 | async-start | bytes 65536 | tf_op jit(solution)/shard_map/all_to_all | solution.py:263
  117.3 2.9 %all-to-all-done.4.all_sums = bf16[8,16,128]{2,1,0:T(8,128)(2,1)S(1)} async-done(((bf16[8,16,128]{2,1,0:T(8,128)(2,1)}), bf16[8,16,128]{2,1,0:T(8,128)(2,1)S(1)}, u32[]{:S(2)}, u32[]{:S(2)}) %all-to-all-start.4) | async-done | bytes 32800 | tf_op jit(solution)/shard_map/all_to_all | solution.py:263
  120.2 2.1 %couple.3 = bf16[64,24,128]{2,1,0:T(8,128)(2,1)} custom-call(s32[4,4]{1,0:T(4,128)S(1)} %copy-done.22, bf16[8,16,128]{2,1,0:T(8,128)(2,1)S(1)} %all-to-all-done.4.all_sums, bf16[4,4,128,128]{3,2,1,0:T(8,128)(2,1)S(1)} %copy-done.2, f32[64,128]{1,0:T(8,128)S(1)} %get-tuple-element.26.told, bf16[64,16,128]{2,1,0:T(8,128)(2,1)S(1)} %partners.3, ...), custom_call_target="tpu_custom_call" | custom-call | flops 33554432 | tf_op jit(solution)/shard_map/couple/pallas_call | solution.py:30
  122.3 9.0 %all-to-all-start.5 = ((bf16[64,24,128]{2,1,0:T(8,128)(2,1)}), bf16[64,24,128]{2,1,0:T(8,128)(2,1)S(1)}, u32[]{:S(2)}, u32[]{:S(2)}) async-start(bf16[64,24,128]{2,1,0:T(8,128)(2,1)} %couple.3), calls=%async_computation.5 | async-start | bytes 786432 | tf_op jit(solution)/shard_map/all_to_all | solution.py:263
  131.3 3.4 %collective-permute-start.6 = (bf16[512,256]{1,0:T(8,128)(2,1)}, bf16[512,256]{1,0:T(8,128)(2,1)S(1)}, u32[]{:S(2)}, u32[]{:S(2)}) collective-permute-start(bf16[512,256]{1,0:T(8,128)(2,1)} %collective-permute-done.4.refs_2_), channel_id=1, source_target_pairs={{0,1},{1,2},{2,3},{3,4},{4,5},{5,6},{6,7},{7,8},{8,9},{9,10},{10,1... | collective-permute-start | bytes 786440 | tf_op jit(solution)/shard_map/ppermute | solution.py:259
  134.7 4.6 %collective-permute-start.7 = (bf16[512,256]{1,0:T(8,128)(2,1)}, bf16[512,256]{1,0:T(8,128)(2,1)S(1)}, u32[]{:S(2)}, u32[]{:S(2)}) collective-permute-start(bf16[512,256]{1,0:T(8,128)(2,1)} %collective-permute-done.5.refs_3_), channel_id=1, source_target_pairs={{1,0},{2,1},{3,2},{4,3},{5,4},{6,5},{7,6},{8,7},{9,8},{10,9},{11,1... | collective-permute-start | bytes 786440 | tf_op jit(solution)/shard_map/ppermute | solution.py:259
  139.3 10.6 %collective-permute-done.6.refs_2_ = bf16[512,256]{1,0:T(8,128)(2,1)S(1)} collective-permute-done((bf16[512,256]{1,0:T(8,128)(2,1)}, bf16[512,256]{1,0:T(8,128)(2,1)S(1)}, u32[]{:S(2)}, u32[]{:S(2)}) %collective-permute-start.6) | collective-permute-done | bytes 262176 | tf_op jit(solution)/shard_map/ppermute | solution.py:259
  (77 shorter events, 24.7 us)
Async XLA Ops:
  8.2 25.1 %copy-start.26 = (bf16[768,256]{1,0:T(8,128)(2,1)}, bf16[768,256]{1,0:T(8,128)(2,1)S(1)}, u32[]{:S(2)}) copy-start(bf16[768,256]{1,0:T(8,128)(2,1)S(1)} %get-tuple-element.23.here.refs_1_) | copy-start | bytes 1179652
  8.2 29.8 %all-to-all-start = ((bf16[64,16,128]{2,1,0:T(8,128)(2,1)}), bf16[64,16,128]{2,1,0:T(8,128)(2,1)S(1)}, u32[]{:S(2)}, u32[]{:S(2)}) async-start(bf16[64,16,128]{2,1,0:T(8,128)(2,1)} %get-tuple-element.22), calls=%async_computation | async-start | bytes 524288 | tf_op jit(solution)/shard_map/all_to_all | solution.py:263
  24.6 18.7 %collective-permute-start = (bf16[768,256]{1,0:T(8,128)(2,1)S(1)}, bf16[768,256]{1,0:T(8,128)(2,1)S(1)}, u32[]{:S(2)}, u32[]{:S(2)}) collective-permute-start(bf16[768,256]{1,0:T(8,128)(2,1)S(1)} %get-tuple-element.23.here.refs_1_), channel_id=1, source_target_pairs={{0,1},{1,2},{2,3},{3,4},{4,5},{5,6},{6,7},{7,8},{8,9},{9,10},{10,1... | collective-permute-start | bytes 1179656 | tf_op jit(solution)/shard_map/ppermute | solution.py:259
  28.0 15.3 %collective-permute-start.1 = (bf16[768,256]{1,0:T(8,128)(2,1)S(1)}, bf16[768,256]{1,0:T(8,128)(2,1)S(1)}, u32[]{:S(2)}, u32[]{:S(2)}) collective-permute-start(bf16[768,256]{1,0:T(8,128)(2,1)S(1)} %get-tuple-element.23.here.refs_1_), channel_id=1, source_target_pairs={{1,0},{2,1},{3,2},{4,3},{5,4},{6,5},{7,6},{8,7},{9,8},{10,9},{11,1... | collective-permute-start | bytes 1179656 | tf_op jit(solution)/shard_map/ppermute | solution.py:259
  38.9 4.5 %copy-start.24 = (s32[1,4]{1,0:T(1,128)S(1)}, s32[1,4]{1,0:T(1,128)}, u32[]{:S(2)}) copy-start(s32[1,4]{1,0:T(1,128)} %refs_0_.7) | copy-start | bytes 52
  38.9 9.9 %all-to-all-start.1 = ((bf16[8,16,128]{2,1,0:T(8,128)(2,1)}), bf16[8,16,128]{2,1,0:T(8,128)(2,1)S(1)}, u32[]{:S(2)}, u32[]{:S(2)}) async-start(bf16[8,16,128]{2,1,0:T(8,128)(2,1)} %get-tuple-element.25), calls=%async_computation.1 | async-start | bytes 65536 | tf_op jit(solution)/shard_map/all_to_all | solution.py:263
  44.3 4.4 %copy-start.2 = (bf16[4,4,128,128]{3,2,1,0:T(8,128)(2,1)S(1)}, bf16[4,4,128,128]{3,2,1,0:T(8,128)(2,1)}, u32[]{:S(2)}) copy-start(bf16[4,4,128,128]{3,2,1,0:T(8,128)(2,1)} %blocks.3) | copy-start | bytes 1572868
  46.5 4.4 %copy-start.16 = (f32[512,256]{1,0:T(8,128)}, f32[512,256]{1,0:T(8,128)S(1)}, u32[]{:S(2)}) copy-start(f32[512,256]{1,0:T(8,128)S(1)} %get-tuple-element.28._.refs_2_) | copy-start | bytes 1572868
  46.5 2.2 %copy-start.22 = (s32[4,4]{1,0:T(4,128)S(1)}, s32[4,4]{1,0:T(4,128)}, u32[]{:S(2)}) copy-start(s32[4,4]{1,0:T(4,128)} %far_clusters.3) | copy-start | bytes 196
  50.9 34.1 %copy-start.19 = (bf16[1,128,128]{2,1,0:T(8,128)(2,1)S(1)}, bf16[1,128,128]{2,1,0:T(8,128)(2,1)}, u32[]{:S(2)}) copy-start(bf16[1,128,128]{2,1,0:T(8,128)(2,1)} %transfer.5) | copy-start | bytes 98308
  50.9 34.1 %all-to-all-start.2 = ((bf16[64,24,128]{2,1,0:T(8,128)(2,1)}), bf16[64,24,128]{2,1,0:T(8,128)(2,1)S(1)}, u32[]{:S(2)}, u32[]{:S(2)}) async-start(bf16[64,24,128]{2,1,0:T(8,128)(2,1)} %couple.2), calls=%async_computation.2 | async-start | bytes 786432 | tf_op jit(solution)/shard_map/all_to_all | solution.py:263
  59.7 25.3 %copy-start.1 = (f32[512,256]{1,0:T(8,128)S(1)}, f32[512,256]{1,0:T(8,128)}, u32[]{:S(2)}) copy-start(f32[512,256]{1,0:T(8,128)} %rs.5) | copy-start | bytes 1572868
  59.7 25.3 %copy-start.3 = (bf16[1,4,128,128]{3,2,1,0:T(8,128)(2,1)S(1)}, bf16[1,4,128,128]{3,2,1,0:T(8,128)(2,1)}, u32[]{:S(2)}) copy-start(bf16[1,4,128,128]{3,2,1,0:T(8,128)(2,1)} %couplings.3) | copy-start | bytes 393220
  59.7 21.0 %collective-permute-start.2 = (bf16[768,256]{1,0:T(8,128)(2,1)S(1)}, bf16[768,256]{1,0:T(8,128)(2,1)S(1)}, u32[]{:S(2)}, u32[]{:S(2)}) collective-permute-start(bf16[768,256]{1,0:T(8,128)(2,1)S(1)} %collective-permute-done.refs_3_), channel_id=1, source_target_pairs={{0,1},{1,2},{2,3},{3,4},{4,5},{5,6},{6,7},{7,8},{8,9},{9,10},{10,1... | collective-permute-start | bytes 1179656 | tf_op jit(solution)/shard_map/ppermute | solution.py:259
  63.2 17.5 %collective-permute-start.3 = (bf16[768,256]{1,0:T(8,128)(2,1)S(1)}, bf16[768,256]{1,0:T(8,128)(2,1)S(1)}, u32[]{:S(2)}, u32[]{:S(2)}) collective-permute-start(bf16[768,256]{1,0:T(8,128)(2,1)S(1)} %collective-permute-done.1.refs_4_), channel_id=1, source_target_pairs={{1,0},{2,1},{3,2},{4,3},{5,4},{6,5},{7,6},{8,7},{9,8},{10,9},{11,1... | collective-permute-start | bytes 1179656 | tf_op jit(solution)/shard_map/ppermute | solution.py:259
  80.7 1.0 copy-start.17
  88.2 20.4 %all-to-all-start.3 = ((bf16[64,8,128]{2,1,0:T(8,128)(2,1)}), bf16[64,8,128]{2,1,0:T(8,128)(2,1)S(1)}, u32[]{:S(2)}, u32[]{:S(2)}) async-start(bf16[64,8,128]{2,1,0:T(8,128)(2,1)} %get-tuple-element.31), calls=%async_computation.3 | async-start | bytes 262144 | tf_op jit(solution)/shard_map/all_to_all | solution.py:263
  98.0 17.1 %collective-permute-start.4 = (bf16[512,256]{1,0:T(8,128)(2,1)S(1)}, bf16[512,256]{1,0:T(8,128)(2,1)}, u32[]{:S(2)}, u32[]{:S(2)}) collective-permute-start(bf16[512,256]{1,0:T(8,128)(2,1)S(1)} %get-tuple-element.32.w), channel_id=1, source_target_pairs={{0,1},{1,2},{2,3},{3,4},{4,5},{5,6},{6,7},{7,8},{8,9},{9,10},{10,1... | collective-permute-start | bytes 786440 | tf_op jit(solution)/shard_map/ppermute | solution.py:259
  101.4 13.8 %collective-permute-start.5 = (bf16[512,256]{1,0:T(8,128)(2,1)S(1)}, bf16[512,256]{1,0:T(8,128)(2,1)}, u32[]{:S(2)}, u32[]{:S(2)}) collective-permute-start(bf16[512,256]{1,0:T(8,128)(2,1)S(1)} %get-tuple-element.32.w), channel_id=1, source_target_pairs={{1,0},{2,1},{3,2},{4,3},{5,4},{6,5},{7,6},{8,7},{9,8},{10,9},{11,1... | collective-permute-start | bytes 786440 | tf_op jit(solution)/shard_map/ppermute | solution.py:259
  106.2 8.9 %copy-start.5 = (bf16[512,512]{1,0:T(8,128)(2,1)S(1)}, bf16[512,512]{1,0:T(8,128)(2,1)}, u32[]{:S(2)}) copy-start(bf16[512,512]{1,0:T(8,128)(2,1)} %copy-done.4) | copy-start | bytes 1572868
  109.4 10.7 %all-to-all-start.4 = ((bf16[8,16,128]{2,1,0:T(8,128)(2,1)}), bf16[8,16,128]{2,1,0:T(8,128)(2,1)S(1)}, u32[]{:S(2)}, u32[]{:S(2)}) async-start(bf16[8,16,128]{2,1,0:T(8,128)(2,1)} %get-tuple-element.34), calls=%async_computation.4 | async-start | bytes 65536 | tf_op jit(solution)/shard_map/all_to_all | solution.py:263
  122.3 30.2 %all-to-all-start.5 = ((bf16[64,24,128]{2,1,0:T(8,128)(2,1)}), bf16[64,24,128]{2,1,0:T(8,128)(2,1)S(1)}, u32[]{:S(2)}, u32[]{:S(2)}) async-start(bf16[64,24,128]{2,1,0:T(8,128)(2,1)} %couple.3), calls=%async_computation.5 | async-start | bytes 786432 | tf_op jit(solution)/shard_map/all_to_all | solution.py:263
  131.3 18.5 %collective-permute-start.6 = (bf16[512,256]{1,0:T(8,128)(2,1)}, bf16[512,256]{1,0:T(8,128)(2,1)S(1)}, u32[]{:S(2)}, u32[]{:S(2)}) collective-permute-start(bf16[512,256]{1,0:T(8,128)(2,1)} %collective-permute-done.4.refs_2_), channel_id=1, source_target_pairs={{0,1},{1,2},{2,3},{3,4},{4,5},{5,6},{6,7},{7,8},{8,9},{9,10},{10,1... | collective-permute-start | bytes 786440 | tf_op jit(solution)/shard_map/ppermute | solution.py:259
  134.7 15.2 %collective-permute-start.7 = (bf16[512,256]{1,0:T(8,128)(2,1)}, bf16[512,256]{1,0:T(8,128)(2,1)S(1)}, u32[]{:S(2)}, u32[]{:S(2)}) collective-permute-start(bf16[512,256]{1,0:T(8,128)(2,1)} %collective-permute-done.5.refs_3_), channel_id=1, source_target_pairs={{1,0},{2,1},{3,2},{4,3},{5,4},{6,5},{7,6},{8,7},{9,8},{10,9},{11,1... | collective-permute-start | bytes 786440 | tf_op jit(solution)/shard_map/ppermute | solution.py:259
  (19 other events, 16.9 us)

commit v3 on v2

v3 whole, which is shorter than its diff:
```python
import jax
import jax.numpy as jnp
from jax import lax
from jax.experimental import pallas as pl
from jax.experimental.pallas import tpu as pltpu
from jax.sharding import PartitionSpec as P

LEAF, DIM, OUT, RANK = 512, 64, 256, 128
N_GRP, N_DEV, CPG = 8, 64, 4
FAR1, FAR2 = 4, 4
COLS = OUT // N_DEV
NEAR = (-1, 1, -2, 2)

KERNEL_LOG2 = -1.4426950408889634 / 32.0
GAP, TOP = 0.5, 8.0

F32, BF16 = jnp.float32, jnp.bfloat16
VMEM = pl.BlockSpec(memory_space=pltpu.VMEM)
SMEM = pl.BlockSpec(memory_space=pltpu.SMEM)
ANY = pl.BlockSpec(memory_space=pl.ANY)
HBM = pl.BlockSpec(memory_space=pltpu.HBM)
LIMIT = 32 * 2**20
SHORT, LONG = 10**7, 10**10
ROWS = 128


def dot(a, b, dims=((1,), (0,))):
    return lax.dot_general(a, b, (dims, ((), ())), preferred_element_type=F32)


def call(kernel, name, outs, ins, args, scratch=(), flops=0, aliases=None):
    shapes = [(pltpu.HBM if spec is HBM else jax.ShapeDtypeStruct)(shape, kind) for shape, kind, spec in outs]
    args = [
        pltpu.with_memory_space_constraint(arg, pltpu.HBM) if spec is HBM else arg for arg, spec in zip(args, ins)
    ]
    return pl.pallas_call(
        kernel,
        name=name,
        out_shape=shapes,
        in_specs=ins,
        out_specs=[spec for _, _, spec in outs],
        scratch_shapes=list(scratch),
        input_output_aliases=aliases or {},
        compiler_params=pltpu.CompilerParams(vmem_limit_bytes=LIMIT),
        cost_estimate=pl.CostEstimate(flops=flops, bytes_accessed=0, transcendentals=0),
    )(*args)


def started(pairs, sems, first=0):
    copies = [pltpu.make_async_copy(a, b, sems.at[first + i]) for i, (a, b) in enumerate(pairs)]
    for copy in copies:
        copy.start()
    return copies


def wait(copies):
    for copy in copies:
        copy.wait()


def chebyshev(ridge):
    ridge = jnp.full((1, 1), ridge, F32)
    bottom, top = ridge + GAP, ridge + TOP
    centre, spread = (top + bottom) / 2.0, (top - bottom) / 2.0
    sigma = centre / spread
    rho0 = 1.0 / sigma
    rho1 = 1.0 / (2.0 * sigma - rho0)
    rho2 = 1.0 / (2.0 * sigma - rho1)
    first = (rho1 * rho0, 2.0 * rho1 / spread)
    second = (rho2 * rho1, 2.0 * rho2 / spread)
    return ridge, centre, first, second


def to_owners(values, basis, transfer, staged, rows):
    skeleton = dot(values, basis, ((0,), (0,))).astype(BF16)
    uplift = dot(skeleton, transfer)
    skeleton = skeleton.astype(F32)
    for i in range(COLS):
        part = slice(N_DEV * i, N_DEV * (i + 1))
        staged[pl.ds(i, N_DEV, stride=rows), :] = skeleton[part]
        staged[pl.ds(COLS + i, N_DEV, stride=rows), :] = uplift[part]


def start_kernel(
    ridge, cluster, far_in, rs_in, coords_in, perm_in, basis_in, transfer_in, wc_out, sent_out, placed_out,
    far, rs, coords, perm, basis, transfer, wc, sent, placed, staged, sems,
):
    copies = started(
        (
            (perm_in, perm), (basis_in, basis), (rs_in, rs), (coords_in, coords),
            (transfer_in, transfer), (far_in, far),
        ),
        sems,
    )
    staged[...] = jnp.zeros_like(staged)
    _, centre, _, _ = chebyshev(ridge[0])
    wait(copies[:2])
    point = lax.broadcasted_iota(jnp.int32, (LEAF, LEAF), 0)
    pick = jnp.where(point == perm[...], 1.0, 0.0).astype(BF16)
    basis_here = dot(pick, basis[...]).astype(BF16)
    placed[...] = basis_here
    wait(copies[2:4])
    values = (rs[...] / centre).astype(BF16)
    wc[:LEAF] = values
    high = coords[...].astype(BF16)
    low = (coords[...] - high.astype(F32)).astype(BF16)
    parts = jnp.concatenate([high, low], axis=0)
    wc[LEAF : LEAF + 2 * DIM] = parts[:, :OUT]
    wc[LEAF + 2 * DIM :] = parts[:, OUT:]
    outs = started(((wc, wc_out), (placed, placed_out)), sems, 6)
    wait(copies[4:])
    to_owners(values, basis_here, transfer[0], staged, 16)
    lane = lax.broadcasted_iota(jnp.int32, (N_DEV, RANK), 1)
    told = jnp.where(lane == FAR1, (cluster[0] % CPG).astype(F32), 0.0)
    for k in range(FAR1):
        told = jnp.where(lane == k, (far[0, k] % N_DEV).astype(F32), told)
    staged[pl.ds(8, N_DEV, stride=16), :] = told
    sent[...] = staged[...].astype(BF16).reshape(N_DEV, 16, RANK)
    outs += started(((sent, sent_out),), sems, 8)
    wait(outs)


def owner_sums(staged, rows, told, sums, narrow):
    lane = lax.broadcasted_iota(jnp.int32, (N_DEV, RANK), 1).astype(F32)
    member = jnp.where(lane == told[:, FAR1 : FAR1 + 1], 1.0, 0.0).astype(BF16)
    uplifts = jnp.concatenate(
        [staged[pl.ds(COLS + i, N_DEV, stride=rows), :] for i in range(COLS)], axis=1
    ).astype(BF16)
    total = dot(member, uplifts, ((0,), (0,)))
    for i in range(COLS):
        narrow[pl.ds(CPG * i, CPG), :] = total[:CPG, RANK * i : RANK * (i + 1)]
    out = narrow[...].astype(BF16)
    for g in range(N_GRP):
        sums[g] = out


def sums_first_kernel(arrived, _, sums, told, skeletons, staged, narrow):
    staged[...] = arrived[...].astype(F32).reshape(N_DEV * 16, RANK)
    told[...] = staged[pl.ds(8, N_DEV, stride=16), :]
    owner_sums(staged, 16, told[...], sums, narrow)
    skeletons[...] = jnp.concatenate(
        [staged[pl.ds(i, N_DEV, stride=16), :] for i in range(COLS)], axis=1
    ).astype(BF16)


def sums_kernel(arrived, told, _, sums, skeletons, staged, narrow):
    staged[...] = arrived[...].astype(F32).reshape(N_DEV * 8, RANK)
    owner_sums(staged, 8, told[...], sums, narrow)
    skeletons[...] = jnp.concatenate(
        [staged[pl.ds(i, N_DEV, stride=8), :] for i in range(COLS)], axis=1
    ).astype(BF16)


def partners_kernel(skeletons, told, sent_out, staged, sent, sems):
    lane = lax.broadcasted_iota(jnp.int32, (N_DEV, N_DEV), 1).astype(F32)
    pick = jnp.concatenate(
        [jnp.where(lane == told[:, k : k + 1], 1.0, 0.0) for k in range(FAR1)], axis=0
    ).astype(BF16)
    picked = dot(pick, skeletons[...])
    for k in range(FAR1):
        for i in range(COLS):
            staged[pl.ds(COLS * k + i, N_DEV, stride=16), :] = picked[
                N_DEV * k : N_DEV * (k + 1), RANK * i : RANK * (i + 1)
            ]
    sent[...] = staged[...].reshape(N_DEV, 2, 8, RANK).astype(BF16)
    wait(started(((sent, sent_out.at[:, :2]),), sems))


def couple_kernel(far_clusters, all_sums, blocks, told, _, sent_out, staged, sent, sems):
    rows = COLS * CPG
    sums = all_sums[...].reshape(N_GRP * rows, RANK)
    row = lax.broadcasted_iota(jnp.int32, (rows, N_GRP * rows), 0)
    lane = lax.broadcasted_iota(jnp.int32, (rows, N_GRP * rows), 1)
    column, cluster = row // CPG, row % CPG
    total = jnp.zeros((rows, CPG * RANK), F32)
    for k in range(FAR2):
        target = CPG * column
        for c in range(CPG):
            f = far_clusters[c, k]
            target += jnp.where(cluster == c, rows * (f // CPG) + f % CPG, 0)
        pick = jnp.where(lane == target, 1.0, 0.0).astype(BF16)
        picked = dot(pick, sums).astype(BF16)
        block = blocks[:, k].reshape(CPG * RANK, RANK)
        total += dot(picked, block, ((1,), (1,)))
    coupled = jnp.zeros((rows, RANK), F32)
    own = cluster[:, :RANK]
    for c in range(CPG):
        coupled += jnp.where(own == c, total[:, RANK * c : RANK * (c + 1)], 0.0)
    coupled = coupled.astype(BF16)
    lane = lax.broadcasted_iota(jnp.int32, (N_DEV, rows), 1).astype(F32)
    pick = jnp.concatenate(
        [jnp.where(lane == told[:, FAR1 : FAR1 + 1] + CPG * i, 1.0, 0.0) for i in range(COLS)], axis=0
    ).astype(BF16)
    out = dot(pick, coupled)
    staged[...] = jnp.zeros_like(staged)
    for i in range(COLS):
        staged[pl.ds(i, N_DEV, stride=8), :] = out[N_DEV * i : N_DEV * (i + 1)]
    sent[...] = staged[...].reshape(N_DEV, 8, RANK).astype(BF16)
    wait(started(((sent, sent_out.at[:, 2]),), sems))


def local_field(arrived, couplings, transfer, staged):
    staged[...] = arrived[...].astype(F32).reshape(N_DEV * 24, RANK)
    local = jnp.zeros((RANK, OUT), F32)
    for k in range(FAR1 + 1):
        skeleton = jnp.concatenate(
            [staged[pl.ds(COLS * k + i, N_DEV, stride=24), :] for i in range(COLS)], axis=0
        ).astype(BF16)
        local += dot(couplings[0, k] if k < FAR1 else transfer[0], skeleton, ((1,), (1,)))
    return local.astype(BF16)


def middle_kernel(
    ridge, arrived, couplings, transfer, basis, near, rs_in, w_out, sent_out, r1_out,
    rs, w, sent, r1, staged, staged_out, sems,
):
    copies = started(((rs_in, rs),), sems)
    ridge, centre, (mul, add), _ = chebyshev(ridge[0])
    local = local_field(arrived, couplings, transfer, staged)
    wait(copies)
    outs = []
    for n, r in enumerate(range(0, LEAF, ROWS)):
        part = slice(r, r + ROWS)
        here = rs[part]
        d1 = here / centre
        residual = here - (ridge * d1 + (near[part] + dot(basis[part], local)))
        r1[part] = residual
        w[part] = (mul * d1 + add * residual).astype(BF16)
        at = pl.ds(r, ROWS)
        outs += started(((r1.at[at], r1_out.at[at]), (w.at[at], w_out.at[at])), sems, 1 + 2 * n)
    to_owners(w[...], basis[...], transfer[0], staged_out, 8)
    sent[...] = staged_out[...].astype(BF16).reshape(N_DEV, 8, RANK)
    outs += started(((sent, sent_out),), sems, 9)
    wait(outs)


def end_kernel(
    ridge, arrived, couplings, transfer, basis, near, rs_in, r1_in, solution_out, residual_out,
    rs, r1, solution, residual, staged, sems,
):
    copies = started(((rs_in, rs), (r1_in, r1)), sems)
    ridge, centre, (mul1, add1), (mul, add) = chebyshev(ridge[0])
    local = local_field(arrived, couplings, transfer, staged)
    wait(copies)
    outs = []
    for n, r in enumerate(range(0, LEAF, ROWS)):
        part = slice(r, r + ROWS)
        d1 = rs[part] / centre
        d2 = mul1 * d1 + add1 * r1[part]
        r2 = r1[part] - (ridge * d2 + (near[part] + dot(basis[part], local)))
        residual[part] = r2
        solution[part] = d1 + d2 + (mul * d2 + add * r2)
        at = pl.ds(r, ROWS)
        outs += started(
            ((residual.at[at], residual_out.at[at]), (solution.at[at], solution_out.at[at])), sems, 2 + 2 * n
        )
    wait(outs)


def coordinates(held):
    parts = jnp.concatenate([held[: 2 * DIM], held[2 * DIM :]], axis=1)
    high, low = parts[:DIM], parts[DIM:]
    points = high.astype(F32) + low.astype(F32)
    return high, low, jnp.sum(points * points, axis=0, keepdims=True) * KERNEL_LOG2


def listed(near_list, offset):
    leaf = lax.axis_index("grp") * N_DEV + lax.axis_index("dev")
    hit = near_list[0, 0] == leaf + offset
    for k in range(1, len(NEAR)):
        hit = hit | (near_list[0, k] == leaf + offset)
    return hit


def block_times(here, there, values, total, fresh):
    high, low, norm = here
    left = jnp.concatenate([high, high, low, low], axis=0)
    column = jnp.broadcast_to(norm, (RANK, LEAF)).T[:, :1]
    high, low, across = there
    right = jnp.concatenate([high, low, high, low], axis=0)
    step = 128
    for r in range(0, LEAF, step):
        part = slice(r, r + step)
        inner = dot(left[:, part], right, ((0,), (0,)))
        entries = jnp.exp2((column[part] + across) - (2.0 * KERNEL_LOG2) * inner).astype(BF16)
        product = dot(entries, values)
        total[part] = product if fresh else total[part] + product


def near_own_kernel(places_in, values_in, total, places, values, sems):
    wait(started(((places_in.at[pl.ds(LEAF, 4 * DIM)], places), (values_in.at[pl.ds(0, LEAF)], values)), sems))
    mine = coordinates(places[...])
    block_times(mine, mine, values[...], total, True)


def near_pair_kernel(offsets, near_list, places_in, before, p1, v1, p2, v2, _, total, places, values, sems):
    copies = started([(p.at[pl.ds(LEAF, 4 * DIM)], places.at[i]) for i, p in enumerate((places_in, p1, p2))], sems)
    copies += started([(v.at[pl.ds(0, LEAF)], values.at[i]) for i, v in enumerate((v1, v2))], sems, 3)
    total[...] = before[...]
    wait(copies)
    mine = coordinates(places[0])
    for i, offset in enumerate(offsets):

        @pl.when(listed(near_list, offset))
        def _():
            block_times(mine, coordinates(places[1 + i]), values[i], total, False)


def from_behind(shard, by):
    pairs = [(i, i + by) for i in range(N_DEV) if 0 <= i + by < N_DEV]
    return lax.ppermute(shard, "dev", pairs)


def from_near(shard, after):
    shard, _ = lax.optimization_barrier((shard, after))
    return [from_behind(shard, -offset) for offset in NEAR]


def exchanged(blocks, axis):
    return lax.all_to_all(blocks, axis, split_axis=0, concat_axis=0, tiled=True)


def body(
    coords,
    right_side,
    leaf_perm,
    near_list,
    far_leaves,
    couplings,
    transfer,
    leaf_basis,
    cluster_of,
    far_clusters,
    cluster_couplings,
    ridge_weight,
):
    ridge = ridge_weight.reshape(1)
    field, dma = (LEAF, OUT), pltpu.SemaphoreType.DMA
    rows24 = pltpu.VMEM((N_DEV * 24, RANK), F32)
    rows16 = pltpu.VMEM((N_DEV * 16, RANK), F32)
    rows8 = pltpu.VMEM((N_DEV * 8, RANK), F32)
    narrow = pltpu.VMEM((COLS * CPG, RANK), F32)
    places = pltpu.VMEM((4 * DIM, OUT), BF16)

    wc, sent, basis = call(
        start_kernel,
        "start",
        [
            ((LEAF + 4 * DIM, OUT), BF16, HBM),
            ((N_DEV, 16, RANK), BF16, HBM),
            ((LEAF, RANK), BF16, HBM),
        ],
        [SMEM] * 2 + [HBM] * 6,
        (ridge, cluster_of, far_leaves, right_side, coords.T, leaf_perm, leaf_basis, transfer),
        [
            pltpu.SMEM((1, FAR1), jnp.int32),
            pltpu.VMEM(field, F32),
            pltpu.VMEM((DIM, LEAF), F32),
            pltpu.VMEM((1, LEAF), jnp.int32),
            pltpu.VMEM((LEAF, RANK), BF16),
            pltpu.VMEM((1, RANK, RANK), BF16),
            pltpu.VMEM((LEAF + 4 * DIM, OUT), BF16),
            pltpu.VMEM((N_DEV, 16, RANK), BF16),
            pltpu.VMEM((LEAF, RANK), BF16),
            rows16,
            dma((9,)),
        ],
        SHORT,
    )

    def near_own(values):
        (near,) = call(
            near_own_kernel,
            "near_own",
            [(field, F32, VMEM)],
            [HBM] * 2,
            (wc, values),
            [places, pltpu.VMEM(field, BF16), dma((2,))],
            SHORT,
        )
        return near

    def near_pair(at, near, first, fields, after, flops):
        (near,) = call(
            lambda *refs: near_pair_kernel(NEAR[at : at + 2], *refs),
            f"near_pair_{at}",
            [(field, F32, VMEM)],
            [SMEM, HBM, VMEM] + [ANY] * 5,
            (near_list, wc, near, first[at], fields[at], first[at + 1], fields[at + 1], after),
            [pltpu.VMEM((3, 4 * DIM, OUT), BF16), pltpu.VMEM((2, *field), BF16), dma((5,))],
            flops,
        )
        return near

    def through_owners(sums, skeletons):
        all_sums = exchanged(sums, "grp")
        (partners,) = call(
            partners_kernel,
            "partners",
            [((N_DEV, 3, 8, RANK), BF16, HBM)],
            [VMEM] * 2,
            (skeletons, told),
            [rows16, pltpu.VMEM((N_DEV, 2, 8, RANK), BF16), dma((1,))],
            SHORT,
        )
        (sent,) = call(
            couple_kernel,
            "couple",
            [((N_DEV, 3, 8, RANK), BF16, HBM)],
            [SMEM] + [VMEM] * 3 + [HBM],
            (far_clusters, all_sums, cluster_couplings, told, partners),
            [rows8, pltpu.VMEM((N_DEV, 8, RANK), BF16), dma((1,))],
            SHORT,
            {4: 0},
        )
        return sent, exchanged(sent, "dev")

    arrived = exchanged(sent, "dev")
    near = near_own(wc)
    first = from_near(wc, near)
    sums, told, skeletons = call(
        sums_first_kernel,
        "sums_first",
        [((N_GRP, 16, RANK), BF16, VMEM), ((N_DEV, RANK), F32, VMEM), ((N_DEV, COLS * RANK), BF16, VMEM)],
        [VMEM, ANY],
        (arrived, near),
        [rows16, narrow],
        SHORT,
    )
    sent, arrived = through_owners(sums, skeletons)
    near = near_pair(0, near, first, first, sent, SHORT)
    near = near_pair(2, near, first, first, sent, LONG)
    w, sent, r1 = call(
        middle_kernel,
        "middle",
        [(field, BF16, HBM), ((N_DEV, 8, RANK), BF16, HBM), (field, F32, HBM)],
        [SMEM] + [VMEM] * 5 + [HBM],
        (ridge, arrived, couplings, transfer, basis, near, right_side),
        [
            pltpu.VMEM(field, F32),
            pltpu.VMEM(field, BF16),
            pltpu.VMEM((N_DEV, 8, RANK), BF16),
            pltpu.VMEM(field, F32),
            rows24,
            rows8,
            dma((10,)),
        ],
        SHORT,
    )
    arrived = exchanged(sent, "dev")
    near = near_own(w)
    fields = from_near(w, near)
    sums, skeletons = call(
        sums_kernel,
        "sums",
        [((N_GRP, 16, RANK), BF16, VMEM), ((N_DEV, COLS * RANK), BF16, VMEM)],
        [VMEM, VMEM, ANY],
        (arrived, told, near),
        [rows8, narrow],
        SHORT,
    )
    sent, arrived = through_owners(sums, skeletons)
    near = near_pair(0, near, first, fields, sent, SHORT)
    near = near_pair(2, near, first, fields, sent, LONG)
    return tuple(
        call(
            end_kernel,
            "end",
            [(field, F32, HBM), (field, F32, HBM)],
            [SMEM] + [VMEM] * 5 + [HBM] * 2,
            (ridge, arrived, couplings, transfer, basis, near, right_side, r1),
            [pltpu.VMEM(field, F32)] * 4 + [rows24, dma((10,))],
            SHORT,
        )
    )


def solution(mesh):
    placed = (
        P(("grp", "dev"), None),
        P(("grp", "dev"), None),
        P(("grp", "dev"), None),
        P(("grp", "dev"), None),
        P(("grp", "dev"), None),
        P(("grp", "dev"), None, None, None),
        P(("grp", "dev"), None, None),
        P(("grp", "dev"), None),
        P(("grp", "dev")),
        P("grp", None),
        P("grp", None, None, None),
        P(),
    )
    return jax.shard_map(
        body,
        mesh=mesh,
        in_specs=placed,
        out_specs=(P(("grp", "dev"), None), P(("grp", "dev"), None)),
        check_vma=False,
    )
```

time: 157 us -> 150 us (0.955)
  the two profiles are of different devices: /device:TPU:24 before, /device:TPU:16 now
where the time goes in v3:
time: 150 us; the launch traced here: 149 us
  starting transfers between devices  85.1 us (57%)
  waiting for transfers between devices  32.2 us (21%)
  Pallas kernels  29 us (19%)
  between operations  2.5 us (2%)
    all_to_all x6, starting transfers between devices, exchanged(): return lax.all_to_all(blocks, axis, split_axis=0, concat_axis=0, tiled=True)  51.4 us
    ppermute x8, starting transfers between devices, from_behind(): return lax.ppermute(shard, 'dev', pairs)  33.7 us
    all_to_all x6, waiting for transfers between devices, exchanged(): return lax.all_to_all(blocks, axis, split_axis=0, concat_axis=0, tiled=True)  32.2 us
    pallas_call x15, Pallas kernels, call(): pl.pallas_call(kernel, name=name, out_shape=shapes, in_specs=ins, out_spe...  29 us
  transfers between devices with their start and end apart: 14, of which 4 were waited for; matrix products, arithmetic and copies ran while one was open for 0% of the time, Pallas kernels for 14%

profile of v3, /device:TPU:16, one launch (start us, length us, event | category | flops | bytes accessed | tf_op | source)
XLA Modules:
  0.0 148.8 jit_solution(9805252128195016765)
XLA Ops:
  1.9 2.6 %start.1 = (bf16[768,256]{1,0:T(8,128)(2,1)}, bf16[64,16,128]{2,1,0:T(8,128)(2,1)}, bf16[512,128]{1,0:T(8,128)(2,1)}) custom-call(f32[1]{0:T(128)} %bitcast.2.ridge, s32[1]{0:T(128)S(6)} %copy.18.cluster, s32[1,4]{1,0:T(1,128)} %far_in.1, f32[512,256]{1,0:T(8,128)} %rs_in.5, f32[64,512]{1,0:T(8,128)} %bitcast.5, s32[1,512]{1,0:T(1,128)} %perm_in.1, ...), custom_call_target="tpu_custom_call" | custom-call | flops 10000000 | tf_op jit(solution)/shard_map/start/pallas_call | solution.py:36
  4.5 16.5 %all-to-all-start = ((bf16[64,16,128]{2,1,0:T(8,128)(2,1)}), bf16[64,16,128]{2,1,0:T(8,128)(2,1)S(1)}, u32[]{:S(2)}, u32[]{:S(2)}) async-start(bf16[64,16,128]{2,1,0:T(8,128)(2,1)} %get-tuple-element.15), calls=%async_computation | async-start | bytes 524288 | tf_op jit(solution)/shard_map/all_to_all | solution.py:320
  22.8 3.5 %collective-permute-start = (bf16[768,256]{1,0:T(8,128)(2,1)}, bf16[768,256]{1,0:T(8,128)(2,1)S(1)}, u32[]{:S(2)}, u32[]{:S(2)}) collective-permute-start(bf16[768,256]{1,0:T(8,128)(2,1)} %get-tuple-element.21.places_in.values_in.refs_1_), channel_id=1, source_target_pairs={{0,1},{1,2},{2,3},{3,4},{4,5},{5,6},{6,7},{7,8},{8,9},{9,10},{10,1... | collective-permute-start | bytes 1179656 | tf_op jit(solution)/shard_map/ppermute | solution.py:311
  26.3 4.6 %collective-permute-start.1 = (bf16[768,256]{1,0:T(8,128)(2,1)}, bf16[768,256]{1,0:T(8,128)(2,1)S(1)}, u32[]{:S(2)}, u32[]{:S(2)}) collective-permute-start(bf16[768,256]{1,0:T(8,128)(2,1)} %get-tuple-element.21.places_in.values_in.refs_1_), channel_id=1, source_target_pairs={{1,0},{2,1},{3,2},{4,3},{5,4},{6,5},{7,6},{8,7},{9,8},{10,9},{11,1... | collective-permute-start | bytes 1179656 | tf_op jit(solution)/shard_map/ppermute | solution.py:311
  33.1 6.7 %collective-permute-start.3 = (bf16[768,256]{1,0:T(8,128)(2,1)}, bf16[768,256]{1,0:T(8,128)(2,1)}, u32[]{:S(2)}, u32[]{:S(2)}) collective-permute-start(bf16[768,256]{1,0:T(8,128)(2,1)} %get-tuple-element.21.places_in.values_in.refs_1_), channel_id=1, source_target_pairs={{2,0},{3,1},{4,2},{5,3},{6,4},{7,5},{8,6},{9,7},{10,8},{11,9},{12,... | collective-permute-start | bytes 1179656 | tf_op jit(solution)/shard_map/ppermute | solution.py:311
  40.7 4.3 %all-to-all-start.1 = ((bf16[8,16,128]{2,1,0:T(8,128)(2,1)}), bf16[8,16,128]{2,1,0:T(8,128)(2,1)S(1)}, u32[]{:S(2)}, u32[]{:S(2)}) async-start(bf16[8,16,128]{2,1,0:T(8,128)(2,1)} %get-tuple-element.17), calls=%async_computation.1 | async-start | bytes 65536 | tf_op jit(solution)/shard_map/all_to_all | solution.py:320
  46.1 4.4 %all-to-all-done.1.all_sums = bf16[8,16,128]{2,1,0:T(8,128)(2,1)S(1)} async-done(((bf16[8,16,128]{2,1,0:T(8,128)(2,1)}), bf16[8,16,128]{2,1,0:T(8,128)(2,1)S(1)}, u32[]{:S(2)}, u32[]{:S(2)}) %all-to-all-start.1) | async-done | bytes 32800 | tf_op jit(solution)/shard_map/all_to_all | solution.py:320
  52.5 11.0 %all-to-all-start.2 = ((bf16[64,3,8,128]{3,2,1,0:T(8,128)(2,1)}), bf16[64,3,8,128]{3,2,1,0:T(8,128)(2,1)S(1)}, u32[]{:S(2)}, u32[]{:S(2)}) async-start(bf16[64,3,8,128]{3,2,1,0:T(8,128)(2,1)} %couple.2.refs_7_), calls=%async_computation.2 | async-start | bytes 786432 | tf_op jit(solution)/shard_map/all_to_all | solution.py:320
  63.5 2.3 %near_pair_0.2.refs_2_ = f32[512,256]{1,0:T(8,128)S(1)} custom-call(s32[1,4]{1,0:T(1,128)S(1)} %copy-done.7, bf16[768,256]{1,0:T(8,128)(2,1)} %get-tuple-element.21.places_in.values_in.refs_1_, f32[512,256]{1,0:T(8,128)S(1)} %near_own.2._.refs_2_, bf16[768,256]{1,0:T(8,128)(2,1)S(1)} %collective-permute-done.refs_3_.refs_4_, ...), custom_call_target="tpu_custom_call" | custom-call | flops 10000000 | tf_op jit(solution)/shard_map/near_pair_0/pallas_call | solution.py:36
  65.9 2.6 %near_pair_2.2.near = f32[512,256]{1,0:T(8,128)S(1)} custom-call(s32[1,4]{1,0:T(1,128)S(1)} %copy-done.7, bf16[768,256]{1,0:T(8,128)(2,1)} %get-tuple-element.21.places_in.values_in.refs_1_, f32[512,256]{1,0:T(8,128)S(1)} %near_pair_0.2.refs_2_, bf16[768,256]{1,0:T(8,128)(2,1)S(1)} %collective-permute-done.2.refs_3_.refs_4_, ...), custom_call_target="tpu_custom_call" | custom-call | flops 10000000000 | tf_op jit(solution)/shard_map/near_pair_2/pallas_call | solution.py:36
  68.5 11.9 %all-to-all-done.2.arrived = bf16[64,3,8,128]{3,2,1,0:T(8,128)(2,1)S(1)} async-done(((bf16[64,3,8,128]{3,2,1,0:T(8,128)(2,1)}), bf16[64,3,8,128]{3,2,1,0:T(8,128)(2,1)S(1)}, u32[]{:S(2)}, u32[]{:S(2)}) %all-to-all-start.2) | async-done | bytes 393248 | tf_op jit(solution)/shard_map/all_to_all | solution.py:320
  80.4 2.6 %middle.1 = (bf16[512,256]{1,0:T(8,128)(2,1)}, bf16[64,8,128]{2,1,0:T(8,128)(2,1)}, f32[512,256]{1,0:T(8,128)}) custom-call(f32[1]{0:T(128)} %bitcast.3.ridge, bf16[64,3,8,128]{3,2,1,0:T(8,128)(2,1)S(1)} %all-to-all-done.2.arrived, bf16[1,4,128,128]{3,2,1,0:T(8,128)(2,1)S(1)} %copy-done.3, bf16[1,128,128]{2,1,0:T(8,128)(2,1)S(1)} %copy-done.5, ...), custom_call_target="tpu_custom_call" | custom-call | flops 10000000 | tf_op jit(solution)/shard_map/middle/pallas_call | solution.py:36
  83.0 5.2 %all-to-all-start.3 = ((bf16[64,8,128]{2,1,0:T(8,128)(2,1)}), bf16[64,8,128]{2,1,0:T(8,128)(2,1)S(1)}, u32[]{:S(2)}, u32[]{:S(2)}) async-start(bf16[64,8,128]{2,1,0:T(8,128)(2,1)} %get-tuple-element.22), calls=%async_computation.3 | async-start | bytes 262144 | tf_op jit(solution)/shard_map/all_to_all | solution.py:320
  90.0 3.4 %collective-permute-start.4 = (bf16[512,256]{1,0:T(8,128)(2,1)S(1)}, bf16[512,256]{1,0:T(8,128)(2,1)S(1)}, u32[]{:S(2)}, u32[]{:S(2)}) collective-permute-start(bf16[512,256]{1,0:T(8,128)(2,1)S(1)} %copy-done.10), channel_id=1, source_target_pairs={{0,1},{1,2},{2,3},{3,4},{4,5},{5,6},{6,7},{7,8},{8,9},{9,10},{10,1... | collective-permute-start | bytes 786440 | tf_op jit(solution)/shard_map/ppermute | solution.py:311
  93.4 4.6 %collective-permute-start.5 = (bf16[512,256]{1,0:T(8,128)(2,1)S(1)}, bf16[512,256]{1,0:T(8,128)(2,1)S(1)}, u32[]{:S(2)}, u32[]{:S(2)}) collective-permute-start(bf16[512,256]{1,0:T(8,128)(2,1)S(1)} %copy-done.10), channel_id=1, source_target_pairs={{1,0},{2,1},{3,2},{4,3},{5,4},{6,5},{7,6},{8,7},{9,8},{10,9},{11,1... | collective-permute-start | bytes 786440 | tf_op jit(solution)/shard_map/ppermute | solution.py:311
  98.0 2.2 %collective-permute-start.6 = (bf16[512,256]{1,0:T(8,128)(2,1)S(1)}, bf16[512,256]{1,0:T(8,128)(2,1)}, u32[]{:S(2)}, u32[]{:S(2)}) collective-permute-start(bf16[512,256]{1,0:T(8,128)(2,1)S(1)} %copy-done.10), channel_id=1, source_target_pairs={{0,2},{1,3},{2,4},{3,5},{4,6},{5,7},{6,8},{7,9},{8,10},{9,11},{10,... | collective-permute-start | bytes 786440 | tf_op jit(solution)/shard_map/ppermute | solution.py:311
  100.2 6.7 %collective-permute-start.7 = (bf16[512,256]{1,0:T(8,128)(2,1)S(1)}, bf16[512,256]{1,0:T(8,128)(2,1)}, u32[]{:S(2)}, u32[]{:S(2)}) collective-permute-start(bf16[512,256]{1,0:T(8,128)(2,1)S(1)} %copy-done.10), channel_id=1, source_target_pairs={{2,0},{3,1},{4,2},{5,3},{6,4},{7,5},{8,6},{9,7},{10,8},{11,9},{12,... | collective-permute-start | bytes 786440 | tf_op jit(solution)/shard_map/ppermute | solution.py:311
  107.7 3.3 %all-to-all-start.4 = ((bf16[8,16,128]{2,1,0:T(8,128)(2,1)}), bf16[8,16,128]{2,1,0:T(8,128)(2,1)S(1)}, u32[]{:S(2)}, u32[]{:S(2)}) async-start(bf16[8,16,128]{2,1,0:T(8,128)(2,1)} %get-tuple-element.24), calls=%async_computation.4 | async-start | bytes 65536 | tf_op jit(solution)/shard_map/all_to_all | solution.py:320
  112.1 4.3 %all-to-all-done.4.all_sums = bf16[8,16,128]{2,1,0:T(8,128)(2,1)S(1)} async-done(((bf16[8,16,128]{2,1,0:T(8,128)(2,1)}), bf16[8,16,128]{2,1,0:T(8,128)(2,1)S(1)}, u32[]{:S(2)}, u32[]{:S(2)}) %all-to-all-start.4) | async-done | bytes 32800 | tf_op jit(solution)/shard_map/all_to_all | solution.py:320
  118.4 11.1 %all-to-all-start.5 = ((bf16[64,3,8,128]{3,2,1,0:T(8,128)(2,1)}), bf16[64,3,8,128]{3,2,1,0:T(8,128)(2,1)S(1)}, u32[]{:S(2)}, u32[]{:S(2)}) async-start(bf16[64,3,8,128]{3,2,1,0:T(8,128)(2,1)} %couple.3.refs_7_), calls=%async_computation.5 | async-start | bytes 786432 | tf_op jit(solution)/shard_map/all_to_all | solution.py:320
  129.5 2.3 %near_pair_0.3.refs_2_ = f32[512,256]{1,0:T(8,128)S(1)} custom-call(s32[1,4]{1,0:T(1,128)S(1)} %copy-done.7, bf16[768,256]{1,0:T(8,128)(2,1)} %get-tuple-element.21.places_in.values_in.refs_1_, f32[512,256]{1,0:T(8,128)S(1)} %near_own.3._.refs_2_, bf16[768,256]{1,0:T(8,128)(2,1)S(1)} %collective-permute-done.refs_3_.refs_4_, ...), custom_call_target="tpu_custom_call" | custom-call | flops 10000000 | tf_op jit(solution)/shard_map/near_pair_0/pallas_call | solution.py:36
  131.8 2.6 %near_pair_2.3.near = f32[512,256]{1,0:T(8,128)S(1)} custom-call(s32[1,4]{1,0:T(1,128)S(1)} %copy-done.7, bf16[768,256]{1,0:T(8,128)(2,1)} %get-tuple-element.21.places_in.values_in.refs_1_, f32[512,256]{1,0:T(8,128)S(1)} %near_pair_0.3.refs_2_, bf16[768,256]{1,0:T(8,128)(2,1)S(1)} %copy-done.9, bf16[512,256]{1,0:T(8,128)(2,1)} %collective-permute-done.6.refs_4_, ...), custom_call_target="tpu_custom_call" | custom-call | flops 10000000000 | tf_op jit(solution)/shard_map/near_pair_2/pallas_call | solution.py:36
  134.5 11.6 %all-to-all-done.5.arrived = bf16[64,3,8,128]{3,2,1,0:T(8,128)(2,1)S(1)} async-done(((bf16[64,3,8,128]{3,2,1,0:T(8,128)(2,1)}), bf16[64,3,8,128]{3,2,1,0:T(8,128)(2,1)S(1)}, u32[]{:S(2)}, u32[]{:S(2)}) %all-to-all-start.5) | async-done | bytes 393248 | tf_op jit(solution)/shard_map/all_to_all | solution.py:320
  146.1 2.6 %end.1 = (f32[512,256]{1,0:T(8,128)}, f32[512,256]{1,0:T(8,128)}) custom-call(f32[1]{0:T(128)} %bitcast.4.ridge, bf16[64,3,8,128]{3,2,1,0:T(8,128)(2,1)S(1)} %all-to-all-done.5.arrived, bf16[1,4,128,128]{3,2,1,0:T(8,128)(2,1)S(1)} %copy-done.3, bf16[1,128,128]{2,1,0:T(8,128)(2,1)S(1)} %copy-done.5, bf16[512,128]{1,0:T(8,128)(2,1)S(1)} %copy-done.4, ...), custom_call_target="tpu_custom_call" | custom-call | flops 10000000 | tf_op jit(solution)/shard_map/end/pallas_call | solution.py:36
  (41 shorter events, 13.7 us)
Async XLA Ops:
  4.5 35.2 %all-to-all-start = ((bf16[64,16,128]{2,1,0:T(8,128)(2,1)}), bf16[64,16,128]{2,1,0:T(8,128)(2,1)S(1)}, u32[]{:S(2)}, u32[]{:S(2)}) async-start(bf16[64,16,128]{2,1,0:T(8,128)(2,1)} %get-tuple-element.15), calls=%async_computation | async-start | bytes 524288 | tf_op jit(solution)/shard_map/all_to_all | solution.py:320
  22.8 27.6 %copy-start.2 = (bf16[4,4,128,128]{3,2,1,0:T(8,128)(2,1)S(1)}, bf16[4,4,128,128]{3,2,1,0:T(8,128)(2,1)}, u32[]{:S(2)}) copy-start(bf16[4,4,128,128]{3,2,1,0:T(8,128)(2,1)} %blocks.3) | copy-start | bytes 1572868
  22.8 40.7 %collective-permute-start = (bf16[768,256]{1,0:T(8,128)(2,1)}, bf16[768,256]{1,0:T(8,128)(2,1)S(1)}, u32[]{:S(2)}, u32[]{:S(2)}) collective-permute-start(bf16[768,256]{1,0:T(8,128)(2,1)} %get-tuple-element.21.places_in.values_in.refs_1_), channel_id=1, source_target_pairs={{0,1},{1,2},{2,3},{3,4},{4,5},{5,6},{6,7},{7,8},{8,9},{9,10},{10,1... | collective-permute-start | bytes 1179656 | tf_op jit(solution)/shard_map/ppermute | solution.py:311
  26.3 37.2 %collective-permute-start.1 = (bf16[768,256]{1,0:T(8,128)(2,1)}, bf16[768,256]{1,0:T(8,128)(2,1)S(1)}, u32[]{:S(2)}, u32[]{:S(2)}) collective-permute-start(bf16[768,256]{1,0:T(8,128)(2,1)} %get-tuple-element.21.places_in.values_in.refs_1_), channel_id=1, source_target_pairs={{1,0},{2,1},{3,2},{4,3},{5,4},{6,5},{7,6},{8,7},{9,8},{10,9},{11,1... | collective-permute-start | bytes 1179656 | tf_op jit(solution)/shard_map/ppermute | solution.py:311
  30.9 34.9 %collective-permute-start.2 = (bf16[768,256]{1,0:T(8,128)(2,1)}, bf16[768,256]{1,0:T(8,128)(2,1)S(1)}, u32[]{:S(2)}, u32[]{:S(2)}) collective-permute-start(bf16[768,256]{1,0:T(8,128)(2,1)} %get-tuple-element.21.places_in.values_in.refs_1_), channel_id=1, source_target_pairs={{0,2},{1,3},{2,4},{3,5},{4,6},{5,7},{6,8},{7,9},{8,10},{9,11},{10,... | collective-permute-start | bytes 1179656 | tf_op jit(solution)/shard_map/ppermute | solution.py:311
  33.1 32.8 %collective-permute-start.3 = (bf16[768,256]{1,0:T(8,128)(2,1)}, bf16[768,256]{1,0:T(8,128)(2,1)}, u32[]{:S(2)}, u32[]{:S(2)}) collective-permute-start(bf16[768,256]{1,0:T(8,128)(2,1)} %get-tuple-element.21.places_in.values_in.refs_1_), channel_id=1, source_target_pairs={{2,0},{3,1},{4,2},{5,3},{6,4},{7,5},{8,6},{9,7},{10,8},{11,9},{12,... | collective-permute-start | bytes 1179656 | tf_op jit(solution)/shard_map/ppermute | solution.py:311
  40.7 9.7 %all-to-all-start.1 = ((bf16[8,16,128]{2,1,0:T(8,128)(2,1)}), bf16[8,16,128]{2,1,0:T(8,128)(2,1)S(1)}, u32[]{:S(2)}, u32[]{:S(2)}) async-start(bf16[8,16,128]{2,1,0:T(8,128)(2,1)} %get-tuple-element.17), calls=%async_computation.1 | async-start | bytes 65536 | tf_op jit(solution)/shard_map/all_to_all | solution.py:320
  45.0 5.5 %copy-start.6 = (s32[4,4]{1,0:T(4,128)S(1)}, s32[4,4]{1,0:T(4,128)}, u32[]{:S(2)}) copy-start(s32[4,4]{1,0:T(4,128)} %far_clusters.3) | copy-start | bytes 196
  52.4 11.1 %copy-start.1 = (bf16[64,3,8,128]{3,2,1,0:T(8,128)(2,1)S(1)}, bf16[64,3,8,128]{3,2,1,0:T(8,128)(2,1)}, u32[]{:S(2)}) copy-start(bf16[64,3,8,128]{3,2,1,0:T(8,128)(2,1)} %couple.2.refs_7_) | copy-start | bytes 1179652
  52.4 11.1 %copy-start.7 = (s32[1,4]{1,0:T(1,128)S(1)}, s32[1,4]{1,0:T(1,128)}, u32[]{:S(2)}) copy-start(s32[1,4]{1,0:T(1,128)} %refs_0_.7) | copy-start | bytes 52
  52.5 27.9 %all-to-all-start.2 = ((bf16[64,3,8,128]{3,2,1,0:T(8,128)(2,1)}), bf16[64,3,8,128]{3,2,1,0:T(8,128)(2,1)S(1)}, u32[]{:S(2)}, u32[]{:S(2)}) async-start(bf16[64,3,8,128]{3,2,1,0:T(8,128)(2,1)} %couple.2.refs_7_), calls=%async_computation.2 | async-start | bytes 786432 | tf_op jit(solution)/shard_map/all_to_all | solution.py:320
  65.8 14.6 %copy-start.3 = (bf16[1,4,128,128]{3,2,1,0:T(8,128)(2,1)S(1)}, bf16[1,4,128,128]{3,2,1,0:T(8,128)(2,1)}, u32[]{:S(2)}) copy-start(bf16[1,4,128,128]{3,2,1,0:T(8,128)(2,1)} %couplings.3) | copy-start | bytes 393220
  65.8 14.6 %copy-start.4 = (bf16[512,128]{1,0:T(8,128)(2,1)S(1)}, bf16[512,128]{1,0:T(8,128)(2,1)}, u32[]{:S(2)}) copy-start(bf16[512,128]{1,0:T(8,128)(2,1)} %get-tuple-element.20.basis) | copy-start | bytes 393220
  65.8 14.6 %copy-start.5 = (bf16[1,128,128]{2,1,0:T(8,128)(2,1)S(1)}, bf16[1,128,128]{2,1,0:T(8,128)(2,1)}, u32[]{:S(2)}) copy-start(bf16[1,128,128]{2,1,0:T(8,128)(2,1)} %transfer.3) | copy-start | bytes 98308
  65.9 2.6 %copy-start.8 = (bf16[768,256]{1,0:T(8,128)(2,1)}, bf16[768,256]{1,0:T(8,128)(2,1)S(1)}, u32[]{:S(2)}) copy-start(bf16[768,256]{1,0:T(8,128)(2,1)S(1)} %collective-permute-done.2.refs_3_.refs_4_) | copy-start | bytes 1179652
  83.0 23.8 %all-to-all-start.3 = ((bf16[64,8,128]{2,1,0:T(8,128)(2,1)}), bf16[64,8,128]{2,1,0:T(8,128)(2,1)S(1)}, u32[]{:S(2)}, u32[]{:S(2)}) async-start(bf16[64,8,128]{2,1,0:T(8,128)(2,1)} %get-tuple-element.22), calls=%async_computation.3 | async-start | bytes 262144 | tf_op jit(solution)/shard_map/all_to_all | solution.py:320
  90.0 39.5 %collective-permute-start.4 = (bf16[512,256]{1,0:T(8,128)(2,1)S(1)}, bf16[512,256]{1,0:T(8,128)(2,1)S(1)}, u32[]{:S(2)}, u32[]{:S(2)}) collective-permute-start(bf16[512,256]{1,0:T(8,128)(2,1)S(1)} %copy-done.10), channel_id=1, source_target_pairs={{0,1},{1,2},{2,3},{3,4},{4,5},{5,6},{6,7},{7,8},{8,9},{9,10},{10,1... | collective-permute-start | bytes 786440 | tf_op jit(solution)/shard_map/ppermute | solution.py:311
  93.4 36.1 %collective-permute-start.5 = (bf16[512,256]{1,0:T(8,128)(2,1)S(1)}, bf16[512,256]{1,0:T(8,128)(2,1)S(1)}, u32[]{:S(2)}, u32[]{:S(2)}) collective-permute-start(bf16[512,256]{1,0:T(8,128)(2,1)S(1)} %copy-done.10), channel_id=1, source_target_pairs={{1,0},{2,1},{3,2},{4,3},{5,4},{6,5},{7,6},{8,7},{9,8},{10,9},{11,1... | collective-permute-start | bytes 786440 | tf_op jit(solution)/shard_map/ppermute | solution.py:311
  98.0 33.8 %collective-permute-start.6 = (bf16[512,256]{1,0:T(8,128)(2,1)S(1)}, bf16[512,256]{1,0:T(8,128)(2,1)}, u32[]{:S(2)}, u32[]{:S(2)}) collective-permute-start(bf16[512,256]{1,0:T(8,128)(2,1)S(1)} %copy-done.10), channel_id=1, source_target_pairs={{0,2},{1,3},{2,4},{3,5},{4,6},{5,7},{6,8},{7,9},{8,10},{9,11},{10,... | collective-permute-start | bytes 786440 | tf_op jit(solution)/shard_map/ppermute | solution.py:311
  100.2 31.6 %collective-permute-start.7 = (bf16[512,256]{1,0:T(8,128)(2,1)S(1)}, bf16[512,256]{1,0:T(8,128)(2,1)}, u32[]{:S(2)}, u32[]{:S(2)}) collective-permute-start(bf16[512,256]{1,0:T(8,128)(2,1)S(1)} %copy-done.10), channel_id=1, source_target_pairs={{2,0},{3,1},{4,2},{5,3},{6,4},{7,5},{8,6},{9,7},{10,8},{11,9},{12,... | collective-permute-start | bytes 786440 | tf_op jit(solution)/shard_map/ppermute | solution.py:311
  107.7 8.7 %all-to-all-start.4 = ((bf16[8,16,128]{2,1,0:T(8,128)(2,1)}), bf16[8,16,128]{2,1,0:T(8,128)(2,1)S(1)}, u32[]{:S(2)}, u32[]{:S(2)}) async-start(bf16[8,16,128]{2,1,0:T(8,128)(2,1)} %get-tuple-element.24), calls=%async_computation.4 | async-start | bytes 65536 | tf_op jit(solution)/shard_map/all_to_all | solution.py:320
  118.4 11.1 %copy-start = (bf16[64,3,8,128]{3,2,1,0:T(8,128)(2,1)S(1)}, bf16[64,3,8,128]{3,2,1,0:T(8,128)(2,1)}, u32[]{:S(2)}) copy-start(bf16[64,3,8,128]{3,2,1,0:T(8,128)(2,1)} %couple.3.refs_7_) | copy-start | bytes 1179652
  118.4 27.6 %all-to-all-start.5 = ((bf16[64,3,8,128]{3,2,1,0:T(8,128)(2,1)}), bf16[64,3,8,128]{3,2,1,0:T(8,128)(2,1)S(1)}, u32[]{:S(2)}, u32[]{:S(2)}) async-start(bf16[64,3,8,128]{3,2,1,0:T(8,128)(2,1)} %couple.3.refs_7_), calls=%async_computation.5 | async-start | bytes 786432 | tf_op jit(solution)/shard_map/all_to_all | solution.py:320
  129.5 2.3 %copy-start.9 = (bf16[768,256]{1,0:T(8,128)(2,1)S(1)}, bf16[768,256]{1,0:T(8,128)(2,1)}, u32[]{:S(2)}) copy-start(bf16[768,256]{1,0:T(8,128)(2,1)} %copy-done.8) | copy-start | bytes 1179652
  (1 other events, 1.8 us)

commit v4 on v3

--- a/solution.py
+++ b/solution.py
@@ -9,7 +9,7 @@
 N_GRP, N_DEV, CPG = 8, 64, 4
 FAR1, FAR2 = 4, 4
 COLS = OUT // N_DEV
-NEAR = (-1, 1, -2, 2)
+NEAR = 4
 
 KERNEL_LOG2 = -1.4426950408889634 / 32.0
 GAP, TOP = 0.5, 8.0
@@ -20,7 +20,7 @@
 ANY = pl.BlockSpec(memory_space=pl.ANY)
 HBM = pl.BlockSpec(memory_space=pltpu.HBM)
 LIMIT = 32 * 2**20
-SHORT, LONG = 10**7, 10**10
+SHORT, MID, LONG = 10**7, 10**10, 10**9
 ROWS = 128
 
 
@@ -151,7 +151,7 @@
     ).astype(BF16)
 
 
-def partners_kernel(skeletons, told, sent_out, staged, sent, sems):
+def partners_kernel(skeletons, told, sent_out, done, staged, sent, sems):
     lane = lax.broadcasted_iota(jnp.int32, (N_DEV, N_DEV), 1).astype(F32)
     pick = jnp.concatenate(
         [jnp.where(lane == told[:, k : k + 1], 1.0, 0.0) for k in range(FAR1)], axis=0
@@ -163,6 +163,7 @@
                 N_DEV * k : N_DEV * (k + 1), RANK * i : RANK * (i + 1)
             ]
     sent[...] = staged[...].reshape(N_DEV, 2, 8, RANK).astype(BF16)
+    done[...] = jnp.zeros_like(done)
     wait(started(((sent, sent_out.at[:, :2]),), sems))
 
 
@@ -172,7 +173,7 @@
     row = lax.broadcasted_iota(jnp.int32, (rows, N_GRP * rows), 0)
     lane = lax.broadcasted_iota(jnp.int32, (rows, N_GRP * rows), 1)
     column, cluster = row // CPG, row % CPG
-    total = jnp.zeros((rows, CPG * RANK), F32)
+    total = jnp.zeros((CPG * RANK, rows), F32)
     for k in range(FAR2):
         target = CPG * column
         for c in range(CPG):
@@ -180,12 +181,12 @@
             target += jnp.where(cluster == c, rows * (f // CPG) + f % CPG, 0)
         pick = jnp.where(lane == target, 1.0, 0.0).astype(BF16)
         picked = dot(pick, sums).astype(BF16)
-        block = blocks[:, k].reshape(CPG * RANK, RANK)
-        total += dot(picked, block, ((1,), (1,)))
-    coupled = jnp.zeros((rows, RANK), F32)
-    own = cluster[:, :RANK]
+        total += dot(blocks[:, k].reshape(CPG * RANK, RANK), picked, ((1,), (1,)))
+    own = lax.broadcasted_iota(jnp.int32, (RANK, rows), 1) % CPG
+    coupled = jnp.zeros((RANK, rows), F32)
     for c in range(CPG):
-        coupled += jnp.where(own == c, total[:, RANK * c : RANK * (c + 1)], 0.0)
+        coupled += jnp.where(own == c, total[RANK * c : RANK * (c + 1)], 0.0)
+    coupled = coupled.T
     coupled = coupled.astype(BF16)
     lane = lax.broadcasted_iota(jnp.int32, (N_DEV, rows), 1).astype(F32)
     pick = jnp.concatenate(
@@ -201,13 +202,13 @@
 
 def local_field(arrived, couplings, transfer, staged):
     staged[...] = arrived[...].astype(F32).reshape(N_DEV * 24, RANK)
-    local = jnp.zeros((RANK, OUT), F32)
+    local = jnp.zeros((OUT, RANK), F32)
     for k in range(FAR1 + 1):
         skeleton = jnp.concatenate(
             [staged[pl.ds(COLS * k + i, N_DEV, stride=24), :] for i in range(COLS)], axis=0
         ).astype(BF16)
-        local += dot(couplings[0, k] if k < FAR1 else transfer[0], skeleton, ((1,), (1,)))
-    return local.astype(BF16)
+        local += dot(skeleton, couplings[0, k] if k < FAR1 else transfer[0], ((1,), (1,)))
+    return local.T.astype(BF16)
 
 
 def middle_kernel(
@@ -267,7 +268,7 @@
 def listed(near_list, offset):
     leaf = lax.axis_index("grp") * N_DEV + lax.axis_index("dev")
     hit = near_list[0, 0] == leaf + offset
-    for k in range(1, len(NEAR)):
+    for k in range(1, NEAR):
         hit = hit | (near_list[0, k] == leaf + offset)
     return hit
 
@@ -311,9 +312,9 @@
     return lax.ppermute(shard, "dev", pairs)
 
 
-def from_near(shard, after):
+def from_pair(shard, distance, after):
     shard, _ = lax.optimization_barrier((shard, after))
-    return [from_behind(shard, -offset) for offset in NEAR]
+    return from_behind(shard, distance), from_behind(shard, -distance)
 
 
 def exchanged(blocks, axis):
@@ -380,13 +381,13 @@
         )
         return near
 
-    def near_pair(at, near, first, fields, after, flops):
+    def near_pair(distance, near, first, fields, after, flops):
         (near,) = call(
-            lambda *refs: near_pair_kernel(NEAR[at : at + 2], *refs),
-            f"near_pair_{at}",
+            lambda *refs: near_pair_kernel((-distance, distance), *refs),
+            f"near_pair_{distance}",
             [(field, F32, VMEM)],
             [SMEM, HBM, VMEM] + [ANY] * 5,
-            (near_list, wc, near, first[at], fields[at], first[at + 1], fields[at + 1], after),
+            (near_list, wc, near, first[0], fields[0], first[1], fields[1], after),
             [pltpu.VMEM((3, 4 * DIM, OUT), BF16), pltpu.VMEM((2, *field), BF16), dma((5,))],
             flops,
         )
@@ -394,10 +395,10 @@
 
     def through_owners(sums, skeletons):
         all_sums = exchanged(sums, "grp")
-        (partners,) = call(
+        partners, done = call(
             partners_kernel,
             "partners",
-            [((N_DEV, 3, 8, RANK), BF16, HBM)],
+            [((N_DEV, 3, 8, RANK), BF16, HBM), ((8, RANK), F32, VMEM)],
             [VMEM] * 2,
             (skeletons, told),
             [rows16, pltpu.VMEM((N_DEV, 2, 8, RANK), BF16), dma((1,))],
@@ -413,11 +414,11 @@
             SHORT,
             {4: 0},
         )
-        return sent, exchanged(sent, "dev")
+        return sent, exchanged(sent, "dev"), done
 
     arrived = exchanged(sent, "dev")
     near = near_own(wc)
-    first = from_near(wc, near)
+    first2 = from_pair(wc, 2, near)
     sums, told, skeletons = call(
         sums_first_kernel,
         "sums_first",
@@ -427,9 +428,10 @@
         [rows16, narrow],
         SHORT,
     )
-    sent, arrived = through_owners(sums, skeletons)
-    near = near_pair(0, near, first, first, sent, SHORT)
-    near = near_pair(2, near, first, first, sent, LONG)
+    sent, arrived, done = through_owners(sums, skeletons)
+    first1 = from_pair(wc, 1, done)
+    near = near_pair(2, near, first2, first2, sent, MID)
+    near = near_pair(1, near, first1, first1, sent, LONG)
     w, sent, r1 = call(
         middle_kernel,
         "middle",
@@ -449,7 +451,7 @@
     )
     arrived = exchanged(sent, "dev")
     near = near_own(w)
-    fields = from_near(w, near)
+    fields2 = from_pair(w, 2, near)
     sums, skeletons = call(
         sums_kernel,
         "sums",
@@ -459,9 +461,10 @@
         [rows8, narrow],
         SHORT,
     )
-    sent, arrived = through_owners(sums, skeletons)
-    near = near_pair(0, near, first, fields, sent, SHORT)
-    near = near_pair(2, near, first, fields, sent, LONG)
+    sent, arrived, done = through_owners(sums, skeletons)
+    fields1 = from_pair(w, 1, done)
+    near = near_pair(2, near, first2, fields2, sent, MID)
+    near = near_pair(1, near, first1, fields1, sent, LONG)
     return tuple(
         call(
             end_kernel,

time: 150 us -> 145 us (0.967)
  the two profiles are of different devices: /device:TPU:16 before, /device:TPU:2 now
where the time goes in v4:
time: 145 us; the launch traced here: 144 us
  starting transfers between devices  74.5 us (51%)
  waiting for transfers between devices  38.5 us (27%)
  Pallas kernels  28.1 us (19%)
  between operations  2.47 us (2%)
    all_to_all x6, starting transfers between devices, exchanged(): return lax.all_to_all(blocks, axis, split_axis=0, concat_axis=0, tiled=True)  54.5 us
    all_to_all x6, waiting for transfers between devices, exchanged(): return lax.all_to_all(blocks, axis, split_axis=0, concat_axis=0, tiled=True)  38.5 us
    pallas_call x15, Pallas kernels, call(): pl.pallas_call(kernel, name=name, out_shape=shapes, in_specs=ins, out_spe...  28.1 us
    ppermute x8, starting transfers between devices, from_behind(): return lax.ppermute(shard, 'dev', pairs)  20 us
  transfers between devices with their start and end apart: 14, of which 4 were waited for; matrix products, arithmetic and copies ran while one was open for 0% of the time, Pallas kernels for 14%

profile of v4, /device:TPU:2, one launch (start us, length us, event | category | flops | bytes accessed | tf_op | source)
XLA Modules:
  0.0 143.6 jit_solution(11515803534539816478)
XLA Ops:
  1.9 2.6 %start.1 = (bf16[768,256]{1,0:T(8,128)(2,1)}, bf16[64,16,128]{2,1,0:T(8,128)(2,1)}, bf16[512,128]{1,0:T(8,128)(2,1)}) custom-call(f32[1]{0:T(128)} %bitcast.2.ridge, s32[1]{0:T(128)S(6)} %copy.18.cluster, s32[1,4]{1,0:T(1,128)} %far_in.1, f32[512,256]{1,0:T(8,128)} %rs_in.5, f32[64,512]{1,0:T(8,128)} %bitcast.5, s32[1,512]{1,0:T(1,128)} %perm_in.1, ...), custom_call_target="tpu_custom_call" | custom-call | flops 10000000 | tf_op jit(solution)/shard_map/start/pallas_call | solution.py:36
  4.5 16.6 %all-to-all-start = ((bf16[64,16,128]{2,1,0:T(8,128)(2,1)}), bf16[64,16,128]{2,1,0:T(8,128)(2,1)S(1)}, u32[]{:S(2)}, u32[]{:S(2)}) async-start(bf16[64,16,128]{2,1,0:T(8,128)(2,1)} %get-tuple-element.17), calls=%async_computation | async-start | bytes 524288 | tf_op jit(solution)/shard_map/all_to_all | solution.py:321
  21.2 1.8 %near_own.2._.refs_2_ = f32[512,256]{1,0:T(8,128)S(1)} custom-call(bf16[768,256]{1,0:T(8,128)(2,1)} %get-tuple-element.24.places_in.values_in.refs_1_, bf16[768,256]{1,0:T(8,128)(2,1)} %get-tuple-element.24.places_in.values_in.refs_1_), custom_call_target="tpu_custom_call" | custom-call | flops 10000000 | tf_op jit(solution)/shard_map/near_own/pallas_call | solution.py:36
  22.9 4.5 %collective-permute-start = (bf16[768,256]{1,0:T(8,128)(2,1)}, bf16[768,256]{1,0:T(8,128)(2,1)S(1)}, u32[]{:S(2)}, u32[]{:S(2)}) collective-permute-start(bf16[768,256]{1,0:T(8,128)(2,1)} %get-tuple-element.24.places_in.values_in.refs_1_), channel_id=1, source_target_pairs={{0,2},{1,3},{2,4},{3,5},{4,6},{5,7},{6,8},{7,9},{8,10},{9,11},{10,... | collective-permute-start | bytes 1179656 | tf_op jit(solution)/shard_map/ppermute | solution.py:312
  28.8 7.4 %all-to-all-done.arrived = bf16[64,16,128]{2,1,0:T(8,128)(2,1)S(1)} async-done(((bf16[64,16,128]{2,1,0:T(8,128)(2,1)}), bf16[64,16,128]{2,1,0:T(8,128)(2,1)S(1)}, u32[]{:S(2)}, u32[]{:S(2)}) %all-to-all-start) | async-done | bytes 262176 | tf_op jit(solution)/shard_map/all_to_all | solution.py:321
  37.0 4.8 %all-to-all-start.1 = ((bf16[8,16,128]{2,1,0:T(8,128)(2,1)}), bf16[8,16,128]{2,1,0:T(8,128)(2,1)S(1)}, u32[]{:S(2)}, u32[]{:S(2)}) async-start(bf16[8,16,128]{2,1,0:T(8,128)(2,1)} %get-tuple-element.19), calls=%async_computation.1 | async-start | bytes 65536 | tf_op jit(solution)/shard_map/all_to_all | solution.py:321
  41.9 2.7 %collective-permute-start.2 = (bf16[768,256]{1,0:T(8,128)(2,1)}, bf16[768,256]{1,0:T(8,128)(2,1)S(1)}, u32[]{:S(2)}, u32[]{:S(2)}) collective-permute-start(bf16[768,256]{1,0:T(8,128)(2,1)} %get-tuple-element.24.places_in.values_in.refs_1_), channel_id=1, source_target_pairs={{0,1},{1,2},{2,3},{3,4},{4,5},{5,6},{6,7},{7,8},{8,9},{9,10},{10,1... | collective-permute-start | bytes 1179656 | tf_op jit(solution)/shard_map/ppermute | solution.py:312
  47.6 2.2 %couple.2.refs_7_ = bf16[64,3,8,128]{3,2,1,0:T(8,128)(2,1)} custom-call(s32[4,4]{1,0:T(4,128)S(1)} %copy-done.6, bf16[8,16,128]{2,1,0:T(8,128)(2,1)S(1)} %all-to-all-done.1.all_sums, bf16[4,4,128,128]{3,2,1,0:T(8,128)(2,1)S(1)} %copy-done, f32[64,128]{1,0:T(8,128)S(1)} %get-tuple-element.20.told, ...), custom_call_target="tpu_custom_call", output_to_operand_aliasing={{}: (4, {})} | custom-call | flops 10000000 | tf_op jit(solution)/shard_map/couple/pallas_call | solution.py:36
  49.8 10.8 %all-to-all-start.2 = ((bf16[64,3,8,128]{3,2,1,0:T(8,128)(2,1)}), bf16[64,3,8,128]{3,2,1,0:T(8,128)(2,1)S(1)}, u32[]{:S(2)}, u32[]{:S(2)}) async-start(bf16[64,3,8,128]{3,2,1,0:T(8,128)(2,1)} %couple.2.refs_7_), calls=%async_computation.2 | async-start | bytes 786432 | tf_op jit(solution)/shard_map/all_to_all | solution.py:321
  62.2 1.8 %near_pair_1.2.near = f32[512,256]{1,0:T(8,128)S(1)} custom-call(s32[1,4]{1,0:T(1,128)S(1)} %copy-done.7, bf16[768,256]{1,0:T(8,128)(2,1)} %get-tuple-element.24.places_in.values_in.refs_1_, f32[512,256]{1,0:T(8,128)S(1)} %near_pair_2.2.refs_2_, bf16[768,256]{1,0:T(8,128)(2,1)S(1)} %collective-permute-done.2.refs_3_.refs_4_, ...), custom_call_target="tpu_custom_call" | custom-call | flops 1000000000 | tf_op jit(solution)/shard_map/near_pair_1/pallas_call | solution.py:36
  64.1 13.2 %all-to-all-done.2.arrived = bf16[64,3,8,128]{3,2,1,0:T(8,128)(2,1)S(1)} async-done(((bf16[64,3,8,128]{3,2,1,0:T(8,128)(2,1)}), bf16[64,3,8,128]{3,2,1,0:T(8,128)(2,1)S(1)}, u32[]{:S(2)}, u32[]{:S(2)}) %all-to-all-start.2) | async-done | bytes 393248 | tf_op jit(solution)/shard_map/all_to_all | solution.py:321
  77.3 2.6 %middle.1 = (bf16[512,256]{1,0:T(8,128)(2,1)}, bf16[64,8,128]{2,1,0:T(8,128)(2,1)}, f32[512,256]{1,0:T(8,128)}) custom-call(f32[1]{0:T(128)} %bitcast.3.ridge, bf16[64,3,8,128]{3,2,1,0:T(8,128)(2,1)S(1)} %all-to-all-done.2.arrived, bf16[1,4,128,128]{3,2,1,0:T(8,128)(2,1)S(1)} %copy-done.3, bf16[1,128,128]{2,1,0:T(8,128)(2,1)S(1)} %copy-done.5, ...), custom_call_target="tpu_custom_call" | custom-call | flops 10000000 | tf_op jit(solution)/shard_map/middle/pallas_call | solution.py:36
  79.9 4.9 %all-to-all-start.3 = ((bf16[64,8,128]{2,1,0:T(8,128)(2,1)}), bf16[64,8,128]{2,1,0:T(8,128)(2,1)S(1)}, u32[]{:S(2)}, u32[]{:S(2)}) async-start(bf16[64,8,128]{2,1,0:T(8,128)(2,1)} %get-tuple-element.25), calls=%async_computation.3 | async-start | bytes 262144 | tf_op jit(solution)/shard_map/all_to_all | solution.py:321
  84.9 1.8 %near_own.3._.refs_2_ = f32[512,256]{1,0:T(8,128)S(1)} custom-call(bf16[768,256]{1,0:T(8,128)(2,1)} %get-tuple-element.24.places_in.values_in.refs_1_, bf16[512,256]{1,0:T(8,128)(2,1)} %get-tuple-element.30.values_in), custom_call_target="tpu_custom_call" | custom-call | flops 10000000 | tf_op jit(solution)/shard_map/near_own/pallas_call | solution.py:36
  86.7 4.4 %collective-permute-start.4 = (bf16[512,256]{1,0:T(8,128)(2,1)S(1)}, bf16[512,256]{1,0:T(8,128)(2,1)S(1)}, u32[]{:S(2)}, u32[]{:S(2)}) collective-permute-start(bf16[512,256]{1,0:T(8,128)(2,1)S(1)} %copy-done.8), channel_id=1, source_target_pairs={{0,2},{1,3},{2,4},{3,5},{4,6},{5,7},{6,8},{7,9},{8,10},{9,11},{10,... | collective-permute-start | bytes 786440 | tf_op jit(solution)/shard_map/ppermute | solution.py:312
  92.4 5.1 %all-to-all-done.3.arrived = bf16[64,8,128]{2,1,0:T(8,128)(2,1)S(1)} async-done(((bf16[64,8,128]{2,1,0:T(8,128)(2,1)}), bf16[64,8,128]{2,1,0:T(8,128)(2,1)S(1)}, u32[]{:S(2)}, u32[]{:S(2)}) %all-to-all-start.3) | async-done | bytes 131104 | tf_op jit(solution)/shard_map/all_to_all | solution.py:321
  98.4 4.8 %all-to-all-start.4 = ((bf16[8,16,128]{2,1,0:T(8,128)(2,1)}), bf16[8,16,128]{2,1,0:T(8,128)(2,1)S(1)}, u32[]{:S(2)}, u32[]{:S(2)}) async-start(bf16[8,16,128]{2,1,0:T(8,128)(2,1)} %get-tuple-element.27), calls=%async_computation.4 | async-start | bytes 65536 | tf_op jit(solution)/shard_map/all_to_all | solution.py:321
  103.2 3.2 %collective-permute-start.6 = (bf16[512,256]{1,0:T(8,128)(2,1)S(1)}, bf16[512,256]{1,0:T(8,128)(2,1)}, u32[]{:S(2)}, u32[]{:S(2)}) collective-permute-start(bf16[512,256]{1,0:T(8,128)(2,1)S(1)} %copy-done.8), channel_id=1, source_target_pairs={{0,1},{1,2},{2,3},{3,4},{4,5},{5,6},{6,7},{7,8},{8,9},{9,10},{10,1... | collective-permute-start | bytes 786440 | tf_op jit(solution)/shard_map/ppermute | solution.py:312
  109.4 2.2 %couple.3.refs_7_ = bf16[64,3,8,128]{3,2,1,0:T(8,128)(2,1)} custom-call(s32[4,4]{1,0:T(4,128)S(1)} %copy-done.6, bf16[8,16,128]{2,1,0:T(8,128)(2,1)S(1)} %all-to-all-done.4.all_sums, bf16[4,4,128,128]{3,2,1,0:T(8,128)(2,1)S(1)} %copy-done, f32[64,128]{1,0:T(8,128)S(1)} %get-tuple-element.20.told, ...), custom_call_target="tpu_custom_call", output_to_operand_aliasing={{}: (4, {})} | custom-call | flops 10000000 | tf_op jit(solution)/shard_map/couple/pallas_call | solution.py:36
  111.6 12.5 %all-to-all-start.5 = ((bf16[64,3,8,128]{3,2,1,0:T(8,128)(2,1)}), bf16[64,3,8,128]{3,2,1,0:T(8,128)(2,1)S(1)}, u32[]{:S(2)}, u32[]{:S(2)}) async-start(bf16[64,3,8,128]{3,2,1,0:T(8,128)(2,1)} %couple.3.refs_7_), calls=%async_computation.5 | async-start | bytes 786432 | tf_op jit(solution)/shard_map/all_to_all | solution.py:321
  124.2 2.0 %near_pair_2.3.refs_2_ = f32[512,256]{1,0:T(8,128)S(1)} custom-call(s32[1,4]{1,0:T(1,128)S(1)} %copy-done.7, bf16[768,256]{1,0:T(8,128)(2,1)} %get-tuple-element.24.places_in.values_in.refs_1_, f32[512,256]{1,0:T(8,128)S(1)} %near_own.3._.refs_2_, bf16[768,256]{1,0:T(8,128)(2,1)S(1)} %collective-permute-done.refs_3_.refs_4_, ...), custom_call_target="tpu_custom_call" | custom-call | flops 10000000000 | tf_op jit(solution)/shard_map/near_pair_2/pallas_call | solution.py:36
  126.1 1.9 %near_pair_1.3.near = f32[512,256]{1,0:T(8,128)S(1)} custom-call(s32[1,4]{1,0:T(1,128)S(1)} %copy-done.7, bf16[768,256]{1,0:T(8,128)(2,1)} %get-tuple-element.24.places_in.values_in.refs_1_, f32[512,256]{1,0:T(8,128)S(1)} %near_pair_2.3.refs_2_, bf16[768,256]{1,0:T(8,128)(2,1)S(1)} %collective-permute-done.2.refs_3_.refs_4_, ...), custom_call_target="tpu_custom_call" | custom-call | flops 1000000000 | tf_op jit(solution)/shard_map/near_pair_1/pallas_call | solution.py:36
  128.1 12.8 %all-to-all-done.5.arrived = bf16[64,3,8,128]{3,2,1,0:T(8,128)(2,1)S(1)} async-done(((bf16[64,3,8,128]{3,2,1,0:T(8,128)(2,1)}), bf16[64,3,8,128]{3,2,1,0:T(8,128)(2,1)S(1)}, u32[]{:S(2)}, u32[]{:S(2)}) %all-to-all-start.5) | async-done | bytes 393248 | tf_op jit(solution)/shard_map/all_to_all | solution.py:321
  140.8 2.6 %end.1 = (f32[512,256]{1,0:T(8,128)}, f32[512,256]{1,0:T(8,128)}) custom-call(f32[1]{0:T(128)} %bitcast.4.ridge, bf16[64,3,8,128]{3,2,1,0:T(8,128)(2,1)S(1)} %all-to-all-done.5.arrived, bf16[1,4,128,128]{3,2,1,0:T(8,128)(2,1)S(1)} %copy-done.3, bf16[1,128,128]{2,1,0:T(8,128)(2,1)S(1)} %copy-done.5, bf16[512,128]{1,0:T(8,128)(2,1)S(1)} %copy-done.4, ...), custom_call_target="tpu_custom_call" | custom-call | flops 10000000 | tf_op jit(solution)/shard_map/end/pallas_call | solution.py:36
  (37 shorter events, 11.9 us)
Async XLA Ops:
  4.5 31.6 %all-to-all-start = ((bf16[64,16,128]{2,1,0:T(8,128)(2,1)}), bf16[64,16,128]{2,1,0:T(8,128)(2,1)S(1)}, u32[]{:S(2)}, u32[]{:S(2)}) async-start(bf16[64,16,128]{2,1,0:T(8,128)(2,1)} %get-tuple-element.17), calls=%async_computation | async-start | bytes 524288 | tf_op jit(solution)/shard_map/all_to_all | solution.py:321
  22.9 24.7 %copy-start = (bf16[4,4,128,128]{3,2,1,0:T(8,128)(2,1)S(1)}, bf16[4,4,128,128]{3,2,1,0:T(8,128)(2,1)}, u32[]{:S(2)}) copy-start(bf16[4,4,128,128]{3,2,1,0:T(8,128)(2,1)} %blocks.3) | copy-start | bytes 1572868
  22.9 37.7 %collective-permute-start = (bf16[768,256]{1,0:T(8,128)(2,1)}, bf16[768,256]{1,0:T(8,128)(2,1)S(1)}, u32[]{:S(2)}, u32[]{:S(2)}) collective-permute-start(bf16[768,256]{1,0:T(8,128)(2,1)} %get-tuple-element.24.places_in.values_in.refs_1_), channel_id=1, source_target_pairs={{0,2},{1,3},{2,4},{3,5},{4,6},{5,7},{6,8},{7,9},{8,10},{9,11},{10,... | collective-permute-start | bytes 1179656 | tf_op jit(solution)/shard_map/ppermute | solution.py:312
  27.5 33.1 %collective-permute-start.1 = (bf16[768,256]{1,0:T(8,128)(2,1)}, bf16[768,256]{1,0:T(8,128)(2,1)S(1)}, u32[]{:S(2)}, u32[]{:S(2)}) collective-permute-start(bf16[768,256]{1,0:T(8,128)(2,1)} %get-tuple-element.24.places_in.values_in.refs_1_), channel_id=1, source_target_pairs={{2,0},{3,1},{4,2},{5,3},{6,4},{7,5},{8,6},{9,7},{10,8},{11,9},{12,... | collective-permute-start | bytes 1179656 | tf_op jit(solution)/shard_map/ppermute | solution.py:312
  37.0 10.5 %all-to-all-start.1 = ((bf16[8,16,128]{2,1,0:T(8,128)(2,1)}), bf16[8,16,128]{2,1,0:T(8,128)(2,1)S(1)}, u32[]{:S(2)}, u32[]{:S(2)}) async-start(bf16[8,16,128]{2,1,0:T(8,128)(2,1)} %get-tuple-element.19), calls=%async_computation.1 | async-start | bytes 65536 | tf_op jit(solution)/shard_map/all_to_all | solution.py:321
  41.9 20.4 %collective-permute-start.2 = (bf16[768,256]{1,0:T(8,128)(2,1)}, bf16[768,256]{1,0:T(8,128)(2,1)S(1)}, u32[]{:S(2)}, u32[]{:S(2)}) collective-permute-start(bf16[768,256]{1,0:T(8,128)(2,1)} %get-tuple-element.24.places_in.values_in.refs_1_), channel_id=1, source_target_pairs={{0,1},{1,2},{2,3},{3,4},{4,5},{5,6},{6,7},{7,8},{8,9},{9,10},{10,1... | collective-permute-start | bytes 1179656 | tf_op jit(solution)/shard_map/ppermute | solution.py:312
  44.6 17.7 %collective-permute-start.3 = (bf16[768,256]{1,0:T(8,128)(2,1)}, bf16[768,256]{1,0:T(8,128)(2,1)}, u32[]{:S(2)}, u32[]{:S(2)}) collective-permute-start(bf16[768,256]{1,0:T(8,128)(2,1)} %get-tuple-element.24.places_in.values_in.refs_1_), channel_id=1, source_target_pairs={{1,0},{2,1},{3,2},{4,3},{5,4},{6,5},{7,6},{8,7},{9,8},{10,9},{11,1... | collective-permute-start | bytes 1179656 | tf_op jit(solution)/shard_map/ppermute | solution.py:312
  45.9 1.7 %copy-start.6 = (s32[4,4]{1,0:T(4,128)S(1)}, s32[4,4]{1,0:T(4,128)}, u32[]{:S(2)}) copy-start(s32[4,4]{1,0:T(4,128)} %far_clusters.3) | copy-start | bytes 196
  49.8 10.8 %copy-start.2 = (bf16[64,3,8,128]{3,2,1,0:T(8,128)(2,1)S(1)}, bf16[64,3,8,128]{3,2,1,0:T(8,128)(2,1)}, u32[]{:S(2)}) copy-start(bf16[64,3,8,128]{3,2,1,0:T(8,128)(2,1)} %couple.2.refs_7_) | copy-start | bytes 1179652
  49.8 10.8 %copy-start.7 = (s32[1,4]{1,0:T(1,128)S(1)}, s32[1,4]{1,0:T(1,128)}, u32[]{:S(2)}) copy-start(s32[1,4]{1,0:T(1,128)} %refs_0_.7) | copy-start | bytes 52
  49.8 27.5 %all-to-all-start.2 = ((bf16[64,3,8,128]{3,2,1,0:T(8,128)(2,1)}), bf16[64,3,8,128]{3,2,1,0:T(8,128)(2,1)S(1)}, u32[]{:S(2)}, u32[]{:S(2)}) async-start(bf16[64,3,8,128]{3,2,1,0:T(8,128)(2,1)} %couple.2.refs_7_), calls=%async_computation.2 | async-start | bytes 786432 | tf_op jit(solution)/shard_map/all_to_all | solution.py:321
  62.2 15.1 %copy-start.3 = (bf16[1,4,128,128]{3,2,1,0:T(8,128)(2,1)S(1)}, bf16[1,4,128,128]{3,2,1,0:T(8,128)(2,1)}, u32[]{:S(2)}) copy-start(bf16[1,4,128,128]{3,2,1,0:T(8,128)(2,1)} %couplings.3) | copy-start | bytes 393220
  62.2 15.1 %copy-start.4 = (bf16[512,128]{1,0:T(8,128)(2,1)S(1)}, bf16[512,128]{1,0:T(8,128)(2,1)}, u32[]{:S(2)}) copy-start(bf16[512,128]{1,0:T(8,128)(2,1)} %get-tuple-element.23.basis) | copy-start | bytes 393220
  62.2 15.1 %copy-start.5 = (bf16[1,128,128]{2,1,0:T(8,128)(2,1)S(1)}, bf16[1,128,128]{2,1,0:T(8,128)(2,1)}, u32[]{:S(2)}) copy-start(bf16[1,128,128]{2,1,0:T(8,128)(2,1)} %transfer.3) | copy-start | bytes 98308
  79.9 17.6 %all-to-all-start.3 = ((bf16[64,8,128]{2,1,0:T(8,128)(2,1)}), bf16[64,8,128]{2,1,0:T(8,128)(2,1)S(1)}, u32[]{:S(2)}, u32[]{:S(2)}) async-start(bf16[64,8,128]{2,1,0:T(8,128)(2,1)} %get-tuple-element.25), calls=%async_computation.3 | async-start | bytes 262144 | tf_op jit(solution)/shard_map/all_to_all | solution.py:321
  84.9 1.8 %copy-start.8 = (bf16[512,256]{1,0:T(8,128)(2,1)S(1)}, bf16[512,256]{1,0:T(8,128)(2,1)}, u32[]{:S(2)}) copy-start(bf16[512,256]{1,0:T(8,128)(2,1)} %get-tuple-element.30.values_in) | copy-start | bytes 786436
  86.7 37.4 %collective-permute-start.4 = (bf16[512,256]{1,0:T(8,128)(2,1)S(1)}, bf16[512,256]{1,0:T(8,128)(2,1)S(1)}, u32[]{:S(2)}, u32[]{:S(2)}) collective-permute-start(bf16[512,256]{1,0:T(8,128)(2,1)S(1)} %copy-done.8), channel_id=1, source_target_pairs={{0,2},{1,3},{2,4},{3,5},{4,6},{5,7},{6,8},{7,9},{8,10},{9,11},{10,... | collective-permute-start | bytes 786440 | tf_op jit(solution)/shard_map/ppermute | solution.py:312
  91.1 33.1 %collective-permute-start.5 = (bf16[512,256]{1,0:T(8,128)(2,1)S(1)}, bf16[512,256]{1,0:T(8,128)(2,1)}, u32[]{:S(2)}, u32[]{:S(2)}) collective-permute-start(bf16[512,256]{1,0:T(8,128)(2,1)S(1)} %copy-done.8), channel_id=1, source_target_pairs={{2,0},{3,1},{4,2},{5,3},{6,4},{7,5},{8,6},{9,7},{10,8},{11,9},{12,... | collective-permute-start | bytes 786440 | tf_op jit(solution)/shard_map/ppermute | solution.py:312
  98.4 11.0 %all-to-all-start.4 = ((bf16[8,16,128]{2,1,0:T(8,128)(2,1)}), bf16[8,16,128]{2,1,0:T(8,128)(2,1)S(1)}, u32[]{:S(2)}, u32[]{:S(2)}) async-start(bf16[8,16,128]{2,1,0:T(8,128)(2,1)} %get-tuple-element.27), calls=%async_computation.4 | async-start | bytes 65536 | tf_op jit(solution)/shard_map/all_to_all | solution.py:321
  103.2 22.9 %collective-permute-start.6 = (bf16[512,256]{1,0:T(8,128)(2,1)S(1)}, bf16[512,256]{1,0:T(8,128)(2,1)}, u32[]{:S(2)}, u32[]{:S(2)}) collective-permute-start(bf16[512,256]{1,0:T(8,128)(2,1)S(1)} %copy-done.8), channel_id=1, source_target_pairs={{0,1},{1,2},{2,3},{3,4},{4,5},{5,6},{6,7},{7,8},{8,9},{9,10},{10,1... | collective-permute-start | bytes 786440 | tf_op jit(solution)/shard_map/ppermute | solution.py:312
  106.4 19.7 %collective-permute-start.7 = (bf16[512,256]{1,0:T(8,128)(2,1)S(1)}, bf16[512,256]{1,0:T(8,128)(2,1)}, u32[]{:S(2)}, u32[]{:S(2)}) collective-permute-start(bf16[512,256]{1,0:T(8,128)(2,1)S(1)} %copy-done.8), channel_id=1, source_target_pairs={{1,0},{2,1},{3,2},{4,3},{5,4},{6,5},{7,6},{8,7},{9,8},{10,9},{11,1... | collective-permute-start | bytes 786440 | tf_op jit(solution)/shard_map/ppermute | solution.py:312
  111.6 12.6 %copy-start.1 = (bf16[64,3,8,128]{3,2,1,0:T(8,128)(2,1)S(1)}, bf16[64,3,8,128]{3,2,1,0:T(8,128)(2,1)}, u32[]{:S(2)}) copy-start(bf16[64,3,8,128]{3,2,1,0:T(8,128)(2,1)} %couple.3.refs_7_) | copy-start | bytes 1179652
  111.6 29.2 %all-to-all-start.5 = ((bf16[64,3,8,128]{3,2,1,0:T(8,128)(2,1)}), bf16[64,3,8,128]{3,2,1,0:T(8,128)(2,1)S(1)}, u32[]{:S(2)}, u32[]{:S(2)}) async-start(bf16[64,3,8,128]{3,2,1,0:T(8,128)(2,1)} %couple.3.refs_7_), calls=%async_computation.5 | async-start | bytes 786432 | tf_op jit(solution)/shard_map/all_to_all | solution.py:321

commit v5 on v4

--- a/solution.py
+++ b/solution.py
@@ -151,7 +151,7 @@
     ).astype(BF16)
 
 
-def partners_kernel(skeletons, told, sent_out, done, staged, sent, sems):
+def partners_kernel(skeletons, told, sent_out, staged, sent, sems):
     lane = lax.broadcasted_iota(jnp.int32, (N_DEV, N_DEV), 1).astype(F32)
     pick = jnp.concatenate(
         [jnp.where(lane == told[:, k : k + 1], 1.0, 0.0) for k in range(FAR1)], axis=0
@@ -163,7 +163,6 @@
                 N_DEV * k : N_DEV * (k + 1), RANK * i : RANK * (i + 1)
             ]
     sent[...] = staged[...].reshape(N_DEV, 2, 8, RANK).astype(BF16)
-    done[...] = jnp.zeros_like(done)
     wait(started(((sent, sent_out.at[:, :2]),), sems))
 
 
@@ -395,10 +394,10 @@
 
     def through_owners(sums, skeletons):
         all_sums = exchanged(sums, "grp")
-        partners, done = call(
+        (partners,) = call(
             partners_kernel,
             "partners",
-            [((N_DEV, 3, 8, RANK), BF16, HBM), ((8, RANK), F32, VMEM)],
+            [((N_DEV, 3, 8, RANK), BF16, HBM)],
             [VMEM] * 2,
             (skeletons, told),
             [rows16, pltpu.VMEM((N_DEV, 2, 8, RANK), BF16), dma((1,))],
@@ -414,7 +413,7 @@
             SHORT,
             {4: 0},
         )
-        return sent, exchanged(sent, "dev"), done
+        return sent, exchanged(sent, "dev")
 
     arrived = exchanged(sent, "dev")
     near = near_own(wc)
@@ -428,8 +427,8 @@
         [rows16, narrow],
         SHORT,
     )
-    sent, arrived, done = through_owners(sums, skeletons)
-    first1 = from_pair(wc, 1, done)
+    sent, arrived = through_owners(sums, skeletons)
+    first1 = from_pair(wc, 1, sent)
     near = near_pair(2, near, first2, first2, sent, MID)
     near = near_pair(1, near, first1, first1, sent, LONG)
     w, sent, r1 = call(
@@ -461,8 +460,8 @@
         [rows8, narrow],
         SHORT,
     )
-    sent, arrived, done = through_owners(sums, skeletons)
-    fields1 = from_pair(w, 1, done)
+    sent, arrived = through_owners(sums, skeletons)
+    fields1 = from_pair(w, 1, sent)
     near = near_pair(2, near, first2, fields2, sent, MID)
     near = near_pair(1, near, first1, fields1, sent, LONG)
     return tuple(

time: 145 us -> 151 us (1.041)
  the two profiles are of different devices: /device:TPU:2 before, /device:TPU:24 now
where the time goes in v5:
time: 151 us; the launch traced here: 150 us
  starting transfers between devices  80.9 us (54%)
  waiting for transfers between devices  34 us (23%)
  Pallas kernels  32.1 us (21%)
  between operations  2.45 us (2%)
    all_to_all x6, starting transfers between devices, exchanged(): return lax.all_to_all(blocks, axis, split_axis=0, concat_axis=0, tiled=True)  52.9 us
    pallas_call x15, Pallas kernels, call(): pl.pallas_call(kernel, name=name, out_shape=shapes, in_specs=ins, out_spe...  32.1 us
    ppermute x8, starting transfers between devices, from_behind(): return lax.ppermute(shard, 'dev', pairs)  28 us
    ppermute x8, waiting for transfers between devices, from_behind(): return lax.ppermute(shard, 'dev', pairs)  20.3 us
    all_to_all x6, waiting for transfers between devices, exchanged(): return lax.all_to_all(blocks, axis, split_axis=0, concat_axis=0, tiled=True)  13.7 us
  transfers between devices with their start and end apart: 14, of which 8 were waited for; matrix products, arithmetic and copies ran while one was open for 0% of the time, Pallas kernels for 16%

profile of v5, /device:TPU:24, one launch (start us, length us, event | category | flops | bytes accessed | tf_op | source)
XLA Modules:
  0.0 150.3 jit_solution(3523445257262826340)
XLA Ops:
  1.9 2.6 %start.1 = (bf16[768,256]{1,0:T(8,128)(2,1)}, bf16[64,16,128]{2,1,0:T(8,128)(2,1)}, bf16[512,128]{1,0:T(8,128)(2,1)}) custom-call(f32[1]{0:T(128)} %bitcast.2.ridge, s32[1]{0:T(128)S(6)} %copy.18.cluster, s32[1,4]{1,0:T(1,128)} %far_in.1, f32[512,256]{1,0:T(8,128)} %rs_in.5, f32[64,512]{1,0:T(8,128)} %bitcast.5, s32[1,512]{1,0:T(1,128)} %perm_in.1, ...), custom_call_target="tpu_custom_call" | custom-call | flops 10000000 | tf_op jit(solution)/shard_map/start/pallas_call | solution.py:36
  4.5 16.4 %all-to-all-start = ((bf16[64,16,128]{2,1,0:T(8,128)(2,1)}), bf16[64,16,128]{2,1,0:T(8,128)(2,1)S(1)}, u32[]{:S(2)}, u32[]{:S(2)}) async-start(bf16[64,16,128]{2,1,0:T(8,128)(2,1)} %get-tuple-element.17), calls=%async_computation | async-start | bytes 524288 | tf_op jit(solution)/shard_map/all_to_all | solution.py:320
  22.7 5.6 %collective-permute-start.1 = (bf16[768,256]{1,0:T(8,128)(2,1)}, bf16[768,256]{1,0:T(8,128)(2,1)S(1)}, u32[]{:S(2)}, u32[]{:S(2)}) collective-permute-start(bf16[768,256]{1,0:T(8,128)(2,1)} %get-tuple-element.24.places_in.values_in.refs_1_), channel_id=1, source_target_pairs={{2,0},{3,1},{4,2},{5,3},{6,4},{7,5},{8,6},{9,7},{10,8},{11,9},{12,... | collective-permute-start | bytes 1179656 | tf_op jit(solution)/shard_map/ppermute | solution.py:311
  30.3 3.8 %all-to-all-done.arrived = bf16[64,16,128]{2,1,0:T(8,128)(2,1)S(1)} async-done(((bf16[64,16,128]{2,1,0:T(8,128)(2,1)}), bf16[64,16,128]{2,1,0:T(8,128)(2,1)S(1)}, u32[]{:S(2)}, u32[]{:S(2)}) %all-to-all-start) | async-done | bytes 262176 | tf_op jit(solution)/shard_map/all_to_all | solution.py:320
  35.0 4.3 %all-to-all-start.1 = ((bf16[8,16,128]{2,1,0:T(8,128)(2,1)}), bf16[8,16,128]{2,1,0:T(8,128)(2,1)S(1)}, u32[]{:S(2)}, u32[]{:S(2)}) async-start(bf16[8,16,128]{2,1,0:T(8,128)(2,1)} %get-tuple-element.19), calls=%async_computation.1 | async-start | bytes 65536 | tf_op jit(solution)/shard_map/all_to_all | solution.py:320
  40.4 4.4 %all-to-all-done.1.all_sums = bf16[8,16,128]{2,1,0:T(8,128)(2,1)S(1)} async-done(((bf16[8,16,128]{2,1,0:T(8,128)(2,1)}), bf16[8,16,128]{2,1,0:T(8,128)(2,1)S(1)}, u32[]{:S(2)}, u32[]{:S(2)}) %all-to-all-start.1) | async-done | bytes 32800 | tf_op jit(solution)/shard_map/all_to_all | solution.py:320
  47.0 8.7 %all-to-all-start.2 = ((bf16[64,3,8,128]{3,2,1,0:T(8,128)(2,1)}), bf16[64,3,8,128]{3,2,1,0:T(8,128)(2,1)S(1)}, u32[]{:S(2)}, u32[]{:S(2)}) async-start(bf16[64,3,8,128]{3,2,1,0:T(8,128)(2,1)} %couple.2.refs_7_), calls=%async_computation.2 | async-start | bytes 786432 | tf_op jit(solution)/shard_map/all_to_all | solution.py:320
  55.7 4.6 %collective-permute-start.3 = (bf16[768,256]{1,0:T(8,128)(2,1)}, bf16[768,256]{1,0:T(8,128)(2,1)S(1)}, u32[]{:S(2)}, u32[]{:S(2)}) collective-permute-start(bf16[768,256]{1,0:T(8,128)(2,1)} %get-tuple-element.24.places_in.values_in.refs_1_), channel_id=1, source_target_pairs={{1,0},{2,1},{3,2},{4,3},{5,4},{6,5},{7,6},{8,7},{9,8},{10,9},{11,1... | collective-permute-start | bytes 1179656 | tf_op jit(solution)/shard_map/ppermute | solution.py:311
  62.2 3.0 %near_pair_2.2.refs_2_ = f32[512,256]{1,0:T(8,128)S(1)} custom-call(s32[1,4]{1,0:T(1,128)S(1)} %copy-done.9, bf16[768,256]{1,0:T(8,128)(2,1)} %get-tuple-element.24.places_in.values_in.refs_1_, f32[512,256]{1,0:T(8,128)S(1)} %near_own.2._.refs_2_, bf16[768,256]{1,0:T(8,128)(2,1)S(1)} %collective-permute-done.refs_3_.refs_4_, ...), custom_call_target="tpu_custom_call" | custom-call | flops 10000000000 | tf_op jit(solution)/shard_map/near_pair_2/pallas_call | solution.py:36
  65.3 9.6 %collective-permute-done.3.refs_5_.refs_6_ = bf16[768,256]{1,0:T(8,128)(2,1)S(1)} collective-permute-done((bf16[768,256]{1,0:T(8,128)(2,1)}, bf16[768,256]{1,0:T(8,128)(2,1)S(1)}, u32[]{:S(2)}, u32[]{:S(2)}) %collective-permute-start.3) | collective-permute-done | bytes 393248 | tf_op jit(solution)/shard_map/ppermute | solution.py:311
  74.8 2.4 %collective-permute-done.2.refs_3_.refs_4_ = bf16[768,256]{1,0:T(8,128)(2,1)S(1)} collective-permute-done((bf16[768,256]{1,0:T(8,128)(2,1)}, bf16[768,256]{1,0:T(8,128)(2,1)S(1)}, u32[]{:S(2)}, u32[]{:S(2)}) %collective-permute-start.2) | collective-permute-done | bytes 393248 | tf_op jit(solution)/shard_map/ppermute | solution.py:311
  77.2 3.0 %near_pair_1.2.near = f32[512,256]{1,0:T(8,128)S(1)} custom-call(s32[1,4]{1,0:T(1,128)S(1)} %copy-done.9, bf16[768,256]{1,0:T(8,128)(2,1)} %get-tuple-element.24.places_in.values_in.refs_1_, f32[512,256]{1,0:T(8,128)S(1)} %near_pair_2.2.refs_2_, bf16[768,256]{1,0:T(8,128)(2,1)S(1)} %collective-permute-done.2.refs_3_.refs_4_, ...), custom_call_target="tpu_custom_call" | custom-call | flops 1000000000 | tf_op jit(solution)/shard_map/near_pair_1/pallas_call | solution.py:36
  81.0 2.6 %middle.1 = (bf16[512,256]{1,0:T(8,128)(2,1)}, bf16[64,8,128]{2,1,0:T(8,128)(2,1)}, f32[512,256]{1,0:T(8,128)}) custom-call(f32[1]{0:T(128)} %bitcast.3.ridge, bf16[64,3,8,128]{3,2,1,0:T(8,128)(2,1)S(1)} %all-to-all-done.2.arrived, bf16[1,4,128,128]{3,2,1,0:T(8,128)(2,1)S(1)} %copy-done.3, bf16[1,128,128]{2,1,0:T(8,128)(2,1)S(1)} %copy-done.5, ...), custom_call_target="tpu_custom_call" | custom-call | flops 10000000 | tf_op jit(solution)/shard_map/middle/pallas_call | solution.py:36
  83.6 8.8 %all-to-all-start.3 = ((bf16[64,8,128]{2,1,0:T(8,128)(2,1)}), bf16[64,8,128]{2,1,0:T(8,128)(2,1)S(1)}, u32[]{:S(2)}, u32[]{:S(2)}) async-start(bf16[64,8,128]{2,1,0:T(8,128)(2,1)} %get-tuple-element.25), calls=%async_computation.3 | async-start | bytes 262144 | tf_op jit(solution)/shard_map/all_to_all | solution.py:320
  94.3 5.5 %collective-permute-start.5 = (bf16[512,256]{1,0:T(8,128)(2,1)S(1)}, bf16[512,256]{1,0:T(8,128)(2,1)}, u32[]{:S(2)}, u32[]{:S(2)}) collective-permute-start(bf16[512,256]{1,0:T(8,128)(2,1)S(1)} %copy-done.10), channel_id=1, source_target_pairs={{2,0},{3,1},{4,2},{5,3},{6,4},{7,5},{8,6},{9,7},{10,8},{11,9},{12,... | collective-permute-start | bytes 786440 | tf_op jit(solution)/shard_map/ppermute | solution.py:311
  103.8 3.3 %all-to-all-start.4 = ((bf16[8,16,128]{2,1,0:T(8,128)(2,1)}), bf16[8,16,128]{2,1,0:T(8,128)(2,1)S(1)}, u32[]{:S(2)}, u32[]{:S(2)}) async-start(bf16[8,16,128]{2,1,0:T(8,128)(2,1)} %get-tuple-element.27), calls=%async_computation.4 | async-start | bytes 65536 | tf_op jit(solution)/shard_map/all_to_all | solution.py:320
  108.2 4.3 %all-to-all-done.4.all_sums = bf16[8,16,128]{2,1,0:T(8,128)(2,1)S(1)} async-done(((bf16[8,16,128]{2,1,0:T(8,128)(2,1)}), bf16[8,16,128]{2,1,0:T(8,128)(2,1)S(1)}, u32[]{:S(2)}, u32[]{:S(2)}) %all-to-all-start.4) | async-done | bytes 32800 | tf_op jit(solution)/shard_map/all_to_all | solution.py:320
  114.7 11.3 %all-to-all-start.5 = ((bf16[64,3,8,128]{3,2,1,0:T(8,128)(2,1)}), bf16[64,3,8,128]{3,2,1,0:T(8,128)(2,1)S(1)}, u32[]{:S(2)}, u32[]{:S(2)}) async-start(bf16[64,3,8,128]{3,2,1,0:T(8,128)(2,1)} %couple.3.refs_7_), calls=%async_computation.5 | async-start | bytes 786432 | tf_op jit(solution)/shard_map/all_to_all | solution.py:320
  126.0 4.7 %collective-permute-start.7 = (bf16[512,256]{1,0:T(8,128)(2,1)S(1)}, bf16[512,256]{1,0:T(8,128)(2,1)S(1)}, u32[]{:S(2)}, u32[]{:S(2)}) collective-permute-start(bf16[512,256]{1,0:T(8,128)(2,1)S(1)} %copy-done.10), channel_id=1, source_target_pairs={{1,0},{2,1},{3,2},{4,3},{5,4},{6,5},{7,6},{8,7},{9,8},{10,9},{11,1... | collective-permute-start | bytes 786440 | tf_op jit(solution)/shard_map/ppermute | solution.py:311
  132.7 3.5 %near_pair_2.3.refs_2_ = f32[512,256]{1,0:T(8,128)S(1)} custom-call(s32[1,4]{1,0:T(1,128)S(1)} %copy-done.9, bf16[768,256]{1,0:T(8,128)(2,1)} %get-tuple-element.24.places_in.values_in.refs_1_, f32[512,256]{1,0:T(8,128)S(1)} %near_own.3._.refs_2_, bf16[768,256]{1,0:T(8,128)(2,1)S(1)} %collective-permute-done.refs_3_.refs_4_, ...), custom_call_target="tpu_custom_call" | custom-call | flops 10000000000 | tf_op jit(solution)/shard_map/near_pair_2/pallas_call | solution.py:36
  136.2 6.0 %collective-permute-done.7.refs_6_ = bf16[512,256]{1,0:T(8,128)(2,1)S(1)} collective-permute-done((bf16[512,256]{1,0:T(8,128)(2,1)S(1)}, bf16[512,256]{1,0:T(8,128)(2,1)S(1)}, u32[]{:S(2)}, u32[]{:S(2)}) %collective-permute-start.7) | collective-permute-done | bytes 262176 | tf_op jit(solution)/shard_map/ppermute | solution.py:311
  142.2 2.3 %collective-permute-done.6.refs_4_ = bf16[512,256]{1,0:T(8,128)(2,1)S(1)} collective-permute-done((bf16[512,256]{1,0:T(8,128)(2,1)S(1)}, bf16[512,256]{1,0:T(8,128)(2,1)S(1)}, u32[]{:S(2)}, u32[]{:S(2)}) %collective-permute-start.6) | collective-permute-done | bytes 262176 | tf_op jit(solution)/shard_map/ppermute | solution.py:311
  144.5 3.0 %near_pair_1.3.near = f32[512,256]{1,0:T(8,128)S(1)} custom-call(s32[1,4]{1,0:T(1,128)S(1)} %copy-done.9, bf16[768,256]{1,0:T(8,128)(2,1)} %get-tuple-element.24.places_in.values_in.refs_1_, f32[512,256]{1,0:T(8,128)S(1)} %near_pair_2.3.refs_2_, bf16[768,256]{1,0:T(8,128)(2,1)S(1)} %copy-done.8, bf16[512,256]{1,0:T(8,128)(2,1)S(1)} %collective-permute-done.6.refs_4_, ...), custom_call_target="tpu_custom_call" | custom-call | flops 1000000000 | tf_op jit(solution)/shard_map/near_pair_1/pallas_call | solution.py:36
  147.5 2.6 %end.1 = (f32[512,256]{1,0:T(8,128)}, f32[512,256]{1,0:T(8,128)}) custom-call(f32[1]{0:T(128)} %bitcast.4.ridge, bf16[64,3,8,128]{3,2,1,0:T(8,128)(2,1)S(1)} %all-to-all-done.5.arrived, bf16[1,4,128,128]{3,2,1,0:T(8,128)(2,1)S(1)} %copy-done.3, bf16[1,128,128]{2,1,0:T(8,128)(2,1)S(1)} %copy-done.5, bf16[512,128]{1,0:T(8,128)(2,1)S(1)} %copy-done.4, ...), custom_call_target="tpu_custom_call" | custom-call | flops 10000000 | tf_op jit(solution)/shard_map/end/pallas_call | solution.py:36
  (41 shorter events, 21.5 us)
Async XLA Ops:
  4.5 29.6 %all-to-all-start = ((bf16[64,16,128]{2,1,0:T(8,128)(2,1)}), bf16[64,16,128]{2,1,0:T(8,128)(2,1)S(1)}, u32[]{:S(2)}, u32[]{:S(2)}) async-start(bf16[64,16,128]{2,1,0:T(8,128)(2,1)} %get-tuple-element.17), calls=%async_computation | async-start | bytes 524288 | tf_op jit(solution)/shard_map/all_to_all | solution.py:320
  22.7 22.0 %copy-start.2 = (bf16[4,4,128,128]{3,2,1,0:T(8,128)(2,1)S(1)}, bf16[4,4,128,128]{3,2,1,0:T(8,128)(2,1)}, u32[]{:S(2)}) copy-start(bf16[4,4,128,128]{3,2,1,0:T(8,128)(2,1)} %blocks.3) | copy-start | bytes 1572868
  22.7 39.4 %collective-permute-start.1 = (bf16[768,256]{1,0:T(8,128)(2,1)}, bf16[768,256]{1,0:T(8,128)(2,1)S(1)}, u32[]{:S(2)}, u32[]{:S(2)}) collective-permute-start(bf16[768,256]{1,0:T(8,128)(2,1)} %get-tuple-element.24.places_in.values_in.refs_1_), channel_id=1, source_target_pairs={{2,0},{3,1},{4,2},{5,3},{6,4},{7,5},{8,6},{9,7},{10,8},{11,9},{12,... | collective-permute-start | bytes 1179656 | tf_op jit(solution)/shard_map/ppermute | solution.py:311
  28.4 33.8 %collective-permute-start = (bf16[768,256]{1,0:T(8,128)(2,1)}, bf16[768,256]{1,0:T(8,128)(2,1)S(1)}, u32[]{:S(2)}, u32[]{:S(2)}) collective-permute-start(bf16[768,256]{1,0:T(8,128)(2,1)} %get-tuple-element.24.places_in.values_in.refs_1_), channel_id=1, source_target_pairs={{0,2},{1,3},{2,4},{3,5},{4,6},{5,7},{6,8},{7,9},{8,10},{9,11},{10,... | collective-permute-start | bytes 1179656 | tf_op jit(solution)/shard_map/ppermute | solution.py:311
  35.0 9.7 %all-to-all-start.1 = ((bf16[8,16,128]{2,1,0:T(8,128)(2,1)}), bf16[8,16,128]{2,1,0:T(8,128)(2,1)S(1)}, u32[]{:S(2)}, u32[]{:S(2)}) async-start(bf16[8,16,128]{2,1,0:T(8,128)(2,1)} %get-tuple-element.19), calls=%async_computation.1 | async-start | bytes 65536 | tf_op jit(solution)/shard_map/all_to_all | solution.py:320
  39.3 5.5 %copy-start.6 = (s32[4,4]{1,0:T(4,128)S(1)}, s32[4,4]{1,0:T(4,128)}, u32[]{:S(2)}) copy-start(s32[4,4]{1,0:T(4,128)} %far_clusters.3) | copy-start | bytes 196
  47.0 15.2 %copy-start.1 = (bf16[64,3,8,128]{3,2,1,0:T(8,128)(2,1)S(1)}, bf16[64,3,8,128]{3,2,1,0:T(8,128)(2,1)}, u32[]{:S(2)}) copy-start(bf16[64,3,8,128]{3,2,1,0:T(8,128)(2,1)} %couple.2.refs_7_) | copy-start | bytes 1179652
  47.0 15.2 %copy-start.9 = (s32[1,4]{1,0:T(1,128)S(1)}, s32[1,4]{1,0:T(1,128)}, u32[]{:S(2)}) copy-start(s32[1,4]{1,0:T(1,128)} %refs_0_.7) | copy-start | bytes 52
  47.0 34.0 %all-to-all-start.2 = ((bf16[64,3,8,128]{3,2,1,0:T(8,128)(2,1)}), bf16[64,3,8,128]{3,2,1,0:T(8,128)(2,1)S(1)}, u32[]{:S(2)}, u32[]{:S(2)}) async-start(bf16[64,3,8,128]{3,2,1,0:T(8,128)(2,1)} %couple.2.refs_7_), calls=%async_computation.2 | async-start | bytes 786432 | tf_op jit(solution)/shard_map/all_to_all | solution.py:320
  55.7 19.2 %collective-permute-start.3 = (bf16[768,256]{1,0:T(8,128)(2,1)}, bf16[768,256]{1,0:T(8,128)(2,1)S(1)}, u32[]{:S(2)}, u32[]{:S(2)}) collective-permute-start(bf16[768,256]{1,0:T(8,128)(2,1)} %get-tuple-element.24.places_in.values_in.refs_1_), channel_id=1, source_target_pairs={{1,0},{2,1},{3,2},{4,3},{5,4},{6,5},{7,6},{8,7},{9,8},{10,9},{11,1... | collective-permute-start | bytes 1179656 | tf_op jit(solution)/shard_map/ppermute | solution.py:311
  60.2 17.0 %collective-permute-start.2 = (bf16[768,256]{1,0:T(8,128)(2,1)}, bf16[768,256]{1,0:T(8,128)(2,1)S(1)}, u32[]{:S(2)}, u32[]{:S(2)}) collective-permute-start(bf16[768,256]{1,0:T(8,128)(2,1)} %get-tuple-element.24.places_in.values_in.refs_1_), channel_id=1, source_target_pairs={{0,1},{1,2},{2,3},{3,4},{4,5},{5,6},{6,7},{7,8},{8,9},{9,10},{10,1... | collective-permute-start | bytes 1179656 | tf_op jit(solution)/shard_map/ppermute | solution.py:311
  65.2 15.8 %copy-start.3 = (bf16[1,4,128,128]{3,2,1,0:T(8,128)(2,1)S(1)}, bf16[1,4,128,128]{3,2,1,0:T(8,128)(2,1)}, u32[]{:S(2)}) copy-start(bf16[1,4,128,128]{3,2,1,0:T(8,128)(2,1)} %couplings.3) | copy-start | bytes 393220
  65.2 15.8 %copy-start.4 = (bf16[512,128]{1,0:T(8,128)(2,1)S(1)}, bf16[512,128]{1,0:T(8,128)(2,1)}, u32[]{:S(2)}) copy-start(bf16[512,128]{1,0:T(8,128)(2,1)} %get-tuple-element.22.basis) | copy-start | bytes 393220
  65.2 15.7 %copy-start.5 = (bf16[1,128,128]{2,1,0:T(8,128)(2,1)S(1)}, bf16[1,128,128]{2,1,0:T(8,128)(2,1)}, u32[]{:S(2)}) copy-start(bf16[1,128,128]{2,1,0:T(8,128)(2,1)} %transfer.3) | copy-start | bytes 98308
  83.6 19.3 %all-to-all-start.3 = ((bf16[64,8,128]{2,1,0:T(8,128)(2,1)}), bf16[64,8,128]{2,1,0:T(8,128)(2,1)S(1)}, u32[]{:S(2)}, u32[]{:S(2)}) async-start(bf16[64,8,128]{2,1,0:T(8,128)(2,1)} %get-tuple-element.25), calls=%async_computation.3 | async-start | bytes 262144 | tf_op jit(solution)/shard_map/all_to_all | solution.py:320
  92.5 1.8 %copy-start.10 = (bf16[512,256]{1,0:T(8,128)(2,1)S(1)}, bf16[512,256]{1,0:T(8,128)(2,1)}, u32[]{:S(2)}) copy-start(bf16[512,256]{1,0:T(8,128)(2,1)} %get-tuple-element.30.values_in) | copy-start | bytes 786436
  94.3 38.4 %collective-permute-start.5 = (bf16[512,256]{1,0:T(8,128)(2,1)S(1)}, bf16[512,256]{1,0:T(8,128)(2,1)}, u32[]{:S(2)}, u32[]{:S(2)}) collective-permute-start(bf16[512,256]{1,0:T(8,128)(2,1)S(1)} %copy-done.10), channel_id=1, source_target_pairs={{2,0},{3,1},{4,2},{5,3},{6,4},{7,5},{8,6},{9,7},{10,8},{11,9},{12,... | collective-permute-start | bytes 786440 | tf_op jit(solution)/shard_map/ppermute | solution.py:311
  99.8 32.9 %collective-permute-start.4 = (bf16[512,256]{1,0:T(8,128)(2,1)S(1)}, bf16[512,256]{1,0:T(8,128)(2,1)}, u32[]{:S(2)}, u32[]{:S(2)}) collective-permute-start(bf16[512,256]{1,0:T(8,128)(2,1)S(1)} %copy-done.10), channel_id=1, source_target_pairs={{0,2},{1,3},{2,4},{3,5},{4,6},{5,7},{6,8},{7,9},{8,10},{9,11},{10,... | collective-permute-start | bytes 786440 | tf_op jit(solution)/shard_map/ppermute | solution.py:311
  103.8 8.7 %all-to-all-start.4 = ((bf16[8,16,128]{2,1,0:T(8,128)(2,1)}), bf16[8,16,128]{2,1,0:T(8,128)(2,1)S(1)}, u32[]{:S(2)}, u32[]{:S(2)}) async-start(bf16[8,16,128]{2,1,0:T(8,128)(2,1)} %get-tuple-element.27), calls=%async_computation.4 | async-start | bytes 65536 | tf_op jit(solution)/shard_map/all_to_all | solution.py:320
  114.7 18.0 %copy-start = (bf16[64,3,8,128]{3,2,1,0:T(8,128)(2,1)S(1)}, bf16[64,3,8,128]{3,2,1,0:T(8,128)(2,1)}, u32[]{:S(2)}) copy-start(bf16[64,3,8,128]{3,2,1,0:T(8,128)(2,1)} %couple.3.refs_7_) | copy-start | bytes 1179652
  114.7 32.8 %all-to-all-start.5 = ((bf16[64,3,8,128]{3,2,1,0:T(8,128)(2,1)}), bf16[64,3,8,128]{3,2,1,0:T(8,128)(2,1)S(1)}, u32[]{:S(2)}, u32[]{:S(2)}) async-start(bf16[64,3,8,128]{3,2,1,0:T(8,128)(2,1)} %couple.3.refs_7_), calls=%async_computation.5 | async-start | bytes 786432 | tf_op jit(solution)/shard_map/all_to_all | solution.py:320
  126.0 18.5 %copy-start.8 = (bf16[768,256]{1,0:T(8,128)(2,1)S(1)}, bf16[768,256]{1,0:T(8,128)(2,1)}, u32[]{:S(2)}) copy-start(bf16[768,256]{1,0:T(8,128)(2,1)} %copy-done.7) | copy-start | bytes 1179652
  126.0 16.2 %collective-permute-start.7 = (bf16[512,256]{1,0:T(8,128)(2,1)S(1)}, bf16[512,256]{1,0:T(8,128)(2,1)S(1)}, u32[]{:S(2)}, u32[]{:S(2)}) collective-permute-start(bf16[512,256]{1,0:T(8,128)(2,1)S(1)} %copy-done.10), channel_id=1, source_target_pairs={{1,0},{2,1},{3,2},{4,3},{5,4},{6,5},{7,6},{8,7},{9,8},{10,9},{11,1... | collective-permute-start | bytes 786440 | tf_op jit(solution)/shard_map/ppermute | solution.py:311
  130.7 13.8 %collective-permute-start.6 = (bf16[512,256]{1,0:T(8,128)(2,1)S(1)}, bf16[512,256]{1,0:T(8,128)(2,1)S(1)}, u32[]{:S(2)}, u32[]{:S(2)}) collective-permute-start(bf16[512,256]{1,0:T(8,128)(2,1)S(1)} %copy-done.10), channel_id=1, source_target_pairs={{0,1},{1,2},{2,3},{3,4},{4,5},{5,6},{6,7},{7,8},{8,9},{9,10},{10,1... | collective-permute-start | bytes 786440 | tf_op jit(solution)/shard_map/ppermute | solution.py:311
  (1 other events, 0.8 us)

commit v6 on v4

--- a/solution.py
+++ b/solution.py
@@ -288,18 +288,18 @@
         total[part] = product if fresh else total[part] + product
 
 
-def near_own_kernel(places_in, values_in, total, places, values, sems):
-    wait(started(((places_in.at[pl.ds(LEAF, 4 * DIM)], places), (values_in.at[pl.ds(0, LEAF)], values)), sems))
-    mine = coordinates(places[...])
-    block_times(mine, mine, values[...], total, True)
-
-
-def near_pair_kernel(offsets, near_list, places_in, before, p1, v1, p2, v2, _, total, places, values, sems):
-    copies = started([(p.at[pl.ds(LEAF, 4 * DIM)], places.at[i]) for i, p in enumerate((places_in, p1, p2))], sems)
-    copies += started([(v.at[pl.ds(0, LEAF)], values.at[i]) for i, v in enumerate((v1, v2))], sems, 3)
-    total[...] = before[...]
+def near_kernel(offsets, own, near_list, places_in, before, p1, v1, p2, v2, _, total, places, values, sems):
+    pairs = [(p.at[pl.ds(LEAF, 4 * DIM)], places.at[i]) for i, p in enumerate((places_in, p1, p2))]
+    pairs += [(v.at[pl.ds(0, LEAF)], values.at[i]) for i, v in enumerate((v1, v2))]
+    if own:
+        pairs.append((before.at[pl.ds(0, LEAF)], values.at[2]))
+    else:
+        pairs.append((before, total))
+    copies = started(pairs, sems)
     wait(copies)
     mine = coordinates(places[0])
+    if own:
+        block_times(mine, mine, values[2], total, True)
     for i, offset in enumerate(offsets):
 
         @pl.when(listed(near_list, offset))
@@ -307,14 +307,18 @@
             block_times(mine, coordinates(places[1 + i]), values[i], total, False)
 
 
+def mark_kernel(_, mark):
+    mark[...] = jnp.zeros_like(mark)
+
+
 def from_behind(shard, by):
     pairs = [(i, i + by) for i in range(N_DEV) if 0 <= i + by < N_DEV]
     return lax.ppermute(shard, "dev", pairs)
 
 
-def from_pair(shard, distance, after):
-    shard, _ = lax.optimization_barrier((shard, after))
-    return from_behind(shard, distance), from_behind(shard, -distance)
+def passed_on(pair, after):
+    behind, ahead, _ = lax.optimization_barrier((*pair, after))
+    return from_behind(behind, 1), from_behind(ahead, -1)
 
 
 def exchanged(blocks, axis):
@@ -341,7 +345,6 @@
     rows16 = pltpu.VMEM((N_DEV * 16, RANK), F32)
     rows8 = pltpu.VMEM((N_DEV * 8, RANK), F32)
     narrow = pltpu.VMEM((COLS * CPG, RANK), F32)
-    places = pltpu.VMEM((4 * DIM, OUT), BF16)
 
     wc, sent, basis = call(
         start_kernel,
@@ -369,29 +372,21 @@
         SHORT,
     )
 
-    def near_own(values):
+    def near_with(distance, own, before, first, fields, after, flops):
         (near,) = call(
-            near_own_kernel,
-            "near_own",
+            lambda *refs: near_kernel((-distance, distance), own, *refs),
+            f"near_{distance}",
             [(field, F32, VMEM)],
-            [HBM] * 2,
-            (wc, values),
-            [places, pltpu.VMEM(field, BF16), dma((2,))],
-            SHORT,
-        )
-        return near
-
-    def near_pair(distance, near, first, fields, after, flops):
-        (near,) = call(
-            lambda *refs: near_pair_kernel((-distance, distance), *refs),
-            f"near_pair_{distance}",
-            [(field, F32, VMEM)],
-            [SMEM, HBM, VMEM] + [ANY] * 5,
-            (near_list, wc, near, first[0], fields[0], first[1], fields[1], after),
-            [pltpu.VMEM((3, 4 * DIM, OUT), BF16), pltpu.VMEM((2, *field), BF16), dma((5,))],
+            [SMEM, HBM] + [ANY] * 6,
+            (near_list, wc, before, first[0], fields[0], first[1], fields[1], after),
+            [pltpu.VMEM((3, 4 * DIM, OUT), BF16), pltpu.VMEM((3, *field), BF16), dma((6,))],
             flops,
         )
         return near
+
+    def marked(shard):
+        (mark,) = call(mark_kernel, "mark", [((8, RANK), F32, VMEM)], [ANY], (shard,), flops=SHORT)
+        return mark
 
     def through_owners(sums, skeletons):
         all_sums = exchanged(sums, "grp")
@@ -417,21 +412,21 @@
         return sent, exchanged(sent, "dev"), done
 
     arrived = exchanged(sent, "dev")
-    near = near_own(wc)
-    first2 = from_pair(wc, 2, near)
+    mark = marked(wc)
+    first1 = passed_on((wc, wc), mark)
     sums, told, skeletons = call(
         sums_first_kernel,
         "sums_first",
         [((N_GRP, 16, RANK), BF16, VMEM), ((N_DEV, RANK), F32, VMEM), ((N_DEV, COLS * RANK), BF16, VMEM)],
         [VMEM, ANY],
-        (arrived, near),
+        (arrived, mark),
         [rows16, narrow],
         SHORT,
     )
     sent, arrived, done = through_owners(sums, skeletons)
-    first1 = from_pair(wc, 1, done)
-    near = near_pair(2, near, first2, first2, sent, MID)
-    near = near_pair(1, near, first1, first1, sent, LONG)
+    first2 = passed_on(first1, done)
+    near = near_with(1, True, wc, first1, first1, sent, MID)
+    near = near_with(2, False, near, first2, first2, sent, LONG)
     w, sent, r1 = call(
         middle_kernel,
         "middle",
@@ -450,21 +445,21 @@
         SHORT,
     )
     arrived = exchanged(sent, "dev")
-    near = near_own(w)
-    fields2 = from_pair(w, 2, near)
+    mark = marked(w)
+    fields1 = passed_on((w, w), mark)
     sums, skeletons = call(
         sums_kernel,
         "sums",
         [((N_GRP, 16, RANK), BF16, VMEM), ((N_DEV, COLS * RANK), BF16, VMEM)],
         [VMEM, VMEM, ANY],
-        (arrived, told, near),
+        (arrived, told, mark),
         [rows8, narrow],
         SHORT,
     )
     sent, arrived, done = through_owners(sums, skeletons)
-    fields1 = from_pair(w, 1, done)
-    near = near_pair(2, near, first2, fields2, sent, MID)
-    near = near_pair(1, near, first1, fields1, sent, LONG)
+    fields2 = passed_on(fields1, done)
+    near = near_with(1, True, w, first1, fields1, sent, MID)
+    near = near_with(2, False, near, first2, fields2, sent, LONG)
     return tuple(
         call(
             end_kernel,

time: 145 us -> 141 us (0.972)
  starting transfers between devices: 74.5 us -> 69.5 us
  Pallas kernels: 28.1 us -> 26.3 us
  local copies, waits for them, and re-layouts: 0.05 us -> 1.79 us
  waiting for transfers between devices: 38.5 us -> 40 us
    all_to_all x6, starting transfers between devices: 54.5 us -> 51.2 us  [exchanged(): return lax.all_to_all(blocks, axis, split_axis=0, concat_axis=0, tiled=True)]
    ppermute x8, starting transfers between devices: 20 us -> 18.2 us  [from_behind(): return lax.ppermute(shard, 'dev', pairs)]
    unnamed x18 -> x26, local copies, waits for them, and re-layouts: 0.05 us -> 1.79 us
    pallas_call x15, Pallas kernels: 28.1 us -> 26.3 us  [call(): pl.pallas_call(kernel, name=name, out_shape=shapes, in_specs=ins, out_spe...]
    all_to_all x6, waiting for transfers between devices: 38.5 us -> 40 us  [exchanged(): return lax.all_to_all(blocks, axis, split_axis=0, concat_axis=0, tiled=True)]
  transfers between devices with their start and end apart: 14 -> 14, of which waited for: 4 -> 4; matrix products, arithmetic and copies ran while one was open for 0% -> 0% of each run, Pallas kernels for 14% -> 13%
where the time goes in v6:
time: 141 us; the launch traced here: 140 us
  starting transfers between devices  69.5 us (49%)
  waiting for transfers between devices  40 us (28%)
  Pallas kernels  26.3 us (19%)
  between operations  2.49 us (2%)
  local copies, waits for them, and re-layouts  1.79 us (1%)
    all_to_all x6, starting transfers between devices, exchanged(): return lax.all_to_all(blocks, axis, split_axis=0, concat_axis=0, tiled=True)  51.2 us
    all_to_all x6, waiting for transfers between devices, exchanged(): return lax.all_to_all(blocks, axis, split_axis=0, concat_axis=0, tiled=True)  40 us
    pallas_call x15, Pallas kernels, call(): pl.pallas_call(kernel, name=name, out_shape=shapes, in_specs=ins, out_spe...  26.3 us
    ppermute x8, starting transfers between devices, from_behind(): return lax.ppermute(shard, 'dev', pairs)  18.2 us
  transfers between devices with their start and end apart: 14, of which 4 were waited for; matrix products, arithmetic and copies ran while one was open for 0% of the time, Pallas kernels for 13%

profile of v6, /device:TPU:2, one launch (start us, length us, event | category | flops | bytes accessed | tf_op | source)
XLA Modules:
  0.0 140.1 jit_solution(9469211086055507944)
XLA Ops:
  1.9 2.6 %start.1 = (bf16[768,256]{1,0:T(8,128)(2,1)}, bf16[64,16,128]{2,1,0:T(8,128)(2,1)}, bf16[512,128]{1,0:T(8,128)(2,1)}) custom-call(f32[1]{0:T(128)} %bitcast.2.ridge, s32[1]{0:T(128)S(6)} %copy.18.cluster, s32[1,4]{1,0:T(1,128)} %far_in.1, f32[512,256]{1,0:T(8,128)} %rs_in.5, f32[64,512]{1,0:T(8,128)} %bitcast.5, s32[1,512]{1,0:T(1,128)} %perm_in.1, ...), custom_call_target="tpu_custom_call" | custom-call | flops 10000000 | tf_op jit(solution)/shard_map/start/pallas_call | solution.py:36
  4.6 16.7 %all-to-all-start = ((bf16[64,16,128]{2,1,0:T(8,128)(2,1)}), bf16[64,16,128]{2,1,0:T(8,128)(2,1)S(1)}, u32[]{:S(2)}, u32[]{:S(2)}) async-start(bf16[64,16,128]{2,1,0:T(8,128)(2,1)} %get-tuple-element.23), calls=%async_computation | async-start | bytes 524288 | tf_op jit(solution)/shard_map/all_to_all | solution.py:325
  21.3 3.6 %collective-permute-start = (bf16[768,256]{1,0:T(8,128)(2,1)S(1)}, bf16[768,256]{1,0:T(8,128)(2,1)S(1)}, u32[]{:S(2)}, u32[]{:S(2)}) collective-permute-start(bf16[768,256]{1,0:T(8,128)(2,1)S(1)} %copy-done.5), channel_id=1, source_target_pairs={{0,1},{1,2},{2,3},{3,4},{4,5},{5,6},{6,7},{7,8},{8,9},{9,10},{10,1... | collective-permute-start | bytes 1179656 | tf_op jit(solution)/shard_map/ppermute | solution.py:316
  26.3 10.0 %all-to-all-done.arrived = bf16[64,16,128]{2,1,0:T(8,128)(2,1)S(1)} async-done(((bf16[64,16,128]{2,1,0:T(8,128)(2,1)}), bf16[64,16,128]{2,1,0:T(8,128)(2,1)S(1)}, u32[]{:S(2)}, u32[]{:S(2)}) %all-to-all-start) | async-done | bytes 262176 | tf_op jit(solution)/shard_map/all_to_all | solution.py:325
  37.2 4.8 %all-to-all-start.1 = ((bf16[8,16,128]{2,1,0:T(8,128)(2,1)}), bf16[8,16,128]{2,1,0:T(8,128)(2,1)S(1)}, u32[]{:S(2)}, u32[]{:S(2)}) async-start(bf16[8,16,128]{2,1,0:T(8,128)(2,1)} %get-tuple-element.25), calls=%async_computation.1 | async-start | bytes 65536 | tf_op jit(solution)/shard_map/all_to_all | solution.py:325
  42.0 2.7 %collective-permute-start.2 = (bf16[768,256]{1,0:T(8,128)(2,1)S(1)}, bf16[768,256]{1,0:T(8,128)(2,1)S(1)}, u32[]{:S(2)}, u32[]{:S(2)}) collective-permute-start(bf16[768,256]{1,0:T(8,128)(2,1)S(1)} %collective-permute-done.refs_3_.refs_4_), channel_id=1, source_target_pairs={{0,1},{1,2},{2,3},{3,4},{4,5},{5,6},{6,7},{7,8},{8,9},{9,10},{10,1... | collective-permute-start | bytes 1179656 | tf_op jit(solution)/shard_map/ppermute | solution.py:316
  46.0 1.7 %partners.2 = (bf16[64,3,8,128]{3,2,1,0:T(8,128)(2,1)}, f32[8,128]{1,0:T(8,128)}) custom-call(bf16[64,512]{1,0:T(8,128)(2,1)S(1)} %get-tuple-element.27.skeletons, f32[64,128]{1,0:T(8,128)S(1)} %get-tuple-element.26.told), custom_call_target="tpu_custom_call" | custom-call | flops 10000000 | tf_op jit(solution)/shard_map/partners/pallas_call | solution.py:36
  47.7 2.2 %couple.2.refs_7_ = bf16[64,3,8,128]{3,2,1,0:T(8,128)(2,1)} custom-call(s32[4,4]{1,0:T(4,128)S(1)} %copy-done.8, bf16[8,16,128]{2,1,0:T(8,128)(2,1)S(1)} %all-to-all-done.1.all_sums, bf16[4,4,128,128]{3,2,1,0:T(8,128)(2,1)S(1)} %copy-done, f32[64,128]{1,0:T(8,128)S(1)} %get-tuple-element.26.told, ...), custom_call_target="tpu_custom_call", output_to_operand_aliasing={{}: (4, {})} | custom-call | flops 10000000 | tf_op jit(solution)/shard_map/couple/pallas_call | solution.py:36
  49.9 10.4 %all-to-all-start.2 = ((bf16[64,3,8,128]{3,2,1,0:T(8,128)(2,1)}), bf16[64,3,8,128]{3,2,1,0:T(8,128)(2,1)S(1)}, u32[]{:S(2)}, u32[]{:S(2)}) async-start(bf16[64,3,8,128]{3,2,1,0:T(8,128)(2,1)} %couple.2.refs_7_), calls=%async_computation.2 | async-start | bytes 786432 | tf_op jit(solution)/shard_map/all_to_all | solution.py:325
  60.4 2.7 %near_1.2.refs_2_ = f32[512,256]{1,0:T(8,128)S(1)} custom-call(s32[1,4]{1,0:T(1,128)S(1)} %copy-done.12, bf16[768,256]{1,0:T(8,128)(2,1)} %get-tuple-element.31._.refs_1_.refs_2_, bf16[768,256]{1,0:T(8,128)(2,1)} %get-tuple-element.31._.refs_1_.refs_2_, bf16[768,256]{1,0:T(8,128)(2,1)S(1)} %collective-permute-done.refs_3_.refs_4_, ...), custom_call_target="tpu_custom_call" | custom-call | flops 10000000000 | tf_op jit(solution)/shard_map/near_1/pallas_call | solution.py:36
  64.8 1.8 %near_2.2.near = f32[512,256]{1,0:T(8,128)S(1)} custom-call(s32[1,4]{1,0:T(1,128)S(1)} %copy-done.12, bf16[768,256]{1,0:T(8,128)(2,1)} %get-tuple-element.31._.refs_1_.refs_2_, f32[512,256]{1,0:T(8,128)S(1)} %near_1.2.refs_2_, bf16[768,256]{1,0:T(8,128)(2,1)S(1)} %copy-done.10, bf16[768,256]{1,0:T(8,128)(2,1)S(1)} %copy-done.10, ...), custom_call_target="tpu_custom_call" | custom-call | flops 1000000000 | tf_op jit(solution)/shard_map/near_2/pallas_call | solution.py:36
  66.7 10.0 %all-to-all-done.2.arrived = bf16[64,3,8,128]{3,2,1,0:T(8,128)(2,1)S(1)} async-done(((bf16[64,3,8,128]{3,2,1,0:T(8,128)(2,1)}), bf16[64,3,8,128]{3,2,1,0:T(8,128)(2,1)S(1)}, u32[]{:S(2)}, u32[]{:S(2)}) %all-to-all-start.2) | async-done | bytes 393248 | tf_op jit(solution)/shard_map/all_to_all | solution.py:325
  76.7 2.6 %middle.1 = (bf16[512,256]{1,0:T(8,128)(2,1)}, bf16[64,8,128]{2,1,0:T(8,128)(2,1)}, f32[512,256]{1,0:T(8,128)}) custom-call(f32[1]{0:T(128)} %bitcast.3.ridge, bf16[64,3,8,128]{3,2,1,0:T(8,128)(2,1)S(1)} %all-to-all-done.2.arrived, bf16[1,4,128,128]{3,2,1,0:T(8,128)(2,1)S(1)} %copy-done.3, bf16[1,128,128]{2,1,0:T(8,128)(2,1)S(1)} %copy-done.6, ...), custom_call_target="tpu_custom_call" | custom-call | flops 10000000 | tf_op jit(solution)/shard_map/middle/pallas_call | solution.py:36
  79.3 4.7 %all-to-all-start.3 = ((bf16[64,8,128]{2,1,0:T(8,128)(2,1)}), bf16[64,8,128]{2,1,0:T(8,128)(2,1)S(1)}, u32[]{:S(2)}, u32[]{:S(2)}) async-start(bf16[64,8,128]{2,1,0:T(8,128)(2,1)} %get-tuple-element.34), calls=%async_computation.3 | async-start | bytes 262144 | tf_op jit(solution)/shard_map/all_to_all | solution.py:325
  84.1 3.4 %collective-permute-start.4 = (bf16[512,256]{1,0:T(8,128)(2,1)S(1)}, bf16[512,256]{1,0:T(8,128)(2,1)S(1)}, u32[]{:S(2)}, u32[]{:S(2)}) collective-permute-start(bf16[512,256]{1,0:T(8,128)(2,1)S(1)} %copy-done.7), channel_id=1, source_target_pairs={{0,1},{1,2},{2,3},{3,4},{4,5},{5,6},{6,7},{7,8},{8,9},{9,10},{10,1... | collective-permute-start | bytes 786440 | tf_op jit(solution)/shard_map/ppermute | solution.py:316
  88.9 8.1 %all-to-all-done.3.arrived = bf16[64,8,128]{2,1,0:T(8,128)(2,1)S(1)} async-done(((bf16[64,8,128]{2,1,0:T(8,128)(2,1)}), bf16[64,8,128]{2,1,0:T(8,128)(2,1)S(1)}, u32[]{:S(2)}, u32[]{:S(2)}) %all-to-all-start.3) | async-done | bytes 131104 | tf_op jit(solution)/shard_map/all_to_all | solution.py:325
  97.8 4.6 %all-to-all-start.4 = ((bf16[8,16,128]{2,1,0:T(8,128)(2,1)}), bf16[8,16,128]{2,1,0:T(8,128)(2,1)S(1)}, u32[]{:S(2)}, u32[]{:S(2)}) async-start(bf16[8,16,128]{2,1,0:T(8,128)(2,1)} %get-tuple-element.36), calls=%async_computation.4 | async-start | bytes 65536 | tf_op jit(solution)/shard_map/all_to_all | solution.py:325
  104.1 3.3 %collective-permute-start.6 = (bf16[512,256]{1,0:T(8,128)(2,1)S(1)}, bf16[512,256]{1,0:T(8,128)(2,1)}, u32[]{:S(2)}, u32[]{:S(2)}) collective-permute-start(bf16[512,256]{1,0:T(8,128)(2,1)S(1)} %collective-permute-done.4.refs_4_), channel_id=1, source_target_pairs={{0,1},{1,2},{2,3},{3,4},{4,5},{5,6},{6,7},{7,8},{8,9},{9,10},{10,1... | collective-permute-start | bytes 786440 | tf_op jit(solution)/shard_map/ppermute | solution.py:316
  108.7 2.2 %couple.3.refs_7_ = bf16[64,3,8,128]{3,2,1,0:T(8,128)(2,1)} custom-call(s32[4,4]{1,0:T(4,128)S(1)} %copy-done.8, bf16[8,16,128]{2,1,0:T(8,128)(2,1)S(1)} %all-to-all-done.4.all_sums, bf16[4,4,128,128]{3,2,1,0:T(8,128)(2,1)S(1)} %copy-done, f32[64,128]{1,0:T(8,128)S(1)} %get-tuple-element.26.told, ...), custom_call_target="tpu_custom_call", output_to_operand_aliasing={{}: (4, {})} | custom-call | flops 10000000 | tf_op jit(solution)/shard_map/couple/pallas_call | solution.py:36
  110.9 9.9 %all-to-all-start.5 = ((bf16[64,3,8,128]{3,2,1,0:T(8,128)(2,1)}), bf16[64,3,8,128]{3,2,1,0:T(8,128)(2,1)S(1)}, u32[]{:S(2)}, u32[]{:S(2)}) async-start(bf16[64,3,8,128]{3,2,1,0:T(8,128)(2,1)} %couple.3.refs_7_), calls=%async_computation.5 | async-start | bytes 786432 | tf_op jit(solution)/shard_map/all_to_all | solution.py:325
  120.9 2.6 %near_1.3.refs_2_ = f32[512,256]{1,0:T(8,128)S(1)} custom-call(s32[1,4]{1,0:T(1,128)S(1)} %copy-done.12, bf16[768,256]{1,0:T(8,128)(2,1)} %get-tuple-element.31._.refs_1_.refs_2_, bf16[512,256]{1,0:T(8,128)(2,1)S(1)} %copy-done.7, bf16[768,256]{1,0:T(8,128)(2,1)S(1)} %collective-permute-done.refs_3_.refs_4_, ...), custom_call_target="tpu_custom_call" | custom-call | flops 10000000000 | tf_op jit(solution)/shard_map/near_1/pallas_call | solution.py:36
  123.5 1.9 %near_2.3.near = f32[512,256]{1,0:T(8,128)S(1)} custom-call(s32[1,4]{1,0:T(1,128)S(1)} %copy-done.12, bf16[768,256]{1,0:T(8,128)(2,1)} %get-tuple-element.31._.refs_1_.refs_2_, f32[512,256]{1,0:T(8,128)S(1)} %near_1.3.refs_2_, bf16[768,256]{1,0:T(8,128)(2,1)S(1)} %copy-done.11, bf16[512,256]{1,0:T(8,128)(2,1)} %collective-permute-done.6.refs_4_, ...), custom_call_target="tpu_custom_call" | custom-call | flops 1000000000 | tf_op jit(solution)/shard_map/near_2/pallas_call | solution.py:36
  125.5 11.9 %all-to-all-done.5.arrived = bf16[64,3,8,128]{3,2,1,0:T(8,128)(2,1)S(1)} async-done(((bf16[64,3,8,128]{3,2,1,0:T(8,128)(2,1)}), bf16[64,3,8,128]{3,2,1,0:T(8,128)(2,1)S(1)}, u32[]{:S(2)}, u32[]{:S(2)}) %all-to-all-start.5) | async-done | bytes 393248 | tf_op jit(solution)/shard_map/all_to_all | solution.py:325
  137.3 2.6 %end.1 = (f32[512,256]{1,0:T(8,128)}, f32[512,256]{1,0:T(8,128)}) custom-call(f32[1]{0:T(128)} %bitcast.4.ridge, bf16[64,3,8,128]{3,2,1,0:T(8,128)(2,1)S(1)} %all-to-all-done.5.arrived, bf16[1,4,128,128]{3,2,1,0:T(8,128)(2,1)S(1)} %copy-done.3, bf16[1,128,128]{2,1,0:T(8,128)(2,1)S(1)} %copy-done.6, bf16[512,128]{1,0:T(8,128)(2,1)S(1)} %copy-done.4, ...), custom_call_target="tpu_custom_call" | custom-call | flops 10000000 | tf_op jit(solution)/shard_map/end/pallas_call | solution.py:36
  (45 shorter events, 10.4 us)
Async XLA Ops:
  4.5 16.8 %copy-start.5 = (bf16[768,256]{1,0:T(8,128)(2,1)S(1)}, bf16[768,256]{1,0:T(8,128)(2,1)}, u32[]{:S(2)}) copy-start(bf16[768,256]{1,0:T(8,128)(2,1)} %get-tuple-element.31._.refs_1_.refs_2_) | copy-start | bytes 1179652
  4.6 31.7 %all-to-all-start = ((bf16[64,16,128]{2,1,0:T(8,128)(2,1)}), bf16[64,16,128]{2,1,0:T(8,128)(2,1)S(1)}, u32[]{:S(2)}, u32[]{:S(2)}) async-start(bf16[64,16,128]{2,1,0:T(8,128)(2,1)} %get-tuple-element.23), calls=%async_computation | async-start | bytes 524288 | tf_op jit(solution)/shard_map/all_to_all | solution.py:325
  21.3 26.4 %copy-start = (bf16[4,4,128,128]{3,2,1,0:T(8,128)(2,1)S(1)}, bf16[4,4,128,128]{3,2,1,0:T(8,128)(2,1)}, u32[]{:S(2)}) copy-start(bf16[4,4,128,128]{3,2,1,0:T(8,128)(2,1)} %blocks.3) | copy-start | bytes 1572868
  21.3 20.7 %collective-permute-start = (bf16[768,256]{1,0:T(8,128)(2,1)S(1)}, bf16[768,256]{1,0:T(8,128)(2,1)S(1)}, u32[]{:S(2)}, u32[]{:S(2)}) collective-permute-start(bf16[768,256]{1,0:T(8,128)(2,1)S(1)} %copy-done.5), channel_id=1, source_target_pairs={{0,1},{1,2},{2,3},{3,4},{4,5},{5,6},{6,7},{7,8},{8,9},{9,10},{10,1... | collective-permute-start | bytes 1179656 | tf_op jit(solution)/shard_map/ppermute | solution.py:316
  25.0 17.0 %collective-permute-start.1 = (bf16[768,256]{1,0:T(8,128)(2,1)S(1)}, bf16[768,256]{1,0:T(8,128)(2,1)S(1)}, u32[]{:S(2)}, u32[]{:S(2)}) collective-permute-start(bf16[768,256]{1,0:T(8,128)(2,1)S(1)} %copy-done.5), channel_id=1, source_target_pairs={{1,0},{2,1},{3,2},{4,3},{5,4},{6,5},{7,6},{8,7},{9,8},{10,9},{11,1... | collective-permute-start | bytes 1179656 | tf_op jit(solution)/shard_map/ppermute | solution.py:316
  37.2 10.5 %all-to-all-start.1 = ((bf16[8,16,128]{2,1,0:T(8,128)(2,1)}), bf16[8,16,128]{2,1,0:T(8,128)(2,1)S(1)}, u32[]{:S(2)}, u32[]{:S(2)}) async-start(bf16[8,16,128]{2,1,0:T(8,128)(2,1)} %get-tuple-element.25), calls=%async_computation.1 | async-start | bytes 65536 | tf_op jit(solution)/shard_map/all_to_all | solution.py:325
  42.0 21.1 %collective-permute-start.2 = (bf16[768,256]{1,0:T(8,128)(2,1)S(1)}, bf16[768,256]{1,0:T(8,128)(2,1)S(1)}, u32[]{:S(2)}, u32[]{:S(2)}) collective-permute-start(bf16[768,256]{1,0:T(8,128)(2,1)S(1)} %collective-permute-done.refs_3_.refs_4_), channel_id=1, source_target_pairs={{0,1},{1,2},{2,3},{3,4},{4,5},{5,6},{6,7},{7,8},{8,9},{9,10},{10,1... | collective-permute-start | bytes 1179656 | tf_op jit(solution)/shard_map/ppermute | solution.py:316
  44.7 19.1 %collective-permute-start.3 = (bf16[768,256]{1,0:T(8,128)(2,1)S(1)}, bf16[768,256]{1,0:T(8,128)(2,1)}, u32[]{:S(2)}, u32[]{:S(2)}) collective-permute-start(bf16[768,256]{1,0:T(8,128)(2,1)S(1)} %collective-permute-done.1.refs_5_.refs_6_), channel_id=1, source_target_pairs={{1,0},{2,1},{3,2},{4,3},{5,4},{6,5},{7,6},{8,7},{9,8},{10,9},{11,1... | collective-permute-start | bytes 1179656 | tf_op jit(solution)/shard_map/ppermute | solution.py:316
  49.9 10.4 %copy-start.2 = (bf16[64,3,8,128]{3,2,1,0:T(8,128)(2,1)S(1)}, bf16[64,3,8,128]{3,2,1,0:T(8,128)(2,1)}, u32[]{:S(2)}) copy-start(bf16[64,3,8,128]{3,2,1,0:T(8,128)(2,1)} %couple.2.refs_7_) | copy-start | bytes 1179652
  49.9 10.4 %copy-start.12 = (s32[1,4]{1,0:T(1,128)S(1)}, s32[1,4]{1,0:T(1,128)}, u32[]{:S(2)}) copy-start(s32[1,4]{1,0:T(1,128)} %refs_0_.7) | copy-start | bytes 52
  49.9 26.7 %all-to-all-start.2 = ((bf16[64,3,8,128]{3,2,1,0:T(8,128)(2,1)}), bf16[64,3,8,128]{3,2,1,0:T(8,128)(2,1)S(1)}, u32[]{:S(2)}, u32[]{:S(2)}) async-start(bf16[64,3,8,128]{3,2,1,0:T(8,128)(2,1)} %couple.2.refs_7_), calls=%async_computation.2 | async-start | bytes 786432 | tf_op jit(solution)/shard_map/all_to_all | solution.py:325
  63.0 13.6 %copy-start.3 = (bf16[1,4,128,128]{3,2,1,0:T(8,128)(2,1)S(1)}, bf16[1,4,128,128]{3,2,1,0:T(8,128)(2,1)}, u32[]{:S(2)}) copy-start(bf16[1,4,128,128]{3,2,1,0:T(8,128)(2,1)} %couplings.3) | copy-start | bytes 393220
  63.0 13.6 %copy-start.4 = (bf16[512,128]{1,0:T(8,128)(2,1)S(1)}, bf16[512,128]{1,0:T(8,128)(2,1)}, u32[]{:S(2)}) copy-start(bf16[512,128]{1,0:T(8,128)(2,1)} %get-tuple-element.29.basis) | copy-start | bytes 393220
  63.1 13.6 %copy-start.6 = (bf16[1,128,128]{2,1,0:T(8,128)(2,1)S(1)}, bf16[1,128,128]{2,1,0:T(8,128)(2,1)}, u32[]{:S(2)}) copy-start(bf16[1,128,128]{2,1,0:T(8,128)(2,1)} %transfer.3) | copy-start | bytes 98308
  79.3 4.8 %copy-start.7 = (bf16[512,256]{1,0:T(8,128)(2,1)S(1)}, bf16[512,256]{1,0:T(8,128)(2,1)}, u32[]{:S(2)}) copy-start(bf16[512,256]{1,0:T(8,128)(2,1)} %get-tuple-element.40._.refs_2_) | copy-start | bytes 786436
  79.3 17.6 %all-to-all-start.3 = ((bf16[64,8,128]{2,1,0:T(8,128)(2,1)}), bf16[64,8,128]{2,1,0:T(8,128)(2,1)S(1)}, u32[]{:S(2)}, u32[]{:S(2)}) async-start(bf16[64,8,128]{2,1,0:T(8,128)(2,1)} %get-tuple-element.34), calls=%async_computation.3 | async-start | bytes 262144 | tf_op jit(solution)/shard_map/all_to_all | solution.py:325
  84.1 20.0 %collective-permute-start.4 = (bf16[512,256]{1,0:T(8,128)(2,1)S(1)}, bf16[512,256]{1,0:T(8,128)(2,1)S(1)}, u32[]{:S(2)}, u32[]{:S(2)}) collective-permute-start(bf16[512,256]{1,0:T(8,128)(2,1)S(1)} %copy-done.7), channel_id=1, source_target_pairs={{0,1},{1,2},{2,3},{3,4},{4,5},{5,6},{6,7},{7,8},{8,9},{9,10},{10,1... | collective-permute-start | bytes 786440 | tf_op jit(solution)/shard_map/ppermute | solution.py:316
  87.6 16.5 %collective-permute-start.5 = (bf16[512,256]{1,0:T(8,128)(2,1)S(1)}, bf16[512,256]{1,0:T(8,128)(2,1)}, u32[]{:S(2)}, u32[]{:S(2)}) collective-permute-start(bf16[512,256]{1,0:T(8,128)(2,1)S(1)} %copy-done.7), channel_id=1, source_target_pairs={{1,0},{2,1},{3,2},{4,3},{5,4},{6,5},{7,6},{8,7},{9,8},{10,9},{11,1... | collective-permute-start | bytes 786440 | tf_op jit(solution)/shard_map/ppermute | solution.py:316
  97.8 10.9 %all-to-all-start.4 = ((bf16[8,16,128]{2,1,0:T(8,128)(2,1)}), bf16[8,16,128]{2,1,0:T(8,128)(2,1)S(1)}, u32[]{:S(2)}, u32[]{:S(2)}) async-start(bf16[8,16,128]{2,1,0:T(8,128)(2,1)} %get-tuple-element.36), calls=%async_computation.4 | async-start | bytes 65536 | tf_op jit(solution)/shard_map/all_to_all | solution.py:325
  104.1 19.4 %collective-permute-start.6 = (bf16[512,256]{1,0:T(8,128)(2,1)S(1)}, bf16[512,256]{1,0:T(8,128)(2,1)}, u32[]{:S(2)}, u32[]{:S(2)}) collective-permute-start(bf16[512,256]{1,0:T(8,128)(2,1)S(1)} %collective-permute-done.4.refs_4_), channel_id=1, source_target_pairs={{0,1},{1,2},{2,3},{3,4},{4,5},{5,6},{6,7},{7,8},{8,9},{9,10},{10,1... | collective-permute-start | bytes 786440 | tf_op jit(solution)/shard_map/ppermute | solution.py:316
  107.4 16.1 %collective-permute-start.7 = (bf16[512,256]{1,0:T(8,128)(2,1)}, bf16[512,256]{1,0:T(8,128)(2,1)}, u32[]{:S(2)}, u32[]{:S(2)}) collective-permute-start(bf16[512,256]{1,0:T(8,128)(2,1)} %collective-permute-done.5.refs_6_), channel_id=1, source_target_pairs={{1,0},{2,1},{3,2},{4,3},{5,4},{6,5},{7,6},{8,7},{9,8},{10,9},{11,1... | collective-permute-start | bytes 786440 | tf_op jit(solution)/shard_map/ppermute | solution.py:316
  110.9 9.9 %copy-start.1 = (bf16[64,3,8,128]{3,2,1,0:T(8,128)(2,1)S(1)}, bf16[64,3,8,128]{3,2,1,0:T(8,128)(2,1)}, u32[]{:S(2)}) copy-start(bf16[64,3,8,128]{3,2,1,0:T(8,128)(2,1)} %couple.3.refs_7_) | copy-start | bytes 1179652
  110.9 26.4 %all-to-all-start.5 = ((bf16[64,3,8,128]{3,2,1,0:T(8,128)(2,1)}), bf16[64,3,8,128]{3,2,1,0:T(8,128)(2,1)S(1)}, u32[]{:S(2)}, u32[]{:S(2)}) async-start(bf16[64,3,8,128]{3,2,1,0:T(8,128)(2,1)} %couple.3.refs_7_), calls=%async_computation.5 | async-start | bytes 786432 | tf_op jit(solution)/shard_map/all_to_all | solution.py:325
  120.9 2.7 %copy-start.11 = (bf16[768,256]{1,0:T(8,128)(2,1)S(1)}, bf16[768,256]{1,0:T(8,128)(2,1)}, u32[]{:S(2)}) copy-start(bf16[768,256]{1,0:T(8,128)(2,1)} %copy-done.9) | copy-start | bytes 1179652
  (3 other events, 3.4 us)

commit v7 on v6

--- a/solution.py
+++ b/solution.py
@@ -82,8 +82,8 @@
 
 
 def start_kernel(
-    ridge, cluster, far_in, rs_in, coords_in, perm_in, basis_in, transfer_in, wc_out, sent_out, placed_out,
-    far, rs, coords, perm, basis, transfer, wc, sent, placed, staged, sems,
+    ridge, cluster, far_in, rs_in, coords_in, perm_in, basis_in, transfer_in, wc_out, sent_out, placed,
+    far, rs, coords, perm, basis, transfer, wc, sent, staged, sems,
 ):
     copies = started(
         (
@@ -107,7 +107,7 @@
     parts = jnp.concatenate([high, low], axis=0)
     wc[LEAF : LEAF + 2 * DIM] = parts[:, :OUT]
     wc[LEAF + 2 * DIM :] = parts[:, OUT:]
-    outs = started(((wc, wc_out), (placed, placed_out)), sems, 6)
+    outs = started(((wc, wc_out),), sems, 6)
     wait(copies[4:])
     to_owners(values, basis_here, transfer[0], staged, 16)
     lane = lax.broadcasted_iota(jnp.int32, (N_DEV, RANK), 1)
@@ -159,101 +159,76 @@
     picked = dot(pick, skeletons[...])
     for k in range(FAR1):
         for i in range(COLS):
-            staged[pl.ds(COLS * k + i, N_DEV, stride=16), :] = picked[
+            staged[:, i, RANK * k : RANK * (k + 1)] = picked[
                 N_DEV * k : N_DEV * (k + 1), RANK * i : RANK * (i + 1)
             ]
-    sent[...] = staged[...].reshape(N_DEV, 2, 8, RANK).astype(BF16)
+    sent[...] = staged[...].astype(BF16)
     done[...] = jnp.zeros_like(done)
-    wait(started(((sent, sent_out.at[:, :2]),), sems))
-
-
-def couple_kernel(far_clusters, all_sums, blocks, told, _, sent_out, staged, sent, sems):
+    wait(started(((sent, sent_out.at[:, :, pl.ds(0, FAR1 * RANK)]),), sems))
+
+
+def couple_kernel(picks, all_sums, blocks, told, _, sent_out, staged, sent, sems):
     rows = COLS * CPG
-    sums = all_sums[...].reshape(N_GRP * rows, RANK)
-    row = lax.broadcasted_iota(jnp.int32, (rows, N_GRP * rows), 0)
-    lane = lax.broadcasted_iota(jnp.int32, (rows, N_GRP * rows), 1)
-    column, cluster = row // CPG, row % CPG
+    picked = dot(picks[...], all_sums[...].reshape(N_GRP * rows, RANK)).astype(BF16)
     total = jnp.zeros((CPG * RANK, rows), F32)
     for k in range(FAR2):
-        target = CPG * column
-        for c in range(CPG):
-            f = far_clusters[c, k]
-            target += jnp.where(cluster == c, rows * (f // CPG) + f % CPG, 0)
-        pick = jnp.where(lane == target, 1.0, 0.0).astype(BF16)
-        picked = dot(pick, sums).astype(BF16)
-        total += dot(blocks[:, k].reshape(CPG * RANK, RANK), picked, ((1,), (1,)))
+        block = blocks[:, k].reshape(CPG * RANK, RANK)
+        total += dot(block, picked[rows * k : rows * (k + 1)], ((1,), (1,)))
     own = lax.broadcasted_iota(jnp.int32, (RANK, rows), 1) % CPG
     coupled = jnp.zeros((RANK, rows), F32)
     for c in range(CPG):
         coupled += jnp.where(own == c, total[RANK * c : RANK * (c + 1)], 0.0)
-    coupled = coupled.T
-    coupled = coupled.astype(BF16)
+    coupled = coupled.T.astype(BF16)
     lane = lax.broadcasted_iota(jnp.int32, (N_DEV, rows), 1).astype(F32)
     pick = jnp.concatenate(
         [jnp.where(lane == told[:, FAR1 : FAR1 + 1] + CPG * i, 1.0, 0.0) for i in range(COLS)], axis=0
     ).astype(BF16)
     out = dot(pick, coupled)
-    staged[...] = jnp.zeros_like(staged)
     for i in range(COLS):
-        staged[pl.ds(i, N_DEV, stride=8), :] = out[N_DEV * i : N_DEV * (i + 1)]
-    sent[...] = staged[...].reshape(N_DEV, 8, RANK).astype(BF16)
-    wait(started(((sent, sent_out.at[:, 2]),), sems))
+        staged[:, i, :] = out[N_DEV * i : N_DEV * (i + 1)]
+    sent[...] = staged[...].astype(BF16)
+    wait(started(((sent, sent_out.at[:, :, pl.ds(FAR1 * RANK, RANK)]),), sems))
 
 
 def local_field(arrived, couplings, transfer, staged):
-    staged[...] = arrived[...].astype(F32).reshape(N_DEV * 24, RANK)
+    staged[...] = arrived[...].astype(F32)
     local = jnp.zeros((OUT, RANK), F32)
     for k in range(FAR1 + 1):
         skeleton = jnp.concatenate(
-            [staged[pl.ds(COLS * k + i, N_DEV, stride=24), :] for i in range(COLS)], axis=0
+            [staged[:, i, RANK * k : RANK * (k + 1)] for i in range(COLS)], axis=0
         ).astype(BF16)
         local += dot(skeleton, couplings[0, k] if k < FAR1 else transfer[0], ((1,), (1,)))
     return local.T.astype(BF16)
 
 
 def middle_kernel(
-    ridge, arrived, couplings, transfer, basis, near, rs_in, w_out, sent_out, r1_out,
-    rs, w, sent, r1, staged, staged_out, sems,
+    arrived, couplings, transfer, basis, residual, direction, factor, w, sent_out, r1, sent, staged, staged_out, sems
 ):
-    copies = started(((rs_in, rs),), sems)
-    ridge, centre, (mul, add), _ = chebyshev(ridge[0])
     local = local_field(arrived, couplings, transfer, staged)
-    wait(copies)
+    for r in range(0, LEAF, ROWS):
+        part = slice(r, r + ROWS)
+        far = dot(basis[part], local)
+        r1[part] = residual[part] - far
+        w[part] = (direction[part] - factor[:1, :1] * far).astype(BF16)
+    to_owners(w[...], basis[...], transfer[0], staged_out, 8)
+    sent[...] = staged_out[...].astype(BF16).reshape(N_DEV, 8, RANK)
+    wait(started(((sent, sent_out),), sems))
+
+
+def end_kernel(
+    arrived, couplings, transfer, basis, before_r, before_s, factor, solution_out, residual_out,
+    solution, residual, staged, sems,
+):
+    local = local_field(arrived, couplings, transfer, staged)
     outs = []
     for n, r in enumerate(range(0, LEAF, ROWS)):
         part = slice(r, r + ROWS)
-        here = rs[part]
-        d1 = here / centre
-        residual = here - (ridge * d1 + (near[part] + dot(basis[part], local)))
-        r1[part] = residual
-        w[part] = (mul * d1 + add * residual).astype(BF16)
-        at = pl.ds(r, ROWS)
-        outs += started(((r1.at[at], r1_out.at[at]), (w.at[at], w_out.at[at])), sems, 1 + 2 * n)
-    to_owners(w[...], basis[...], transfer[0], staged_out, 8)
-    sent[...] = staged_out[...].astype(BF16).reshape(N_DEV, 8, RANK)
-    outs += started(((sent, sent_out),), sems, 9)
-    wait(outs)
-
-
-def end_kernel(
-    ridge, arrived, couplings, transfer, basis, near, rs_in, r1_in, solution_out, residual_out,
-    rs, r1, solution, residual, staged, sems,
-):
-    copies = started(((rs_in, rs), (r1_in, r1)), sems)
-    ridge, centre, (mul1, add1), (mul, add) = chebyshev(ridge[0])
-    local = local_field(arrived, couplings, transfer, staged)
-    wait(copies)
-    outs = []
-    for n, r in enumerate(range(0, LEAF, ROWS)):
-        part = slice(r, r + ROWS)
-        d1 = rs[part] / centre
-        d2 = mul1 * d1 + add1 * r1[part]
-        r2 = r1[part] - (ridge * d2 + (near[part] + dot(basis[part], local)))
-        residual[part] = r2
-        solution[part] = d1 + d2 + (mul * d2 + add * r2)
+        far = dot(basis[part], local)
+        residual[part] = before_r[part] - far
+        solution[part] = before_s[part] - factor[:1, :1] * far
         at = pl.ds(r, ROWS)
         outs += started(
-            ((residual.at[at], residual_out.at[at]), (solution.at[at], solution_out.at[at])), sems, 2 + 2 * n
+            ((residual.at[at], residual_out.at[at]), (solution.at[at], solution_out.at[at])), sems, 2 * n
         )
     wait(outs)
 
@@ -288,18 +263,7 @@
         total[part] = product if fresh else total[part] + product
 
 
-def near_kernel(offsets, own, near_list, places_in, before, p1, v1, p2, v2, _, total, places, values, sems):
-    pairs = [(p.at[pl.ds(LEAF, 4 * DIM)], places.at[i]) for i, p in enumerate((places_in, p1, p2))]
-    pairs += [(v.at[pl.ds(0, LEAF)], values.at[i]) for i, v in enumerate((v1, v2))]
-    if own:
-        pairs.append((before.at[pl.ds(0, LEAF)], values.at[2]))
-    else:
-        pairs.append((before, total))
-    copies = started(pairs, sems)
-    wait(copies)
-    mine = coordinates(places[0])
-    if own:
-        block_times(mine, mine, values[2], total, True)
+def near_products(offsets, near_list, mine, places, values, total):
     for i, offset in enumerate(offsets):
 
         @pl.when(listed(near_list, offset))
@@ -307,8 +271,58 @@
             block_times(mine, coordinates(places[1 + i]), values[i], total, False)
 
 
+def near_pairs(places_in, p1, v1, p2, v2, places, values):
+    pairs = [(p.at[pl.ds(LEAF, 4 * DIM)], places.at[i]) for i, p in enumerate((places_in, p1, p2))]
+    return pairs + [(v.at[pl.ds(0, LEAF)], values.at[i]) for i, v in enumerate((v1, v2))]
+
+
+def near_1_kernel(near_list, places_in, own, p1, v1, p2, v2, _, total, places, values, sems):
+    pairs = near_pairs(places_in, p1, v1, p2, v2, places, values)
+    wait(started([*pairs, (own.at[pl.ds(0, LEAF)], values.at[2])], sems))
+    mine = coordinates(places[0])
+    block_times(mine, mine, values[2], total, True)
+    near_products((-1, 1), near_list, mine, places, values, total)
+
+
+def near_2_kernel(
+    last, ridge, near_list, places_in, before, p1, v1, p2, v2, rs_in, r1, residual, other, factor,
+    total, places, values, rs, sems,
+):
+    pairs = near_pairs(places_in, p1, v1, p2, v2, places, values)
+    copies = started([*pairs, (before, total), (rs_in, rs)], sems)
+    if last:
+        copies += started(((r1, residual),), sems, 7)
+    wait(copies)
+    near_products((-2, 2), near_list, coordinates(places[0]), places, values, total)
+    ridge, centre, first, second = chebyshev(ridge[0])
+    d1 = rs[...] / centre
+    if last:
+        d2 = first[0] * d1 + first[1] * residual[...]
+        left = residual[...] - (ridge * d2 + total[...])
+        other[...] = d1 + d2 + (second[0] * d2 + second[1] * left)
+        factor[...] = jnp.broadcast_to(second[1], factor.shape)
+    else:
+        left = rs[...] - (ridge * d1 + total[...])
+        other[...] = first[0] * d1 + first[1] * left
+        factor[...] = jnp.broadcast_to(first[1], factor.shape)
+    residual[...] = left
+
+
 def mark_kernel(_, mark):
     mark[...] = jnp.zeros_like(mark)
+
+
+def prepare_kernel(far_clusters, _, picks):
+    rows = COLS * CPG
+    row = lax.broadcasted_iota(jnp.int32, (rows, N_GRP * rows), 0)
+    lane = lax.broadcasted_iota(jnp.int32, (rows, N_GRP * rows), 1)
+    column, cluster = row // CPG, row % CPG
+    for k in range(FAR2):
+        target = CPG * column
+        for c in range(CPG):
+            f = far_clusters[c, k]
+            target += jnp.where(cluster == c, rows * (f // CPG) + f % CPG, 0)
+        picks[rows * k : rows * (k + 1)] = jnp.where(lane == target, 1.0, 0.0).astype(BF16)
 
 
 def from_behind(shard, by):
@@ -341,7 +355,8 @@
 ):
     ridge = ridge_weight.reshape(1)
     field, dma = (LEAF, OUT), pltpu.SemaphoreType.DMA
-    rows24 = pltpu.VMEM((N_DEV * 24, RANK), F32)
+    payload, partner = (N_DEV, COLS, (FAR1 + 1) * RANK), (N_DEV, COLS, FAR1 * RANK)
+    wide = pltpu.VMEM(payload, F32)
     rows16 = pltpu.VMEM((N_DEV * 16, RANK), F32)
     rows8 = pltpu.VMEM((N_DEV * 8, RANK), F32)
     narrow = pltpu.VMEM((COLS * CPG, RANK), F32)
@@ -352,7 +367,7 @@
         [
             ((LEAF + 4 * DIM, OUT), BF16, HBM),
             ((N_DEV, 16, RANK), BF16, HBM),
-            ((LEAF, RANK), BF16, HBM),
+            ((LEAF, RANK), BF16, VMEM),
         ],
         [SMEM] * 2 + [HBM] * 6,
         (ridge, cluster_of, far_leaves, right_side, coords.T, leaf_perm, leaf_basis, transfer),
@@ -365,24 +380,40 @@
             pltpu.VMEM((1, RANK, RANK), BF16),
             pltpu.VMEM((LEAF + 4 * DIM, OUT), BF16),
             pltpu.VMEM((N_DEV, 16, RANK), BF16),
-            pltpu.VMEM((LEAF, RANK), BF16),
             rows16,
             dma((9,)),
         ],
         SHORT,
     )
 
-    def near_with(distance, own, before, first, fields, after, flops):
+    def near_1(own, first, fields, after):
         (near,) = call(
-            lambda *refs: near_kernel((-distance, distance), own, *refs),
-            f"near_{distance}",
+            near_1_kernel,
+            "near_1",
             [(field, F32, VMEM)],
             [SMEM, HBM] + [ANY] * 6,
-            (near_list, wc, before, first[0], fields[0], first[1], fields[1], after),
+            (near_list, wc, own, first[0], fields[0], first[1], fields[1], after),
             [pltpu.VMEM((3, 4 * DIM, OUT), BF16), pltpu.VMEM((3, *field), BF16), dma((6,))],
-            flops,
+            MID,
         )
         return near
+
+    def near_2(last, near, first, fields, r1):
+        return call(
+            lambda *refs: near_2_kernel(last, *refs),
+            "near_2",
+            [(field, F32, VMEM), (field, F32, VMEM), ((8, RANK), F32, VMEM)],
+            [SMEM, SMEM, HBM] + [ANY] * 5 + [HBM, ANY],
+            (ridge, near_list, wc, near, first[0], fields[0], first[1], fields[1], right_side, r1),
+            [
+                pltpu.VMEM(field, F32),
+                pltpu.VMEM((3, 4 * DIM, OUT), BF16),
+                pltpu.VMEM((2, *field), BF16),
+                pltpu.VMEM(field, F32),
+                dma((8,)),
+            ],
+            LONG,
+        )
 
     def marked(shard):
         (mark,) = call(mark_kernel, "mark", [((8, RANK), F32, VMEM)], [ANY], (shard,), flops=SHORT)
@@ -393,55 +424,54 @@
         partners, done = call(
             partners_kernel,
             "partners",
-            [((N_DEV, 3, 8, RANK), BF16, HBM), ((8, RANK), F32, VMEM)],
+            [(payload, BF16, HBM), ((8, RANK), F32, VMEM)],
             [VMEM] * 2,
             (skeletons, told),
-            [rows16, pltpu.VMEM((N_DEV, 2, 8, RANK), BF16), dma((1,))],
+            [pltpu.VMEM(partner, F32), pltpu.VMEM(partner, BF16), dma((1,))],
             SHORT,
         )
         (sent,) = call(
             couple_kernel,
             "couple",
-            [((N_DEV, 3, 8, RANK), BF16, HBM)],
-            [SMEM] + [VMEM] * 3 + [HBM],
-            (far_clusters, all_sums, cluster_couplings, told, partners),
-            [rows8, pltpu.VMEM((N_DEV, 8, RANK), BF16), dma((1,))],
+            [(payload, BF16, HBM)],
+            [VMEM] * 4 + [HBM],
+            (picks, all_sums, cluster_couplings, told, partners),
+            [pltpu.VMEM((N_DEV, COLS, RANK), F32), pltpu.VMEM((N_DEV, COLS, RANK), BF16), dma((1,))],
             SHORT,
             {4: 0},
         )
         return sent, exchanged(sent, "dev"), done
 
     arrived = exchanged(sent, "dev")
-    mark = marked(wc)
-    first1 = passed_on((wc, wc), mark)
+    (picks,) = call(
+        prepare_kernel,
+        "prepare",
+        [((FAR2 * COLS * CPG, N_GRP * COLS * CPG), BF16, VMEM)],
+        [SMEM, ANY],
+        (far_clusters, wc),
+        flops=SHORT,
+    )
+    first1 = passed_on((wc, wc), picks)
     sums, told, skeletons = call(
         sums_first_kernel,
         "sums_first",
         [((N_GRP, 16, RANK), BF16, VMEM), ((N_DEV, RANK), F32, VMEM), ((N_DEV, COLS * RANK), BF16, VMEM)],
         [VMEM, ANY],
-        (arrived, mark),
+        (arrived, picks),
         [rows16, narrow],
         SHORT,
     )
     sent, arrived, done = through_owners(sums, skeletons)
     first2 = passed_on(first1, done)
-    near = near_with(1, True, wc, first1, first1, sent, MID)
-    near = near_with(2, False, near, first2, first2, sent, LONG)
+    near = near_1(wc, first1, first1, sent)
+    residual, direction, factor = near_2(False, near, first2, first2, near)
     w, sent, r1 = call(
         middle_kernel,
         "middle",
-        [(field, BF16, HBM), ((N_DEV, 8, RANK), BF16, HBM), (field, F32, HBM)],
-        [SMEM] + [VMEM] * 5 + [HBM],
-        (ridge, arrived, couplings, transfer, basis, near, right_side),
-        [
-            pltpu.VMEM(field, F32),
-            pltpu.VMEM(field, BF16),
-            pltpu.VMEM((N_DEV, 8, RANK), BF16),
-            pltpu.VMEM(field, F32),
-            rows24,
-            rows8,
-            dma((10,)),
-        ],
+        [(field, BF16, VMEM), ((N_DEV, 8, RANK), BF16, HBM), (field, F32, VMEM)],
+        [VMEM] * 7,
+        (arrived, couplings, transfer, basis, residual, direction, factor),
+        [pltpu.VMEM((N_DEV, 8, RANK), BF16), wide, rows8, dma((1,))],
         SHORT,
     )
     arrived = exchanged(sent, "dev")
@@ -458,16 +488,16 @@
     )
     sent, arrived, done = through_owners(sums, skeletons)
     fields2 = passed_on(fields1, done)
-    near = near_with(1, True, w, first1, fields1, sent, MID)
-    near = near_with(2, False, near, first2, fields2, sent, LONG)
+    near = near_1(w, first1, fields1, sent)
+    residual, total, factor = near_2(True, near, first2, fields2, r1)
     return tuple(
         call(
             end_kernel,
             "end",
             [(field, F32, HBM), (field, F32, HBM)],
-            [SMEM] + [VMEM] * 5 + [HBM] * 2,
-            (ridge, arrived, couplings, transfer, basis, near, right_side, r1),
-            [pltpu.VMEM(field, F32)] * 4 + [rows24, dma((10,))],
+            [VMEM] * 7,
+            (arrived, couplings, transfer, basis, residual, total, factor),
+            [pltpu.VMEM(field, F32)] * 2 + [wide, dma((8,))],
             SHORT,
         )
     )

time: 141 us -> 139 us (0.986)
  waiting for transfers between devices: 40 us -> 33.8 us
  starting transfers between devices: 69.5 us -> 72.1 us
    all_to_all x6, waiting for transfers between devices: 40 us -> 33.7 us  [exchanged(): return lax.all_to_all(blocks, axis, split_axis=0, concat_axis=0, tiled=True)]
    all_to_all x6, starting transfers between devices: 51.2 us -> 54 us  [exchanged(): return lax.all_to_all(blocks, axis, split_axis=0, concat_axis=0, tiled=True)]
  transfers between devices with their start and end apart: 14 -> 14, of which waited for: 4 -> 4; matrix products, arithmetic and copies ran while one was open for 0% -> 0% of each run, Pallas kernels for 13% -> 15%
where the time goes in v7:
time: 139 us; the launch traced here: 138 us
  starting transfers between devices  72.1 us (52%)
  waiting for transfers between devices  33.8 us (24%)
  Pallas kernels  27.5 us (20%)
  between operations  2.55 us (2%)
  local copies, waits for them, and re-layouts  1.84 us (1%)
    all_to_all x6, starting transfers between devices, exchanged(): return lax.all_to_all(blocks, axis, split_axis=0, concat_axis=0, tiled=True)  54 us
    all_to_all x6, waiting for transfers between devices, exchanged(): return lax.all_to_all(blocks, axis, split_axis=0, concat_axis=0, tiled=True)  33.7 us
    pallas_call x15, Pallas kernels, call(): pl.pallas_call(kernel, name=name, out_shape=shapes, in_specs=ins, out_spe...  27.5 us
    ppermute x8, starting transfers between devices, from_behind(): return lax.ppermute(shard, 'dev', pairs)  18.1 us
  transfers between devices with their start and end apart: 14, of which 4 were waited for; matrix products, arithmetic and copies ran while one was open for 0% of the time, Pallas kernels for 15%

profile of v7, /device:TPU:2, one launch (start us, length us, event | category | flops | bytes accessed | tf_op | source)
XLA Modules:
  0.0 137.7 jit_solution(6391622069438751505)
XLA Ops:
  1.9 2.6 %start.1 = (bf16[768,256]{1,0:T(8,128)(2,1)}, bf16[64,16,128]{2,1,0:T(8,128)(2,1)}, bf16[512,128]{1,0:T(8,128)(2,1)S(1)}) custom-call(f32[1]{0:T(128)} %bitcast.2.ridge, s32[1]{0:T(128)S(6)} %copy.18.cluster, s32[1,4]{1,0:T(1,128)} %far_in.1, f32[512,256]{1,0:T(8,128)} %refs_8_.3, f32[64,512]{1,0:T(8,128)} %bitcast.5, s32[1,512]{1,0:T(1,128)} %perm_in.1, ...), custom_call_target="tpu_custom_call" | custom-call | flops 10000000 | tf_op jit(solution)/shard_map/start/pallas_call | solution.py:36
  4.6 16.7 %all-to-all-start = ((bf16[64,16,128]{2,1,0:T(8,128)(2,1)}), bf16[64,16,128]{2,1,0:T(8,128)(2,1)S(1)}, u32[]{:S(2)}, u32[]{:S(2)}) async-start(bf16[64,16,128]{2,1,0:T(8,128)(2,1)} %get-tuple-element.30), calls=%async_computation | async-start | bytes 524288 | tf_op jit(solution)/shard_map/all_to_all | solution.py:339
  22.0 3.5 %collective-permute-start = (bf16[768,256]{1,0:T(8,128)(2,1)S(1)}, bf16[768,256]{1,0:T(8,128)(2,1)S(1)}, u32[]{:S(2)}, u32[]{:S(2)}) collective-permute-start(bf16[768,256]{1,0:T(8,128)(2,1)S(1)} %copy-done.4), channel_id=1, source_target_pairs={{0,1},{1,2},{2,3},{3,4},{4,5},{5,6},{6,7},{7,8},{8,9},{9,10},{10,1... | collective-permute-start | bytes 1179656 | tf_op jit(solution)/shard_map/ppermute | solution.py:330
  26.8 9.5 %all-to-all-done.arrived = bf16[64,16,128]{2,1,0:T(8,128)(2,1)S(1)} async-done(((bf16[64,16,128]{2,1,0:T(8,128)(2,1)}), bf16[64,16,128]{2,1,0:T(8,128)(2,1)S(1)}, u32[]{:S(2)}, u32[]{:S(2)}) %all-to-all-start) | async-done | bytes 262176 | tf_op jit(solution)/shard_map/all_to_all | solution.py:339
  37.2 4.8 %all-to-all-start.1 = ((bf16[8,16,128]{2,1,0:T(8,128)(2,1)}), bf16[8,16,128]{2,1,0:T(8,128)(2,1)S(1)}, u32[]{:S(2)}, u32[]{:S(2)}) async-start(bf16[8,16,128]{2,1,0:T(8,128)(2,1)} %get-tuple-element.31), calls=%async_computation.1 | async-start | bytes 65536 | tf_op jit(solution)/shard_map/all_to_all | solution.py:339
  42.1 2.7 %collective-permute-start.2 = (bf16[768,256]{1,0:T(8,128)(2,1)S(1)}, bf16[768,256]{1,0:T(8,128)(2,1)S(1)}, u32[]{:S(2)}, u32[]{:S(2)}) collective-permute-start(bf16[768,256]{1,0:T(8,128)(2,1)S(1)} %collective-permute-done.p1.v1), channel_id=1, source_target_pairs={{0,1},{1,2},{2,3},{3,4},{4,5},{5,6},{6,7},{7,8},{8,9},{9,10},{10,1... | collective-permute-start | bytes 1179656 | tf_op jit(solution)/shard_map/ppermute | solution.py:330
  46.1 1.9 %partners.2 = (bf16[64,4,640]{2,1,0:T(4,128)(2,1)}, f32[8,128]{1,0:T(8,128)}) custom-call(bf16[64,512]{1,0:T(8,128)(2,1)S(1)} %get-tuple-element.33.skeletons, f32[64,128]{1,0:T(8,128)S(1)} %get-tuple-element.32.told), custom_call_target="tpu_custom_call" | custom-call | flops 10000000 | tf_op jit(solution)/shard_map/partners/pallas_call | solution.py:36
  49.3 10.9 %all-to-all-start.2 = ((bf16[64,4,640]{2,1,0:T(4,128)(2,1)}), bf16[64,4,640]{2,1,0:T(4,128)(2,1)S(1)}, u32[]{:S(2)}, u32[]{:S(2)}) async-start(bf16[64,4,640]{2,1,0:T(4,128)(2,1)} %couple.2._), calls=%async_computation.2 | async-start | bytes 655360 | tf_op jit(solution)/shard_map/all_to_all | solution.py:339
  60.3 3.2 %near_1.2.refs_3_.refs_9_ = f32[512,256]{1,0:T(8,128)S(1)} custom-call(s32[1,4]{1,0:T(1,128)S(1)} %copy-done.16, bf16[768,256]{1,0:T(8,128)(2,1)} %get-tuple-element.37._.places_in.own.refs_2_, bf16[768,256]{1,0:T(8,128)(2,1)} %get-tuple-element.37._.places_in.own.refs_2_, bf16[768,256]{1,0:T(8,128)(2,1)S(1)} %collective-permute-done.p1.v1, ...), custom_call_target="tpu_custom_call" | custom-call | flops 10000000000 | tf_op jit(solution)/shard_map/near_1/pallas_call | solution.py:36
  65.3 3.0 %near_2.2 = (f32[512,256]{1,0:T(8,128)S(1)}, f32[512,256]{1,0:T(8,128)S(1)}, f32[8,128]{1,0:T(8,128)S(1)}) custom-call(f32[1]{0:T(128)} %bitcast.3.refs_0_, s32[1,4]{1,0:T(1,128)S(1)} %copy-done.16, bf16[768,256]{1,0:T(8,128)(2,1)} %get-tuple-element.37._.places_in.own.refs_2_, f32[512,256]{1,0:T(8,128)S(1)} %near_1.2.refs_3_.refs_9_, ...), custom_call_target="tpu_custom_call" | custom-call | flops 1000000000 | tf_op jit(solution)/shard_map/near_2/pallas_call | solution.py:36
  68.3 6.8 %all-to-all-done.2.arrived = bf16[64,4,640]{2,1,0:T(4,128)(2,1)S(1)} async-done(((bf16[64,4,640]{2,1,0:T(4,128)(2,1)}), bf16[64,4,640]{2,1,0:T(4,128)(2,1)S(1)}, u32[]{:S(2)}, u32[]{:S(2)}) %all-to-all-start.2) | async-done | bytes 327712 | tf_op jit(solution)/shard_map/all_to_all | solution.py:339
  75.1 2.0 %middle.1 = (bf16[512,256]{1,0:T(8,128)(2,1)S(1)}, bf16[64,8,128]{2,1,0:T(8,128)(2,1)}, f32[512,256]{1,0:T(8,128)S(1)}) custom-call(bf16[64,4,640]{2,1,0:T(4,128)(2,1)S(1)} %all-to-all-done.2.arrived, bf16[1,4,128,128]{3,2,1,0:T(8,128)(2,1)S(1)} %copy-done.3, bf16[1,128,128]{2,1,0:T(8,128)(2,1)S(1)} %copy-done.5, ...), custom_call_target="tpu_custom_call" | custom-call | flops 10000000 | tf_op jit(solution)/shard_map/middle/pallas_call | solution.py:36
  77.1 7.2 %all-to-all-start.3 = ((bf16[64,8,128]{2,1,0:T(8,128)(2,1)}), bf16[64,8,128]{2,1,0:T(8,128)(2,1)S(1)}, u32[]{:S(2)}, u32[]{:S(2)}) async-start(bf16[64,8,128]{2,1,0:T(8,128)(2,1)} %get-tuple-element.43), calls=%async_computation.3 | async-start | bytes 262144 | tf_op jit(solution)/shard_map/all_to_all | solution.py:339
  84.3 3.5 %collective-permute-start.4 = (bf16[512,256]{1,0:T(8,128)(2,1)S(1)}, bf16[512,256]{1,0:T(8,128)(2,1)S(1)}, u32[]{:S(2)}, u32[]{:S(2)}) collective-permute-start(bf16[512,256]{1,0:T(8,128)(2,1)S(1)} %get-tuple-element.49._.own), channel_id=1, source_target_pairs={{0,1},{1,2},{2,3},{3,4},{4,5},{5,6},{6,7},{7,8},{8,9},{9,10},{10,1... | collective-permute-start | bytes 786440 | tf_op jit(solution)/shard_map/ppermute | solution.py:330
  89.1 7.8 %all-to-all-done.3.arrived = bf16[64,8,128]{2,1,0:T(8,128)(2,1)S(1)} async-done(((bf16[64,8,128]{2,1,0:T(8,128)(2,1)}), bf16[64,8,128]{2,1,0:T(8,128)(2,1)S(1)}, u32[]{:S(2)}, u32[]{:S(2)}) %all-to-all-start.3) | async-done | bytes 131104 | tf_op jit(solution)/shard_map/all_to_all | solution.py:339
  97.8 4.6 %all-to-all-start.4 = ((bf16[8,16,128]{2,1,0:T(8,128)(2,1)}), bf16[8,16,128]{2,1,0:T(8,128)(2,1)S(1)}, u32[]{:S(2)}, u32[]{:S(2)}) async-start(bf16[8,16,128]{2,1,0:T(8,128)(2,1)} %get-tuple-element.45), calls=%async_computation.4 | async-start | bytes 65536 | tf_op jit(solution)/shard_map/all_to_all | solution.py:339
  102.3 1.9 %partners.3 = (bf16[64,4,640]{2,1,0:T(4,128)(2,1)}, f32[8,128]{1,0:T(8,128)}) custom-call(bf16[64,512]{1,0:T(8,128)(2,1)S(1)} %get-tuple-element.46.skeletons, f32[64,128]{1,0:T(8,128)S(1)} %get-tuple-element.32.told), custom_call_target="tpu_custom_call" | custom-call | flops 10000000 | tf_op jit(solution)/shard_map/partners/pallas_call | solution.py:36
  104.2 3.3 %collective-permute-start.6 = (bf16[512,256]{1,0:T(8,128)(2,1)S(1)}, bf16[512,256]{1,0:T(8,128)(2,1)}, u32[]{:S(2)}, u32[]{:S(2)}) collective-permute-start(bf16[512,256]{1,0:T(8,128)(2,1)S(1)} %collective-permute-done.4.v1), channel_id=1, source_target_pairs={{0,1},{1,2},{2,3},{3,4},{4,5},{5,6},{6,7},{7,8},{8,9},{9,10},{10,1... | collective-permute-start | bytes 786440 | tf_op jit(solution)/shard_map/ppermute | solution.py:330
  108.9 1.3 couple.3._
  110.2 9.8 %all-to-all-start.5 = ((bf16[64,4,640]{2,1,0:T(4,128)(2,1)}), bf16[64,4,640]{2,1,0:T(4,128)(2,1)S(1)}, u32[]{:S(2)}, u32[]{:S(2)}) async-start(bf16[64,4,640]{2,1,0:T(4,128)(2,1)} %couple.3._), calls=%async_computation.5 | async-start | bytes 655360 | tf_op jit(solution)/shard_map/all_to_all | solution.py:339
  120.0 2.8 %near_1.3.refs_3_ = f32[512,256]{1,0:T(8,128)S(1)} custom-call(s32[1,4]{1,0:T(1,128)S(1)} %copy-done.16, bf16[768,256]{1,0:T(8,128)(2,1)} %get-tuple-element.37._.places_in.own.refs_2_, bf16[512,256]{1,0:T(8,128)(2,1)S(1)} %get-tuple-element.49._.own, bf16[768,256]{1,0:T(8,128)(2,1)S(1)} %copy-done.8, bf16[512,256]{1,0:T(8,128)(2,1)S(1)} %collective-permute-done.4.v1, ...), custom_call_target="tpu_custom_call" | custom-call | flops 10000000000 | tf_op jit(solution)/shard_map/near_1/pallas_call | solution.py:36
  122.9 3.2 %near_2.3 = (f32[512,256]{1,0:T(8,128)S(1)}, f32[512,256]{1,0:T(8,128)S(1)}, f32[8,128]{1,0:T(8,128)S(1)}) custom-call(f32[1]{0:T(128)} %bitcast.4.refs_0_, s32[1,4]{1,0:T(1,128)S(1)} %copy-done.16, bf16[768,256]{1,0:T(8,128)(2,1)} %get-tuple-element.37._.places_in.own.refs_2_, f32[512,256]{1,0:T(8,128)S(1)} %near_1.3.refs_3_, ...), custom_call_target="tpu_custom_call" | custom-call | flops 1000000000 | tf_op jit(solution)/shard_map/near_2/pallas_call | solution.py:36
  126.1 9.6 %all-to-all-done.5.arrived = bf16[64,4,640]{2,1,0:T(4,128)(2,1)S(1)} async-done(((bf16[64,4,640]{2,1,0:T(4,128)(2,1)}), bf16[64,4,640]{2,1,0:T(4,128)(2,1)S(1)}, u32[]{:S(2)}, u32[]{:S(2)}) %all-to-all-start.5) | async-done | bytes 327712 | tf_op jit(solution)/shard_map/all_to_all | solution.py:339
  135.7 1.8 %end.1 = (f32[512,256]{1,0:T(8,128)}, f32[512,256]{1,0:T(8,128)}) custom-call(bf16[64,4,640]{2,1,0:T(4,128)(2,1)S(1)} %all-to-all-done.5.arrived, bf16[1,4,128,128]{3,2,1,0:T(8,128)(2,1)S(1)} %copy-done.3, bf16[1,128,128]{2,1,0:T(8,128)(2,1)S(1)} %copy-done.5, bf16[512,128]{1,0:T(8,128)(2,1)S(1)} %get-tuple-element.35.basis, ...), custom_call_target="tpu_custom_call" | custom-call | flops 10000000 | tf_op jit(solution)/shard_map/end/pallas_call | solution.py:36
  (53 shorter events, 10.8 us)
Async XLA Ops:
  4.5 16.8 %copy-start.4 = (bf16[768,256]{1,0:T(8,128)(2,1)S(1)}, bf16[768,256]{1,0:T(8,128)(2,1)}, u32[]{:S(2)}) copy-start(bf16[768,256]{1,0:T(8,128)(2,1)} %get-tuple-element.37._.places_in.own.refs_2_) | copy-start | bytes 1179652
  4.6 16.8 %copy-start.6 = (s32[4,4]{1,0:T(4,128)S(1)}, s32[4,4]{1,0:T(4,128)}, u32[]{:S(2)}) copy-start(s32[4,4]{1,0:T(4,128)} %far_clusters.1) | copy-start | bytes 196
  4.6 31.7 %all-to-all-start = ((bf16[64,16,128]{2,1,0:T(8,128)(2,1)}), bf16[64,16,128]{2,1,0:T(8,128)(2,1)S(1)}, u32[]{:S(2)}, u32[]{:S(2)}) async-start(bf16[64,16,128]{2,1,0:T(8,128)(2,1)} %get-tuple-element.30), calls=%async_computation | async-start | bytes 524288 | tf_op jit(solution)/shard_map/all_to_all | solution.py:339
  21.3 26.6 %copy-start = (bf16[4,4,128,128]{3,2,1,0:T(8,128)(2,1)S(1)}, bf16[4,4,128,128]{3,2,1,0:T(8,128)(2,1)}, u32[]{:S(2)}) copy-start(bf16[4,4,128,128]{3,2,1,0:T(8,128)(2,1)} %blocks.3) | copy-start | bytes 1572868
  22.0 20.0 %collective-permute-start = (bf16[768,256]{1,0:T(8,128)(2,1)S(1)}, bf16[768,256]{1,0:T(8,128)(2,1)S(1)}, u32[]{:S(2)}, u32[]{:S(2)}) collective-permute-start(bf16[768,256]{1,0:T(8,128)(2,1)S(1)} %copy-done.4), channel_id=1, source_target_pairs={{0,1},{1,2},{2,3},{3,4},{4,5},{5,6},{6,7},{7,8},{8,9},{9,10},{10,1... | collective-permute-start | bytes 1179656 | tf_op jit(solution)/shard_map/ppermute | solution.py:330
  25.5 16.5 %collective-permute-start.1 = (bf16[768,256]{1,0:T(8,128)(2,1)S(1)}, bf16[768,256]{1,0:T(8,128)(2,1)S(1)}, u32[]{:S(2)}, u32[]{:S(2)}) collective-permute-start(bf16[768,256]{1,0:T(8,128)(2,1)S(1)} %copy-done.4), channel_id=1, source_target_pairs={{1,0},{2,1},{3,2},{4,3},{5,4},{6,5},{7,6},{8,7},{9,8},{10,9},{11,1... | collective-permute-start | bytes 1179656 | tf_op jit(solution)/shard_map/ppermute | solution.py:330
  37.2 10.7 %all-to-all-start.1 = ((bf16[8,16,128]{2,1,0:T(8,128)(2,1)}), bf16[8,16,128]{2,1,0:T(8,128)(2,1)S(1)}, u32[]{:S(2)}, u32[]{:S(2)}) async-start(bf16[8,16,128]{2,1,0:T(8,128)(2,1)} %get-tuple-element.31), calls=%async_computation.1 | async-start | bytes 65536 | tf_op jit(solution)/shard_map/all_to_all | solution.py:339
  42.0 18.2 %copy-start.7 = (bf16[768,256]{1,0:T(8,128)(2,1)}, bf16[768,256]{1,0:T(8,128)(2,1)S(1)}, u32[]{:S(2)}) copy-start(bf16[768,256]{1,0:T(8,128)(2,1)S(1)} %collective-permute-done.p1.v1) | copy-start | bytes 1179652
  42.1 18.2 %copy-start.9 = (bf16[768,256]{1,0:T(8,128)(2,1)}, bf16[768,256]{1,0:T(8,128)(2,1)S(1)}, u32[]{:S(2)}) copy-start(bf16[768,256]{1,0:T(8,128)(2,1)S(1)} %collective-permute-done.1.p2.v2) | copy-start | bytes 1179652
  42.1 21.4 %collective-permute-start.2 = (bf16[768,256]{1,0:T(8,128)(2,1)S(1)}, bf16[768,256]{1,0:T(8,128)(2,1)S(1)}, u32[]{:S(2)}, u32[]{:S(2)}) collective-permute-start(bf16[768,256]{1,0:T(8,128)(2,1)S(1)} %collective-permute-done.p1.v1), channel_id=1, source_target_pairs={{0,1},{1,2},{2,3},{3,4},{4,5},{5,6},{6,7},{7,8},{8,9},{9,10},{10,1... | collective-permute-start | bytes 1179656 | tf_op jit(solution)/shard_map/ppermute | solution.py:330
  44.8 18.8 %collective-permute-start.3 = (bf16[768,256]{1,0:T(8,128)(2,1)S(1)}, bf16[768,256]{1,0:T(8,128)(2,1)S(1)}, u32[]{:S(2)}, u32[]{:S(2)}) collective-permute-start(bf16[768,256]{1,0:T(8,128)(2,1)S(1)} %collective-permute-done.1.p2.v2), channel_id=1, source_target_pairs={{1,0},{2,1},{3,2},{4,3},{5,4},{6,5},{7,6},{8,7},{9,8},{10,9},{11,1... | collective-permute-start | bytes 1179656 | tf_op jit(solution)/shard_map/ppermute | solution.py:330
  49.3 11.0 %copy-start.2 = (bf16[64,4,640]{2,1,0:T(4,128)(2,1)S(1)}, bf16[64,4,640]{2,1,0:T(4,128)(2,1)}, u32[]{:S(2)}) copy-start(bf16[64,4,640]{2,1,0:T(4,128)(2,1)} %couple.2._) | copy-start | bytes 983044
  49.3 11.0 %copy-start.16 = (s32[1,4]{1,0:T(1,128)S(1)}, s32[1,4]{1,0:T(1,128)}, u32[]{:S(2)}) copy-start(s32[1,4]{1,0:T(1,128)} %refs_1_.3) | copy-start | bytes 52
  49.3 25.8 %all-to-all-start.2 = ((bf16[64,4,640]{2,1,0:T(4,128)(2,1)}), bf16[64,4,640]{2,1,0:T(4,128)(2,1)S(1)}, u32[]{:S(2)}, u32[]{:S(2)}) async-start(bf16[64,4,640]{2,1,0:T(4,128)(2,1)} %couple.2._), calls=%async_computation.2 | async-start | bytes 655360 | tf_op jit(solution)/shard_map/all_to_all | solution.py:339
  77.1 19.8 %all-to-all-start.3 = ((bf16[64,8,128]{2,1,0:T(8,128)(2,1)}), bf16[64,8,128]{2,1,0:T(8,128)(2,1)S(1)}, u32[]{:S(2)}, u32[]{:S(2)}) async-start(bf16[64,8,128]{2,1,0:T(8,128)(2,1)} %get-tuple-element.43), calls=%async_computation.3 | async-start | bytes 262144 | tf_op jit(solution)/shard_map/all_to_all | solution.py:339
  84.3 19.9 %collective-permute-start.4 = (bf16[512,256]{1,0:T(8,128)(2,1)S(1)}, bf16[512,256]{1,0:T(8,128)(2,1)S(1)}, u32[]{:S(2)}, u32[]{:S(2)}) collective-permute-start(bf16[512,256]{1,0:T(8,128)(2,1)S(1)} %get-tuple-element.49._.own), channel_id=1, source_target_pairs={{0,1},{1,2},{2,3},{3,4},{4,5},{5,6},{6,7},{7,8},{8,9},{9,10},{10,1... | collective-permute-start | bytes 786440 | tf_op jit(solution)/shard_map/ppermute | solution.py:330
  87.8 16.5 %collective-permute-start.5 = (bf16[512,256]{1,0:T(8,128)(2,1)S(1)}, bf16[512,256]{1,0:T(8,128)(2,1)S(1)}, u32[]{:S(2)}, u32[]{:S(2)}) collective-permute-start(bf16[512,256]{1,0:T(8,128)(2,1)S(1)} %get-tuple-element.49._.own), channel_id=1, source_target_pairs={{1,0},{2,1},{3,2},{4,3},{5,4},{6,5},{7,6},{8,7},{9,8},{10,9},{11,1... | collective-permute-start | bytes 786440 | tf_op jit(solution)/shard_map/ppermute | solution.py:330
  97.8 11.1 %all-to-all-start.4 = ((bf16[8,16,128]{2,1,0:T(8,128)(2,1)}), bf16[8,16,128]{2,1,0:T(8,128)(2,1)S(1)}, u32[]{:S(2)}, u32[]{:S(2)}) async-start(bf16[8,16,128]{2,1,0:T(8,128)(2,1)} %get-tuple-element.45), calls=%async_computation.4 | async-start | bytes 65536 | tf_op jit(solution)/shard_map/all_to_all | solution.py:339
  104.2 18.6 %collective-permute-start.6 = (bf16[512,256]{1,0:T(8,128)(2,1)S(1)}, bf16[512,256]{1,0:T(8,128)(2,1)}, u32[]{:S(2)}, u32[]{:S(2)}) collective-permute-start(bf16[512,256]{1,0:T(8,128)(2,1)S(1)} %collective-permute-done.4.v1), channel_id=1, source_target_pairs={{0,1},{1,2},{2,3},{3,4},{4,5},{5,6},{6,7},{7,8},{8,9},{9,10},{10,1... | collective-permute-start | bytes 786440 | tf_op jit(solution)/shard_map/ppermute | solution.py:330
  107.5 15.3 %collective-permute-start.7 = (bf16[512,256]{1,0:T(8,128)(2,1)S(1)}, bf16[512,256]{1,0:T(8,128)(2,1)}, u32[]{:S(2)}, u32[]{:S(2)}) collective-permute-start(bf16[512,256]{1,0:T(8,128)(2,1)S(1)} %collective-permute-done.5.v2), channel_id=1, source_target_pairs={{1,0},{2,1},{3,2},{4,3},{5,4},{6,5},{7,6},{8,7},{9,8},{10,9},{11,1... | collective-permute-start | bytes 786440 | tf_op jit(solution)/shard_map/ppermute | solution.py:330
  108.8 11.2 %copy-start.8 = (bf16[768,256]{1,0:T(8,128)(2,1)S(1)}, bf16[768,256]{1,0:T(8,128)(2,1)}, u32[]{:S(2)}) copy-start(bf16[768,256]{1,0:T(8,128)(2,1)} %copy-done.7) | copy-start | bytes 1179652
  108.8 11.2 %copy-start.10 = (bf16[768,256]{1,0:T(8,128)(2,1)S(1)}, bf16[768,256]{1,0:T(8,128)(2,1)}, u32[]{:S(2)}) copy-start(bf16[768,256]{1,0:T(8,128)(2,1)} %copy-done.9) | copy-start | bytes 1179652
  110.2 9.8 %copy-start.1 = (bf16[64,4,640]{2,1,0:T(4,128)(2,1)S(1)}, bf16[64,4,640]{2,1,0:T(4,128)(2,1)}, u32[]{:S(2)}) copy-start(bf16[64,4,640]{2,1,0:T(4,128)(2,1)} %couple.3._) | copy-start | bytes 983044
  110.2 25.5 %all-to-all-start.5 = ((bf16[64,4,640]{2,1,0:T(4,128)(2,1)}), bf16[64,4,640]{2,1,0:T(4,128)(2,1)S(1)}, u32[]{:S(2)}, u32[]{:S(2)}) async-start(bf16[64,4,640]{2,1,0:T(4,128)(2,1)} %couple.3._), calls=%async_computation.5 | async-start | bytes 655360 | tf_op jit(solution)/shard_map/all_to_all | solution.py:339
  (7 other events, 31.8 us)

commit v8 on v7

--- a/solution.py
+++ b/solution.py
@@ -28,7 +28,7 @@
     return lax.dot_general(a, b, (dims, ((), ())), preferred_element_type=F32)
 
 
-def call(kernel, name, outs, ins, args, scratch=(), flops=0, aliases=None):
+def call(kernel, name, outs, ins, args, scratch=(), flops=0):
     shapes = [(pltpu.HBM if spec is HBM else jax.ShapeDtypeStruct)(shape, kind) for shape, kind, spec in outs]
     args = [
         pltpu.with_memory_space_constraint(arg, pltpu.HBM) if spec is HBM else arg for arg, spec in zip(args, ins)
@@ -40,7 +40,6 @@
         in_specs=ins,
         out_specs=[spec for _, _, spec in outs],
         scratch_shapes=list(scratch),
-        input_output_aliases=aliases or {},
         compiler_params=pltpu.CompilerParams(vmem_limit_bytes=LIMIT),
         cost_estimate=pl.CostEstimate(flops=flops, bytes_accessed=0, transcendentals=0),
     )(*args)
@@ -151,7 +150,7 @@
     ).astype(BF16)
 
 
-def partners_kernel(skeletons, told, sent_out, done, staged, sent, sems):
+def partners_kernel(skeletons, told, sent, staged):
     lane = lax.broadcasted_iota(jnp.int32, (N_DEV, N_DEV), 1).astype(F32)
     pick = jnp.concatenate(
         [jnp.where(lane == told[:, k : k + 1], 1.0, 0.0) for k in range(FAR1)], axis=0
@@ -163,11 +162,10 @@
                 N_DEV * k : N_DEV * (k + 1), RANK * i : RANK * (i + 1)
             ]
     sent[...] = staged[...].astype(BF16)
-    done[...] = jnp.zeros_like(done)
-    wait(started(((sent, sent_out.at[:, :, pl.ds(0, FAR1 * RANK)]),), sems))
-
-
-def couple_kernel(picks, all_sums, blocks, told, _, sent_out, staged, sent, sems):
+
+
+def couple_kernel(picks, all_sums, blocks, told, partners, sent_out, staged, sent, sems):
+    copies = started(((partners, sent_out.at[:, :, pl.ds(0, FAR1 * RANK)]),), sems)
     rows = COLS * CPG
     picked = dot(picks[...], all_sums[...].reshape(N_GRP * rows, RANK)).astype(BF16)
     total = jnp.zeros((CPG * RANK, rows), F32)
@@ -187,7 +185,7 @@
     for i in range(COLS):
         staged[:, i, :] = out[N_DEV * i : N_DEV * (i + 1)]
     sent[...] = staged[...].astype(BF16)
-    wait(started(((sent, sent_out.at[:, :, pl.ds(FAR1 * RANK, RANK)]),), sems))
+    wait(copies + started(((sent, sent_out.at[:, :, pl.ds(FAR1 * RANK, RANK)]),), sems, 1))
 
 
 def local_field(arrived, couplings, transfer, staged):
@@ -263,8 +261,9 @@
         total[part] = product if fresh else total[part] + product
 
 
-def near_products(offsets, near_list, mine, places, values, total):
-    for i, offset in enumerate(offsets):
+def near_products(distance, near_list, mine, places, values, total):
+    ahead = distance * (1 - 2 * (lax.axis_index("dev") % 2))
+    for i, offset in enumerate((ahead, -ahead)):
 
         @pl.when(listed(near_list, offset))
         def _():
@@ -281,7 +280,7 @@
     wait(started([*pairs, (own.at[pl.ds(0, LEAF)], values.at[2])], sems))
     mine = coordinates(places[0])
     block_times(mine, mine, values[2], total, True)
-    near_products((-1, 1), near_list, mine, places, values, total)
+    near_products(1, near_list, mine, places, values, total)
 
 
 def near_2_kernel(
@@ -293,7 +292,7 @@
     if last:
         copies += started(((r1, residual),), sems, 7)
     wait(copies)
-    near_products((-2, 2), near_list, coordinates(places[0]), places, values, total)
+    near_products(2, near_list, coordinates(places[0]), places, values, total)
     ridge, centre, first, second = chebyshev(ridge[0])
     d1 = rs[...] / centre
     if last:
@@ -325,14 +324,11 @@
         picks[rows * k : rows * (k + 1)] = jnp.where(lane == target, 1.0, 0.0).astype(BF16)
 
 
-def from_behind(shard, by):
-    pairs = [(i, i + by) for i in range(N_DEV) if 0 <= i + by < N_DEV]
-    return lax.ppermute(shard, "dev", pairs)
-
-
-def passed_on(pair, after):
-    behind, ahead, _ = lax.optimization_barrier((*pair, after))
-    return from_behind(behind, 1), from_behind(ahead, -1)
+def swapped(pair, after):
+    one, two, _ = lax.optimization_barrier((*pair, after))
+    inner = [(i, i ^ 1) for i in range(N_DEV)]
+    outer = [(i, ((i + 1) ^ 1) - 1) for i in range(1, N_DEV - 1)]
+    return lax.ppermute(one, "dev", inner), lax.ppermute(two, "dev", outer)
 
 
 def exchanged(blocks, axis):
@@ -421,26 +417,25 @@
 
     def through_owners(sums, skeletons):
         all_sums = exchanged(sums, "grp")
-        partners, done = call(
+        (partners,) = call(
             partners_kernel,
             "partners",
-            [(payload, BF16, HBM), ((8, RANK), F32, VMEM)],
+            [(partner, BF16, VMEM)],
             [VMEM] * 2,
             (skeletons, told),
-            [pltpu.VMEM(partner, F32), pltpu.VMEM(partner, BF16), dma((1,))],
+            [pltpu.VMEM(partner, F32)],
             SHORT,
         )
         (sent,) = call(
             couple_kernel,
             "couple",
             [(payload, BF16, HBM)],
-            [VMEM] * 4 + [HBM],
+            [VMEM] * 5,
             (picks, all_sums, cluster_couplings, told, partners),
-            [pltpu.VMEM((N_DEV, COLS, RANK), F32), pltpu.VMEM((N_DEV, COLS, RANK), BF16), dma((1,))],
+            [pltpu.VMEM((N_DEV, COLS, RANK), F32), pltpu.VMEM((N_DEV, COLS, RANK), BF16), dma((2,))],
             SHORT,
-            {4: 0},
         )
-        return sent, exchanged(sent, "dev"), done
+        return sent, exchanged(sent, "dev")
 
     arrived = exchanged(sent, "dev")
     (picks,) = call(
@@ -451,7 +446,7 @@
         (far_clusters, wc),
         flops=SHORT,
     )
-    first1 = passed_on((wc, wc), picks)
+    first1 = swapped((wc, wc), picks)
     sums, told, skeletons = call(
         sums_first_kernel,
         "sums_first",
@@ -461,8 +456,8 @@
         [rows16, narrow],
         SHORT,
     )
-    sent, arrived, done = through_owners(sums, skeletons)
-    first2 = passed_on(first1, done)
+    sent, arrived = through_owners(sums, skeletons)
+    first2 = swapped(first1[::-1], sums)
     near = near_1(wc, first1, first1, sent)
     residual, direction, factor = near_2(False, near, first2, first2, near)
     w, sent, r1 = call(
@@ -476,7 +471,7 @@
     )
     arrived = exchanged(sent, "dev")
     mark = marked(w)
-    fields1 = passed_on((w, w), mark)
+    fields1 = swapped((w, w), mark)
     sums, skeletons = call(
         sums_kernel,
         "sums",
@@ -486,8 +481,8 @@
         [rows8, narrow],
         SHORT,
     )
-    sent, arrived, done = through_owners(sums, skeletons)
-    fields2 = passed_on(fields1, done)
+    sent, arrived = through_owners(sums, skeletons)
+    fields2 = swapped(fields1[::-1], sums)
     near = near_1(w, first1, fields1, sent)
     residual, total, factor = near_2(True, near, first2, fields2, r1)
     return tuple(

time: 139 us -> 132 us (0.950)
  starting transfers between devices: 72.1 us -> 67.4 us
  Pallas kernels: 27.5 us -> 23.8 us
  waiting for transfers between devices: 33.8 us -> 36 us
    pallas_call x15, Pallas kernels: 27.5 us -> 23.8 us  [call(): pl.pallas_call(kernel, name=name, out_shape=shapes, in_specs=ins, out_spe...]
    ppermute x8, starting transfers between devices: 18.1 us -> 15.7 us  [swapped(): return (lax.ppermute(one, 'dev', inner), lax.ppermute(two, 'dev', outer))]
    all_to_all x6, waiting for transfers between devices: 33.7 us -> 36 us  [exchanged(): return lax.all_to_all(blocks, axis, split_axis=0, concat_axis=0, tiled=True)]
    all_to_all x6, starting transfers between devices: 54 us -> 51.7 us  [exchanged(): return lax.all_to_all(blocks, axis, split_axis=0, concat_axis=0, tiled=True)]
  transfers between devices with their start and end apart: 14 -> 14, of which waited for: 4 -> 4; matrix products, arithmetic and copies ran while one was open for 0% -> 0% of each run, Pallas kernels for 15% -> 13%
where the time goes in v8:
time: 132 us
  starting transfers between devices  67.4 us (51%)
  waiting for transfers between devices  36 us (27%)
  Pallas kernels  23.8 us (18%)
  between operations  2.51 us (2%)
  local copies, waits for them, and re-layouts  1.84 us (1%)
    all_to_all x6, starting transfers between devices, exchanged(): return lax.all_to_all(blocks, axis, split_axis=0, concat_axis=0, tiled=True)  51.7 us
    all_to_all x6, waiting for transfers between devices, exchanged(): return lax.all_to_all(blocks, axis, split_axis=0, concat_axis=0, tiled=True)  36 us
    pallas_call x15, Pallas kernels, call(): pl.pallas_call(kernel, name=name, out_shape=shapes, in_specs=ins, out_spe...  23.8 us
    ppermute x8, starting transfers between devices, swapped(): return (lax.ppermute(one, 'dev', inner), lax.ppermute(two, 'dev', outer))  15.7 us
  transfers between devices with their start and end apart: 14, of which 4 were waited for; matrix products, arithmetic and copies ran while one was open for 0% of the time, Pallas kernels for 13%

profile of v8, /device:TPU:2, one launch (start us, length us, event | category | flops | bytes accessed | tf_op | source)
XLA Modules:
  0.0 131.5 jit_solution(16241259678265419807)
XLA Ops:
  1.9 2.6 %start.1 = (bf16[768,256]{1,0:T(8,128)(2,1)}, bf16[64,16,128]{2,1,0:T(8,128)(2,1)}, bf16[512,128]{1,0:T(8,128)(2,1)S(1)}) custom-call(f32[1]{0:T(128)} %bitcast.2.ridge, s32[1]{0:T(128)S(6)} %copy.14.cluster, s32[1,4]{1,0:T(1,128)} %far_in.1, f32[512,256]{1,0:T(8,128)} %refs_8_.3, f32[64,512]{1,0:T(8,128)} %bitcast.5, s32[1,512]{1,0:T(1,128)} %perm_in.1, ...), custom_call_target="tpu_custom_call" | custom-call | flops 10000000 | tf_op jit(solution)/shard_map/start/pallas_call | solution.py:36
  4.6 16.7 %all-to-all-start = ((bf16[64,16,128]{2,1,0:T(8,128)(2,1)}), bf16[64,16,128]{2,1,0:T(8,128)(2,1)S(1)}, u32[]{:S(2)}, u32[]{:S(2)}) async-start(bf16[64,16,128]{2,1,0:T(8,128)(2,1)} %get-tuple-element.28), calls=%async_computation | async-start | bytes 524288 | tf_op jit(solution)/shard_map/all_to_all | solution.py:335
  22.0 3.5 %collective-permute-start = (bf16[768,256]{1,0:T(8,128)(2,1)S(1)}, bf16[768,256]{1,0:T(8,128)(2,1)S(1)}, u32[]{:S(2)}, u32[]{:S(2)}) collective-permute-start(bf16[768,256]{1,0:T(8,128)(2,1)S(1)} %copy-done.4), channel_id=1, source_target_pairs={{0,1},{1,0},{2,3},{3,2},{4,5},{5,4},{6,7},{7,6},{8,9},{9,8},{10,11... | collective-permute-start | bytes 1179656 | tf_op jit(solution)/shard_map/ppermute | solution.py:331
  26.2 10.1 %all-to-all-done.arrived = bf16[64,16,128]{2,1,0:T(8,128)(2,1)S(1)} async-done(((bf16[64,16,128]{2,1,0:T(8,128)(2,1)}), bf16[64,16,128]{2,1,0:T(8,128)(2,1)S(1)}, u32[]{:S(2)}, u32[]{:S(2)}) %all-to-all-start) | async-done | bytes 262176 | tf_op jit(solution)/shard_map/all_to_all | solution.py:335
  37.2 4.8 %all-to-all-start.1 = ((bf16[8,16,128]{2,1,0:T(8,128)(2,1)}), bf16[8,16,128]{2,1,0:T(8,128)(2,1)S(1)}, u32[]{:S(2)}, u32[]{:S(2)}) async-start(bf16[8,16,128]{2,1,0:T(8,128)(2,1)} %get-tuple-element.29), calls=%async_computation.1 | async-start | bytes 65536 | tf_op jit(solution)/shard_map/all_to_all | solution.py:335
  42.1 2.7 %collective-permute-start.2 = (bf16[768,256]{1,0:T(8,128)(2,1)S(1)}, bf16[768,256]{1,0:T(8,128)(2,1)S(1)}, u32[]{:S(2)}, u32[]{:S(2)}) collective-permute-start(bf16[768,256]{1,0:T(8,128)(2,1)S(1)} %collective-permute-done.1.p2.v2), channel_id=1, source_target_pairs={{0,1},{1,0},{2,3},{3,2},{4,5},{5,4},{6,7},{7,6},{8,9},{9,8},{10,11... | collective-permute-start | bytes 1179656 | tf_op jit(solution)/shard_map/ppermute | solution.py:331
  46.0 1.4 %couple.2._ = bf16[64,4,640]{2,1,0:T(4,128)(2,1)} custom-call(bf16[64,128]{1,0:T(8,128)(2,1)S(1)} %prepare.1._.picks, bf16[8,16,128]{2,1,0:T(8,128)(2,1)S(1)} %all-to-all-done.1.all_sums, bf16[4,4,128,128]{3,2,1,0:T(8,128)(2,1)S(1)} %copy-done, f32[64,128]{1,0:T(8,128)S(1)} %get-tuple-element.30.told, bf16[64,4,512]{2,1,0:T(4,128)(2,1)S(1)} %partners.2), custom_call_target="tpu_custom_call" | custom-call | flops 10000000 | tf_op jit(solution)/shard_map/couple/pallas_call | solution.py:36
  47.4 10.9 %all-to-all-start.2 = ((bf16[64,4,640]{2,1,0:T(4,128)(2,1)}), bf16[64,4,640]{2,1,0:T(4,128)(2,1)S(1)}, u32[]{:S(2)}, u32[]{:S(2)}) async-start(bf16[64,4,640]{2,1,0:T(4,128)(2,1)} %couple.2._), calls=%async_computation.2 | async-start | bytes 655360 | tf_op jit(solution)/shard_map/all_to_all | solution.py:335
  58.4 2.7 %near_1.2.refs_3_.refs_9_ = f32[512,256]{1,0:T(8,128)S(1)} custom-call(s32[1,4]{1,0:T(1,128)S(1)} %copy-done.16, bf16[768,256]{1,0:T(8,128)(2,1)} %get-tuple-element.34._.places_in.own.refs_2_, bf16[768,256]{1,0:T(8,128)(2,1)} %get-tuple-element.34._.places_in.own.refs_2_, bf16[768,256]{1,0:T(8,128)(2,1)S(1)} %collective-permute-done.p1.v1, ...), custom_call_target="tpu_custom_call" | custom-call | flops 10000000000 | tf_op jit(solution)/shard_map/near_1/pallas_call | solution.py:36
  62.8 3.0 %near_2.2 = (f32[512,256]{1,0:T(8,128)S(1)}, f32[512,256]{1,0:T(8,128)S(1)}, f32[8,128]{1,0:T(8,128)S(1)}) custom-call(f32[1]{0:T(128)} %bitcast.3.refs_0_, s32[1,4]{1,0:T(1,128)S(1)} %copy-done.16, bf16[768,256]{1,0:T(8,128)(2,1)} %get-tuple-element.34._.places_in.own.refs_2_, f32[512,256]{1,0:T(8,128)S(1)} %near_1.2.refs_3_.refs_9_, ...), custom_call_target="tpu_custom_call" | custom-call | flops 1000000000 | tf_op jit(solution)/shard_map/near_2/pallas_call | solution.py:36
  65.8 7.2 %all-to-all-done.2.arrived = bf16[64,4,640]{2,1,0:T(4,128)(2,1)S(1)} async-done(((bf16[64,4,640]{2,1,0:T(4,128)(2,1)}), bf16[64,4,640]{2,1,0:T(4,128)(2,1)S(1)}, u32[]{:S(2)}, u32[]{:S(2)}) %all-to-all-start.2) | async-done | bytes 327712 | tf_op jit(solution)/shard_map/all_to_all | solution.py:335
  73.1 2.0 %middle.1 = (bf16[512,256]{1,0:T(8,128)(2,1)S(1)}, bf16[64,8,128]{2,1,0:T(8,128)(2,1)}, f32[512,256]{1,0:T(8,128)S(1)}) custom-call(bf16[64,4,640]{2,1,0:T(4,128)(2,1)S(1)} %all-to-all-done.2.arrived, bf16[1,4,128,128]{3,2,1,0:T(8,128)(2,1)S(1)} %copy-done.3, bf16[1,128,128]{2,1,0:T(8,128)(2,1)S(1)} %copy-done.5, ...), custom_call_target="tpu_custom_call" | custom-call | flops 10000000 | tf_op jit(solution)/shard_map/middle/pallas_call | solution.py:36
  75.1 6.4 %all-to-all-start.3 = ((bf16[64,8,128]{2,1,0:T(8,128)(2,1)}), bf16[64,8,128]{2,1,0:T(8,128)(2,1)S(1)}, u32[]{:S(2)}, u32[]{:S(2)}) async-start(bf16[64,8,128]{2,1,0:T(8,128)(2,1)} %get-tuple-element.40), calls=%async_computation.3 | async-start | bytes 262144 | tf_op jit(solution)/shard_map/all_to_all | solution.py:335
  81.4 3.5 %collective-permute-start.4 = (bf16[512,256]{1,0:T(8,128)(2,1)S(1)}, bf16[512,256]{1,0:T(8,128)(2,1)S(1)}, u32[]{:S(2)}, u32[]{:S(2)}) collective-permute-start(bf16[512,256]{1,0:T(8,128)(2,1)S(1)} %get-tuple-element.45._.own), channel_id=1, source_target_pairs={{0,1},{1,0},{2,3},{3,2},{4,5},{5,4},{6,7},{7,6},{8,9},{9,8},{10,11... | collective-permute-start | bytes 786440 | tf_op jit(solution)/shard_map/ppermute | solution.py:331
  85.6 8.5 %all-to-all-done.3.arrived = bf16[64,8,128]{2,1,0:T(8,128)(2,1)S(1)} async-done(((bf16[64,8,128]{2,1,0:T(8,128)(2,1)}), bf16[64,8,128]{2,1,0:T(8,128)(2,1)S(1)}, u32[]{:S(2)}, u32[]{:S(2)}) %all-to-all-start.3) | async-done | bytes 131104 | tf_op jit(solution)/shard_map/all_to_all | solution.py:335
  94.9 4.9 %all-to-all-start.4 = ((bf16[8,16,128]{2,1,0:T(8,128)(2,1)}), bf16[8,16,128]{2,1,0:T(8,128)(2,1)S(1)}, u32[]{:S(2)}, u32[]{:S(2)}) async-start(bf16[8,16,128]{2,1,0:T(8,128)(2,1)} %get-tuple-element.42), calls=%async_computation.4 | async-start | bytes 65536 | tf_op jit(solution)/shard_map/all_to_all | solution.py:335
  100.4 2.6 %collective-permute-start.6 = (bf16[512,256]{1,0:T(8,128)(2,1)S(1)}, bf16[512,256]{1,0:T(8,128)(2,1)}, u32[]{:S(2)}, u32[]{:S(2)}) collective-permute-start(bf16[512,256]{1,0:T(8,128)(2,1)S(1)} %collective-permute-done.5.v2), channel_id=1, source_target_pairs={{0,1},{1,0},{2,3},{3,2},{4,5},{5,4},{6,7},{7,6},{8,9},{9,8},{10,11... | collective-permute-start | bytes 786440 | tf_op jit(solution)/shard_map/ppermute | solution.py:331
  103.0 1.4 %collective-permute-start.7 = (bf16[512,256]{1,0:T(8,128)(2,1)S(1)}, bf16[512,256]{1,0:T(8,128)(2,1)}, u32[]{:S(2)}, u32[]{:S(2)}) collective-permute-start(bf16[512,256]{1,0:T(8,128)(2,1)S(1)} %collective-permute-done.4.v1), channel_id=1, source_target_pairs={{1,2},{2,1},{3,4},{4,3},{5,6},{6,5},{7,8},{8,7},{9,10},{10,9},{11,... | collective-permute-start | bytes 786440 | tf_op jit(solution)/shard_map/ppermute | solution.py:331
  104.4 1.4 %couple.3._ = bf16[64,4,640]{2,1,0:T(4,128)(2,1)} custom-call(bf16[64,128]{1,0:T(8,128)(2,1)S(1)} %prepare.1._.picks, bf16[8,16,128]{2,1,0:T(8,128)(2,1)S(1)} %all-to-all-done.4.all_sums, bf16[4,4,128,128]{3,2,1,0:T(8,128)(2,1)S(1)} %copy-done, f32[64,128]{1,0:T(8,128)S(1)} %get-tuple-element.30.told, bf16[64,4,512]{2,1,0:T(4,128)(2,1)S(1)} %partners.3), custom_call_target="tpu_custom_call" | custom-call | flops 10000000 | tf_op jit(solution)/shard_map/couple/pallas_call | solution.py:36
  105.8 8.0 %all-to-all-start.5 = ((bf16[64,4,640]{2,1,0:T(4,128)(2,1)}), bf16[64,4,640]{2,1,0:T(4,128)(2,1)S(1)}, u32[]{:S(2)}, u32[]{:S(2)}) async-start(bf16[64,4,640]{2,1,0:T(4,128)(2,1)} %couple.3._), calls=%async_computation.5 | async-start | bytes 655360 | tf_op jit(solution)/shard_map/all_to_all | solution.py:335
  113.9 2.2 %near_1.3.refs_3_ = f32[512,256]{1,0:T(8,128)S(1)} custom-call(s32[1,4]{1,0:T(1,128)S(1)} %copy-done.16, bf16[768,256]{1,0:T(8,128)(2,1)} %get-tuple-element.34._.places_in.own.refs_2_, bf16[512,256]{1,0:T(8,128)(2,1)S(1)} %get-tuple-element.45._.own, bf16[768,256]{1,0:T(8,128)(2,1)S(1)} %copy-done.8, bf16[512,256]{1,0:T(8,128)(2,1)S(1)} %collective-permute-done.4.v1, ...), custom_call_target="tpu_custom_call" | custom-call | flops 10000000000 | tf_op jit(solution)/shard_map/near_1/pallas_call | solution.py:36
  116.2 3.2 %near_2.3 = (f32[512,256]{1,0:T(8,128)S(1)}, f32[512,256]{1,0:T(8,128)S(1)}, f32[8,128]{1,0:T(8,128)S(1)}) custom-call(f32[1]{0:T(128)} %bitcast.4.refs_0_, s32[1,4]{1,0:T(1,128)S(1)} %copy-done.16, bf16[768,256]{1,0:T(8,128)(2,1)} %get-tuple-element.34._.places_in.own.refs_2_, f32[512,256]{1,0:T(8,128)S(1)} %near_1.3.refs_3_, ...), custom_call_target="tpu_custom_call" | custom-call | flops 1000000000 | tf_op jit(solution)/shard_map/near_2/pallas_call | solution.py:36
  119.3 10.2 %all-to-all-done.5.arrived = bf16[64,4,640]{2,1,0:T(4,128)(2,1)S(1)} async-done(((bf16[64,4,640]{2,1,0:T(4,128)(2,1)}), bf16[64,4,640]{2,1,0:T(4,128)(2,1)S(1)}, u32[]{:S(2)}, u32[]{:S(2)}) %all-to-all-start.5) | async-done | bytes 327712 | tf_op jit(solution)/shard_map/all_to_all | solution.py:335
  129.5 1.8 %end.1 = (f32[512,256]{1,0:T(8,128)}, f32[512,256]{1,0:T(8,128)}) custom-call(bf16[64,4,640]{2,1,0:T(4,128)(2,1)S(1)} %all-to-all-done.5.arrived, bf16[1,4,128,128]{3,2,1,0:T(8,128)(2,1)S(1)} %copy-done.3, bf16[1,128,128]{2,1,0:T(8,128)(2,1)S(1)} %copy-done.5, bf16[512,128]{1,0:T(8,128)(2,1)S(1)} %get-tuple-element.32.basis, ...), custom_call_target="tpu_custom_call" | custom-call | flops 10000000 | tf_op jit(solution)/shard_map/end/pallas_call | solution.py:36
  (53 shorter events, 7.5 us)
Async XLA Ops:
  4.5 16.8 %copy-start.4 = (bf16[768,256]{1,0:T(8,128)(2,1)S(1)}, bf16[768,256]{1,0:T(8,128)(2,1)}, u32[]{:S(2)}) copy-start(bf16[768,256]{1,0:T(8,128)(2,1)} %get-tuple-element.34._.places_in.own.refs_2_) | copy-start | bytes 1179652
  4.6 16.8 %copy-start.6 = (s32[4,4]{1,0:T(4,128)S(1)}, s32[4,4]{1,0:T(4,128)}, u32[]{:S(2)}) copy-start(s32[4,4]{1,0:T(4,128)} %far_clusters.1) | copy-start | bytes 196
  4.6 31.7 %all-to-all-start = ((bf16[64,16,128]{2,1,0:T(8,128)(2,1)}), bf16[64,16,128]{2,1,0:T(8,128)(2,1)S(1)}, u32[]{:S(2)}, u32[]{:S(2)}) async-start(bf16[64,16,128]{2,1,0:T(8,128)(2,1)} %get-tuple-element.28), calls=%async_computation | async-start | bytes 524288 | tf_op jit(solution)/shard_map/all_to_all | solution.py:335
  21.3 24.7 %copy-start = (bf16[4,4,128,128]{3,2,1,0:T(8,128)(2,1)S(1)}, bf16[4,4,128,128]{3,2,1,0:T(8,128)(2,1)}, u32[]{:S(2)}) copy-start(bf16[4,4,128,128]{3,2,1,0:T(8,128)(2,1)} %blocks.3) | copy-start | bytes 1572868
  22.0 20.0 %collective-permute-start = (bf16[768,256]{1,0:T(8,128)(2,1)S(1)}, bf16[768,256]{1,0:T(8,128)(2,1)S(1)}, u32[]{:S(2)}, u32[]{:S(2)}) collective-permute-start(bf16[768,256]{1,0:T(8,128)(2,1)S(1)} %copy-done.4), channel_id=1, source_target_pairs={{0,1},{1,0},{2,3},{3,2},{4,5},{5,4},{6,7},{7,6},{8,9},{9,8},{10,11... | collective-permute-start | bytes 1179656 | tf_op jit(solution)/shard_map/ppermute | solution.py:331
  25.5 16.5 %collective-permute-start.1 = (bf16[768,256]{1,0:T(8,128)(2,1)S(1)}, bf16[768,256]{1,0:T(8,128)(2,1)S(1)}, u32[]{:S(2)}, u32[]{:S(2)}) collective-permute-start(bf16[768,256]{1,0:T(8,128)(2,1)S(1)} %copy-done.4), channel_id=1, source_target_pairs={{1,2},{2,1},{3,4},{4,3},{5,6},{6,5},{7,8},{8,7},{9,10},{10,9},{11,... | collective-permute-start | bytes 1179656 | tf_op jit(solution)/shard_map/ppermute | solution.py:331
  37.2 8.8 %all-to-all-start.1 = ((bf16[8,16,128]{2,1,0:T(8,128)(2,1)}), bf16[8,16,128]{2,1,0:T(8,128)(2,1)S(1)}, u32[]{:S(2)}, u32[]{:S(2)}) async-start(bf16[8,16,128]{2,1,0:T(8,128)(2,1)} %get-tuple-element.29), calls=%async_computation.1 | async-start | bytes 65536 | tf_op jit(solution)/shard_map/all_to_all | solution.py:335
  42.0 16.3 %copy-start.7 = (bf16[768,256]{1,0:T(8,128)(2,1)}, bf16[768,256]{1,0:T(8,128)(2,1)S(1)}, u32[]{:S(2)}) copy-start(bf16[768,256]{1,0:T(8,128)(2,1)S(1)} %collective-permute-done.p1.v1) | copy-start | bytes 1179652
  42.0 16.3 %copy-start.9 = (bf16[768,256]{1,0:T(8,128)(2,1)}, bf16[768,256]{1,0:T(8,128)(2,1)S(1)}, u32[]{:S(2)}) copy-start(bf16[768,256]{1,0:T(8,128)(2,1)S(1)} %collective-permute-done.1.p2.v2) | copy-start | bytes 1179652
  42.1 19.0 %collective-permute-start.2 = (bf16[768,256]{1,0:T(8,128)(2,1)S(1)}, bf16[768,256]{1,0:T(8,128)(2,1)S(1)}, u32[]{:S(2)}, u32[]{:S(2)}) collective-permute-start(bf16[768,256]{1,0:T(8,128)(2,1)S(1)} %collective-permute-done.1.p2.v2), channel_id=1, source_target_pairs={{0,1},{1,0},{2,3},{3,2},{4,5},{5,4},{6,7},{7,6},{8,9},{9,8},{10,11... | collective-permute-start | bytes 1179656 | tf_op jit(solution)/shard_map/ppermute | solution.py:331
  44.7 16.3 %collective-permute-start.3 = (bf16[768,256]{1,0:T(8,128)(2,1)S(1)}, bf16[768,256]{1,0:T(8,128)(2,1)S(1)}, u32[]{:S(2)}, u32[]{:S(2)}) collective-permute-start(bf16[768,256]{1,0:T(8,128)(2,1)S(1)} %collective-permute-done.p1.v1), channel_id=1, source_target_pairs={{1,2},{2,1},{3,4},{4,3},{5,6},{6,5},{7,8},{8,7},{9,10},{10,9},{11,... | collective-permute-start | bytes 1179656 | tf_op jit(solution)/shard_map/ppermute | solution.py:331
  47.4 10.9 %copy-start.2 = (bf16[64,4,640]{2,1,0:T(4,128)(2,1)S(1)}, bf16[64,4,640]{2,1,0:T(4,128)(2,1)}, u32[]{:S(2)}) copy-start(bf16[64,4,640]{2,1,0:T(4,128)(2,1)} %couple.2._) | copy-start | bytes 983044
  47.4 10.9 %copy-start.16 = (s32[1,4]{1,0:T(1,128)S(1)}, s32[1,4]{1,0:T(1,128)}, u32[]{:S(2)}) copy-start(s32[1,4]{1,0:T(1,128)} %refs_1_.3) | copy-start | bytes 52
  47.4 25.7 %all-to-all-start.2 = ((bf16[64,4,640]{2,1,0:T(4,128)(2,1)}), bf16[64,4,640]{2,1,0:T(4,128)(2,1)S(1)}, u32[]{:S(2)}, u32[]{:S(2)}) async-start(bf16[64,4,640]{2,1,0:T(4,128)(2,1)} %couple.2._), calls=%async_computation.2 | async-start | bytes 655360 | tf_op jit(solution)/shard_map/all_to_all | solution.py:335
  62.8 10.2 %copy-start.3 = (bf16[1,4,128,128]{3,2,1,0:T(8,128)(2,1)S(1)}, bf16[1,4,128,128]{3,2,1,0:T(8,128)(2,1)}, u32[]{:S(2)}) copy-start(bf16[1,4,128,128]{3,2,1,0:T(8,128)(2,1)} %couplings.3) | copy-start | bytes 393220
  62.8 10.2 %copy-start.5 = (bf16[1,128,128]{2,1,0:T(8,128)(2,1)S(1)}, bf16[1,128,128]{2,1,0:T(8,128)(2,1)}, u32[]{:S(2)}) copy-start(bf16[1,128,128]{2,1,0:T(8,128)(2,1)} %transfer.3) | copy-start | bytes 98308
  75.1 19.0 %all-to-all-start.3 = ((bf16[64,8,128]{2,1,0:T(8,128)(2,1)}), bf16[64,8,128]{2,1,0:T(8,128)(2,1)S(1)}, u32[]{:S(2)}, u32[]{:S(2)}) async-start(bf16[64,8,128]{2,1,0:T(8,128)(2,1)} %get-tuple-element.40), calls=%async_computation.3 | async-start | bytes 262144 | tf_op jit(solution)/shard_map/all_to_all | solution.py:335
  81.4 18.9 %collective-permute-start.4 = (bf16[512,256]{1,0:T(8,128)(2,1)S(1)}, bf16[512,256]{1,0:T(8,128)(2,1)S(1)}, u32[]{:S(2)}, u32[]{:S(2)}) collective-permute-start(bf16[512,256]{1,0:T(8,128)(2,1)S(1)} %get-tuple-element.45._.own), channel_id=1, source_target_pairs={{0,1},{1,0},{2,3},{3,2},{4,5},{5,4},{6,7},{7,6},{8,9},{9,8},{10,11... | collective-permute-start | bytes 786440 | tf_op jit(solution)/shard_map/ppermute | solution.py:331
  84.9 15.5 %collective-permute-start.5 = (bf16[512,256]{1,0:T(8,128)(2,1)S(1)}, bf16[512,256]{1,0:T(8,128)(2,1)S(1)}, u32[]{:S(2)}, u32[]{:S(2)}) collective-permute-start(bf16[512,256]{1,0:T(8,128)(2,1)S(1)} %get-tuple-element.45._.own), channel_id=1, source_target_pairs={{1,2},{2,1},{3,4},{4,3},{5,6},{6,5},{7,8},{8,7},{9,10},{10,9},{11,... | collective-permute-start | bytes 786440 | tf_op jit(solution)/shard_map/ppermute | solution.py:331
  94.9 9.5 %all-to-all-start.4 = ((bf16[8,16,128]{2,1,0:T(8,128)(2,1)}), bf16[8,16,128]{2,1,0:T(8,128)(2,1)S(1)}, u32[]{:S(2)}, u32[]{:S(2)}) async-start(bf16[8,16,128]{2,1,0:T(8,128)(2,1)} %get-tuple-element.42), calls=%async_computation.4 | async-start | bytes 65536 | tf_op jit(solution)/shard_map/all_to_all | solution.py:335
  100.4 15.7 %collective-permute-start.6 = (bf16[512,256]{1,0:T(8,128)(2,1)S(1)}, bf16[512,256]{1,0:T(8,128)(2,1)}, u32[]{:S(2)}, u32[]{:S(2)}) collective-permute-start(bf16[512,256]{1,0:T(8,128)(2,1)S(1)} %collective-permute-done.5.v2), channel_id=1, source_target_pairs={{0,1},{1,0},{2,3},{3,2},{4,5},{5,4},{6,7},{7,6},{8,9},{9,8},{10,11... | collective-permute-start | bytes 786440 | tf_op jit(solution)/shard_map/ppermute | solution.py:331
  103.0 13.1 %collective-permute-start.7 = (bf16[512,256]{1,0:T(8,128)(2,1)S(1)}, bf16[512,256]{1,0:T(8,128)(2,1)}, u32[]{:S(2)}, u32[]{:S(2)}) collective-permute-start(bf16[512,256]{1,0:T(8,128)(2,1)S(1)} %collective-permute-done.4.v1), channel_id=1, source_target_pairs={{1,2},{2,1},{3,4},{4,3},{5,6},{6,5},{7,8},{8,7},{9,10},{10,9},{11,... | collective-permute-start | bytes 786440 | tf_op jit(solution)/shard_map/ppermute | solution.py:331
  104.4 9.4 %copy-start.10 = (bf16[768,256]{1,0:T(8,128)(2,1)S(1)}, bf16[768,256]{1,0:T(8,128)(2,1)}, u32[]{:S(2)}) copy-start(bf16[768,256]{1,0:T(8,128)(2,1)} %copy-done.9) | copy-start | bytes 1179652
  105.8 23.7 %all-to-all-start.5 = ((bf16[64,4,640]{2,1,0:T(4,128)(2,1)}), bf16[64,4,640]{2,1,0:T(4,128)(2,1)S(1)}, u32[]{:S(2)}, u32[]{:S(2)}) async-start(bf16[64,4,640]{2,1,0:T(4,128)(2,1)} %couple.3._), calls=%async_computation.5 | async-start | bytes 655360 | tf_op jit(solution)/shard_map/all_to_all | solution.py:335
  (7 other events, 28.6 us)

commit v9 on v8

--- a/solution.py
+++ b/solution.py
@@ -70,84 +70,78 @@
     return ridge, centre, first, second
 
 
-def to_owners(values, basis, transfer, staged, rows):
+def to_owners(values, basis, transfer, staged):
     skeleton = dot(values, basis, ((0,), (0,))).astype(BF16)
     uplift = dot(skeleton, transfer)
     skeleton = skeleton.astype(F32)
     for i in range(COLS):
         part = slice(N_DEV * i, N_DEV * (i + 1))
-        staged[pl.ds(i, N_DEV, stride=rows), :] = skeleton[part]
-        staged[pl.ds(COLS + i, N_DEV, stride=rows), :] = uplift[part]
+        staged[:, i, :RANK] = skeleton[part]
+        staged[:, i, RANK : 2 * RANK] = uplift[part]
 
 
 def start_kernel(
     ridge, cluster, far_in, rs_in, coords_in, perm_in, basis_in, transfer_in, wc_out, sent_out, placed,
     far, rs, coords, perm, basis, transfer, wc, sent, staged, sems,
 ):
-    copies = started(
-        (
-            (perm_in, perm), (basis_in, basis), (rs_in, rs), (coords_in, coords),
-            (transfer_in, transfer), (far_in, far),
-        ),
-        sems,
-    )
-    staged[...] = jnp.zeros_like(staged)
+    parts = [pl.ds(r, ROWS) for r in range(0, LEAF, ROWS)]
+    copies = started(((perm_in, perm), (basis_in, basis)), sems)
+    copies += started([(rs_in.at[part], rs.at[part]) for part in parts], sems, 2)
+    copies += started(((transfer_in, transfer), (coords_in, coords), (far_in, far)), sems, 6)
     _, centre, _, _ = chebyshev(ridge[0])
     wait(copies[:2])
     point = lax.broadcasted_iota(jnp.int32, (LEAF, LEAF), 0)
     pick = jnp.where(point == perm[...], 1.0, 0.0).astype(BF16)
     basis_here = dot(pick, basis[...]).astype(BF16)
     placed[...] = basis_here
-    wait(copies[2:4])
+    wait(copies[2:6])
     values = (rs[...] / centre).astype(BF16)
     wc[:LEAF] = values
-    high = coords[...].astype(BF16)
-    low = (coords[...] - high.astype(F32)).astype(BF16)
-    parts = jnp.concatenate([high, low], axis=0)
-    wc[LEAF : LEAF + 2 * DIM] = parts[:, :OUT]
-    wc[LEAF + 2 * DIM :] = parts[:, OUT:]
-    outs = started(((wc, wc_out),), sems, 6)
-    wait(copies[4:])
-    to_owners(values, basis_here, transfer[0], staged, 16)
+    outs = started(((wc.at[pl.ds(0, LEAF)], wc_out.at[pl.ds(0, LEAF)]),), sems, 9)
+    wait(copies[6:])
+    to_owners(values, basis_here, transfer[0], staged)
     lane = lax.broadcasted_iota(jnp.int32, (N_DEV, RANK), 1)
     told = jnp.where(lane == FAR1, (cluster[0] % CPG).astype(F32), 0.0)
     for k in range(FAR1):
         told = jnp.where(lane == k, (far[0, k] % N_DEV).astype(F32), told)
-    staged[pl.ds(8, N_DEV, stride=16), :] = told
-    sent[...] = staged[...].astype(BF16).reshape(N_DEV, 16, RANK)
-    outs += started(((sent, sent_out),), sems, 8)
+    for i in range(COLS):
+        staged[:, i, 2 * RANK :] = told
+    sent[...] = staged[...].astype(BF16)
+    outs += started(((sent, sent_out),), sems, 10)
+    high = coords[...].astype(BF16)
+    low = (coords[...] - high.astype(F32)).astype(BF16)
+    both = jnp.concatenate([high, low], axis=0)
+    wc[LEAF : LEAF + 2 * DIM] = both[:, :OUT]
+    wc[LEAF + 2 * DIM :] = both[:, OUT:]
+    rest = pl.ds(LEAF, 4 * DIM)
+    outs += started(((wc.at[rest], wc_out.at[rest]),), sems, 11)
     wait(outs)
 
 
-def owner_sums(staged, rows, told, sums, narrow):
+def owner_sums(staged, told, sums_out, skeletons, narrow, sums, sems):
     lane = lax.broadcasted_iota(jnp.int32, (N_DEV, RANK), 1).astype(F32)
     member = jnp.where(lane == told[:, FAR1 : FAR1 + 1], 1.0, 0.0).astype(BF16)
-    uplifts = jnp.concatenate(
-        [staged[pl.ds(COLS + i, N_DEV, stride=rows), :] for i in range(COLS)], axis=1
-    ).astype(BF16)
+    uplifts = jnp.concatenate([staged[:, i, RANK : 2 * RANK] for i in range(COLS)], axis=1).astype(BF16)
     total = dot(member, uplifts, ((0,), (0,)))
     for i in range(COLS):
         narrow[pl.ds(CPG * i, CPG), :] = total[:CPG, RANK * i : RANK * (i + 1)]
     out = narrow[...].astype(BF16)
     for g in range(N_GRP):
         sums[g] = out
-
-
-def sums_first_kernel(arrived, _, sums, told, skeletons, staged, narrow):
-    staged[...] = arrived[...].astype(F32).reshape(N_DEV * 16, RANK)
-    told[...] = staged[pl.ds(8, N_DEV, stride=16), :]
-    owner_sums(staged, 16, told[...], sums, narrow)
-    skeletons[...] = jnp.concatenate(
-        [staged[pl.ds(i, N_DEV, stride=16), :] for i in range(COLS)], axis=1
-    ).astype(BF16)
-
-
-def sums_kernel(arrived, told, _, sums, skeletons, staged, narrow):
-    staged[...] = arrived[...].astype(F32).reshape(N_DEV * 8, RANK)
-    owner_sums(staged, 8, told[...], sums, narrow)
-    skeletons[...] = jnp.concatenate(
-        [staged[pl.ds(i, N_DEV, stride=8), :] for i in range(COLS)], axis=1
-    ).astype(BF16)
+    copies = started(((sums, sums_out),), sems)
+    skeletons[...] = jnp.concatenate([staged[:, i, :RANK] for i in range(COLS)], axis=1).astype(BF16)
+    wait(copies)
+
+
+def sums_first_kernel(arrived, _, sums_out, told, skeletons, staged, narrow, sums, sems):
+    staged[...] = arrived[...].astype(F32)
+    told[...] = staged[:, 0, 2 * RANK :]
+    owner_sums(staged, told[...], sums_out, skeletons, narrow, sums, sems)
+
+
+def sums_kernel(arrived, told, _, sums_out, skeletons, staged, narrow, sums, sems):
+    staged[...] = arrived[...].astype(F32)
+    owner_sums(staged, told[...], sums_out, skeletons, narrow, sums, sems)
 
 
 def partners_kernel(skeletons, told, sent, staged):
@@ -208,8 +202,8 @@
         far = dot(basis[part], local)
         r1[part] = residual[part] - far
         w[part] = (direction[part] - factor[:1, :1] * far).astype(BF16)
-    to_owners(w[...], basis[...], transfer[0], staged_out, 8)
-    sent[...] = staged_out[...].astype(BF16).reshape(N_DEV, 8, RANK)
+    to_owners(w[...], basis[...], transfer[0], staged_out)
+    sent[...] = staged_out[...].astype(BF16)
     wait(started(((sent, sent_out),), sems))
 
 
@@ -353,16 +347,16 @@
     field, dma = (LEAF, OUT), pltpu.SemaphoreType.DMA
     payload, partner = (N_DEV, COLS, (FAR1 + 1) * RANK), (N_DEV, COLS, FAR1 * RANK)
     wide = pltpu.VMEM(payload, F32)
-    rows16 = pltpu.VMEM((N_DEV * 16, RANK), F32)
-    rows8 = pltpu.VMEM((N_DEV * 8, RANK), F32)
-    narrow = pltpu.VMEM((COLS * CPG, RANK), F32)
+    told_too, upward = (N_DEV, COLS, 3 * RANK), (N_DEV, COLS, 2 * RANK)
+    sums_shape = (N_GRP, COLS * CPG, RANK)
+    narrow = [pltpu.VMEM((COLS * CPG, RANK), F32), pltpu.VMEM(sums_shape, BF16), dma((1,))]
 
     wc, sent, basis = call(
         start_kernel,
         "start",
         [
             ((LEAF + 4 * DIM, OUT), BF16, HBM),
-            ((N_DEV, 16, RANK), BF16, HBM),
+            (told_too, BF16, HBM),
             ((LEAF, RANK), BF16, VMEM),
         ],
         [SMEM] * 2 + [HBM] * 6,
@@ -375,9 +369,9 @@
             pltpu.VMEM((LEAF, RANK), BF16),
             pltpu.VMEM((1, RANK, RANK), BF16),
             pltpu.VMEM((LEAF + 4 * DIM, OUT), BF16),
-            pltpu.VMEM((N_DEV, 16, RANK), BF16),
-            rows16,
-            dma((9,)),
+            pltpu.VMEM(told_too, BF16),
+            pltpu.VMEM(told_too, F32),
+            dma((12,)),
         ],
         SHORT,
     )
@@ -387,7 +381,7 @@
             near_1_kernel,
             "near_1",
             [(field, F32, VMEM)],
-            [SMEM, HBM] + [ANY] * 6,
+            [SMEM, HBM] + [ANY] * 5 + [HBM],
             (near_list, wc, own, first[0], fields[0], first[1], fields[1], after),
             [pltpu.VMEM((3, 4 * DIM, OUT), BF16), pltpu.VMEM((3, *field), BF16), dma((6,))],
             MID,
@@ -442,7 +436,7 @@
         prepare_kernel,
         "prepare",
         [((FAR2 * COLS * CPG, N_GRP * COLS * CPG), BF16, VMEM)],
-        [SMEM, ANY],
+        [SMEM, HBM],
         (far_clusters, wc),
         flops=SHORT,
     )
@@ -450,10 +444,10 @@
     sums, told, skeletons = call(
         sums_first_kernel,
         "sums_first",
-        [((N_GRP, 16, RANK), BF16, VMEM), ((N_DEV, RANK), F32, VMEM), ((N_DEV, COLS * RANK), BF16, VMEM)],
+        [(sums_shape, BF16, HBM), ((N_DEV, RANK), F32, VMEM), ((N_DEV, COLS * RANK), BF16, VMEM)],
         [VMEM, ANY],
         (arrived, picks),
-        [rows16, narrow],
+        [pltpu.VMEM(told_too, F32), *narrow],
         SHORT,
     )
     sent, arrived = through_owners(sums, skeletons)
@@ -463,10 +457,10 @@
     w, sent, r1 = call(
         middle_kernel,
         "middle",
-        [(field, BF16, VMEM), ((N_DEV, 8, RANK), BF16, HBM), (field, F32, VMEM)],
+        [(field, BF16, VMEM), (upward, BF16, HBM), (field, F32, VMEM)],
         [VMEM] * 7,
         (arrived, couplings, transfer, basis, residual, direction, factor),
-        [pltpu.VMEM((N_DEV, 8, RANK), BF16), wide, rows8, dma((1,))],
+        [pltpu.VMEM(upward, BF16), wide, pltpu.VMEM(upward, F32), dma((1,))],
         SHORT,
     )
     arrived = exchanged(sent, "dev")
@@ -475,10 +469,10 @@
     sums, skeletons = call(
         sums_kernel,
         "sums",
-        [((N_GRP, 16, RANK), BF16, VMEM), ((N_DEV, COLS * RANK), BF16, VMEM)],
+        [(sums_shape, BF16, HBM), ((N_DEV, COLS * RANK), BF16, VMEM)],
         [VMEM, VMEM, ANY],
         (arrived, told, mark),
-        [rows8, narrow],
+        [pltpu.VMEM(upward, F32), *narrow],
         SHORT,
     )
     sent, arrived = through_owners(sums, skeletons)

time: 132 us -> 132 us (level)
  waiting for transfers between devices: 36 us -> 31.8 us
  starting transfers between devices: 67.4 us -> 69.6 us
  Pallas kernels: 23.8 us -> 25.6 us
    all_to_all x6, waiting for transfers between devices: 36 us -> 31.8 us  [exchanged(): return lax.all_to_all(blocks, axis, split_axis=0, concat_axis=0, tiled=True)]
    pallas_call x15, Pallas kernels: 23.8 us -> 25.6 us  [call(): pl.pallas_call(kernel, name=name, out_shape=shapes, in_specs=ins, out_spe...]
    all_to_all x6, starting transfers between devices: 51.7 us -> 53.4 us  [exchanged(): return lax.all_to_all(blocks, axis, split_axis=0, concat_axis=0, tiled=True)]
  transfers between devices with their start and end apart: 14 -> 14, of which waited for: 4 -> 5; matrix products, arithmetic and copies ran while one was open for 0% -> 0% of each run, Pallas kernels for 13% -> 14%
where the time goes in v9:
time: 132 us; the launch traced here: 131 us
  starting transfers between devices  69.6 us (53%)
  waiting for transfers between devices  31.8 us (24%)
  Pallas kernels  25.6 us (19%)
  between operations  2.48 us (2%)
  local copies, waits for them, and re-layouts  1.82 us (1%)
    all_to_all x6, starting transfers between devices, exchanged(): return lax.all_to_all(blocks, axis, split_axis=0, concat_axis=0, tiled=True)  53.4 us
    all_to_all x6, waiting for transfers between devices, exchanged(): return lax.all_to_all(blocks, axis, split_axis=0, concat_axis=0, tiled=True)  31.8 us
    pallas_call x15, Pallas kernels, call(): pl.pallas_call(kernel, name=name, out_shape=shapes, in_specs=ins, out_spe...  25.6 us
    ppermute x8, starting transfers between devices, swapped(): return (lax.ppermute(one, 'dev', inner), lax.ppermute(two, 'dev', outer))  16.2 us
  transfers between devices with their start and end apart: 14, of which 5 were waited for; matrix products, arithmetic and copies ran while one was open for 0% of the time, Pallas kernels for 14%

profile of v9, /device:TPU:2, one launch (start us, length us, event | category | flops | bytes accessed | tf_op | source)
XLA Modules:
  0.0 131.3 jit_solution(2515547537431975512)
XLA Ops:
  1.9 2.8 %start.1 = (bf16[768,256]{1,0:T(8,128)(2,1)}, bf16[64,4,384]{2,1,0:T(4,128)(2,1)}, bf16[512,128]{1,0:T(8,128)(2,1)S(1)}) custom-call(f32[1]{0:T(128)} %bitcast.2.ridge, s32[1]{0:T(128)S(6)} %copy.14.cluster, s32[1,4]{1,0:T(1,128)} %far_in.1, f32[512,256]{1,0:T(8,128)} %refs_8_.3, f32[64,512]{1,0:T(8,128)} %bitcast.5, s32[1,512]{1,0:T(1,128)} %perm_in.1, ...), custom_call_target="tpu_custom_call" | custom-call | flops 10000000 | tf_op jit(solution)/shard_map/start/pallas_call | solution.py:36
  4.7 16.7 %all-to-all-start = ((bf16[64,4,384]{2,1,0:T(4,128)(2,1)}), bf16[64,4,384]{2,1,0:T(4,128)(2,1)S(1)}, u32[]{:S(2)}, u32[]{:S(2)}) async-start(bf16[64,4,384]{2,1,0:T(4,128)(2,1)} %get-tuple-element.28), calls=%async_computation | async-start | bytes 393216 | tf_op jit(solution)/shard_map/all_to_all | solution.py:329
  22.1 3.5 %collective-permute-start = (bf16[768,256]{1,0:T(8,128)(2,1)S(1)}, bf16[768,256]{1,0:T(8,128)(2,1)S(1)}, u32[]{:S(2)}, u32[]{:S(2)}) collective-permute-start(bf16[768,256]{1,0:T(8,128)(2,1)S(1)} %copy-done.12), channel_id=1, source_target_pairs={{0,1},{1,0},{2,3},{3,2},{4,5},{5,4},{6,7},{7,6},{8,9},{9,8},{10,11... | collective-permute-start | bytes 1179656 | tf_op jit(solution)/shard_map/ppermute | solution.py:325
  26.3 9.0 %all-to-all-done.arrived = bf16[64,4,384]{2,1,0:T(4,128)(2,1)S(1)} async-done(((bf16[64,4,384]{2,1,0:T(4,128)(2,1)}), bf16[64,4,384]{2,1,0:T(4,128)(2,1)S(1)}, u32[]{:S(2)}, u32[]{:S(2)}) %all-to-all-start) | async-done | bytes 196640 | tf_op jit(solution)/shard_map/all_to_all | solution.py:329
  36.3 4.8 %all-to-all-start.1 = ((bf16[8,16,128]{2,1,0:T(8,128)(2,1)}), bf16[8,16,128]{2,1,0:T(8,128)(2,1)S(1)}, u32[]{:S(2)}, u32[]{:S(2)}) async-start(bf16[8,16,128]{2,1,0:T(8,128)(2,1)} %get-tuple-element.29), calls=%async_computation.1 | async-start | bytes 65536 | tf_op jit(solution)/shard_map/all_to_all | solution.py:329
  41.7 2.5 %collective-permute-start.2 = (bf16[768,256]{1,0:T(8,128)(2,1)S(1)}, bf16[768,256]{1,0:T(8,128)(2,1)S(1)}, u32[]{:S(2)}, u32[]{:S(2)}) collective-permute-start(bf16[768,256]{1,0:T(8,128)(2,1)S(1)} %collective-permute-done.1.p2.v2), channel_id=1, source_target_pairs={{0,1},{1,0},{2,3},{3,2},{4,5},{5,4},{6,7},{7,6},{8,9},{9,8},{10,11... | collective-permute-start | bytes 1179656 | tf_op jit(solution)/shard_map/ppermute | solution.py:325
  45.1 1.4 %couple.2._ = bf16[64,4,640]{2,1,0:T(4,128)(2,1)} custom-call(bf16[64,128]{1,0:T(8,128)(2,1)S(1)} %prepare.1._.picks, bf16[8,16,128]{2,1,0:T(8,128)(2,1)S(1)} %all-to-all-done.1.all_sums, bf16[4,4,128,128]{3,2,1,0:T(8,128)(2,1)S(1)} %copy-done, f32[64,128]{1,0:T(8,128)S(1)} %get-tuple-element.30.told, bf16[64,4,512]{2,1,0:T(4,128)(2,1)S(1)} %partners.2), custom_call_target="tpu_custom_call" | custom-call | flops 10000000 | tf_op jit(solution)/shard_map/couple/pallas_call | solution.py:36
  46.5 11.2 %all-to-all-start.2 = ((bf16[64,4,640]{2,1,0:T(4,128)(2,1)}), bf16[64,4,640]{2,1,0:T(4,128)(2,1)S(1)}, u32[]{:S(2)}, u32[]{:S(2)}) async-start(bf16[64,4,640]{2,1,0:T(4,128)(2,1)} %couple.2._), calls=%async_computation.2 | async-start | bytes 655360 | tf_op jit(solution)/shard_map/all_to_all | solution.py:329
  57.8 3.1 %near_1.2.refs_3_.refs_9_ = f32[512,256]{1,0:T(8,128)S(1)} custom-call(s32[1,4]{1,0:T(1,128)S(1)} %copy-done.11, bf16[768,256]{1,0:T(8,128)(2,1)} %get-tuple-element.34._.places_in.own.refs_2_, bf16[768,256]{1,0:T(8,128)(2,1)} %get-tuple-element.34._.places_in.own.refs_2_, bf16[768,256]{1,0:T(8,128)(2,1)S(1)} %collective-permute-done.p1.v1, ...), custom_call_target="tpu_custom_call" | custom-call | flops 10000000000 | tf_op jit(solution)/shard_map/near_1/pallas_call | solution.py:36
  62.7 3.0 %near_2.2 = (f32[512,256]{1,0:T(8,128)S(1)}, f32[512,256]{1,0:T(8,128)S(1)}, f32[8,128]{1,0:T(8,128)S(1)}) custom-call(f32[1]{0:T(128)} %bitcast.3.refs_0_, s32[1,4]{1,0:T(1,128)S(1)} %copy-done.11, bf16[768,256]{1,0:T(8,128)(2,1)} %get-tuple-element.34._.places_in.own.refs_2_, f32[512,256]{1,0:T(8,128)S(1)} %near_1.2.refs_3_.refs_9_, ...), custom_call_target="tpu_custom_call" | custom-call | flops 1000000000 | tf_op jit(solution)/shard_map/near_2/pallas_call | solution.py:36
  65.7 6.0 %all-to-all-done.2.arrived = bf16[64,4,640]{2,1,0:T(4,128)(2,1)S(1)} async-done(((bf16[64,4,640]{2,1,0:T(4,128)(2,1)}), bf16[64,4,640]{2,1,0:T(4,128)(2,1)S(1)}, u32[]{:S(2)}, u32[]{:S(2)}) %all-to-all-start.2) | async-done | bytes 327712 | tf_op jit(solution)/shard_map/all_to_all | solution.py:329
  71.7 2.0 %middle.1 = (bf16[512,256]{1,0:T(8,128)(2,1)S(1)}, bf16[64,4,256]{2,1,0:T(4,128)(2,1)}, f32[512,256]{1,0:T(8,128)S(1)}) custom-call(bf16[64,4,640]{2,1,0:T(4,128)(2,1)S(1)} %all-to-all-done.2.arrived, bf16[1,4,128,128]{3,2,1,0:T(8,128)(2,1)S(1)} %copy-done.1, bf16[1,128,128]{2,1,0:T(8,128)(2,1)S(1)} %copy-done.2, ...), custom_call_target="tpu_custom_call" | custom-call | flops 10000000 | tf_op jit(solution)/shard_map/middle/pallas_call | solution.py:36
  73.8 8.0 %all-to-all-start.3 = ((bf16[64,4,256]{2,1,0:T(4,128)(2,1)}), bf16[64,4,256]{2,1,0:T(4,128)(2,1)S(1)}, u32[]{:S(2)}, u32[]{:S(2)}) async-start(bf16[64,4,256]{2,1,0:T(4,128)(2,1)} %get-tuple-element.40), calls=%async_computation.3 | async-start | bytes 262144 | tf_op jit(solution)/shard_map/all_to_all | solution.py:329
  81.8 3.5 %collective-permute-start.4 = (bf16[512,256]{1,0:T(8,128)(2,1)S(1)}, bf16[512,256]{1,0:T(8,128)(2,1)S(1)}, u32[]{:S(2)}, u32[]{:S(2)}) collective-permute-start(bf16[512,256]{1,0:T(8,128)(2,1)S(1)} %get-tuple-element.45._.own), channel_id=1, source_target_pairs={{0,1},{1,0},{2,3},{3,2},{4,5},{5,4},{6,7},{7,6},{8,9},{9,8},{10,11... | collective-permute-start | bytes 786440 | tf_op jit(solution)/shard_map/ppermute | solution.py:325
  85.3 1.4 %collective-permute-start.5 = (bf16[512,256]{1,0:T(8,128)(2,1)S(1)}, bf16[512,256]{1,0:T(8,128)(2,1)}, u32[]{:S(2)}, u32[]{:S(2)}) collective-permute-start(bf16[512,256]{1,0:T(8,128)(2,1)S(1)} %get-tuple-element.45._.own), channel_id=1, source_target_pairs={{1,2},{2,1},{3,4},{4,3},{5,6},{6,5},{7,8},{8,7},{9,10},{10,9},{11,... | collective-permute-start | bytes 786440 | tf_op jit(solution)/shard_map/ppermute | solution.py:325
  86.7 7.8 %all-to-all-done.3.arrived = bf16[64,4,256]{2,1,0:T(4,128)(2,1)S(1)} async-done(((bf16[64,4,256]{2,1,0:T(4,128)(2,1)}), bf16[64,4,256]{2,1,0:T(4,128)(2,1)S(1)}, u32[]{:S(2)}, u32[]{:S(2)}) %all-to-all-start.3) | async-done | bytes 131104 | tf_op jit(solution)/shard_map/all_to_all | solution.py:329
  95.4 4.0 %all-to-all-start.4 = ((bf16[8,16,128]{2,1,0:T(8,128)(2,1)}), bf16[8,16,128]{2,1,0:T(8,128)(2,1)S(1)}, u32[]{:S(2)}, u32[]{:S(2)}) async-start(bf16[8,16,128]{2,1,0:T(8,128)(2,1)} %get-tuple-element.42), calls=%async_computation.4 | async-start | bytes 65536 | tf_op jit(solution)/shard_map/all_to_all | solution.py:329
  100.0 2.6 %collective-permute-start.6 = (bf16[512,256]{1,0:T(8,128)(2,1)}, bf16[512,256]{1,0:T(8,128)(2,1)}, u32[]{:S(2)}, u32[]{:S(2)}) collective-permute-start(bf16[512,256]{1,0:T(8,128)(2,1)} %collective-permute-done.5.v2), channel_id=1, source_target_pairs={{0,1},{1,0},{2,3},{3,2},{4,5},{5,4},{6,7},{7,6},{8,9},{9,8},{10,11... | collective-permute-start | bytes 786440 | tf_op jit(solution)/shard_map/ppermute | solution.py:325
  104.0 1.4 %couple.3._ = bf16[64,4,640]{2,1,0:T(4,128)(2,1)} custom-call(bf16[64,128]{1,0:T(8,128)(2,1)S(1)} %prepare.1._.picks, bf16[8,16,128]{2,1,0:T(8,128)(2,1)S(1)} %all-to-all-done.4.all_sums, bf16[4,4,128,128]{3,2,1,0:T(8,128)(2,1)S(1)} %copy-done, f32[64,128]{1,0:T(8,128)S(1)} %get-tuple-element.30.told, bf16[64,4,512]{2,1,0:T(4,128)(2,1)S(1)} %partners.3), custom_call_target="tpu_custom_call" | custom-call | flops 10000000 | tf_op jit(solution)/shard_map/couple/pallas_call | solution.py:36
  105.4 8.6 %all-to-all-start.5 = ((bf16[64,4,640]{2,1,0:T(4,128)(2,1)}), bf16[64,4,640]{2,1,0:T(4,128)(2,1)S(1)}, u32[]{:S(2)}, u32[]{:S(2)}) async-start(bf16[64,4,640]{2,1,0:T(4,128)(2,1)} %couple.3._), calls=%async_computation.5 | async-start | bytes 655360 | tf_op jit(solution)/shard_map/all_to_all | solution.py:329
  114.0 3.1 %near_1.3.refs_3_ = f32[512,256]{1,0:T(8,128)S(1)} custom-call(s32[1,4]{1,0:T(1,128)S(1)} %copy-done.11, bf16[768,256]{1,0:T(8,128)(2,1)} %get-tuple-element.34._.places_in.own.refs_2_, bf16[512,256]{1,0:T(8,128)(2,1)S(1)} %get-tuple-element.45._.own, bf16[768,256]{1,0:T(8,128)(2,1)S(1)} %collective-permute-done.p1.v1, ...), custom_call_target="tpu_custom_call" | custom-call | flops 10000000000 | tf_op jit(solution)/shard_map/near_1/pallas_call | solution.py:36
  117.2 3.2 %near_2.3 = (f32[512,256]{1,0:T(8,128)S(1)}, f32[512,256]{1,0:T(8,128)S(1)}, f32[8,128]{1,0:T(8,128)S(1)}) custom-call(f32[1]{0:T(128)} %bitcast.4.refs_0_, s32[1,4]{1,0:T(1,128)S(1)} %copy-done.11, bf16[768,256]{1,0:T(8,128)(2,1)} %get-tuple-element.34._.places_in.own.refs_2_, f32[512,256]{1,0:T(8,128)S(1)} %near_1.3.refs_3_, ...), custom_call_target="tpu_custom_call" | custom-call | flops 1000000000 | tf_op jit(solution)/shard_map/near_2/pallas_call | solution.py:36
  120.4 8.9 %all-to-all-done.5.arrived = bf16[64,4,640]{2,1,0:T(4,128)(2,1)S(1)} async-done(((bf16[64,4,640]{2,1,0:T(4,128)(2,1)}), bf16[64,4,640]{2,1,0:T(4,128)(2,1)S(1)}, u32[]{:S(2)}, u32[]{:S(2)}) %all-to-all-start.5) | async-done | bytes 327712 | tf_op jit(solution)/shard_map/all_to_all | solution.py:329
  129.3 1.9 %end.1 = (f32[512,256]{1,0:T(8,128)}, f32[512,256]{1,0:T(8,128)}) custom-call(bf16[64,4,640]{2,1,0:T(4,128)(2,1)S(1)} %all-to-all-done.5.arrived, bf16[1,4,128,128]{3,2,1,0:T(8,128)(2,1)S(1)} %copy-done.1, bf16[1,128,128]{2,1,0:T(8,128)(2,1)S(1)} %copy-done.2, bf16[512,128]{1,0:T(8,128)(2,1)S(1)} %get-tuple-element.32.basis, ...), custom_call_target="tpu_custom_call" | custom-call | flops 10000000 | tf_op jit(solution)/shard_map/end/pallas_call | solution.py:36
  (45 shorter events, 8.5 us)
Async XLA Ops:
  4.7 16.8 %copy-start.3 = (s32[4,4]{1,0:T(4,128)S(1)}, s32[4,4]{1,0:T(4,128)}, u32[]{:S(2)}) copy-start(s32[4,4]{1,0:T(4,128)} %far_clusters.1) | copy-start | bytes 196
  4.7 17.4 %copy-start.12 = (bf16[768,256]{1,0:T(8,128)(2,1)S(1)}, bf16[768,256]{1,0:T(8,128)(2,1)}, u32[]{:S(2)}) copy-start(bf16[768,256]{1,0:T(8,128)(2,1)} %get-tuple-element.34._.places_in.own.refs_2_) | copy-start | bytes 1179652
  4.7 30.6 %all-to-all-start = ((bf16[64,4,384]{2,1,0:T(4,128)(2,1)}), bf16[64,4,384]{2,1,0:T(4,128)(2,1)S(1)}, u32[]{:S(2)}, u32[]{:S(2)}) async-start(bf16[64,4,384]{2,1,0:T(4,128)(2,1)} %get-tuple-element.28), calls=%async_computation | async-start | bytes 393216 | tf_op jit(solution)/shard_map/all_to_all | solution.py:329
  21.5 23.7 %copy-start = (bf16[4,4,128,128]{3,2,1,0:T(8,128)(2,1)S(1)}, bf16[4,4,128,128]{3,2,1,0:T(8,128)(2,1)}, u32[]{:S(2)}) copy-start(bf16[4,4,128,128]{3,2,1,0:T(8,128)(2,1)} %blocks.3) | copy-start | bytes 1572868
  22.1 19.6 %collective-permute-start = (bf16[768,256]{1,0:T(8,128)(2,1)S(1)}, bf16[768,256]{1,0:T(8,128)(2,1)S(1)}, u32[]{:S(2)}, u32[]{:S(2)}) collective-permute-start(bf16[768,256]{1,0:T(8,128)(2,1)S(1)} %copy-done.12), channel_id=1, source_target_pairs={{0,1},{1,0},{2,3},{3,2},{4,5},{5,4},{6,7},{7,6},{8,9},{9,8},{10,11... | collective-permute-start | bytes 1179656 | tf_op jit(solution)/shard_map/ppermute | solution.py:325
  25.6 16.1 %collective-permute-start.1 = (bf16[768,256]{1,0:T(8,128)(2,1)S(1)}, bf16[768,256]{1,0:T(8,128)(2,1)S(1)}, u32[]{:S(2)}, u32[]{:S(2)}) collective-permute-start(bf16[768,256]{1,0:T(8,128)(2,1)S(1)} %copy-done.12), channel_id=1, source_target_pairs={{1,2},{2,1},{3,4},{4,3},{5,6},{6,5},{7,8},{8,7},{9,10},{10,9},{11,... | collective-permute-start | bytes 1179656 | tf_op jit(solution)/shard_map/ppermute | solution.py:325
  36.3 8.8 %all-to-all-start.1 = ((bf16[8,16,128]{2,1,0:T(8,128)(2,1)}), bf16[8,16,128]{2,1,0:T(8,128)(2,1)S(1)}, u32[]{:S(2)}, u32[]{:S(2)}) async-start(bf16[8,16,128]{2,1,0:T(8,128)(2,1)} %get-tuple-element.29), calls=%async_computation.1 | async-start | bytes 65536 | tf_op jit(solution)/shard_map/all_to_all | solution.py:329
  41.7 16.0 %copy-start.4 = (bf16[768,256]{1,0:T(8,128)(2,1)}, bf16[768,256]{1,0:T(8,128)(2,1)S(1)}, u32[]{:S(2)}) copy-start(bf16[768,256]{1,0:T(8,128)(2,1)S(1)} %collective-permute-done.1.p2.v2) | copy-start | bytes 1179652
  41.7 19.2 %collective-permute-start.2 = (bf16[768,256]{1,0:T(8,128)(2,1)S(1)}, bf16[768,256]{1,0:T(8,128)(2,1)S(1)}, u32[]{:S(2)}, u32[]{:S(2)}) collective-permute-start(bf16[768,256]{1,0:T(8,128)(2,1)S(1)} %collective-permute-done.1.p2.v2), channel_id=1, source_target_pairs={{0,1},{1,0},{2,3},{3,2},{4,5},{5,4},{6,7},{7,6},{8,9},{9,8},{10,11... | collective-permute-start | bytes 1179656 | tf_op jit(solution)/shard_map/ppermute | solution.py:325
  44.3 16.7 %collective-permute-start.3 = (bf16[768,256]{1,0:T(8,128)(2,1)S(1)}, bf16[768,256]{1,0:T(8,128)(2,1)S(1)}, u32[]{:S(2)}, u32[]{:S(2)}) collective-permute-start(bf16[768,256]{1,0:T(8,128)(2,1)S(1)} %collective-permute-done.p1.v1), channel_id=1, source_target_pairs={{1,2},{2,1},{3,4},{4,3},{5,6},{6,5},{7,8},{8,7},{9,10},{10,9},{11,... | collective-permute-start | bytes 1179656 | tf_op jit(solution)/shard_map/ppermute | solution.py:325
  46.5 11.2 %copy-start.11 = (s32[1,4]{1,0:T(1,128)S(1)}, s32[1,4]{1,0:T(1,128)}, u32[]{:S(2)}) copy-start(s32[1,4]{1,0:T(1,128)} %refs_1_.3) | copy-start | bytes 52
  46.5 25.2 %all-to-all-start.2 = ((bf16[64,4,640]{2,1,0:T(4,128)(2,1)}), bf16[64,4,640]{2,1,0:T(4,128)(2,1)S(1)}, u32[]{:S(2)}, u32[]{:S(2)}) async-start(bf16[64,4,640]{2,1,0:T(4,128)(2,1)} %couple.2._), calls=%async_computation.2 | async-start | bytes 655360 | tf_op jit(solution)/shard_map/all_to_all | solution.py:329
  60.9 4.8 %copy-start.6 = (bf16[768,256]{1,0:T(8,128)(2,1)}, bf16[768,256]{1,0:T(8,128)(2,1)S(1)}, u32[]{:S(2)}) copy-start(bf16[768,256]{1,0:T(8,128)(2,1)S(1)} %collective-permute-done.2.refs_4_.refs_5_) | copy-start | bytes 1179652
  62.7 9.0 %copy-start.1 = (bf16[1,4,128,128]{3,2,1,0:T(8,128)(2,1)S(1)}, bf16[1,4,128,128]{3,2,1,0:T(8,128)(2,1)}, u32[]{:S(2)}) copy-start(bf16[1,4,128,128]{3,2,1,0:T(8,128)(2,1)} %couplings.3) | copy-start | bytes 393220
  62.7 9.0 %copy-start.2 = (bf16[1,128,128]{2,1,0:T(8,128)(2,1)S(1)}, bf16[1,128,128]{2,1,0:T(8,128)(2,1)}, u32[]{:S(2)}) copy-start(bf16[1,128,128]{2,1,0:T(8,128)(2,1)} %transfer.3) | copy-start | bytes 98308
  73.8 20.7 %all-to-all-start.3 = ((bf16[64,4,256]{2,1,0:T(4,128)(2,1)}), bf16[64,4,256]{2,1,0:T(4,128)(2,1)S(1)}, u32[]{:S(2)}, u32[]{:S(2)}) async-start(bf16[64,4,256]{2,1,0:T(4,128)(2,1)} %get-tuple-element.40), calls=%async_computation.3 | async-start | bytes 262144 | tf_op jit(solution)/shard_map/all_to_all | solution.py:329
  81.8 18.2 %collective-permute-start.4 = (bf16[512,256]{1,0:T(8,128)(2,1)S(1)}, bf16[512,256]{1,0:T(8,128)(2,1)S(1)}, u32[]{:S(2)}, u32[]{:S(2)}) collective-permute-start(bf16[512,256]{1,0:T(8,128)(2,1)S(1)} %get-tuple-element.45._.own), channel_id=1, source_target_pairs={{0,1},{1,0},{2,3},{3,2},{4,5},{5,4},{6,7},{7,6},{8,9},{9,8},{10,11... | collective-permute-start | bytes 786440 | tf_op jit(solution)/shard_map/ppermute | solution.py:325
  85.3 14.7 %collective-permute-start.5 = (bf16[512,256]{1,0:T(8,128)(2,1)S(1)}, bf16[512,256]{1,0:T(8,128)(2,1)}, u32[]{:S(2)}, u32[]{:S(2)}) collective-permute-start(bf16[512,256]{1,0:T(8,128)(2,1)S(1)} %get-tuple-element.45._.own), channel_id=1, source_target_pairs={{1,2},{2,1},{3,4},{4,3},{5,6},{6,5},{7,8},{8,7},{9,10},{10,9},{11,... | collective-permute-start | bytes 786440 | tf_op jit(solution)/shard_map/ppermute | solution.py:325
  95.4 8.6 %all-to-all-start.4 = ((bf16[8,16,128]{2,1,0:T(8,128)(2,1)}), bf16[8,16,128]{2,1,0:T(8,128)(2,1)S(1)}, u32[]{:S(2)}, u32[]{:S(2)}) async-start(bf16[8,16,128]{2,1,0:T(8,128)(2,1)} %get-tuple-element.42), calls=%async_computation.4 | async-start | bytes 65536 | tf_op jit(solution)/shard_map/all_to_all | solution.py:329
  100.0 17.1 %collective-permute-start.6 = (bf16[512,256]{1,0:T(8,128)(2,1)}, bf16[512,256]{1,0:T(8,128)(2,1)}, u32[]{:S(2)}, u32[]{:S(2)}) collective-permute-start(bf16[512,256]{1,0:T(8,128)(2,1)} %collective-permute-done.5.v2), channel_id=1, source_target_pairs={{0,1},{1,0},{2,3},{3,2},{4,5},{5,4},{6,7},{7,6},{8,9},{9,8},{10,11... | collective-permute-start | bytes 786440 | tf_op jit(solution)/shard_map/ppermute | solution.py:325
  102.6 14.6 %collective-permute-start.7 = (bf16[512,256]{1,0:T(8,128)(2,1)S(1)}, bf16[512,256]{1,0:T(8,128)(2,1)}, u32[]{:S(2)}, u32[]{:S(2)}) collective-permute-start(bf16[512,256]{1,0:T(8,128)(2,1)S(1)} %collective-permute-done.4.v1), channel_id=1, source_target_pairs={{1,2},{2,1},{3,4},{4,3},{5,6},{6,5},{7,8},{8,7},{9,10},{10,9},{11,... | collective-permute-start | bytes 786440 | tf_op jit(solution)/shard_map/ppermute | solution.py:325
  105.4 8.6 %copy-start.5 = (bf16[768,256]{1,0:T(8,128)(2,1)S(1)}, bf16[768,256]{1,0:T(8,128)(2,1)}, u32[]{:S(2)}) copy-start(bf16[768,256]{1,0:T(8,128)(2,1)} %copy-done.4) | copy-start | bytes 1179652
  105.4 23.9 %all-to-all-start.5 = ((bf16[64,4,640]{2,1,0:T(4,128)(2,1)}), bf16[64,4,640]{2,1,0:T(4,128)(2,1)S(1)}, u32[]{:S(2)}, u32[]{:S(2)}) async-start(bf16[64,4,640]{2,1,0:T(4,128)(2,1)} %couple.3._), calls=%async_computation.5 | async-start | bytes 655360 | tf_op jit(solution)/shard_map/all_to_all | solution.py:329
  114.0 3.2 %copy-start.7 = (bf16[768,256]{1,0:T(8,128)(2,1)S(1)}, bf16[768,256]{1,0:T(8,128)(2,1)}, u32[]{:S(2)}) copy-start(bf16[768,256]{1,0:T(8,128)(2,1)} %copy-done.6) | copy-start | bytes 1179652
  (3 other events, 5.0 us)

commit v10 on v9

--- a/solution.py
+++ b/solution.py
@@ -20,7 +20,7 @@
 ANY = pl.BlockSpec(memory_space=pl.ANY)
 HBM = pl.BlockSpec(memory_space=pltpu.HBM)
 LIMIT = 32 * 2**20
-SHORT, MID, LONG = 10**7, 10**10, 10**9
+SHORT, MID, LONG = 10**7, 10**9, 10**10
 ROWS = 128
 
 
@@ -84,21 +84,24 @@
     ridge, cluster, far_in, rs_in, coords_in, perm_in, basis_in, transfer_in, wc_out, sent_out, placed,
     far, rs, coords, perm, basis, transfer, wc, sent, staged, sems,
 ):
-    parts = [pl.ds(r, ROWS) for r in range(0, LEAF, ROWS)]
-    copies = started(((perm_in, perm), (basis_in, basis)), sems)
-    copies += started([(rs_in.at[part], rs.at[part]) for part in parts], sems, 2)
-    copies += started(((transfer_in, transfer), (coords_in, coords), (far_in, far)), sems, 6)
+    copies = started(
+        (
+            (perm_in, perm), (basis_in, basis), (rs_in, rs), (transfer_in, transfer),
+            (coords_in, coords), (far_in, far),
+        ),
+        sems,
+    )
     _, centre, _, _ = chebyshev(ridge[0])
     wait(copies[:2])
     point = lax.broadcasted_iota(jnp.int32, (LEAF, LEAF), 0)
     pick = jnp.where(point == perm[...], 1.0, 0.0).astype(BF16)
     basis_here = dot(pick, basis[...]).astype(BF16)
     placed[...] = basis_here
-    wait(copies[2:6])
+    wait(copies[2:3])
     values = (rs[...] / centre).astype(BF16)
     wc[:LEAF] = values
-    outs = started(((wc.at[pl.ds(0, LEAF)], wc_out.at[pl.ds(0, LEAF)]),), sems, 9)
-    wait(copies[6:])
+    outs = started(((wc.at[pl.ds(0, LEAF)], wc_out.at[pl.ds(0, LEAF)]),), sems, 6)
+    wait(copies[3:])
     to_owners(values, basis_here, transfer[0], staged)
     lane = lax.broadcasted_iota(jnp.int32, (N_DEV, RANK), 1)
     told = jnp.where(lane == FAR1, (cluster[0] % CPG).astype(F32), 0.0)
@@ -107,14 +110,14 @@
     for i in range(COLS):
         staged[:, i, 2 * RANK :] = told
     sent[...] = staged[...].astype(BF16)
-    outs += started(((sent, sent_out),), sems, 10)
+    outs += started(((sent, sent_out),), sems, 7)
     high = coords[...].astype(BF16)
     low = (coords[...] - high.astype(F32)).astype(BF16)
     both = jnp.concatenate([high, low], axis=0)
     wc[LEAF : LEAF + 2 * DIM] = both[:, :OUT]
     wc[LEAF + 2 * DIM :] = both[:, OUT:]
     rest = pl.ds(LEAF, 4 * DIM)
-    outs += started(((wc.at[rest], wc_out.at[rest]),), sems, 11)
+    outs += started(((wc.at[rest], wc_out.at[rest]),), sems, 8)
     wait(outs)
 
 
@@ -133,13 +136,13 @@
     wait(copies)
 
 
-def sums_first_kernel(arrived, _, sums_out, told, skeletons, staged, narrow, sums, sems):
+def sums_first_kernel(arrived, sums_out, told, skeletons, staged, narrow, sums, sems):
     staged[...] = arrived[...].astype(F32)
     told[...] = staged[:, 0, 2 * RANK :]
     owner_sums(staged, told[...], sums_out, skeletons, narrow, sums, sems)
 
 
-def sums_kernel(arrived, told, _, sums_out, skeletons, staged, narrow, sums, sems):
+def sums_kernel(arrived, told, sums_out, skeletons, staged, narrow, sums, sems):
     staged[...] = arrived[...].astype(F32)
     owner_sums(staged, told[...], sums_out, skeletons, narrow, sums, sems)
 
@@ -301,11 +304,7 @@
     residual[...] = left
 
 
-def mark_kernel(_, mark):
-    mark[...] = jnp.zeros_like(mark)
-
-
-def prepare_kernel(far_clusters, _, picks):
+def prepare_kernel(far_clusters, picks):
     rows = COLS * CPG
     row = lax.broadcasted_iota(jnp.int32, (rows, N_GRP * rows), 0)
     lane = lax.broadcasted_iota(jnp.int32, (rows, N_GRP * rows), 1)
@@ -318,8 +317,7 @@
         picks[rows * k : rows * (k + 1)] = jnp.where(lane == target, 1.0, 0.0).astype(BF16)
 
 
-def swapped(pair, after):
-    one, two, _ = lax.optimization_barrier((*pair, after))
+def swapped(one, two):
     inner = [(i, i ^ 1) for i in range(N_DEV)]
     outer = [(i, ((i + 1) ^ 1) - 1) for i in range(1, N_DEV - 1)]
     return lax.ppermute(one, "dev", inner), lax.ppermute(two, "dev", outer)
@@ -371,7 +369,7 @@
             pltpu.VMEM((LEAF + 4 * DIM, OUT), BF16),
             pltpu.VMEM(told_too, BF16),
             pltpu.VMEM(told_too, F32),
-            dma((12,)),
+            dma((9,)),
         ],
         SHORT,
     )
@@ -404,10 +402,6 @@
             ],
             LONG,
         )
-
-    def marked(shard):
-        (mark,) = call(mark_kernel, "mark", [((8, RANK), F32, VMEM)], [ANY], (shard,), flops=SHORT)
-        return mark
 
     def through_owners(sums, skeletons):
         all_sums = exchanged(sums, "grp")
@@ -436,22 +430,22 @@
         prepare_kernel,
         "prepare",
         [((FAR2 * COLS * CPG, N_GRP * COLS * CPG), BF16, VMEM)],
-        [SMEM, HBM],
-        (far_clusters, wc),
+        [SMEM],
+        (far_clusters,),
         flops=SHORT,
     )
-    first1 = swapped((wc, wc), picks)
+    first1 = swapped(wc, wc)
     sums, told, skeletons = call(
         sums_first_kernel,
         "sums_first",
         [(sums_shape, BF16, HBM), ((N_DEV, RANK), F32, VMEM), ((N_DEV, COLS * RANK), BF16, VMEM)],
-        [VMEM, ANY],
-        (arrived, picks),
+        [VMEM],
+        (arrived,),
         [pltpu.VMEM(told_too, F32), *narrow],
         SHORT,
     )
     sent, arrived = through_owners(sums, skeletons)
-    first2 = swapped(first1[::-1], sums)
+    first2 = swapped(*first1[::-1])
     near = near_1(wc, first1, first1, sent)
     residual, direction, factor = near_2(False, near, first2, first2, near)
     w, sent, r1 = call(
@@ -464,19 +458,18 @@
         SHORT,
     )
     arrived = exchanged(sent, "dev")
-    mark = marked(w)
-    fields1 = swapped((w, w), mark)
+    fields1 = swapped(w, w)
     sums, skeletons = call(
         sums_kernel,
         "sums",
         [(sums_shape, BF16, HBM), ((N_DEV, COLS * RANK), BF16, VMEM)],
-        [VMEM, VMEM, ANY],
-        (arrived, told, mark),
+        [VMEM, VMEM],
+        (arrived, told),
         [pltpu.VMEM(upward, F32), *narrow],
         SHORT,
     )
     sent, arrived = through_owners(sums, skeletons)
-    fields2 = swapped(fields1[::-1], sums)
+    fields2 = swapped(*fields1[::-1])
     near = near_1(w, first1, fields1, sent)
     residual, total, factor = near_2(True, near, first2, fields2, r1)
     return tuple(

time: 132 us -> 136 us (1.030)
  the two profiles are of different devices: /device:TPU:2 before, /device:TPU:16 now
where the time goes in v10:
time: 136 us; the launch traced here: 135 us
  starting transfers between devices  72.2 us (53%)
  waiting for transfers between devices  32.8 us (24%)
  Pallas kernels  25.6 us (19%)
  between operations  2.47 us (2%)
  local copies, waits for them, and re-layouts  1.78 us (1%)
    all_to_all x6, starting transfers between devices, exchanged(): return lax.all_to_all(blocks, axis, split_axis=0, concat_axis=0, tiled=True)  38.7 us
    ppermute x8, starting transfers between devices, swapped(): return (lax.ppermute(one, 'dev', inner), lax.ppermute(two, 'dev', outer))  33.5 us
    all_to_all x6, waiting for transfers between devices, exchanged(): return lax.all_to_all(blocks, axis, split_axis=0, concat_axis=0, tiled=True)  32.8 us
    pallas_call x14, Pallas kernels, call(): pl.pallas_call(kernel, name=name, out_shape=shapes, in_specs=ins, out_spe...  25.6 us
  transfers between devices with their start and end apart: 14, of which 6 were waited for; matrix products, arithmetic and copies ran while one was open for 0% of the time, Pallas kernels for 14%

profile of v10, /device:TPU:16, one launch (start us, length us, event | category | flops | bytes accessed | tf_op | source)
XLA Modules:
  0.0 134.9 jit_solution(8311331109396401148)
XLA Ops:
  1.9 2.7 %start.1 = (bf16[768,256]{1,0:T(8,128)(2,1)}, bf16[64,4,384]{2,1,0:T(4,128)(2,1)}, bf16[512,128]{1,0:T(8,128)(2,1)S(1)}) custom-call(f32[1]{0:T(128)} %bitcast.2.ridge, s32[1]{0:T(128)S(6)} %copy.14.cluster, s32[1,4]{1,0:T(1,128)} %far_in.1, f32[512,256]{1,0:T(8,128)} %refs_8_.3, f32[64,512]{1,0:T(8,128)} %bitcast.5, s32[1,512]{1,0:T(1,128)} %perm_in.1, ...), custom_call_target="tpu_custom_call" | custom-call | flops 10000000 | tf_op jit(solution)/shard_map/start/pallas_call | solution.py:36
  4.7 10.8 %collective-permute-start.1 = (bf16[768,256]{1,0:T(8,128)(2,1)}, bf16[768,256]{1,0:T(8,128)(2,1)S(1)}, u32[]{:S(2)}, u32[]{:S(2)}) collective-permute-start(bf16[768,256]{1,0:T(8,128)(2,1)} %get-tuple-element.24.places_in.own.refs_2_), channel_id=1, source_target_pairs={{1,2},{2,1},{3,4},{4,3},{5,6},{6,5},{7,8},{8,7},{9,10},{10,9},{11,... | collective-permute-start | bytes 1179656 | tf_op jit(solution)/shard_map/ppermute | solution.py:323
  17.4 10.6 %all-to-all-start = ((bf16[64,4,384]{2,1,0:T(4,128)(2,1)}), bf16[64,4,384]{2,1,0:T(4,128)(2,1)S(1)}, u32[]{:S(2)}, u32[]{:S(2)}) async-start(bf16[64,4,384]{2,1,0:T(4,128)(2,1)} %get-tuple-element.19), calls=%async_computation | async-start | bytes 393216 | tf_op jit(solution)/shard_map/all_to_all | solution.py:327
  28.1 3.4 %collective-permute-start.2 = (bf16[768,256]{1,0:T(8,128)(2,1)S(1)}, bf16[768,256]{1,0:T(8,128)(2,1)S(1)}, u32[]{:S(2)}, u32[]{:S(2)}) collective-permute-start(bf16[768,256]{1,0:T(8,128)(2,1)S(1)} %collective-permute-done.1.p2.v2), channel_id=1, source_target_pairs={{0,1},{1,0},{2,3},{3,2},{4,5},{5,4},{6,7},{7,6},{8,9},{9,8},{10,11... | collective-permute-start | bytes 1179656 | tf_op jit(solution)/shard_map/ppermute | solution.py:323
  31.5 4.6 %collective-permute-start.3 = (bf16[768,256]{1,0:T(8,128)(2,1)S(1)}, bf16[768,256]{1,0:T(8,128)(2,1)S(1)}, u32[]{:S(2)}, u32[]{:S(2)}) collective-permute-start(bf16[768,256]{1,0:T(8,128)(2,1)S(1)} %collective-permute-done.p1.v1), channel_id=1, source_target_pairs={{1,2},{2,1},{3,4},{4,3},{5,6},{6,5},{7,8},{8,7},{9,10},{10,9},{11,... | collective-permute-start | bytes 1179656 | tf_op jit(solution)/shard_map/ppermute | solution.py:323
  36.0 4.1 %all-to-all-done.arrived = bf16[64,4,384]{2,1,0:T(4,128)(2,1)S(1)} async-done(((bf16[64,4,384]{2,1,0:T(4,128)(2,1)}), bf16[64,4,384]{2,1,0:T(4,128)(2,1)S(1)}, u32[]{:S(2)}, u32[]{:S(2)}) %all-to-all-start) | async-done | bytes 196640 | tf_op jit(solution)/shard_map/all_to_all | solution.py:327
  41.2 4.3 %all-to-all-start.1 = ((bf16[8,16,128]{2,1,0:T(8,128)(2,1)}), bf16[8,16,128]{2,1,0:T(8,128)(2,1)S(1)}, u32[]{:S(2)}, u32[]{:S(2)}) async-start(bf16[8,16,128]{2,1,0:T(8,128)(2,1)} %get-tuple-element.20), calls=%async_computation.1 | async-start | bytes 65536 | tf_op jit(solution)/shard_map/all_to_all | solution.py:327
  46.7 4.2 %all-to-all-done.1.all_sums = bf16[8,16,128]{2,1,0:T(8,128)(2,1)S(1)} async-done(((bf16[8,16,128]{2,1,0:T(8,128)(2,1)}), bf16[8,16,128]{2,1,0:T(8,128)(2,1)S(1)}, u32[]{:S(2)}, u32[]{:S(2)}) %all-to-all-start.1) | async-done | bytes 32800 | tf_op jit(solution)/shard_map/all_to_all | solution.py:327
  52.3 5.8 %all-to-all-start.2 = ((bf16[64,4,640]{2,1,0:T(4,128)(2,1)}), bf16[64,4,640]{2,1,0:T(4,128)(2,1)S(1)}, u32[]{:S(2)}, u32[]{:S(2)}) async-start(bf16[64,4,640]{2,1,0:T(4,128)(2,1)} %couple.2._), calls=%async_computation.2 | async-start | bytes 655360 | tf_op jit(solution)/shard_map/all_to_all | solution.py:327
  58.1 3.2 %near_1.2.refs_3_.refs_9_ = f32[512,256]{1,0:T(8,128)S(1)} custom-call(s32[1,4]{1,0:T(1,128)S(1)} %copy-done.11, bf16[768,256]{1,0:T(8,128)(2,1)} %get-tuple-element.24.places_in.own.refs_2_, bf16[768,256]{1,0:T(8,128)(2,1)} %get-tuple-element.24.places_in.own.refs_2_, bf16[768,256]{1,0:T(8,128)(2,1)S(1)} %collective-permute-done.p1.v1, ...), custom_call_target="tpu_custom_call" | custom-call | flops 1000000000 | tf_op jit(solution)/shard_map/near_1/pallas_call | solution.py:36
  63.1 3.0 %near_2.2 = (f32[512,256]{1,0:T(8,128)S(1)}, f32[512,256]{1,0:T(8,128)S(1)}, f32[8,128]{1,0:T(8,128)S(1)}) custom-call(f32[1]{0:T(128)} %bitcast.3.refs_0_, s32[1,4]{1,0:T(1,128)S(1)} %copy-done.11, bf16[768,256]{1,0:T(8,128)(2,1)} %get-tuple-element.24.places_in.own.refs_2_, f32[512,256]{1,0:T(8,128)S(1)} %near_1.2.refs_3_.refs_9_, ...), custom_call_target="tpu_custom_call" | custom-call | flops 10000000000 | tf_op jit(solution)/shard_map/near_2/pallas_call | solution.py:36
  66.1 7.5 %all-to-all-done.2.arrived = bf16[64,4,640]{2,1,0:T(4,128)(2,1)S(1)} async-done(((bf16[64,4,640]{2,1,0:T(4,128)(2,1)}), bf16[64,4,640]{2,1,0:T(4,128)(2,1)S(1)}, u32[]{:S(2)}, u32[]{:S(2)}) %all-to-all-start.2) | async-done | bytes 327712 | tf_op jit(solution)/shard_map/all_to_all | solution.py:327
  73.7 2.0 %middle.1 = (bf16[512,256]{1,0:T(8,128)(2,1)S(1)}, bf16[64,4,256]{2,1,0:T(4,128)(2,1)}, f32[512,256]{1,0:T(8,128)S(1)}) custom-call(bf16[64,4,640]{2,1,0:T(4,128)(2,1)S(1)} %all-to-all-done.2.arrived, bf16[1,4,128,128]{3,2,1,0:T(8,128)(2,1)S(1)} %copy-done.1, bf16[1,128,128]{2,1,0:T(8,128)(2,1)S(1)} %copy-done.2, ...), custom_call_target="tpu_custom_call" | custom-call | flops 10000000 | tf_op jit(solution)/shard_map/middle/pallas_call | solution.py:36
  75.7 2.9 %collective-permute-start.5 = (bf16[512,256]{1,0:T(8,128)(2,1)S(1)}, bf16[512,256]{1,0:T(8,128)(2,1)}, u32[]{:S(2)}, u32[]{:S(2)}) collective-permute-start(bf16[512,256]{1,0:T(8,128)(2,1)S(1)} %get-tuple-element.31.own), channel_id=1, source_target_pairs={{1,2},{2,1},{3,4},{4,3},{5,6},{6,5},{7,8},{8,7},{9,10},{10,9},{11,... | collective-permute-start | bytes 786440 | tf_op jit(solution)/shard_map/ppermute | solution.py:323
  80.6 8.1 %all-to-all-start.3 = ((bf16[64,4,256]{2,1,0:T(4,128)(2,1)}), bf16[64,4,256]{2,1,0:T(4,128)(2,1)S(1)}, u32[]{:S(2)}, u32[]{:S(2)}) async-start(bf16[64,4,256]{2,1,0:T(4,128)(2,1)} %get-tuple-element.28), calls=%async_computation.3 | async-start | bytes 262144 | tf_op jit(solution)/shard_map/all_to_all | solution.py:327
  88.6 3.4 %collective-permute-start.6 = (bf16[512,256]{1,0:T(8,128)(2,1)}, bf16[512,256]{1,0:T(8,128)(2,1)}, u32[]{:S(2)}, u32[]{:S(2)}) collective-permute-start(bf16[512,256]{1,0:T(8,128)(2,1)} %collective-permute-done.5.v2), channel_id=1, source_target_pairs={{0,1},{1,0},{2,3},{3,2},{4,5},{5,4},{6,7},{7,6},{8,9},{9,8},{10,11... | collective-permute-start | bytes 786440 | tf_op jit(solution)/shard_map/ppermute | solution.py:323
  92.0 4.6 %collective-permute-start.7 = (bf16[512,256]{1,0:T(8,128)(2,1)}, bf16[512,256]{1,0:T(8,128)(2,1)}, u32[]{:S(2)}, u32[]{:S(2)}) collective-permute-start(bf16[512,256]{1,0:T(8,128)(2,1)} %collective-permute-done.4.v1), channel_id=1, source_target_pairs={{1,2},{2,1},{3,4},{4,3},{5,6},{6,5},{7,8},{8,7},{9,10},{10,9},{11,... | collective-permute-start | bytes 786440 | tf_op jit(solution)/shard_map/ppermute | solution.py:323
  96.6 3.3 %all-to-all-done.3.arrived = bf16[64,4,256]{2,1,0:T(4,128)(2,1)S(1)} async-done(((bf16[64,4,256]{2,1,0:T(4,128)(2,1)}), bf16[64,4,256]{2,1,0:T(4,128)(2,1)S(1)}, u32[]{:S(2)}, u32[]{:S(2)}) %all-to-all-start.3) | async-done | bytes 131104 | tf_op jit(solution)/shard_map/all_to_all | solution.py:327
  100.8 3.3 %all-to-all-start.4 = ((bf16[8,16,128]{2,1,0:T(8,128)(2,1)}), bf16[8,16,128]{2,1,0:T(8,128)(2,1)S(1)}, u32[]{:S(2)}, u32[]{:S(2)}) async-start(bf16[8,16,128]{2,1,0:T(8,128)(2,1)} %get-tuple-element.29), calls=%async_computation.4 | async-start | bytes 65536 | tf_op jit(solution)/shard_map/all_to_all | solution.py:327
  104.8 4.8 %all-to-all-done.4.all_sums = bf16[8,16,128]{2,1,0:T(8,128)(2,1)S(1)} async-done(((bf16[8,16,128]{2,1,0:T(8,128)(2,1)}), bf16[8,16,128]{2,1,0:T(8,128)(2,1)S(1)}, u32[]{:S(2)}, u32[]{:S(2)}) %all-to-all-start.4) | async-done | bytes 32800 | tf_op jit(solution)/shard_map/all_to_all | solution.py:327
  110.9 6.6 %all-to-all-start.5 = ((bf16[64,4,640]{2,1,0:T(4,128)(2,1)}), bf16[64,4,640]{2,1,0:T(4,128)(2,1)S(1)}, u32[]{:S(2)}, u32[]{:S(2)}) async-start(bf16[64,4,640]{2,1,0:T(4,128)(2,1)} %couple.3._), calls=%async_computation.5 | async-start | bytes 655360 | tf_op jit(solution)/shard_map/all_to_all | solution.py:327
  117.6 3.3 %near_1.3.refs_3_ = f32[512,256]{1,0:T(8,128)S(1)} custom-call(s32[1,4]{1,0:T(1,128)S(1)} %copy-done.11, bf16[768,256]{1,0:T(8,128)(2,1)} %get-tuple-element.24.places_in.own.refs_2_, bf16[512,256]{1,0:T(8,128)(2,1)S(1)} %get-tuple-element.31.own, bf16[768,256]{1,0:T(8,128)(2,1)S(1)} %copy-done.6, bf16[512,256]{1,0:T(8,128)(2,1)} %collective-permute-done.4.v1, ...), custom_call_target="tpu_custom_call" | custom-call | flops 1000000000 | tf_op jit(solution)/shard_map/near_1/pallas_call | solution.py:36
  120.8 3.2 %near_2.3 = (f32[512,256]{1,0:T(8,128)S(1)}, f32[512,256]{1,0:T(8,128)S(1)}, f32[8,128]{1,0:T(8,128)S(1)}) custom-call(f32[1]{0:T(128)} %bitcast.4.refs_0_, s32[1,4]{1,0:T(1,128)S(1)} %copy-done.11, bf16[768,256]{1,0:T(8,128)(2,1)} %get-tuple-element.24.places_in.own.refs_2_, f32[512,256]{1,0:T(8,128)S(1)} %near_1.3.refs_3_, ...), custom_call_target="tpu_custom_call" | custom-call | flops 10000000000 | tf_op jit(solution)/shard_map/near_2/pallas_call | solution.py:36
  124.0 8.8 %all-to-all-done.5.arrived = bf16[64,4,640]{2,1,0:T(4,128)(2,1)S(1)} async-done(((bf16[64,4,640]{2,1,0:T(4,128)(2,1)}), bf16[64,4,640]{2,1,0:T(4,128)(2,1)S(1)}, u32[]{:S(2)}, u32[]{:S(2)}) %all-to-all-start.5) | async-done | bytes 327712 | tf_op jit(solution)/shard_map/all_to_all | solution.py:327
  (42 shorter events, 13.9 us)
Async XLA Ops:
  4.7 23.4 %collective-permute-start.1 = (bf16[768,256]{1,0:T(8,128)(2,1)}, bf16[768,256]{1,0:T(8,128)(2,1)S(1)}, u32[]{:S(2)}, u32[]{:S(2)}) collective-permute-start(bf16[768,256]{1,0:T(8,128)(2,1)} %get-tuple-element.24.places_in.own.refs_2_), channel_id=1, source_target_pairs={{1,2},{2,1},{3,4},{4,3},{5,6},{6,5},{7,8},{8,7},{9,10},{10,9},{11,... | collective-permute-start | bytes 1179656 | tf_op jit(solution)/shard_map/ppermute | solution.py:323
  15.5 15.9 %collective-permute-start = (bf16[768,256]{1,0:T(8,128)(2,1)}, bf16[768,256]{1,0:T(8,128)(2,1)S(1)}, u32[]{:S(2)}, u32[]{:S(2)}) collective-permute-start(bf16[768,256]{1,0:T(8,128)(2,1)} %get-tuple-element.24.places_in.own.refs_2_), channel_id=1, source_target_pairs={{0,1},{1,0},{2,3},{3,2},{4,5},{5,4},{6,7},{7,6},{8,9},{9,8},{10,11... | collective-permute-start | bytes 1179656 | tf_op jit(solution)/shard_map/ppermute | solution.py:323
  17.4 33.5 %copy-start = (bf16[4,4,128,128]{3,2,1,0:T(8,128)(2,1)S(1)}, bf16[4,4,128,128]{3,2,1,0:T(8,128)(2,1)}, u32[]{:S(2)}) copy-start(bf16[4,4,128,128]{3,2,1,0:T(8,128)(2,1)} %blocks.3) | copy-start | bytes 1572868
  17.4 22.7 %all-to-all-start = ((bf16[64,4,384]{2,1,0:T(4,128)(2,1)}), bf16[64,4,384]{2,1,0:T(4,128)(2,1)S(1)}, u32[]{:S(2)}, u32[]{:S(2)}) async-start(bf16[64,4,384]{2,1,0:T(4,128)(2,1)} %get-tuple-element.19), calls=%async_computation | async-start | bytes 393216 | tf_op jit(solution)/shard_map/all_to_all | solution.py:327
  28.0 30.1 %copy-start.3 = (bf16[768,256]{1,0:T(8,128)(2,1)}, bf16[768,256]{1,0:T(8,128)(2,1)S(1)}, u32[]{:S(2)}) copy-start(bf16[768,256]{1,0:T(8,128)(2,1)S(1)} %collective-permute-done.1.p2.v2) | copy-start | bytes 1179652
  28.1 33.3 %collective-permute-start.2 = (bf16[768,256]{1,0:T(8,128)(2,1)S(1)}, bf16[768,256]{1,0:T(8,128)(2,1)S(1)}, u32[]{:S(2)}, u32[]{:S(2)}) collective-permute-start(bf16[768,256]{1,0:T(8,128)(2,1)S(1)} %collective-permute-done.1.p2.v2), channel_id=1, source_target_pairs={{0,1},{1,0},{2,3},{3,2},{4,5},{5,4},{6,7},{7,6},{8,9},{9,8},{10,11... | collective-permute-start | bytes 1179656 | tf_op jit(solution)/shard_map/ppermute | solution.py:323
  31.4 26.7 %copy-start.5 = (bf16[768,256]{1,0:T(8,128)(2,1)}, bf16[768,256]{1,0:T(8,128)(2,1)S(1)}, u32[]{:S(2)}) copy-start(bf16[768,256]{1,0:T(8,128)(2,1)S(1)} %collective-permute-done.p1.v1) | copy-start | bytes 1179652
  31.5 29.9 %collective-permute-start.3 = (bf16[768,256]{1,0:T(8,128)(2,1)S(1)}, bf16[768,256]{1,0:T(8,128)(2,1)S(1)}, u32[]{:S(2)}, u32[]{:S(2)}) collective-permute-start(bf16[768,256]{1,0:T(8,128)(2,1)S(1)} %collective-permute-done.p1.v1), channel_id=1, source_target_pairs={{1,2},{2,1},{3,4},{4,3},{5,6},{6,5},{7,8},{8,7},{9,10},{10,9},{11,... | collective-permute-start | bytes 1179656 | tf_op jit(solution)/shard_map/ppermute | solution.py:323
  41.2 4.3 %copy-start.10 = (s32[4,4]{1,0:T(4,128)S(1)}, s32[4,4]{1,0:T(4,128)}, u32[]{:S(2)}) copy-start(s32[4,4]{1,0:T(4,128)} %far_clusters.1) | copy-start | bytes 196
  41.2 9.8 %all-to-all-start.1 = ((bf16[8,16,128]{2,1,0:T(8,128)(2,1)}), bf16[8,16,128]{2,1,0:T(8,128)(2,1)S(1)}, u32[]{:S(2)}, u32[]{:S(2)}) async-start(bf16[8,16,128]{2,1,0:T(8,128)(2,1)} %get-tuple-element.20), calls=%async_computation.1 | async-start | bytes 65536 | tf_op jit(solution)/shard_map/all_to_all | solution.py:327
  52.3 5.8 %copy-start.11 = (s32[1,4]{1,0:T(1,128)S(1)}, s32[1,4]{1,0:T(1,128)}, u32[]{:S(2)}) copy-start(s32[1,4]{1,0:T(1,128)} %refs_1_.3) | copy-start | bytes 52
  52.3 21.3 %all-to-all-start.2 = ((bf16[64,4,640]{2,1,0:T(4,128)(2,1)}), bf16[64,4,640]{2,1,0:T(4,128)(2,1)S(1)}, u32[]{:S(2)}, u32[]{:S(2)}) async-start(bf16[64,4,640]{2,1,0:T(4,128)(2,1)} %couple.2._), calls=%async_computation.2 | async-start | bytes 655360 | tf_op jit(solution)/shard_map/all_to_all | solution.py:327
  63.1 10.5 %copy-start.1 = (bf16[1,4,128,128]{3,2,1,0:T(8,128)(2,1)S(1)}, bf16[1,4,128,128]{3,2,1,0:T(8,128)(2,1)}, u32[]{:S(2)}) copy-start(bf16[1,4,128,128]{3,2,1,0:T(8,128)(2,1)} %couplings.3) | copy-start | bytes 393220
  63.1 10.5 %copy-start.2 = (bf16[1,128,128]{2,1,0:T(8,128)(2,1)S(1)}, bf16[1,128,128]{2,1,0:T(8,128)(2,1)}, u32[]{:S(2)}) copy-start(bf16[1,128,128]{2,1,0:T(8,128)(2,1)} %transfer.3) | copy-start | bytes 98308
  75.7 12.9 %collective-permute-start.5 = (bf16[512,256]{1,0:T(8,128)(2,1)S(1)}, bf16[512,256]{1,0:T(8,128)(2,1)}, u32[]{:S(2)}, u32[]{:S(2)}) collective-permute-start(bf16[512,256]{1,0:T(8,128)(2,1)S(1)} %get-tuple-element.31.own), channel_id=1, source_target_pairs={{1,2},{2,1},{3,4},{4,3},{5,6},{6,5},{7,8},{8,7},{9,10},{10,9},{11,... | collective-permute-start | bytes 786440 | tf_op jit(solution)/shard_map/ppermute | solution.py:323
  78.6 13.4 %collective-permute-start.4 = (bf16[512,256]{1,0:T(8,128)(2,1)S(1)}, bf16[512,256]{1,0:T(8,128)(2,1)}, u32[]{:S(2)}, u32[]{:S(2)}) collective-permute-start(bf16[512,256]{1,0:T(8,128)(2,1)S(1)} %get-tuple-element.31.own), channel_id=1, source_target_pairs={{0,1},{1,0},{2,3},{3,2},{4,5},{5,4},{6,7},{7,6},{8,9},{9,8},{10,11... | collective-permute-start | bytes 786440 | tf_op jit(solution)/shard_map/ppermute | solution.py:323
  80.6 19.3 %all-to-all-start.3 = ((bf16[64,4,256]{2,1,0:T(4,128)(2,1)}), bf16[64,4,256]{2,1,0:T(4,128)(2,1)S(1)}, u32[]{:S(2)}, u32[]{:S(2)}) async-start(bf16[64,4,256]{2,1,0:T(4,128)(2,1)} %get-tuple-element.28), calls=%async_computation.3 | async-start | bytes 262144 | tf_op jit(solution)/shard_map/all_to_all | solution.py:327
  88.6 32.2 %collective-permute-start.6 = (bf16[512,256]{1,0:T(8,128)(2,1)}, bf16[512,256]{1,0:T(8,128)(2,1)}, u32[]{:S(2)}, u32[]{:S(2)}) collective-permute-start(bf16[512,256]{1,0:T(8,128)(2,1)} %collective-permute-done.5.v2), channel_id=1, source_target_pairs={{0,1},{1,0},{2,3},{3,2},{4,5},{5,4},{6,7},{7,6},{8,9},{9,8},{10,11... | collective-permute-start | bytes 786440 | tf_op jit(solution)/shard_map/ppermute | solution.py:323
  92.0 28.8 %collective-permute-start.7 = (bf16[512,256]{1,0:T(8,128)(2,1)}, bf16[512,256]{1,0:T(8,128)(2,1)}, u32[]{:S(2)}, u32[]{:S(2)}) collective-permute-start(bf16[512,256]{1,0:T(8,128)(2,1)} %collective-permute-done.4.v1), channel_id=1, source_target_pairs={{1,2},{2,1},{3,4},{4,3},{5,6},{6,5},{7,8},{8,7},{9,10},{10,9},{11,... | collective-permute-start | bytes 786440 | tf_op jit(solution)/shard_map/ppermute | solution.py:323
  100.8 8.7 %all-to-all-start.4 = ((bf16[8,16,128]{2,1,0:T(8,128)(2,1)}), bf16[8,16,128]{2,1,0:T(8,128)(2,1)S(1)}, u32[]{:S(2)}, u32[]{:S(2)}) async-start(bf16[8,16,128]{2,1,0:T(8,128)(2,1)} %get-tuple-element.29), calls=%async_computation.4 | async-start | bytes 65536 | tf_op jit(solution)/shard_map/all_to_all | solution.py:327
  109.6 8.0 %copy-start.6 = (bf16[768,256]{1,0:T(8,128)(2,1)S(1)}, bf16[768,256]{1,0:T(8,128)(2,1)}, u32[]{:S(2)}) copy-start(bf16[768,256]{1,0:T(8,128)(2,1)} %copy-done.5) | copy-start | bytes 1179652
  110.9 6.6 %copy-start.4 = (bf16[768,256]{1,0:T(8,128)(2,1)S(1)}, bf16[768,256]{1,0:T(8,128)(2,1)}, u32[]{:S(2)}) copy-start(bf16[768,256]{1,0:T(8,128)(2,1)} %copy-done.3) | copy-start | bytes 1179652
  110.9 21.9 %all-to-all-start.5 = ((bf16[64,4,640]{2,1,0:T(4,128)(2,1)}), bf16[64,4,640]{2,1,0:T(4,128)(2,1)S(1)}, u32[]{:S(2)}, u32[]{:S(2)}) async-start(bf16[64,4,640]{2,1,0:T(4,128)(2,1)} %couple.3._), calls=%async_computation.5 | async-start | bytes 655360 | tf_op jit(solution)/shard_map/all_to_all | solution.py:327
  117.5 3.3 %copy-start.9 = (bf16[768,256]{1,0:T(8,128)(2,1)S(1)}, bf16[768,256]{1,0:T(8,128)(2,1)}, u32[]{:S(2)}) copy-start(bf16[768,256]{1,0:T(8,128)(2,1)} %copy-done.7) | copy-start | bytes 1179652
  (2 other events, 1.7 us)

commit v11 on v10

--- a/solution.py
+++ b/solution.py
@@ -20,7 +20,7 @@
 ANY = pl.BlockSpec(memory_space=pl.ANY)
 HBM = pl.BlockSpec(memory_space=pltpu.HBM)
 LIMIT = 32 * 2**20
-SHORT, MID, LONG = 10**7, 10**9, 10**10
+SHORT, MID, LONG = 10**7, 10**10, 10**10
 ROWS = 128
 
 
@@ -121,7 +121,7 @@
     wait(outs)
 
 
-def owner_sums(staged, told, sums_out, skeletons, narrow, sums, sems):
+def owner_sums(staged, told, sums, skeletons, narrow):
     lane = lax.broadcasted_iota(jnp.int32, (N_DEV, RANK), 1).astype(F32)
     member = jnp.where(lane == told[:, FAR1 : FAR1 + 1], 1.0, 0.0).astype(BF16)
     uplifts = jnp.concatenate([staged[:, i, RANK : 2 * RANK] for i in range(COLS)], axis=1).astype(BF16)
@@ -131,20 +131,18 @@
     out = narrow[...].astype(BF16)
     for g in range(N_GRP):
         sums[g] = out
-    copies = started(((sums, sums_out),), sems)
     skeletons[...] = jnp.concatenate([staged[:, i, :RANK] for i in range(COLS)], axis=1).astype(BF16)
-    wait(copies)
-
-
-def sums_first_kernel(arrived, sums_out, told, skeletons, staged, narrow, sums, sems):
+
+
+def sums_first_kernel(arrived, _, sums, told, skeletons, staged, narrow):
     staged[...] = arrived[...].astype(F32)
     told[...] = staged[:, 0, 2 * RANK :]
-    owner_sums(staged, told[...], sums_out, skeletons, narrow, sums, sems)
-
-
-def sums_kernel(arrived, told, sums_out, skeletons, staged, narrow, sums, sems):
+    owner_sums(staged, told[...], sums, skeletons, narrow)
+
+
+def sums_kernel(arrived, told, sums, skeletons, staged, narrow):
     staged[...] = arrived[...].astype(F32)
-    owner_sums(staged, told[...], sums_out, skeletons, narrow, sums, sems)
+    owner_sums(staged, told[...], sums, skeletons, narrow)
 
 
 def partners_kernel(skeletons, told, sent, staged):
@@ -347,7 +345,7 @@
     wide = pltpu.VMEM(payload, F32)
     told_too, upward = (N_DEV, COLS, 3 * RANK), (N_DEV, COLS, 2 * RANK)
     sums_shape = (N_GRP, COLS * CPG, RANK)
-    narrow = [pltpu.VMEM((COLS * CPG, RANK), F32), pltpu.VMEM(sums_shape, BF16), dma((1,))]
+    narrow = pltpu.VMEM((COLS * CPG, RANK), F32)
 
     wc, sent, basis = call(
         start_kernel,
@@ -438,10 +436,10 @@
     sums, told, skeletons = call(
         sums_first_kernel,
         "sums_first",
-        [(sums_shape, BF16, HBM), ((N_DEV, RANK), F32, VMEM), ((N_DEV, COLS * RANK), BF16, VMEM)],
-        [VMEM],
-        (arrived,),
-        [pltpu.VMEM(told_too, F32), *narrow],
+        [(sums_shape, BF16, VMEM), ((N_DEV, RANK), F32, VMEM), ((N_DEV, COLS * RANK), BF16, VMEM)],
+        [VMEM, ANY],
+        (arrived, picks),
+        [pltpu.VMEM(told_too, F32), narrow],
         SHORT,
     )
     sent, arrived = through_owners(sums, skeletons)
@@ -462,10 +460,10 @@
     sums, skeletons = call(
         sums_kernel,
         "sums",
-        [(sums_shape, BF16, HBM), ((N_DEV, COLS * RANK), BF16, VMEM)],
+        [(sums_shape, BF16, VMEM), ((N_DEV, COLS * RANK), BF16, VMEM)],
         [VMEM, VMEM],
         (arrived, told),
-        [pltpu.VMEM(upward, F32), *narrow],
+        [pltpu.VMEM(upward, F32), narrow],
         SHORT,
     )
     sent, arrived = through_owners(sums, skeletons)

time: 136 us -> 134 us (0.985)
  the two profiles are of different devices: /device:TPU:16 before, /device:TPU:2 now
where the time goes in v11:
time: 134 us; the launch traced here: 133 us
  starting transfers between devices  73.5 us (55%)
  waiting for transfers between devices  29.1 us (22%)
  Pallas kernels  24 us (18%)
  local copies, waits for them, and re-layouts  3.53 us (3%)
  between operations  2.45 us (2%)
    all_to_all x6, starting transfers between devices, exchanged(): return lax.all_to_all(blocks, axis, split_axis=0, concat_axis=0, tiled=True)  52.8 us
    all_to_all x6, waiting for transfers between devices, exchanged(): return lax.all_to_all(blocks, axis, split_axis=0, concat_axis=0, tiled=True)  29.1 us
    pallas_call x14, Pallas kernels, call(): pl.pallas_call(kernel, name=name, out_shape=shapes, in_specs=ins, out_spe...  24 us
    ppermute x8, starting transfers between devices, swapped(): return (lax.ppermute(one, 'dev', inner), lax.ppermute(two, 'dev', outer))  20.7 us
    unnamed x28, local copies, waits for them, and re-layouts  3.53 us
  transfers between devices with their start and end apart: 14, of which 5 were waited for; matrix products, arithmetic and copies ran while one was open for 0% of the time, Pallas kernels for 13%

profile of v11, /device:TPU:2, one launch (start us, length us, event | category | flops | bytes accessed | tf_op | source)
XLA Modules:
  0.0 132.6 jit_solution(11227867356191013207)
XLA Ops:
  1.9 2.7 %start.1 = (bf16[768,256]{1,0:T(8,128)(2,1)}, bf16[64,4,384]{2,1,0:T(4,128)(2,1)}, bf16[512,128]{1,0:T(8,128)(2,1)S(1)}) custom-call(f32[1]{0:T(128)} %bitcast.2.ridge, s32[1]{0:T(128)S(6)} %copy.14.cluster, s32[1,4]{1,0:T(1,128)} %far_in.1, f32[512,256]{1,0:T(8,128)} %refs_8_.3, f32[64,512]{1,0:T(8,128)} %bitcast.5, s32[1,512]{1,0:T(1,128)} %perm_in.1, ...), custom_call_target="tpu_custom_call" | custom-call | flops 10000000 | tf_op jit(solution)/shard_map/start/pallas_call | solution.py:36
  4.7 16.7 %all-to-all-start = ((bf16[64,4,384]{2,1,0:T(4,128)(2,1)}), bf16[64,4,384]{2,1,0:T(4,128)(2,1)S(1)}, u32[]{:S(2)}, u32[]{:S(2)}) async-start(bf16[64,4,384]{2,1,0:T(4,128)(2,1)} %get-tuple-element.19), calls=%async_computation | async-start | bytes 393216 | tf_op jit(solution)/shard_map/all_to_all | solution.py:325
  22.1 6.2 %collective-permute-start = (bf16[768,256]{1,0:T(8,128)(2,1)S(1)}, bf16[768,256]{1,0:T(8,128)(2,1)S(1)}, u32[]{:S(2)}, u32[]{:S(2)}) collective-permute-start(bf16[768,256]{1,0:T(8,128)(2,1)S(1)} %copy-done.13), channel_id=1, source_target_pairs={{0,1},{1,0},{2,3},{3,2},{4,5},{5,4},{6,7},{7,6},{8,9},{9,8},{10,11... | collective-permute-start | bytes 1179656 | tf_op jit(solution)/shard_map/ppermute | solution.py:321
  29.0 6.3 %all-to-all-done.arrived = bf16[64,4,384]{2,1,0:T(4,128)(2,1)S(1)} async-done(((bf16[64,4,384]{2,1,0:T(4,128)(2,1)}), bf16[64,4,384]{2,1,0:T(4,128)(2,1)S(1)}, u32[]{:S(2)}, u32[]{:S(2)}) %all-to-all-start) | async-done | bytes 196640 | tf_op jit(solution)/shard_map/all_to_all | solution.py:325
  36.3 4.8 %all-to-all-start.1 = ((bf16[8,16,128]{2,1,0:T(8,128)(2,1)}), bf16[8,16,128]{2,1,0:T(8,128)(2,1)S(1)}, u32[]{:S(2)}, u32[]{:S(2)}) async-start(bf16[8,16,128]{2,1,0:T(8,128)(2,1)} %get-tuple-element.20), calls=%async_computation.1 | async-start | bytes 65536 | tf_op jit(solution)/shard_map/all_to_all | solution.py:325
  41.7 2.5 %collective-permute-start.2 = (bf16[768,256]{1,0:T(8,128)(2,1)S(1)}, bf16[768,256]{1,0:T(8,128)(2,1)S(1)}, u32[]{:S(2)}, u32[]{:S(2)}) collective-permute-start(bf16[768,256]{1,0:T(8,128)(2,1)S(1)} %collective-permute-done.1.p2.v2), channel_id=1, source_target_pairs={{0,1},{1,0},{2,3},{3,2},{4,5},{5,4},{6,7},{7,6},{8,9},{9,8},{10,11... | collective-permute-start | bytes 1179656 | tf_op jit(solution)/shard_map/ppermute | solution.py:321
  45.1 1.3 %couple.2._ = bf16[64,4,640]{2,1,0:T(4,128)(2,1)} custom-call(bf16[64,128]{1,0:T(8,128)(2,1)S(1)} %prepare.1._.picks, bf16[8,16,128]{2,1,0:T(8,128)(2,1)S(1)} %all-to-all-done.1.all_sums, bf16[4,4,128,128]{3,2,1,0:T(8,128)(2,1)S(1)} %copy-done, f32[64,128]{1,0:T(8,128)S(1)} %get-tuple-element.21.told, bf16[64,4,512]{2,1,0:T(4,128)(2,1)S(1)} %partners.2), custom_call_target="tpu_custom_call" | custom-call | flops 10000000 | tf_op jit(solution)/shard_map/couple/pallas_call | solution.py:36
  46.5 9.2 %all-to-all-start.2 = ((bf16[64,4,640]{2,1,0:T(4,128)(2,1)}), bf16[64,4,640]{2,1,0:T(4,128)(2,1)S(1)}, u32[]{:S(2)}, u32[]{:S(2)}) async-start(bf16[64,4,640]{2,1,0:T(4,128)(2,1)} %couple.2._), calls=%async_computation.2 | async-start | bytes 655360 | tf_op jit(solution)/shard_map/all_to_all | solution.py:325
  55.7 2.7 %near_1.2.refs_3_.refs_9_ = f32[512,256]{1,0:T(8,128)S(1)} custom-call(s32[1,4]{1,0:T(1,128)S(1)} %copy-done.12, bf16[768,256]{1,0:T(8,128)(2,1)} %get-tuple-element.24.places_in.own.refs_2_, bf16[768,256]{1,0:T(8,128)(2,1)} %get-tuple-element.24.places_in.own.refs_2_, bf16[768,256]{1,0:T(8,128)(2,1)S(1)} %collective-permute-done.p1.v1, ...), custom_call_target="tpu_custom_call" | custom-call | flops 10000000000 | tf_op jit(solution)/shard_map/near_1/pallas_call | solution.py:36
  61.8 3.0 %near_2.2 = (f32[512,256]{1,0:T(8,128)S(1)}, f32[512,256]{1,0:T(8,128)S(1)}, f32[8,128]{1,0:T(8,128)S(1)}) custom-call(f32[1]{0:T(128)} %bitcast.3.refs_0_, s32[1,4]{1,0:T(1,128)S(1)} %copy-done.12, bf16[768,256]{1,0:T(8,128)(2,1)} %get-tuple-element.24.places_in.own.refs_2_, f32[512,256]{1,0:T(8,128)S(1)} %near_1.2.refs_3_.refs_9_, ...), custom_call_target="tpu_custom_call" | custom-call | flops 10000000000 | tf_op jit(solution)/shard_map/near_2/pallas_call | solution.py:36
  64.8 6.5 %all-to-all-done.2.arrived = bf16[64,4,640]{2,1,0:T(4,128)(2,1)S(1)} async-done(((bf16[64,4,640]{2,1,0:T(4,128)(2,1)}), bf16[64,4,640]{2,1,0:T(4,128)(2,1)S(1)}, u32[]{:S(2)}, u32[]{:S(2)}) %all-to-all-start.2) | async-done | bytes 327712 | tf_op jit(solution)/shard_map/all_to_all | solution.py:325
  71.3 2.0 %middle.1 = (bf16[512,256]{1,0:T(8,128)(2,1)S(1)}, bf16[64,4,256]{2,1,0:T(4,128)(2,1)}, f32[512,256]{1,0:T(8,128)S(1)}) custom-call(bf16[64,4,640]{2,1,0:T(4,128)(2,1)S(1)} %all-to-all-done.2.arrived, bf16[1,4,128,128]{3,2,1,0:T(8,128)(2,1)S(1)} %copy-done.1, bf16[1,128,128]{2,1,0:T(8,128)(2,1)S(1)} %copy-done.2, ...), custom_call_target="tpu_custom_call" | custom-call | flops 10000000 | tf_op jit(solution)/shard_map/middle/pallas_call | solution.py:36
  73.4 7.2 %all-to-all-start.3 = ((bf16[64,4,256]{2,1,0:T(4,128)(2,1)}), bf16[64,4,256]{2,1,0:T(4,128)(2,1)S(1)}, u32[]{:S(2)}, u32[]{:S(2)}) async-start(bf16[64,4,256]{2,1,0:T(4,128)(2,1)} %get-tuple-element.28), calls=%async_computation.3 | async-start | bytes 262144 | tf_op jit(solution)/shard_map/all_to_all | solution.py:325
  81.3 6.2 %collective-permute-start.4 = (bf16[512,256]{1,0:T(8,128)(2,1)S(1)}, bf16[512,256]{1,0:T(8,128)(2,1)S(1)}, u32[]{:S(2)}, u32[]{:S(2)}) collective-permute-start(bf16[512,256]{1,0:T(8,128)(2,1)S(1)} %get-tuple-element.31.own), channel_id=1, source_target_pairs={{0,1},{1,0},{2,3},{3,2},{4,5},{5,4},{6,7},{7,6},{8,9},{9,8},{10,11... | collective-permute-start | bytes 786440 | tf_op jit(solution)/shard_map/ppermute | solution.py:321
  87.5 5.8 %all-to-all-done.3.arrived = bf16[64,4,256]{2,1,0:T(4,128)(2,1)S(1)} async-done(((bf16[64,4,256]{2,1,0:T(4,128)(2,1)}), bf16[64,4,256]{2,1,0:T(4,128)(2,1)S(1)}, u32[]{:S(2)}, u32[]{:S(2)}) %all-to-all-start.3) | async-done | bytes 131104 | tf_op jit(solution)/shard_map/all_to_all | solution.py:325
  94.2 5.6 %all-to-all-start.4 = ((bf16[8,16,128]{2,1,0:T(8,128)(2,1)}), bf16[8,16,128]{2,1,0:T(8,128)(2,1)S(1)}, u32[]{:S(2)}, u32[]{:S(2)}) async-start(bf16[8,16,128]{2,1,0:T(8,128)(2,1)} %get-tuple-element.29), calls=%async_computation.4 | async-start | bytes 65536 | tf_op jit(solution)/shard_map/all_to_all | solution.py:325
  100.4 2.4 %collective-permute-start.6 = (bf16[512,256]{1,0:T(8,128)(2,1)S(1)}, bf16[512,256]{1,0:T(8,128)(2,1)S(1)}, u32[]{:S(2)}, u32[]{:S(2)}) collective-permute-start(bf16[512,256]{1,0:T(8,128)(2,1)S(1)} %collective-permute-done.5.v2), channel_id=1, source_target_pairs={{0,1},{1,0},{2,3},{3,2},{4,5},{5,4},{6,7},{7,6},{8,9},{9,8},{10,11... | collective-permute-start | bytes 786440 | tf_op jit(solution)/shard_map/ppermute | solution.py:321
  102.9 1.4 %collective-permute-start.7 = (bf16[512,256]{1,0:T(8,128)(2,1)S(1)}, bf16[512,256]{1,0:T(8,128)(2,1)}, u32[]{:S(2)}, u32[]{:S(2)}) collective-permute-start(bf16[512,256]{1,0:T(8,128)(2,1)S(1)} %collective-permute-done.4.v1), channel_id=1, source_target_pairs={{1,2},{2,1},{3,4},{4,3},{5,6},{6,5},{7,8},{8,7},{9,10},{10,9},{11,... | collective-permute-start | bytes 786440 | tf_op jit(solution)/shard_map/ppermute | solution.py:321
  104.2 1.4 %couple.3._ = bf16[64,4,640]{2,1,0:T(4,128)(2,1)} custom-call(bf16[64,128]{1,0:T(8,128)(2,1)S(1)} %prepare.1._.picks, bf16[8,16,128]{2,1,0:T(8,128)(2,1)S(1)} %all-to-all-done.4.all_sums, bf16[4,4,128,128]{3,2,1,0:T(8,128)(2,1)S(1)} %copy-done, f32[64,128]{1,0:T(8,128)S(1)} %get-tuple-element.21.told, bf16[64,4,512]{2,1,0:T(4,128)(2,1)S(1)} %partners.3), custom_call_target="tpu_custom_call" | custom-call | flops 10000000 | tf_op jit(solution)/shard_map/couple/pallas_call | solution.py:36
  105.6 9.2 %all-to-all-start.5 = ((bf16[64,4,640]{2,1,0:T(4,128)(2,1)}), bf16[64,4,640]{2,1,0:T(4,128)(2,1)S(1)}, u32[]{:S(2)}, u32[]{:S(2)}) async-start(bf16[64,4,640]{2,1,0:T(4,128)(2,1)} %couple.3._), calls=%async_computation.5 | async-start | bytes 655360 | tf_op jit(solution)/shard_map/all_to_all | solution.py:325
  114.9 2.2 %near_1.3.refs_3_ = f32[512,256]{1,0:T(8,128)S(1)} custom-call(s32[1,4]{1,0:T(1,128)S(1)} %copy-done.12, bf16[768,256]{1,0:T(8,128)(2,1)} %get-tuple-element.24.places_in.own.refs_2_, bf16[512,256]{1,0:T(8,128)(2,1)S(1)} %get-tuple-element.31.own, bf16[768,256]{1,0:T(8,128)(2,1)S(1)} %copy-done.4, bf16[512,256]{1,0:T(8,128)(2,1)S(1)} %collective-permute-done.4.v1, ...), custom_call_target="tpu_custom_call" | custom-call | flops 10000000000 | tf_op jit(solution)/shard_map/near_1/pallas_call | solution.py:36
  117.2 3.1 %near_2.3 = (f32[512,256]{1,0:T(8,128)S(1)}, f32[512,256]{1,0:T(8,128)S(1)}, f32[8,128]{1,0:T(8,128)S(1)}) custom-call(f32[1]{0:T(128)} %bitcast.4.refs_0_, s32[1,4]{1,0:T(1,128)S(1)} %copy-done.12, bf16[768,256]{1,0:T(8,128)(2,1)} %get-tuple-element.24.places_in.own.refs_2_, f32[512,256]{1,0:T(8,128)S(1)} %near_1.3.refs_3_, bf16[768,256]{1,0:T(8,128)(2,1)S(1)} %copy-done.7, ...), custom_call_target="tpu_custom_call" | custom-call | flops 10000000000 | tf_op jit(solution)/shard_map/near_2/pallas_call | solution.py:36
  120.3 10.3 %all-to-all-done.5.arrived = bf16[64,4,640]{2,1,0:T(4,128)(2,1)S(1)} async-done(((bf16[64,4,640]{2,1,0:T(4,128)(2,1)}), bf16[64,4,640]{2,1,0:T(4,128)(2,1)S(1)}, u32[]{:S(2)}, u32[]{:S(2)}) %all-to-all-start.5) | async-done | bytes 327712 | tf_op jit(solution)/shard_map/all_to_all | solution.py:325
  130.6 1.9 %end.1 = (f32[512,256]{1,0:T(8,128)}, f32[512,256]{1,0:T(8,128)}) custom-call(bf16[64,4,640]{2,1,0:T(4,128)(2,1)S(1)} %all-to-all-done.5.arrived, bf16[1,4,128,128]{3,2,1,0:T(8,128)(2,1)S(1)} %copy-done.1, bf16[1,128,128]{2,1,0:T(8,128)(2,1)S(1)} %copy-done.2, bf16[512,128]{1,0:T(8,128)(2,1)S(1)} %get-tuple-element.23.basis, ...), custom_call_target="tpu_custom_call" | custom-call | flops 10000000 | tf_op jit(solution)/shard_map/end/pallas_call | solution.py:36
  (46 shorter events, 9.5 us)
Async XLA Ops:
  1.9 26.4 %copy-start.11 = (s32[4,4]{1,0:T(4,128)S(1)}, s32[4,4]{1,0:T(4,128)}, u32[]{:S(2)}) copy-start(s32[4,4]{1,0:T(4,128)} %far_clusters.1) | copy-start | bytes 196
  4.7 16.8 %copy-start.13 = (bf16[768,256]{1,0:T(8,128)(2,1)S(1)}, bf16[768,256]{1,0:T(8,128)(2,1)}, u32[]{:S(2)}) copy-start(bf16[768,256]{1,0:T(8,128)(2,1)} %get-tuple-element.24.places_in.own.refs_2_) | copy-start | bytes 1179652
  4.7 40.4 %copy-start = (bf16[4,4,128,128]{3,2,1,0:T(8,128)(2,1)S(1)}, bf16[4,4,128,128]{3,2,1,0:T(8,128)(2,1)}, u32[]{:S(2)}) copy-start(bf16[4,4,128,128]{3,2,1,0:T(8,128)(2,1)} %blocks.3) | copy-start | bytes 1572868
  4.7 30.6 %all-to-all-start = ((bf16[64,4,384]{2,1,0:T(4,128)(2,1)}), bf16[64,4,384]{2,1,0:T(4,128)(2,1)S(1)}, u32[]{:S(2)}, u32[]{:S(2)}) async-start(bf16[64,4,384]{2,1,0:T(4,128)(2,1)} %get-tuple-element.19), calls=%async_computation | async-start | bytes 393216 | tf_op jit(solution)/shard_map/all_to_all | solution.py:325
  21.4 20.2 %collective-permute-start.1 = (bf16[768,256]{1,0:T(8,128)(2,1)S(1)}, bf16[768,256]{1,0:T(8,128)(2,1)S(1)}, u32[]{:S(2)}, u32[]{:S(2)}) collective-permute-start(bf16[768,256]{1,0:T(8,128)(2,1)S(1)} %copy-done.13), channel_id=1, source_target_pairs={{1,2},{2,1},{3,4},{4,3},{5,6},{6,5},{7,8},{8,7},{9,10},{10,9},{11,... | collective-permute-start | bytes 1179656 | tf_op jit(solution)/shard_map/ppermute | solution.py:321
  22.1 22.1 %collective-permute-start = (bf16[768,256]{1,0:T(8,128)(2,1)S(1)}, bf16[768,256]{1,0:T(8,128)(2,1)S(1)}, u32[]{:S(2)}, u32[]{:S(2)}) collective-permute-start(bf16[768,256]{1,0:T(8,128)(2,1)S(1)} %copy-done.13), channel_id=1, source_target_pairs={{0,1},{1,0},{2,3},{3,2},{4,5},{5,4},{6,7},{7,6},{8,9},{9,8},{10,11... | collective-permute-start | bytes 1179656 | tf_op jit(solution)/shard_map/ppermute | solution.py:321
  36.3 8.8 %all-to-all-start.1 = ((bf16[8,16,128]{2,1,0:T(8,128)(2,1)}), bf16[8,16,128]{2,1,0:T(8,128)(2,1)S(1)}, u32[]{:S(2)}, u32[]{:S(2)}) async-start(bf16[8,16,128]{2,1,0:T(8,128)(2,1)} %get-tuple-element.20), calls=%async_computation.1 | async-start | bytes 65536 | tf_op jit(solution)/shard_map/all_to_all | solution.py:325
  41.7 16.7 %collective-permute-start.2 = (bf16[768,256]{1,0:T(8,128)(2,1)S(1)}, bf16[768,256]{1,0:T(8,128)(2,1)S(1)}, u32[]{:S(2)}, u32[]{:S(2)}) collective-permute-start(bf16[768,256]{1,0:T(8,128)(2,1)S(1)} %collective-permute-done.1.p2.v2), channel_id=1, source_target_pairs={{0,1},{1,0},{2,3},{3,2},{4,5},{5,4},{6,7},{7,6},{8,9},{9,8},{10,11... | collective-permute-start | bytes 1179656 | tf_op jit(solution)/shard_map/ppermute | solution.py:321
  44.2 11.4 %copy-start.3 = (bf16[768,256]{1,0:T(8,128)(2,1)}, bf16[768,256]{1,0:T(8,128)(2,1)S(1)}, u32[]{:S(2)}) copy-start(bf16[768,256]{1,0:T(8,128)(2,1)S(1)} %collective-permute-done.p1.v1) | copy-start | bytes 1179652
  44.2 14.9 %collective-permute-start.3 = (bf16[768,256]{1,0:T(8,128)(2,1)S(1)}, bf16[768,256]{1,0:T(8,128)(2,1)S(1)}, u32[]{:S(2)}, u32[]{:S(2)}) collective-permute-start(bf16[768,256]{1,0:T(8,128)(2,1)S(1)} %collective-permute-done.p1.v1), channel_id=1, source_target_pairs={{1,2},{2,1},{3,4},{4,3},{5,6},{6,5},{7,8},{8,7},{9,10},{10,9},{11,... | collective-permute-start | bytes 1179656 | tf_op jit(solution)/shard_map/ppermute | solution.py:321
  46.4 9.2 %copy-start.12 = (s32[1,4]{1,0:T(1,128)S(1)}, s32[1,4]{1,0:T(1,128)}, u32[]{:S(2)}) copy-start(s32[1,4]{1,0:T(1,128)} %refs_1_.3) | copy-start | bytes 52
  46.5 24.9 %all-to-all-start.2 = ((bf16[64,4,640]{2,1,0:T(4,128)(2,1)}), bf16[64,4,640]{2,1,0:T(4,128)(2,1)S(1)}, u32[]{:S(2)}, u32[]{:S(2)}) async-start(bf16[64,4,640]{2,1,0:T(4,128)(2,1)} %couple.2._), calls=%async_computation.2 | async-start | bytes 655360 | tf_op jit(solution)/shard_map/all_to_all | solution.py:325
  61.8 9.5 %copy-start.1 = (bf16[1,4,128,128]{3,2,1,0:T(8,128)(2,1)S(1)}, bf16[1,4,128,128]{3,2,1,0:T(8,128)(2,1)}, u32[]{:S(2)}) copy-start(bf16[1,4,128,128]{3,2,1,0:T(8,128)(2,1)} %couplings.3) | copy-start | bytes 393220
  61.8 9.5 %copy-start.2 = (bf16[1,128,128]{2,1,0:T(8,128)(2,1)S(1)}, bf16[1,128,128]{2,1,0:T(8,128)(2,1)}, u32[]{:S(2)}) copy-start(bf16[1,128,128]{2,1,0:T(8,128)(2,1)} %transfer.3) | copy-start | bytes 98308
  73.4 19.9 %all-to-all-start.3 = ((bf16[64,4,256]{2,1,0:T(4,128)(2,1)}), bf16[64,4,256]{2,1,0:T(4,128)(2,1)S(1)}, u32[]{:S(2)}, u32[]{:S(2)}) async-start(bf16[64,4,256]{2,1,0:T(4,128)(2,1)} %get-tuple-element.28), calls=%async_computation.3 | async-start | bytes 262144 | tf_op jit(solution)/shard_map/all_to_all | solution.py:325
  80.6 19.8 %collective-permute-start.5 = (bf16[512,256]{1,0:T(8,128)(2,1)S(1)}, bf16[512,256]{1,0:T(8,128)(2,1)S(1)}, u32[]{:S(2)}, u32[]{:S(2)}) collective-permute-start(bf16[512,256]{1,0:T(8,128)(2,1)S(1)} %get-tuple-element.31.own), channel_id=1, source_target_pairs={{1,2},{2,1},{3,4},{4,3},{5,6},{6,5},{7,8},{8,7},{9,10},{10,9},{11,... | collective-permute-start | bytes 786440 | tf_op jit(solution)/shard_map/ppermute | solution.py:321
  81.3 21.5 %collective-permute-start.4 = (bf16[512,256]{1,0:T(8,128)(2,1)S(1)}, bf16[512,256]{1,0:T(8,128)(2,1)S(1)}, u32[]{:S(2)}, u32[]{:S(2)}) collective-permute-start(bf16[512,256]{1,0:T(8,128)(2,1)S(1)} %get-tuple-element.31.own), channel_id=1, source_target_pairs={{0,1},{1,0},{2,3},{3,2},{4,5},{5,4},{6,7},{7,6},{8,9},{9,8},{10,11... | collective-permute-start | bytes 786440 | tf_op jit(solution)/shard_map/ppermute | solution.py:321
  94.2 10.0 %all-to-all-start.4 = ((bf16[8,16,128]{2,1,0:T(8,128)(2,1)}), bf16[8,16,128]{2,1,0:T(8,128)(2,1)S(1)}, u32[]{:S(2)}, u32[]{:S(2)}) async-start(bf16[8,16,128]{2,1,0:T(8,128)(2,1)} %get-tuple-element.29), calls=%async_computation.4 | async-start | bytes 65536 | tf_op jit(solution)/shard_map/all_to_all | solution.py:325
  100.4 16.7 %collective-permute-start.6 = (bf16[512,256]{1,0:T(8,128)(2,1)S(1)}, bf16[512,256]{1,0:T(8,128)(2,1)S(1)}, u32[]{:S(2)}, u32[]{:S(2)}) collective-permute-start(bf16[512,256]{1,0:T(8,128)(2,1)S(1)} %collective-permute-done.5.v2), channel_id=1, source_target_pairs={{0,1},{1,0},{2,3},{3,2},{4,5},{5,4},{6,7},{7,6},{8,9},{9,8},{10,11... | collective-permute-start | bytes 786440 | tf_op jit(solution)/shard_map/ppermute | solution.py:321
  102.9 14.3 %collective-permute-start.7 = (bf16[512,256]{1,0:T(8,128)(2,1)S(1)}, bf16[512,256]{1,0:T(8,128)(2,1)}, u32[]{:S(2)}, u32[]{:S(2)}) collective-permute-start(bf16[512,256]{1,0:T(8,128)(2,1)S(1)} %collective-permute-done.4.v1), channel_id=1, source_target_pairs={{1,2},{2,1},{3,4},{4,3},{5,6},{6,5},{7,8},{8,7},{9,10},{10,9},{11,... | collective-permute-start | bytes 786440 | tf_op jit(solution)/shard_map/ppermute | solution.py:321
  105.6 9.3 %copy-start.4 = (bf16[768,256]{1,0:T(8,128)(2,1)S(1)}, bf16[768,256]{1,0:T(8,128)(2,1)}, u32[]{:S(2)}) copy-start(bf16[768,256]{1,0:T(8,128)(2,1)} %copy-done.3) | copy-start | bytes 1179652
  105.6 25.0 %all-to-all-start.5 = ((bf16[64,4,640]{2,1,0:T(4,128)(2,1)}), bf16[64,4,640]{2,1,0:T(4,128)(2,1)S(1)}, u32[]{:S(2)}, u32[]{:S(2)}) async-start(bf16[64,4,640]{2,1,0:T(4,128)(2,1)} %couple.3._), calls=%async_computation.5 | async-start | bytes 655360 | tf_op jit(solution)/shard_map/all_to_all | solution.py:325
  114.9 2.3 %copy-start.7 = (bf16[768,256]{1,0:T(8,128)(2,1)S(1)}, bf16[768,256]{1,0:T(8,128)(2,1)}, u32[]{:S(2)}) copy-start(bf16[768,256]{1,0:T(8,128)(2,1)} %copy-done.5) | copy-start | bytes 1179652
  114.9 2.3 %copy-start.10 = (bf16[768,256]{1,0:T(8,128)(2,1)S(1)}, bf16[768,256]{1,0:T(8,128)(2,1)}, u32[]{:S(2)}) copy-start(bf16[768,256]{1,0:T(8,128)(2,1)} %copy-done.8) | copy-start | bytes 1179652
  (4 other events, 3.5 us)

commit v12 on v11

--- a/solution.py
+++ b/solution.py
@@ -21,6 +21,7 @@
 HBM = pl.BlockSpec(memory_space=pltpu.HBM)
 LIMIT = 32 * 2**20
 SHORT, MID, LONG = 10**7, 10**10, 10**10
+LATER, LAST = 10**10, 10**7
 ROWS = 128
 
 
@@ -256,38 +257,38 @@
         total[part] = product if fresh else total[part] + product
 
 
-def near_products(distance, near_list, mine, places, values, total):
-    ahead = distance * (1 - 2 * (lax.axis_index("dev") % 2))
-    for i, offset in enumerate((ahead, -ahead)):
+def add_near(offsets, near_list, mine, places, values, total):
+    for i, offset in enumerate(offsets):
 
         @pl.when(listed(near_list, offset))
         def _():
             block_times(mine, coordinates(places[1 + i]), values[i], total, False)
 
 
-def near_pairs(places_in, p1, v1, p2, v2, places, values):
-    pairs = [(p.at[pl.ds(LEAF, 4 * DIM)], places.at[i]) for i, p in enumerate((places_in, p1, p2))]
-    return pairs + [(v.at[pl.ds(0, LEAF)], values.at[i]) for i, v in enumerate((v1, v2))]
-
-
-def near_1_kernel(near_list, places_in, own, p1, v1, p2, v2, _, total, places, values, sems):
-    pairs = near_pairs(places_in, p1, v1, p2, v2, places, values)
-    wait(started([*pairs, (own.at[pl.ds(0, LEAF)], values.at[2])], sems))
+def offsets_of(swaps):
+    ahead = 1 - 2 * (lax.axis_index("dev") % 2)
+    return [ahead * way for way in swaps]
+
+
+def near_1_kernel(swaps, near_list, places_in, own, *refs):
+    n = len(swaps)
+    total, places, values, sems = refs[2 * n + 1 :]
+    pairs = [(p.at[pl.ds(LEAF, 4 * DIM)], places.at[i]) for i, p in enumerate((places_in, *refs[: 2 * n : 2]))]
+    pairs += [(v.at[pl.ds(0, LEAF)], values.at[i]) for i, v in enumerate((*refs[1 : 2 * n : 2], own))]
+    wait(started(pairs, sems))
     mine = coordinates(places[0])
-    block_times(mine, mine, values[2], total, True)
-    near_products(1, near_list, mine, places, values, total)
-
-
-def near_2_kernel(
-    last, ridge, near_list, places_in, before, p1, v1, p2, v2, rs_in, r1, residual, other, factor,
-    total, places, values, rs, sems,
-):
-    pairs = near_pairs(places_in, p1, v1, p2, v2, places, values)
-    copies = started([*pairs, (before, total), (rs_in, rs)], sems)
-    if last:
-        copies += started(((r1, residual),), sems, 7)
-    wait(copies)
-    near_products(2, near_list, coordinates(places[0]), places, values, total)
+    block_times(mine, mine, values[n], total, True)
+    add_near(offsets_of(swaps), near_list, mine, places, values, total)
+
+
+def near_2_kernel(swaps, last, ridge, near_list, places_in, before, *refs):
+    n = len(swaps)
+    rs_in, r1, residual, other, factor, total, places, values, rs, sems = refs[2 * n :]
+    pairs = [(p.at[pl.ds(LEAF, 4 * DIM)], places.at[i]) for i, p in enumerate((places_in, *refs[: 2 * n : 2]))]
+    pairs += [(v.at[pl.ds(0, LEAF)], values.at[i]) for i, v in enumerate(refs[1 : 2 * n : 2])]
+    pairs += [(before, total), (rs_in, rs)] + ([(r1, residual)] if last else [])
+    wait(started(pairs, sems))
+    add_near(offsets_of(swaps), near_list, coordinates(places[0]), places, values, total)
     ridge, centre, first, second = chebyshev(ridge[0])
     d1 = rs[...] / centre
     if last:
@@ -372,33 +373,35 @@
         SHORT,
     )
 
-    def near_1(own, first, fields, after):
+    def near_1(swaps, own, first, fields, after, flops):
+        n = len(swaps)
         (near,) = call(
-            near_1_kernel,
+            lambda *refs: near_1_kernel(swaps, *refs),
             "near_1",
             [(field, F32, VMEM)],
-            [SMEM, HBM] + [ANY] * 5 + [HBM],
-            (near_list, wc, own, first[0], fields[0], first[1], fields[1], after),
-            [pltpu.VMEM((3, 4 * DIM, OUT), BF16), pltpu.VMEM((3, *field), BF16), dma((6,))],
-            MID,
+            [SMEM, HBM] + [ANY] * (1 + 2 * n) + [HBM],
+            (near_list, wc, own, *[x for pair in zip(first, fields) for x in pair], after),
+            [pltpu.VMEM((1 + n, 4 * DIM, OUT), BF16), pltpu.VMEM((1 + n, *field), BF16), dma((2 + 2 * n,))],
+            flops,
         )
         return near
 
-    def near_2(last, near, first, fields, r1):
+    def near_2(swaps, last, near, first, fields, r1, flops):
+        n = len(swaps)
         return call(
-            lambda *refs: near_2_kernel(last, *refs),
+            lambda *refs: near_2_kernel(swaps, last, *refs),
             "near_2",
             [(field, F32, VMEM), (field, F32, VMEM), ((8, RANK), F32, VMEM)],
-            [SMEM, SMEM, HBM] + [ANY] * 5 + [HBM, ANY],
-            (ridge, near_list, wc, near, first[0], fields[0], first[1], fields[1], right_side, r1),
+            [SMEM, SMEM, HBM] + [ANY] * (1 + 2 * n) + [HBM, ANY],
+            (ridge, near_list, wc, near, *[x for pair in zip(first, fields) for x in pair], right_side, r1),
             [
                 pltpu.VMEM(field, F32),
-                pltpu.VMEM((3, 4 * DIM, OUT), BF16),
-                pltpu.VMEM((2, *field), BF16),
+                pltpu.VMEM((1 + n, 4 * DIM, OUT), BF16),
+                pltpu.VMEM((n, *field), BF16),
                 pltpu.VMEM(field, F32),
-                dma((8,)),
+                dma((4 + 2 * n,)),
             ],
-            LONG,
+            flops,
         )
 
     def through_owners(sums, skeletons):
@@ -444,8 +447,8 @@
     )
     sent, arrived = through_owners(sums, skeletons)
     first2 = swapped(*first1[::-1])
-    near = near_1(wc, first1, first1, sent)
-    residual, direction, factor = near_2(False, near, first2, first2, near)
+    near = near_1((1, -1), wc, first1, first1, sent, MID)
+    residual, direction, factor = near_2((2, -2), False, near, first2, first2, near, LONG)
     w, sent, r1 = call(
         middle_kernel,
         "middle",
@@ -468,8 +471,8 @@
     )
     sent, arrived = through_owners(sums, skeletons)
     fields2 = swapped(*fields1[::-1])
-    near = near_1(w, first1, fields1, sent)
-    residual, total, factor = near_2(True, near, first2, fields2, r1)
+    near = near_1((1, -1, 2), w, (*first1, first2[0]), (*fields1, fields2[0]), sent, LATER)
+    residual, total, factor = near_2((-2,), True, near, first2[1:], fields2[1:], r1, LAST)
     return tuple(
         call(
             end_kernel,

time: 134 us -> 132 us (0.985)
  the two profiles are of different devices: /device:TPU:2 before, /device:TPU:16 now
where the time goes in v12:
time: 132 us; the launch traced here: 131 us
  starting transfers between devices  72.3 us (55%)
  waiting for transfers between devices  27 us (20%)
  Pallas kernels  26.6 us (20%)
  local copies, waits for them, and re-layouts  2.77 us (2%)
  between operations  2.47 us (2%)
    all_to_all x6, starting transfers between devices, exchanged(): return lax.all_to_all(blocks, axis, split_axis=0, concat_axis=0, tiled=True)  47.9 us
    all_to_all x6, waiting for transfers between devices, exchanged(): return lax.all_to_all(blocks, axis, split_axis=0, concat_axis=0, tiled=True)  27 us
    pallas_call x14, Pallas kernels, call(): pl.pallas_call(kernel, name=name, out_shape=shapes, in_specs=ins, out_spe...  26.6 us
    ppermute x8, starting transfers between devices, swapped(): return (lax.ppermute(one, 'dev', inner), lax.ppermute(two, 'dev', outer))  24.4 us
    unnamed x26, local copies, waits for them, and re-layouts  2.77 us
  transfers between devices with their start and end apart: 14, of which 5 were waited for; matrix products, arithmetic and copies ran while one was open for 0% of the time, Pallas kernels for 15%

profile of v12, /device:TPU:16, one launch (start us, length us, event | category | flops | bytes accessed | tf_op | source)
XLA Modules:
  0.0 131.1 jit_solution(7325194211992771067)
XLA Ops:
  1.9 2.7 %start.1 = (bf16[768,256]{1,0:T(8,128)(2,1)}, bf16[64,4,384]{2,1,0:T(4,128)(2,1)}, bf16[512,128]{1,0:T(8,128)(2,1)S(1)}) custom-call(f32[1]{0:T(128)} %bitcast.2.ridge, s32[1]{0:T(128)S(6)} %copy.14.cluster, s32[1,4]{1,0:T(1,128)} %far_in.1, f32[512,256]{1,0:T(8,128)} %refs_6_.1, f32[64,512]{1,0:T(8,128)} %bitcast.5, s32[1,512]{1,0:T(1,128)} %perm_in.1, ...), custom_call_target="tpu_custom_call" | custom-call | flops 10000000 | tf_op jit(solution)/shard_map/start/pallas_call | solution.py:37
  4.7 16.6 %all-to-all-start = ((bf16[64,4,384]{2,1,0:T(4,128)(2,1)}), bf16[64,4,384]{2,1,0:T(4,128)(2,1)S(1)}, u32[]{:S(2)}, u32[]{:S(2)}) async-start(bf16[64,4,384]{2,1,0:T(4,128)(2,1)} %get-tuple-element.19), calls=%async_computation | async-start | bytes 393216 | tf_op jit(solution)/shard_map/all_to_all | solution.py:326
  21.3 4.6 %collective-permute-start.1 = (bf16[768,256]{1,0:T(8,128)(2,1)S(1)}, bf16[768,256]{1,0:T(8,128)(2,1)S(1)}, u32[]{:S(2)}, u32[]{:S(2)}) collective-permute-start(bf16[768,256]{1,0:T(8,128)(2,1)S(1)} %copy-done.12), channel_id=1, source_target_pairs={{1,2},{2,1},{3,4},{4,3},{5,6},{6,5},{7,8},{8,7},{9,10},{10,9},{11,... | collective-permute-start | bytes 1179656 | tf_op jit(solution)/shard_map/ppermute | solution.py:322
  25.9 2.2 %collective-permute-start = (bf16[768,256]{1,0:T(8,128)(2,1)S(1)}, bf16[768,256]{1,0:T(8,128)(2,1)S(1)}, u32[]{:S(2)}, u32[]{:S(2)}) collective-permute-start(bf16[768,256]{1,0:T(8,128)(2,1)S(1)} %copy-done.12), channel_id=1, source_target_pairs={{0,1},{1,0},{2,3},{3,2},{4,5},{5,4},{6,7},{7,6},{8,9},{9,8},{10,11... | collective-permute-start | bytes 1179656 | tf_op jit(solution)/shard_map/ppermute | solution.py:322
  28.8 5.2 %all-to-all-done.arrived = bf16[64,4,384]{2,1,0:T(4,128)(2,1)S(1)} async-done(((bf16[64,4,384]{2,1,0:T(4,128)(2,1)}), bf16[64,4,384]{2,1,0:T(4,128)(2,1)S(1)}, u32[]{:S(2)}, u32[]{:S(2)}) %all-to-all-start) | async-done | bytes 196640 | tf_op jit(solution)/shard_map/all_to_all | solution.py:326
  34.9 4.3 %all-to-all-start.1 = ((bf16[8,16,128]{2,1,0:T(8,128)(2,1)}), bf16[8,16,128]{2,1,0:T(8,128)(2,1)S(1)}, u32[]{:S(2)}, u32[]{:S(2)}) async-start(bf16[8,16,128]{2,1,0:T(8,128)(2,1)} %get-tuple-element.20), calls=%async_computation.1 | async-start | bytes 65536 | tf_op jit(solution)/shard_map/all_to_all | solution.py:326
  39.8 2.6 %collective-permute-start.2 = (bf16[768,256]{1,0:T(8,128)(2,1)S(1)}, bf16[768,256]{1,0:T(8,128)(2,1)S(1)}, u32[]{:S(2)}, u32[]{:S(2)}) collective-permute-start(bf16[768,256]{1,0:T(8,128)(2,1)S(1)} %collective-permute-done.1.refs_5_.refs_6_), channel_id=1, source_target_pairs={{0,1},{1,0},{2,3},{3,2},{4,5},{5,4},{6,7},{7,6},{8,9},{9,8},{10,11... | collective-permute-start | bytes 1179656 | tf_op jit(solution)/shard_map/ppermute | solution.py:322
  42.5 3.0 %collective-permute-start.3 = (bf16[768,256]{1,0:T(8,128)(2,1)S(1)}, bf16[768,256]{1,0:T(8,128)(2,1)S(1)}, u32[]{:S(2)}, u32[]{:S(2)}) collective-permute-start(bf16[768,256]{1,0:T(8,128)(2,1)S(1)} %collective-permute-done.refs_3_.refs_4_), channel_id=1, source_target_pairs={{1,2},{2,1},{3,4},{4,3},{5,6},{6,5},{7,8},{8,7},{9,10},{10,9},{11,... | collective-permute-start | bytes 1179656 | tf_op jit(solution)/shard_map/ppermute | solution.py:322
  46.9 8.2 %all-to-all-start.2 = ((bf16[64,4,640]{2,1,0:T(4,128)(2,1)}), bf16[64,4,640]{2,1,0:T(4,128)(2,1)S(1)}, u32[]{:S(2)}, u32[]{:S(2)}) async-start(bf16[64,4,640]{2,1,0:T(4,128)(2,1)} %couple.2.refs_7_), calls=%async_computation.2 | async-start | bytes 655360 | tf_op jit(solution)/shard_map/all_to_all | solution.py:326
  55.2 2.7 %near_1.2.refs_3_.refs_9_ = f32[512,256]{1,0:T(8,128)S(1)} custom-call(s32[1,4]{1,0:T(1,128)S(1)} %copy-done.3, bf16[768,256]{1,0:T(8,128)(2,1)} %get-tuple-element.24.refs_1_.refs_2_, bf16[768,256]{1,0:T(8,128)(2,1)} %get-tuple-element.24.refs_1_.refs_2_, bf16[768,256]{1,0:T(8,128)(2,1)S(1)} %collective-permute-done.refs_3_.refs_4_, ...), custom_call_target="tpu_custom_call" | custom-call | flops 10000000000 | tf_op jit(solution)/shard_map/near_1/pallas_call | solution.py:37
  59.6 3.7 %near_2.2 = (f32[512,256]{1,0:T(8,128)S(1)}, f32[512,256]{1,0:T(8,128)S(1)}, f32[8,128]{1,0:T(8,128)S(1)}) custom-call(f32[1]{0:T(128)} %bitcast.3.refs_0_, s32[1,4]{1,0:T(1,128)S(1)} %copy-done.3, bf16[768,256]{1,0:T(8,128)(2,1)} %get-tuple-element.24.refs_1_.refs_2_, f32[512,256]{1,0:T(8,128)S(1)} %near_1.2.refs_3_.refs_9_, ...), custom_call_target="tpu_custom_call" | custom-call | flops 10000000000 | tf_op jit(solution)/shard_map/near_2/pallas_call | solution.py:37
  63.3 7.1 %all-to-all-done.2.arrived = bf16[64,4,640]{2,1,0:T(4,128)(2,1)S(1)} async-done(((bf16[64,4,640]{2,1,0:T(4,128)(2,1)}), bf16[64,4,640]{2,1,0:T(4,128)(2,1)S(1)}, u32[]{:S(2)}, u32[]{:S(2)}) %all-to-all-start.2) | async-done | bytes 327712 | tf_op jit(solution)/shard_map/all_to_all | solution.py:326
  70.4 2.8 %middle.1 = (bf16[512,256]{1,0:T(8,128)(2,1)}, bf16[64,4,256]{2,1,0:T(4,128)(2,1)}, f32[512,256]{1,0:T(8,128)S(1)}) custom-call(bf16[64,4,640]{2,1,0:T(4,128)(2,1)S(1)} %all-to-all-done.2.arrived, bf16[1,4,128,128]{3,2,1,0:T(8,128)(2,1)S(1)} %copy-done.1, bf16[1,128,128]{2,1,0:T(8,128)(2,1)S(1)} %copy-done.2, bf16[512,128]{1,0:T(8,128)(2,1)S(1)} %get-tuple-element.23.basis, ...), custom_call_target="tpu_custom_call" | custom-call | flops 10000000 | tf_op jit(solution)/shard_map/middle/pallas_call | solution.py:37
  73.2 2.9 %collective-permute-start.5 = (bf16[512,256]{1,0:T(8,128)(2,1)}, bf16[512,256]{1,0:T(8,128)(2,1)S(1)}, u32[]{:S(2)}, u32[]{:S(2)}) collective-permute-start(bf16[512,256]{1,0:T(8,128)(2,1)} %get-tuple-element.31.refs_2_), channel_id=1, source_target_pairs={{1,2},{2,1},{3,4},{4,3},{5,6},{6,5},{7,8},{8,7},{9,10},{10,9},{11,... | collective-permute-start | bytes 786440 | tf_op jit(solution)/shard_map/ppermute | solution.py:322
  76.2 6.6 %all-to-all-start.3 = ((bf16[64,4,256]{2,1,0:T(4,128)(2,1)}), bf16[64,4,256]{2,1,0:T(4,128)(2,1)S(1)}, u32[]{:S(2)}, u32[]{:S(2)}) async-start(bf16[64,4,256]{2,1,0:T(4,128)(2,1)} %get-tuple-element.28), calls=%async_computation.3 | async-start | bytes 262144 | tf_op jit(solution)/shard_map/all_to_all | solution.py:326
  82.8 3.4 %collective-permute-start.4 = (bf16[512,256]{1,0:T(8,128)(2,1)}, bf16[512,256]{1,0:T(8,128)(2,1)}, u32[]{:S(2)}, u32[]{:S(2)}) collective-permute-start(bf16[512,256]{1,0:T(8,128)(2,1)} %get-tuple-element.31.refs_2_), channel_id=1, source_target_pairs={{0,1},{1,0},{2,3},{3,2},{4,5},{5,4},{6,7},{7,6},{8,9},{9,8},{10,11... | collective-permute-start | bytes 786440 | tf_op jit(solution)/shard_map/ppermute | solution.py:322
  86.2 2.5 %collective-permute-start.6 = (bf16[512,256]{1,0:T(8,128)(2,1)S(1)}, bf16[512,256]{1,0:T(8,128)(2,1)}, u32[]{:S(2)}, u32[]{:S(2)}) collective-permute-start(bf16[512,256]{1,0:T(8,128)(2,1)S(1)} %collective-permute-done.5.refs_6_), channel_id=1, source_target_pairs={{0,1},{1,0},{2,3},{3,2},{4,5},{5,4},{6,7},{7,6},{8,9},{9,8},{10,11... | collective-permute-start | bytes 786440 | tf_op jit(solution)/shard_map/ppermute | solution.py:322
  88.7 5.3 %all-to-all-done.3.arrived = bf16[64,4,256]{2,1,0:T(4,128)(2,1)S(1)} async-done(((bf16[64,4,256]{2,1,0:T(4,128)(2,1)}), bf16[64,4,256]{2,1,0:T(4,128)(2,1)S(1)}, u32[]{:S(2)}, u32[]{:S(2)}) %all-to-all-start.3) | async-done | bytes 131104 | tf_op jit(solution)/shard_map/all_to_all | solution.py:326
  94.9 4.5 %all-to-all-start.4 = ((bf16[8,16,128]{2,1,0:T(8,128)(2,1)}), bf16[8,16,128]{2,1,0:T(8,128)(2,1)S(1)}, u32[]{:S(2)}, u32[]{:S(2)}) async-start(bf16[8,16,128]{2,1,0:T(8,128)(2,1)} %get-tuple-element.29), calls=%async_computation.4 | async-start | bytes 65536 | tf_op jit(solution)/shard_map/all_to_all | solution.py:326
  100.0 3.3 %collective-permute-start.7 = (bf16[512,256]{1,0:T(8,128)(2,1)}, bf16[512,256]{1,0:T(8,128)(2,1)S(1)}, u32[]{:S(2)}, u32[]{:S(2)}) collective-permute-start(bf16[512,256]{1,0:T(8,128)(2,1)} %collective-permute-done.4.refs_4_), channel_id=1, source_target_pairs={{1,2},{2,1},{3,4},{4,3},{5,6},{6,5},{7,8},{8,7},{9,10},{10,9},{11,... | collective-permute-start | bytes 786440 | tf_op jit(solution)/shard_map/ppermute | solution.py:322
  106.2 7.6 %all-to-all-start.5 = ((bf16[64,4,640]{2,1,0:T(4,128)(2,1)}), bf16[64,4,640]{2,1,0:T(4,128)(2,1)S(1)}, u32[]{:S(2)}, u32[]{:S(2)}) async-start(bf16[64,4,640]{2,1,0:T(4,128)(2,1)} %couple.3.refs_9_), calls=%async_computation.5 | async-start | bytes 655360 | tf_op jit(solution)/shard_map/all_to_all | solution.py:326
  114.9 3.5 %near_1.3.refs_3_ = f32[512,256]{1,0:T(8,128)S(1)} custom-call(s32[1,4]{1,0:T(1,128)S(1)} %copy-done.3, bf16[768,256]{1,0:T(8,128)(2,1)} %get-tuple-element.24.refs_1_.refs_2_, bf16[512,256]{1,0:T(8,128)(2,1)} %get-tuple-element.31.refs_2_, bf16[768,256]{1,0:T(8,128)(2,1)S(1)} %copy-done.7, bf16[512,256]{1,0:T(8,128)(2,1)} %collective-permute-done.4.refs_4_, ...), custom_call_target="tpu_custom_call" | custom-call | flops 10000000000 | tf_op jit(solution)/shard_map/near_1/pallas_call | solution.py:37
  118.4 2.9 %near_2.3 = (f32[512,256]{1,0:T(8,128)S(1)}, f32[512,256]{1,0:T(8,128)S(1)}, f32[8,128]{1,0:T(8,128)S(1)}) custom-call(f32[1]{0:T(128)} %bitcast.4.refs_0_, s32[1,4]{1,0:T(1,128)S(1)} %copy-done.3, bf16[768,256]{1,0:T(8,128)(2,1)} %get-tuple-element.24.refs_1_.refs_2_, f32[512,256]{1,0:T(8,128)S(1)} %near_1.3.refs_3_, ...), custom_call_target="tpu_custom_call" | custom-call | flops 10000000 | tf_op jit(solution)/shard_map/near_2/pallas_call | solution.py:37
  121.3 7.8 %all-to-all-done.5.arrived = bf16[64,4,640]{2,1,0:T(4,128)(2,1)S(1)} async-done(((bf16[64,4,640]{2,1,0:T(4,128)(2,1)}), bf16[64,4,640]{2,1,0:T(4,128)(2,1)S(1)}, u32[]{:S(2)}, u32[]{:S(2)}) %all-to-all-start.5) | async-done | bytes 327712 | tf_op jit(solution)/shard_map/all_to_all | solution.py:326
  (44 shorter events, 12.7 us)
Async XLA Ops:
  1.9 26.2 %copy-start.11 = (s32[4,4]{1,0:T(4,128)S(1)}, s32[4,4]{1,0:T(4,128)}, u32[]{:S(2)}) copy-start(s32[4,4]{1,0:T(4,128)} %far_clusters.1) | copy-start | bytes 196
  4.7 16.7 %copy-start.12 = (bf16[768,256]{1,0:T(8,128)(2,1)S(1)}, bf16[768,256]{1,0:T(8,128)(2,1)}, u32[]{:S(2)}) copy-start(bf16[768,256]{1,0:T(8,128)(2,1)} %get-tuple-element.24.refs_1_.refs_2_) | copy-start | bytes 1179652
  4.7 40.9 %copy-start = (bf16[4,4,128,128]{3,2,1,0:T(8,128)(2,1)S(1)}, bf16[4,4,128,128]{3,2,1,0:T(8,128)(2,1)}, u32[]{:S(2)}) copy-start(bf16[4,4,128,128]{3,2,1,0:T(8,128)(2,1)} %blocks.3) | copy-start | bytes 1572868
  4.7 29.3 %all-to-all-start = ((bf16[64,4,384]{2,1,0:T(4,128)(2,1)}), bf16[64,4,384]{2,1,0:T(4,128)(2,1)S(1)}, u32[]{:S(2)}, u32[]{:S(2)}) async-start(bf16[64,4,384]{2,1,0:T(4,128)(2,1)} %get-tuple-element.19), calls=%async_computation | async-start | bytes 393216 | tf_op jit(solution)/shard_map/all_to_all | solution.py:326
  21.3 18.5 %collective-permute-start.1 = (bf16[768,256]{1,0:T(8,128)(2,1)S(1)}, bf16[768,256]{1,0:T(8,128)(2,1)S(1)}, u32[]{:S(2)}, u32[]{:S(2)}) collective-permute-start(bf16[768,256]{1,0:T(8,128)(2,1)S(1)} %copy-done.12), channel_id=1, source_target_pairs={{1,2},{2,1},{3,4},{4,3},{5,6},{6,5},{7,8},{8,7},{9,10},{10,9},{11,... | collective-permute-start | bytes 1179656 | tf_op jit(solution)/shard_map/ppermute | solution.py:322
  25.9 16.5 %collective-permute-start = (bf16[768,256]{1,0:T(8,128)(2,1)S(1)}, bf16[768,256]{1,0:T(8,128)(2,1)S(1)}, u32[]{:S(2)}, u32[]{:S(2)}) collective-permute-start(bf16[768,256]{1,0:T(8,128)(2,1)S(1)} %copy-done.12), channel_id=1, source_target_pairs={{0,1},{1,0},{2,3},{3,2},{4,5},{5,4},{6,7},{7,6},{8,9},{9,8},{10,11... | collective-permute-start | bytes 1179656 | tf_op jit(solution)/shard_map/ppermute | solution.py:322
  34.9 10.6 %all-to-all-start.1 = ((bf16[8,16,128]{2,1,0:T(8,128)(2,1)}), bf16[8,16,128]{2,1,0:T(8,128)(2,1)S(1)}, u32[]{:S(2)}, u32[]{:S(2)}) async-start(bf16[8,16,128]{2,1,0:T(8,128)(2,1)} %get-tuple-element.20), calls=%async_computation.1 | async-start | bytes 65536 | tf_op jit(solution)/shard_map/all_to_all | solution.py:326
  39.8 15.3 %copy-start.4 = (bf16[768,256]{1,0:T(8,128)(2,1)}, bf16[768,256]{1,0:T(8,128)(2,1)S(1)}, u32[]{:S(2)}) copy-start(bf16[768,256]{1,0:T(8,128)(2,1)S(1)} %collective-permute-done.1.refs_5_.refs_6_) | copy-start | bytes 1179652
  39.8 18.0 %collective-permute-start.2 = (bf16[768,256]{1,0:T(8,128)(2,1)S(1)}, bf16[768,256]{1,0:T(8,128)(2,1)S(1)}, u32[]{:S(2)}, u32[]{:S(2)}) collective-permute-start(bf16[768,256]{1,0:T(8,128)(2,1)S(1)} %collective-permute-done.1.refs_5_.refs_6_), channel_id=1, source_target_pairs={{0,1},{1,0},{2,3},{3,2},{4,5},{5,4},{6,7},{7,6},{8,9},{9,8},{10,11... | collective-permute-start | bytes 1179656 | tf_op jit(solution)/shard_map/ppermute | solution.py:322
  42.4 12.7 %copy-start.6 = (bf16[768,256]{1,0:T(8,128)(2,1)}, bf16[768,256]{1,0:T(8,128)(2,1)S(1)}, u32[]{:S(2)}) copy-start(bf16[768,256]{1,0:T(8,128)(2,1)S(1)} %collective-permute-done.refs_3_.refs_4_) | copy-start | bytes 1179652
  42.5 16.1 %collective-permute-start.3 = (bf16[768,256]{1,0:T(8,128)(2,1)S(1)}, bf16[768,256]{1,0:T(8,128)(2,1)S(1)}, u32[]{:S(2)}, u32[]{:S(2)}) collective-permute-start(bf16[768,256]{1,0:T(8,128)(2,1)S(1)} %collective-permute-done.refs_3_.refs_4_), channel_id=1, source_target_pairs={{1,2},{2,1},{3,4},{4,3},{5,6},{6,5},{7,8},{8,7},{9,10},{10,9},{11,... | collective-permute-start | bytes 1179656 | tf_op jit(solution)/shard_map/ppermute | solution.py:322
  46.9 8.2 %copy-start.3 = (s32[1,4]{1,0:T(1,128)S(1)}, s32[1,4]{1,0:T(1,128)}, u32[]{:S(2)}) copy-start(s32[1,4]{1,0:T(1,128)} %refs_1_.3) | copy-start | bytes 52
  46.9 23.5 %all-to-all-start.2 = ((bf16[64,4,640]{2,1,0:T(4,128)(2,1)}), bf16[64,4,640]{2,1,0:T(4,128)(2,1)S(1)}, u32[]{:S(2)}, u32[]{:S(2)}) async-start(bf16[64,4,640]{2,1,0:T(4,128)(2,1)} %couple.2.refs_7_), calls=%async_computation.2 | async-start | bytes 655360 | tf_op jit(solution)/shard_map/all_to_all | solution.py:326
  59.6 10.8 %copy-start.1 = (bf16[1,4,128,128]{3,2,1,0:T(8,128)(2,1)S(1)}, bf16[1,4,128,128]{3,2,1,0:T(8,128)(2,1)}, u32[]{:S(2)}) copy-start(bf16[1,4,128,128]{3,2,1,0:T(8,128)(2,1)} %couplings.3) | copy-start | bytes 393220
  59.6 10.8 %copy-start.2 = (bf16[1,128,128]{2,1,0:T(8,128)(2,1)S(1)}, bf16[1,128,128]{2,1,0:T(8,128)(2,1)}, u32[]{:S(2)}) copy-start(bf16[1,128,128]{2,1,0:T(8,128)(2,1)} %transfer.3) | copy-start | bytes 98308
  73.2 13.0 %collective-permute-start.5 = (bf16[512,256]{1,0:T(8,128)(2,1)}, bf16[512,256]{1,0:T(8,128)(2,1)S(1)}, u32[]{:S(2)}, u32[]{:S(2)}) collective-permute-start(bf16[512,256]{1,0:T(8,128)(2,1)} %get-tuple-element.31.refs_2_), channel_id=1, source_target_pairs={{1,2},{2,1},{3,4},{4,3},{5,6},{6,5},{7,8},{8,7},{9,10},{10,9},{11,... | collective-permute-start | bytes 786440 | tf_op jit(solution)/shard_map/ppermute | solution.py:322
  76.2 17.8 %all-to-all-start.3 = ((bf16[64,4,256]{2,1,0:T(4,128)(2,1)}), bf16[64,4,256]{2,1,0:T(4,128)(2,1)S(1)}, u32[]{:S(2)}, u32[]{:S(2)}) async-start(bf16[64,4,256]{2,1,0:T(4,128)(2,1)} %get-tuple-element.28), calls=%async_computation.3 | async-start | bytes 262144 | tf_op jit(solution)/shard_map/all_to_all | solution.py:326
  82.8 17.2 %collective-permute-start.4 = (bf16[512,256]{1,0:T(8,128)(2,1)}, bf16[512,256]{1,0:T(8,128)(2,1)}, u32[]{:S(2)}, u32[]{:S(2)}) collective-permute-start(bf16[512,256]{1,0:T(8,128)(2,1)} %get-tuple-element.31.refs_2_), channel_id=1, source_target_pairs={{0,1},{1,0},{2,3},{3,2},{4,5},{5,4},{6,7},{7,6},{8,9},{9,8},{10,11... | collective-permute-start | bytes 786440 | tf_op jit(solution)/shard_map/ppermute | solution.py:322
  86.2 27.7 %collective-permute-start.6 = (bf16[512,256]{1,0:T(8,128)(2,1)S(1)}, bf16[512,256]{1,0:T(8,128)(2,1)}, u32[]{:S(2)}, u32[]{:S(2)}) collective-permute-start(bf16[512,256]{1,0:T(8,128)(2,1)S(1)} %collective-permute-done.5.refs_6_), channel_id=1, source_target_pairs={{0,1},{1,0},{2,3},{3,2},{4,5},{5,4},{6,7},{7,6},{8,9},{9,8},{10,11... | collective-permute-start | bytes 786440 | tf_op jit(solution)/shard_map/ppermute | solution.py:322
  94.9 10.0 %all-to-all-start.4 = ((bf16[8,16,128]{2,1,0:T(8,128)(2,1)}), bf16[8,16,128]{2,1,0:T(8,128)(2,1)S(1)}, u32[]{:S(2)}, u32[]{:S(2)}) async-start(bf16[8,16,128]{2,1,0:T(8,128)(2,1)} %get-tuple-element.29), calls=%async_computation.4 | async-start | bytes 65536 | tf_op jit(solution)/shard_map/all_to_all | solution.py:326
  100.0 18.4 %collective-permute-start.7 = (bf16[512,256]{1,0:T(8,128)(2,1)}, bf16[512,256]{1,0:T(8,128)(2,1)S(1)}, u32[]{:S(2)}, u32[]{:S(2)}) collective-permute-start(bf16[512,256]{1,0:T(8,128)(2,1)} %collective-permute-done.4.refs_4_), channel_id=1, source_target_pairs={{1,2},{2,1},{3,4},{4,3},{5,6},{6,5},{7,8},{8,7},{9,10},{10,9},{11,... | collective-permute-start | bytes 786440 | tf_op jit(solution)/shard_map/ppermute | solution.py:322
  104.8 9.0 %copy-start.7 = (bf16[768,256]{1,0:T(8,128)(2,1)S(1)}, bf16[768,256]{1,0:T(8,128)(2,1)}, u32[]{:S(2)}) copy-start(bf16[768,256]{1,0:T(8,128)(2,1)} %copy-done.6) | copy-start | bytes 1179652
  106.2 7.7 %copy-start.5 = (bf16[768,256]{1,0:T(8,128)(2,1)S(1)}, bf16[768,256]{1,0:T(8,128)(2,1)}, u32[]{:S(2)}) copy-start(bf16[768,256]{1,0:T(8,128)(2,1)} %copy-done.4) | copy-start | bytes 1179652
  106.2 22.9 %all-to-all-start.5 = ((bf16[64,4,640]{2,1,0:T(4,128)(2,1)}), bf16[64,4,640]{2,1,0:T(4,128)(2,1)S(1)}, u32[]{:S(2)}, u32[]{:S(2)}) async-start(bf16[64,4,640]{2,1,0:T(4,128)(2,1)} %couple.3.refs_9_), calls=%async_computation.5 | async-start | bytes 655360 | tf_op jit(solution)/shard_map/all_to_all | solution.py:326
  (3 other events, 2.7 us)

commit v13 on v12

--- a/solution.py
+++ b/solution.py
@@ -20,7 +20,7 @@
 ANY = pl.BlockSpec(memory_space=pl.ANY)
 HBM = pl.BlockSpec(memory_space=pltpu.HBM)
 LIMIT = 32 * 2**20
-SHORT, MID, LONG = 10**7, 10**10, 10**10
+SHORT = 10**7
 LATER, LAST = 10**10, 10**7
 ROWS = 128
 
@@ -447,8 +447,8 @@
     )
     sent, arrived = through_owners(sums, skeletons)
     first2 = swapped(*first1[::-1])
-    near = near_1((1, -1), wc, first1, first1, sent, MID)
-    residual, direction, factor = near_2((2, -2), False, near, first2, first2, near, LONG)
+    near = near_1((1, -1, 2), wc, (*first1, first2[0]), (*first1, first2[0]), sent, LATER)
+    residual, direction, factor = near_2((-2,), False, near, first2[1:], first2[1:], near, LAST)
     w, sent, r1 = call(
         middle_kernel,
         "middle",

time: 132 us -> 132 us (level)
  waiting for transfers between devices: 27 us -> 31.2 us
  starting transfers between devices: 72.3 us -> 70.2 us
  local copies, waits for them, and re-layouts: 2.77 us -> 1.05 us
    all_to_all x6, starting transfers between devices: 47.9 us -> 38.1 us  [exchanged(): return lax.all_to_all(blocks, axis, split_axis=0, concat_axis=0, tiled=True)]
    ppermute x8, starting transfers between devices: 24.4 us -> 32.1 us  [swapped(): return (lax.ppermute(one, 'dev', inner), lax.ppermute(two, 'dev', outer))]
    all_to_all x6, waiting for transfers between devices: 27 us -> 31.2 us  [exchanged(): return lax.all_to_all(blocks, axis, split_axis=0, concat_axis=0, tiled=True)]
    unnamed x26 -> x24, local copies, waits for them, and re-layouts: 2.77 us -> 1.05 us
  transfers between devices with their start and end apart: 14 -> 14, of which waited for: 5 -> 6; matrix products, arithmetic and copies ran while one was open for 0% -> 0% of each run, Pallas kernels for 15% -> 14%
where the time goes in v13:
time: 132 us; the launch traced here: 131 us
  starting transfers between devices  70.2 us (53%)
  waiting for transfers between devices  31.2 us (24%)
  Pallas kernels  25.9 us (20%)
  between operations  2.49 us (2%)
    all_to_all x6, starting transfers between devices, exchanged(): return lax.all_to_all(blocks, axis, split_axis=0, concat_axis=0, tiled=True)  38.1 us
    ppermute x8, starting transfers between devices, swapped(): return (lax.ppermute(one, 'dev', inner), lax.ppermute(two, 'dev', outer))  32.1 us
    all_to_all x6, waiting for transfers between devices, exchanged(): return lax.all_to_all(blocks, axis, split_axis=0, concat_axis=0, tiled=True)  31.2 us
    pallas_call x14, Pallas kernels, call(): pl.pallas_call(kernel, name=name, out_shape=shapes, in_specs=ins, out_spe...  25.9 us
  transfers between devices with their start and end apart: 14, of which 6 were waited for; matrix products, arithmetic and copies ran while one was open for 0% of the time, Pallas kernels for 14%

profile of v13, /device:TPU:16, one launch (start us, length us, event | category | flops | bytes accessed | tf_op | source)
XLA Modules:
  0.0 130.9 jit_solution(14576334439496436975)
XLA Ops:
  1.9 2.7 %start.1 = (bf16[768,256]{1,0:T(8,128)(2,1)}, bf16[64,4,384]{2,1,0:T(4,128)(2,1)}, bf16[512,128]{1,0:T(8,128)(2,1)S(1)}) custom-call(f32[1]{0:T(128)} %bitcast.2.ridge, s32[1]{0:T(128)S(6)} %copy.14.cluster, s32[1,4]{1,0:T(1,128)} %far_in.1, f32[512,256]{1,0:T(8,128)} %refs_6_.3, f32[64,512]{1,0:T(8,128)} %bitcast.5, s32[1,512]{1,0:T(1,128)} %perm_in.1, ...), custom_call_target="tpu_custom_call" | custom-call | flops 10000000 | tf_op jit(solution)/shard_map/start/pallas_call | solution.py:37
  4.7 11.0 %collective-permute-start.1 = (bf16[768,256]{1,0:T(8,128)(2,1)}, bf16[768,256]{1,0:T(8,128)(2,1)S(1)}, u32[]{:S(2)}, u32[]{:S(2)}) collective-permute-start(bf16[768,256]{1,0:T(8,128)(2,1)} %get-tuple-element.24.refs_1_.refs_2_), channel_id=1, source_target_pairs={{1,2},{2,1},{3,4},{4,3},{5,6},{6,5},{7,8},{8,7},{9,10},{10,9},{11,... | collective-permute-start | bytes 1179656 | tf_op jit(solution)/shard_map/ppermute | solution.py:322
  15.7 9.1 %all-to-all-start = ((bf16[64,4,384]{2,1,0:T(4,128)(2,1)}), bf16[64,4,384]{2,1,0:T(4,128)(2,1)S(1)}, u32[]{:S(2)}, u32[]{:S(2)}) async-start(bf16[64,4,384]{2,1,0:T(4,128)(2,1)} %get-tuple-element.19), calls=%async_computation | async-start | bytes 393216 | tf_op jit(solution)/shard_map/all_to_all | solution.py:326
  24.8 3.4 %collective-permute-start = (bf16[768,256]{1,0:T(8,128)(2,1)S(1)}, bf16[768,256]{1,0:T(8,128)(2,1)S(1)}, u32[]{:S(2)}, u32[]{:S(2)}) collective-permute-start(bf16[768,256]{1,0:T(8,128)(2,1)S(1)} %copy-done.11), channel_id=1, source_target_pairs={{0,1},{1,0},{2,3},{3,2},{4,5},{5,4},{6,7},{7,6},{8,9},{9,8},{10,11... | collective-permute-start | bytes 1179656 | tf_op jit(solution)/shard_map/ppermute | solution.py:322
  28.2 2.5 %collective-permute-start.2 = (bf16[768,256]{1,0:T(8,128)(2,1)S(1)}, bf16[768,256]{1,0:T(8,128)(2,1)S(1)}, u32[]{:S(2)}, u32[]{:S(2)}) collective-permute-start(bf16[768,256]{1,0:T(8,128)(2,1)S(1)} %collective-permute-done.1.refs_5_.refs_6_), channel_id=1, source_target_pairs={{0,1},{1,0},{2,3},{3,2},{4,5},{5,4},{6,7},{7,6},{8,9},{9,8},{10,11... | collective-permute-start | bytes 1179656 | tf_op jit(solution)/shard_map/ppermute | solution.py:322
  31.4 5.7 %all-to-all-done.arrived = bf16[64,4,384]{2,1,0:T(4,128)(2,1)S(1)} async-done(((bf16[64,4,384]{2,1,0:T(4,128)(2,1)}), bf16[64,4,384]{2,1,0:T(4,128)(2,1)S(1)}, u32[]{:S(2)}, u32[]{:S(2)}) %all-to-all-start) | async-done | bytes 196640 | tf_op jit(solution)/shard_map/all_to_all | solution.py:326
  38.1 4.3 %all-to-all-start.1 = ((bf16[8,16,128]{2,1,0:T(8,128)(2,1)}), bf16[8,16,128]{2,1,0:T(8,128)(2,1)S(1)}, u32[]{:S(2)}, u32[]{:S(2)}) async-start(bf16[8,16,128]{2,1,0:T(8,128)(2,1)} %get-tuple-element.20), calls=%async_computation.1 | async-start | bytes 65536 | tf_op jit(solution)/shard_map/all_to_all | solution.py:326
  42.9 3.2 %collective-permute-start.3 = (bf16[768,256]{1,0:T(8,128)(2,1)S(1)}, bf16[768,256]{1,0:T(8,128)(2,1)S(1)}, u32[]{:S(2)}, u32[]{:S(2)}) collective-permute-start(bf16[768,256]{1,0:T(8,128)(2,1)S(1)} %collective-permute-done.refs_3_.refs_4_), channel_id=1, source_target_pairs={{1,2},{2,1},{3,4},{4,3},{5,6},{6,5},{7,8},{8,7},{9,10},{10,9},{11,... | collective-permute-start | bytes 1179656 | tf_op jit(solution)/shard_map/ppermute | solution.py:322
  49.2 7.0 %all-to-all-start.2 = ((bf16[64,4,640]{2,1,0:T(4,128)(2,1)}), bf16[64,4,640]{2,1,0:T(4,128)(2,1)S(1)}, u32[]{:S(2)}, u32[]{:S(2)}) async-start(bf16[64,4,640]{2,1,0:T(4,128)(2,1)} %couple.2.refs_9_), calls=%async_computation.2 | async-start | bytes 655360 | tf_op jit(solution)/shard_map/all_to_all | solution.py:326
  56.3 4.0 %near_1.2.refs_3_.refs_7_ = f32[512,256]{1,0:T(8,128)S(1)} custom-call(s32[1,4]{1,0:T(1,128)S(1)} %copy-done.3, bf16[768,256]{1,0:T(8,128)(2,1)} %get-tuple-element.24.refs_1_.refs_2_, bf16[768,256]{1,0:T(8,128)(2,1)} %get-tuple-element.24.refs_1_.refs_2_, bf16[768,256]{1,0:T(8,128)(2,1)S(1)} %collective-permute-done.refs_3_.refs_4_, ...), custom_call_target="tpu_custom_call" | custom-call | flops 10000000000 | tf_op jit(solution)/shard_map/near_1/pallas_call | solution.py:37
  60.3 2.1 %near_2.2 = (f32[512,256]{1,0:T(8,128)S(1)}, f32[512,256]{1,0:T(8,128)S(1)}, f32[8,128]{1,0:T(8,128)S(1)}) custom-call(f32[1]{0:T(128)} %bitcast.3.refs_0_, s32[1,4]{1,0:T(1,128)S(1)} %copy-done.3, bf16[768,256]{1,0:T(8,128)(2,1)} %get-tuple-element.24.refs_1_.refs_2_, f32[512,256]{1,0:T(8,128)S(1)} %near_1.2.refs_3_.refs_7_, ...), custom_call_target="tpu_custom_call" | custom-call | flops 10000000 | tf_op jit(solution)/shard_map/near_2/pallas_call | solution.py:37
  62.4 9.1 %all-to-all-done.2.arrived = bf16[64,4,640]{2,1,0:T(4,128)(2,1)S(1)} async-done(((bf16[64,4,640]{2,1,0:T(4,128)(2,1)}), bf16[64,4,640]{2,1,0:T(4,128)(2,1)S(1)}, u32[]{:S(2)}, u32[]{:S(2)}) %all-to-all-start.2) | async-done | bytes 327712 | tf_op jit(solution)/shard_map/all_to_all | solution.py:326
  71.5 2.7 %middle.1 = (bf16[512,256]{1,0:T(8,128)(2,1)}, bf16[64,4,256]{2,1,0:T(4,128)(2,1)}, f32[512,256]{1,0:T(8,128)S(1)}) custom-call(bf16[64,4,640]{2,1,0:T(4,128)(2,1)S(1)} %all-to-all-done.2.arrived, bf16[1,4,128,128]{3,2,1,0:T(8,128)(2,1)S(1)} %copy-done.1, bf16[1,128,128]{2,1,0:T(8,128)(2,1)S(1)} %copy-done.2, bf16[512,128]{1,0:T(8,128)(2,1)S(1)} %get-tuple-element.23.basis, ...), custom_call_target="tpu_custom_call" | custom-call | flops 10000000 | tf_op jit(solution)/shard_map/middle/pallas_call | solution.py:37
  74.2 2.9 %collective-permute-start.5 = (bf16[512,256]{1,0:T(8,128)(2,1)}, bf16[512,256]{1,0:T(8,128)(2,1)S(1)}, u32[]{:S(2)}, u32[]{:S(2)}) collective-permute-start(bf16[512,256]{1,0:T(8,128)(2,1)} %get-tuple-element.31.refs_2_), channel_id=1, source_target_pairs={{1,2},{2,1},{3,4},{4,3},{5,6},{6,5},{7,8},{8,7},{9,10},{10,9},{11,... | collective-permute-start | bytes 786440 | tf_op jit(solution)/shard_map/ppermute | solution.py:322
  77.2 6.7 %all-to-all-start.3 = ((bf16[64,4,256]{2,1,0:T(4,128)(2,1)}), bf16[64,4,256]{2,1,0:T(4,128)(2,1)S(1)}, u32[]{:S(2)}, u32[]{:S(2)}) async-start(bf16[64,4,256]{2,1,0:T(4,128)(2,1)} %get-tuple-element.28), calls=%async_computation.3 | async-start | bytes 262144 | tf_op jit(solution)/shard_map/all_to_all | solution.py:326
  83.9 3.4 %collective-permute-start.4 = (bf16[512,256]{1,0:T(8,128)(2,1)}, bf16[512,256]{1,0:T(8,128)(2,1)}, u32[]{:S(2)}, u32[]{:S(2)}) collective-permute-start(bf16[512,256]{1,0:T(8,128)(2,1)} %get-tuple-element.31.refs_2_), channel_id=1, source_target_pairs={{0,1},{1,0},{2,3},{3,2},{4,5},{5,4},{6,7},{7,6},{8,9},{9,8},{10,11... | collective-permute-start | bytes 786440 | tf_op jit(solution)/shard_map/ppermute | solution.py:322
  87.3 2.5 %collective-permute-start.6 = (bf16[512,256]{1,0:T(8,128)(2,1)S(1)}, bf16[512,256]{1,0:T(8,128)(2,1)}, u32[]{:S(2)}, u32[]{:S(2)}) collective-permute-start(bf16[512,256]{1,0:T(8,128)(2,1)S(1)} %collective-permute-done.5.refs_6_), channel_id=1, source_target_pairs={{0,1},{1,0},{2,3},{3,2},{4,5},{5,4},{6,7},{7,6},{8,9},{9,8},{10,11... | collective-permute-start | bytes 786440 | tf_op jit(solution)/shard_map/ppermute | solution.py:322
  89.8 5.3 %all-to-all-done.3.arrived = bf16[64,4,256]{2,1,0:T(4,128)(2,1)S(1)} async-done(((bf16[64,4,256]{2,1,0:T(4,128)(2,1)}), bf16[64,4,256]{2,1,0:T(4,128)(2,1)S(1)}, u32[]{:S(2)}, u32[]{:S(2)}) %all-to-all-start.3) | async-done | bytes 131104 | tf_op jit(solution)/shard_map/all_to_all | solution.py:326
  96.0 3.3 %all-to-all-start.4 = ((bf16[8,16,128]{2,1,0:T(8,128)(2,1)}), bf16[8,16,128]{2,1,0:T(8,128)(2,1)S(1)}, u32[]{:S(2)}, u32[]{:S(2)}) async-start(bf16[8,16,128]{2,1,0:T(8,128)(2,1)} %get-tuple-element.29), calls=%async_computation.4 | async-start | bytes 65536 | tf_op jit(solution)/shard_map/all_to_all | solution.py:326
  99.9 3.3 %collective-permute-start.7 = (bf16[512,256]{1,0:T(8,128)(2,1)}, bf16[512,256]{1,0:T(8,128)(2,1)S(1)}, u32[]{:S(2)}, u32[]{:S(2)}) collective-permute-start(bf16[512,256]{1,0:T(8,128)(2,1)} %collective-permute-done.4.refs_4_), channel_id=1, source_target_pairs={{1,2},{2,1},{3,4},{4,3},{5,6},{6,5},{7,8},{8,7},{9,10},{10,9},{11,... | collective-permute-start | bytes 786440 | tf_op jit(solution)/shard_map/ppermute | solution.py:322
  106.0 7.6 %all-to-all-start.5 = ((bf16[64,4,640]{2,1,0:T(4,128)(2,1)}), bf16[64,4,640]{2,1,0:T(4,128)(2,1)S(1)}, u32[]{:S(2)}, u32[]{:S(2)}) async-start(bf16[64,4,640]{2,1,0:T(4,128)(2,1)} %couple.3.refs_9_), calls=%async_computation.5 | async-start | bytes 655360 | tf_op jit(solution)/shard_map/all_to_all | solution.py:326
  114.7 4.1 %near_1.3.refs_3_ = f32[512,256]{1,0:T(8,128)S(1)} custom-call(s32[1,4]{1,0:T(1,128)S(1)} %copy-done.3, bf16[768,256]{1,0:T(8,128)(2,1)} %get-tuple-element.24.refs_1_.refs_2_, bf16[512,256]{1,0:T(8,128)(2,1)} %get-tuple-element.31.refs_2_, bf16[768,256]{1,0:T(8,128)(2,1)S(1)} %copy-done.7, bf16[512,256]{1,0:T(8,128)(2,1)} %collective-permute-done.4.refs_4_, ...), custom_call_target="tpu_custom_call" | custom-call | flops 10000000000 | tf_op jit(solution)/shard_map/near_1/pallas_call | solution.py:37
  118.7 2.2 %near_2.3 = (f32[512,256]{1,0:T(8,128)S(1)}, f32[512,256]{1,0:T(8,128)S(1)}, f32[8,128]{1,0:T(8,128)S(1)}) custom-call(f32[1]{0:T(128)} %bitcast.4.refs_0_, s32[1,4]{1,0:T(1,128)S(1)} %copy-done.3, bf16[768,256]{1,0:T(8,128)(2,1)} %get-tuple-element.24.refs_1_.refs_2_, f32[512,256]{1,0:T(8,128)S(1)} %near_1.3.refs_3_, ...), custom_call_target="tpu_custom_call" | custom-call | flops 10000000 | tf_op jit(solution)/shard_map/near_2/pallas_call | solution.py:37
  120.9 8.0 %all-to-all-done.5.arrived = bf16[64,4,640]{2,1,0:T(4,128)(2,1)S(1)} async-done(((bf16[64,4,640]{2,1,0:T(4,128)(2,1)}), bf16[64,4,640]{2,1,0:T(4,128)(2,1)S(1)}, u32[]{:S(2)}, u32[]{:S(2)}) %all-to-all-start.5) | async-done | bytes 327712 | tf_op jit(solution)/shard_map/all_to_all | solution.py:326
  (42 shorter events, 12.4 us)
Async XLA Ops:
  1.9 28.8 %copy-start.10 = (s32[4,4]{1,0:T(4,128)S(1)}, s32[4,4]{1,0:T(4,128)}, u32[]{:S(2)}) copy-start(s32[4,4]{1,0:T(4,128)} %far_clusters.1) | copy-start | bytes 196
  4.7 20.2 %copy-start.11 = (bf16[768,256]{1,0:T(8,128)(2,1)S(1)}, bf16[768,256]{1,0:T(8,128)(2,1)}, u32[]{:S(2)}) copy-start(bf16[768,256]{1,0:T(8,128)(2,1)} %get-tuple-element.24.refs_1_.refs_2_) | copy-start | bytes 1179652
  4.7 23.5 %collective-permute-start.1 = (bf16[768,256]{1,0:T(8,128)(2,1)}, bf16[768,256]{1,0:T(8,128)(2,1)S(1)}, u32[]{:S(2)}, u32[]{:S(2)}) collective-permute-start(bf16[768,256]{1,0:T(8,128)(2,1)} %get-tuple-element.24.refs_1_.refs_2_), channel_id=1, source_target_pairs={{1,2},{2,1},{3,4},{4,3},{5,6},{6,5},{7,8},{8,7},{9,10},{10,9},{11,... | collective-permute-start | bytes 1179656 | tf_op jit(solution)/shard_map/ppermute | solution.py:322
  15.6 32.2 %copy-start = (bf16[4,4,128,128]{3,2,1,0:T(8,128)(2,1)S(1)}, bf16[4,4,128,128]{3,2,1,0:T(8,128)(2,1)}, u32[]{:S(2)}) copy-start(bf16[4,4,128,128]{3,2,1,0:T(8,128)(2,1)} %blocks.3) | copy-start | bytes 1572868
  15.7 21.4 %all-to-all-start = ((bf16[64,4,384]{2,1,0:T(4,128)(2,1)}), bf16[64,4,384]{2,1,0:T(4,128)(2,1)S(1)}, u32[]{:S(2)}, u32[]{:S(2)}) async-start(bf16[64,4,384]{2,1,0:T(4,128)(2,1)} %get-tuple-element.19), calls=%async_computation | async-start | bytes 393216 | tf_op jit(solution)/shard_map/all_to_all | solution.py:326
  24.8 18.1 %collective-permute-start = (bf16[768,256]{1,0:T(8,128)(2,1)S(1)}, bf16[768,256]{1,0:T(8,128)(2,1)S(1)}, u32[]{:S(2)}, u32[]{:S(2)}) collective-permute-start(bf16[768,256]{1,0:T(8,128)(2,1)S(1)} %copy-done.11), channel_id=1, source_target_pairs={{0,1},{1,0},{2,3},{3,2},{4,5},{5,4},{6,7},{7,6},{8,9},{9,8},{10,11... | collective-permute-start | bytes 1179656 | tf_op jit(solution)/shard_map/ppermute | solution.py:322
  28.2 28.0 %copy-start.4 = (bf16[768,256]{1,0:T(8,128)(2,1)}, bf16[768,256]{1,0:T(8,128)(2,1)S(1)}, u32[]{:S(2)}) copy-start(bf16[768,256]{1,0:T(8,128)(2,1)S(1)} %collective-permute-done.1.refs_5_.refs_6_) | copy-start | bytes 1179652
  28.2 28.0 %collective-permute-start.2 = (bf16[768,256]{1,0:T(8,128)(2,1)S(1)}, bf16[768,256]{1,0:T(8,128)(2,1)S(1)}, u32[]{:S(2)}, u32[]{:S(2)}) collective-permute-start(bf16[768,256]{1,0:T(8,128)(2,1)S(1)} %collective-permute-done.1.refs_5_.refs_6_), channel_id=1, source_target_pairs={{0,1},{1,0},{2,3},{3,2},{4,5},{5,4},{6,7},{7,6},{8,9},{9,8},{10,11... | collective-permute-start | bytes 1179656 | tf_op jit(solution)/shard_map/ppermute | solution.py:322
  38.1 9.7 %all-to-all-start.1 = ((bf16[8,16,128]{2,1,0:T(8,128)(2,1)}), bf16[8,16,128]{2,1,0:T(8,128)(2,1)S(1)}, u32[]{:S(2)}, u32[]{:S(2)}) async-start(bf16[8,16,128]{2,1,0:T(8,128)(2,1)} %get-tuple-element.20), calls=%async_computation.1 | async-start | bytes 65536 | tf_op jit(solution)/shard_map/all_to_all | solution.py:326
  42.9 13.3 %copy-start.6 = (bf16[768,256]{1,0:T(8,128)(2,1)}, bf16[768,256]{1,0:T(8,128)(2,1)S(1)}, u32[]{:S(2)}) copy-start(bf16[768,256]{1,0:T(8,128)(2,1)S(1)} %collective-permute-done.refs_3_.refs_4_) | copy-start | bytes 1179652
  42.9 17.3 %collective-permute-start.3 = (bf16[768,256]{1,0:T(8,128)(2,1)S(1)}, bf16[768,256]{1,0:T(8,128)(2,1)S(1)}, u32[]{:S(2)}, u32[]{:S(2)}) collective-permute-start(bf16[768,256]{1,0:T(8,128)(2,1)S(1)} %collective-permute-done.refs_3_.refs_4_), channel_id=1, source_target_pairs={{1,2},{2,1},{3,4},{4,3},{5,6},{6,5},{7,8},{8,7},{9,10},{10,9},{11,... | collective-permute-start | bytes 1179656 | tf_op jit(solution)/shard_map/ppermute | solution.py:322
  49.2 7.1 %copy-start.3 = (s32[1,4]{1,0:T(1,128)S(1)}, s32[1,4]{1,0:T(1,128)}, u32[]{:S(2)}) copy-start(s32[1,4]{1,0:T(1,128)} %refs_1_.3) | copy-start | bytes 52
  49.2 22.3 %all-to-all-start.2 = ((bf16[64,4,640]{2,1,0:T(4,128)(2,1)}), bf16[64,4,640]{2,1,0:T(4,128)(2,1)S(1)}, u32[]{:S(2)}, u32[]{:S(2)}) async-start(bf16[64,4,640]{2,1,0:T(4,128)(2,1)} %couple.2.refs_9_), calls=%async_computation.2 | async-start | bytes 655360 | tf_op jit(solution)/shard_map/all_to_all | solution.py:326
  60.3 11.2 %copy-start.1 = (bf16[1,4,128,128]{3,2,1,0:T(8,128)(2,1)S(1)}, bf16[1,4,128,128]{3,2,1,0:T(8,128)(2,1)}, u32[]{:S(2)}) copy-start(bf16[1,4,128,128]{3,2,1,0:T(8,128)(2,1)} %couplings.3) | copy-start | bytes 393220
  60.3 11.2 %copy-start.2 = (bf16[1,128,128]{2,1,0:T(8,128)(2,1)S(1)}, bf16[1,128,128]{2,1,0:T(8,128)(2,1)}, u32[]{:S(2)}) copy-start(bf16[1,128,128]{2,1,0:T(8,128)(2,1)} %transfer.3) | copy-start | bytes 98308
  74.2 13.1 %collective-permute-start.5 = (bf16[512,256]{1,0:T(8,128)(2,1)}, bf16[512,256]{1,0:T(8,128)(2,1)S(1)}, u32[]{:S(2)}, u32[]{:S(2)}) collective-permute-start(bf16[512,256]{1,0:T(8,128)(2,1)} %get-tuple-element.31.refs_2_), channel_id=1, source_target_pairs={{1,2},{2,1},{3,4},{4,3},{5,6},{6,5},{7,8},{8,7},{9,10},{10,9},{11,... | collective-permute-start | bytes 786440 | tf_op jit(solution)/shard_map/ppermute | solution.py:322
  77.2 17.9 %all-to-all-start.3 = ((bf16[64,4,256]{2,1,0:T(4,128)(2,1)}), bf16[64,4,256]{2,1,0:T(4,128)(2,1)S(1)}, u32[]{:S(2)}, u32[]{:S(2)}) async-start(bf16[64,4,256]{2,1,0:T(4,128)(2,1)} %get-tuple-element.28), calls=%async_computation.3 | async-start | bytes 262144 | tf_op jit(solution)/shard_map/all_to_all | solution.py:326
  83.9 16.0 %collective-permute-start.4 = (bf16[512,256]{1,0:T(8,128)(2,1)}, bf16[512,256]{1,0:T(8,128)(2,1)}, u32[]{:S(2)}, u32[]{:S(2)}) collective-permute-start(bf16[512,256]{1,0:T(8,128)(2,1)} %get-tuple-element.31.refs_2_), channel_id=1, source_target_pairs={{0,1},{1,0},{2,3},{3,2},{4,5},{5,4},{6,7},{7,6},{8,9},{9,8},{10,11... | collective-permute-start | bytes 786440 | tf_op jit(solution)/shard_map/ppermute | solution.py:322
  87.3 26.4 %collective-permute-start.6 = (bf16[512,256]{1,0:T(8,128)(2,1)S(1)}, bf16[512,256]{1,0:T(8,128)(2,1)}, u32[]{:S(2)}, u32[]{:S(2)}) collective-permute-start(bf16[512,256]{1,0:T(8,128)(2,1)S(1)} %collective-permute-done.5.refs_6_), channel_id=1, source_target_pairs={{0,1},{1,0},{2,3},{3,2},{4,5},{5,4},{6,7},{7,6},{8,9},{9,8},{10,11... | collective-permute-start | bytes 786440 | tf_op jit(solution)/shard_map/ppermute | solution.py:322
  96.0 8.7 %all-to-all-start.4 = ((bf16[8,16,128]{2,1,0:T(8,128)(2,1)}), bf16[8,16,128]{2,1,0:T(8,128)(2,1)S(1)}, u32[]{:S(2)}, u32[]{:S(2)}) async-start(bf16[8,16,128]{2,1,0:T(8,128)(2,1)} %get-tuple-element.29), calls=%async_computation.4 | async-start | bytes 65536 | tf_op jit(solution)/shard_map/all_to_all | solution.py:326
  99.9 18.9 %collective-permute-start.7 = (bf16[512,256]{1,0:T(8,128)(2,1)}, bf16[512,256]{1,0:T(8,128)(2,1)S(1)}, u32[]{:S(2)}, u32[]{:S(2)}) collective-permute-start(bf16[512,256]{1,0:T(8,128)(2,1)} %collective-permute-done.4.refs_4_), channel_id=1, source_target_pairs={{1,2},{2,1},{3,4},{4,3},{5,6},{6,5},{7,8},{8,7},{9,10},{10,9},{11,... | collective-permute-start | bytes 786440 | tf_op jit(solution)/shard_map/ppermute | solution.py:322
  104.7 9.0 %copy-start.7 = (bf16[768,256]{1,0:T(8,128)(2,1)S(1)}, bf16[768,256]{1,0:T(8,128)(2,1)}, u32[]{:S(2)}) copy-start(bf16[768,256]{1,0:T(8,128)(2,1)} %copy-done.6) | copy-start | bytes 1179652
  106.0 7.6 %copy-start.5 = (bf16[768,256]{1,0:T(8,128)(2,1)S(1)}, bf16[768,256]{1,0:T(8,128)(2,1)}, u32[]{:S(2)}) copy-start(bf16[768,256]{1,0:T(8,128)(2,1)} %copy-done.4) | copy-start | bytes 1179652
  106.0 22.8 %all-to-all-start.5 = ((bf16[64,4,640]{2,1,0:T(4,128)(2,1)}), bf16[64,4,640]{2,1,0:T(4,128)(2,1)S(1)}, u32[]{:S(2)}, u32[]{:S(2)}) async-start(bf16[64,4,640]{2,1,0:T(4,128)(2,1)} %couple.3.refs_9_), calls=%async_computation.5 | async-start | bytes 655360 | tf_op jit(solution)/shard_map/all_to_all | solution.py:326
  (2 other events, 5.0 us)
